TPU v7x, 32 devices: a whole 2x2x4 slice. The times are simulated.
32 devices in a mesh: groups: 2 (over x), expert: 16 (over z, y, core).
Axes of the slice: x: 2, y: 2, z: 4, core: 2. Of those that a mesh axis runs over, the one named last changes fastest.
Arguments:
- prefill_tokens: bfloat16 [1024, 7168], P(('groups', 'expert')), parts along dimension 0, may hold values from -6 to 6
- prefill_experts: int32 [1024, 8], P(('groups', 'expert')), parts along dimension 0, may hold values from 0 to 7, as said below
- prefill_gates: int32 [1024, 8], P(('groups', 'expert')), parts along dimension 0, may hold values from 2048 to 65536
- decode_rows: bfloat16 [1024, 7168], P(('groups', 'expert')), parts along dimension 0, may hold values from -6 to 6
- decode_experts: int32 [1024, 8], P(('groups', 'expert')), parts along dimension 0, may hold values from 0 to 7, as said below
- decode_gates: int32 [1024, 8], P(('groups', 'expert')), parts along dimension 0, may hold values from 2048 to 65536
- w_gate_up: bfloat16 [16, 7168, 1024], P('expert'), may hold values from -0.0625 to 0.0625
- w_down: bfloat16 [16, 512, 7168], P('expert'), may hold values from -0.1875 to 0.1875
- queries: bfloat16 [1024, 64, 576], P(('groups', 'expert')), parts along dimension 0, may hold values from -21 to 21
- own_latent: bfloat16 [1024, 576], P(('groups', 'expert')), parts along dimension 0, may hold values from -6 to 6
- latents: bfloat16 [512, 64, 576], P(('groups', 'expert')), parts along dimension 0, may hold values from -6 to 6
- span_owner: int32 [512], P(('groups', 'expert')), parts along dimension 0, may hold values from 0 to 15, as said below
- span_request: int32 [512], P(('groups', 'expert')), parts along dimension 0, may hold values from 0 to 31
- span_length: int32 [512], P(('groups', 'expert')), parts along dimension 0, may hold values from 1 to 64
Outputs:
- prefill_out: bfloat16 [1024, 7168], P(('groups', 'expert')), parts along dimension 0
- decode_out: bfloat16 [1024, 7168], P(('groups', 'expert')), parts along dimension 0
- context: bfloat16 [1024, 64, 512], P(('groups', 'expert')), parts along dimension 0
There are 2 independent parts, one for each index of `groups`. A program takes and returns all parts, laid end to end along the dimension named above; an argument that names none is the same for every part. Nothing has to cross between parts.
Inputs may be any that keep to these rules, and one draw needn't show every extreme that they name: `prefill_experts`: the 8 experts of a row differ. One expert, drawn from the seed and the same for the decode rows, is named by every row; among the rows of one device no expert is named more than 32 times, and the other experts share the remaining picks of that device evenly. `decode_experts`: the 8 experts of a row differ. One expert, drawn from the seed and the same for the prefill tokens, is named by every row; among the rows of one device no expert is named more than 32 times, and the other experts share the remaining picks of that device evenly. `span_owner`: of the blocks of one device, either none or exactly 2 have the same owner; a few owners, drawn from the seed, receive 2 blocks from every device.
All inputs are finite; a program needn't handle non-finite values.
Results may differ from a plain program's by a relative error of at most 0.008.
Values may be sent and summed in bfloat16 or wider, within the bound.
No kernel may reach another device: no remote copies, remote signals or barrier semaphores. Data moves between devices by JAX's collectives and lax.ppermute only.
A program may use at most 256 MiB of HBM per device.

v0:
```python
import jax
import jax.numpy as jnp
from jax import lax
from jax.sharding import PartitionSpec as P

TOP = 8
KV = 512
CAPC = 2


softmax_scale = 192.0 ** (-0.5)
gate_unit = 65536.0
empty_score = -1e30


def half_expert(inputs, gate_up, down_proj):
    leading = inputs.shape[:-1]
    merged = jnp.dot(
        inputs.reshape(-1, inputs.shape[-1]), gate_up, preferred_element_type=jnp.float32
    )
    halfway = down_proj.shape[0]
    hidden = (jax.nn.silu(merged[:, :halfway]) * merged[:, halfway:]).astype(jnp.bfloat16)
    output = jnp.dot(hidden, down_proj, preferred_element_type=jnp.float32).astype(jnp.bfloat16)
    return output.reshape(leading + (down_proj.shape[1],))


def pick_ranks(experts):
    flattened = experts.reshape(-1)
    numbered = jnp.arange(flattened.shape[0])
    earlier = (flattened[None, :] == flattened[:, None]) & (numbered[None, :] < numbered[:, None])
    return (flattened, jnp.sum(earlier, axis=1))


def slot_tokens(flattened, pick_rank, expert_count, capacity):
    matches = (flattened[None, None, :] == jnp.arange(expert_count)[:, None, None]) & (
        pick_rank[None, None, :] == jnp.arange(capacity)[None, :, None]
    )
    token_index = jnp.arange(flattened.shape[0]) // TOP
    tokens = jnp.sum(jnp.where(matches, token_index[None, None, :], 0), axis=2)
    return (tokens, jnp.any(matches, axis=2))


def fetch_rows(source, tokens, filled):
    return jnp.where(filled[:, :, None], source[tokens], jnp.zeros((), source.dtype))


def weighted_rows(values, gate_ints):
    weights = gate_ints.astype(jnp.float32) / gate_unit
    picked = values.reshape(gate_ints.shape + (values.shape[-1],)).astype(jnp.float32)
    return jnp.einsum("rk,rkd->rd", weights, picked).astype(jnp.bfloat16)


def per_device(
    prefill_tokens,
    prefill_experts,
    prefill_gates,
    decode_rows,
    decode_experts,
    decode_gates,
    w_gate_up,
    w_down,
    queries,
    own_latent,
    latents,
    span_owner,
    span_request,
    span_length,
):
    devices = lax.axis_size("expert")
    expert_count = devices // 2
    gate_up = w_gate_up[0]
    down_proj = w_down[0]
    model_width = prefill_tokens.shape[1]
    prefill_count = prefill_tokens.shape[0]
    decode_count = decode_rows.shape[0]
    prefill_flat, prefill_rank = pick_ranks(prefill_experts)
    decode_flat, decode_rank = pick_ranks(decode_experts)
    prefill_slots, prefill_filled = slot_tokens(
        prefill_flat, prefill_rank, expert_count, prefill_count
    )
    decode_slots, decode_filled = slot_tokens(decode_flat, decode_rank, expert_count, decode_count)
    outgoing = jnp.concatenate(
        [
            fetch_rows(
                prefill_tokens,
                jnp.repeat(prefill_slots, 2, axis=0),
                jnp.repeat(prefill_filled, 2, axis=0),
            ),
            fetch_rows(
                decode_rows,
                jnp.repeat(decode_slots, 2, axis=0),
                jnp.repeat(decode_filled, 2, axis=0),
            ),
        ],
        axis=1,
    )
    returned = lax.all_to_all(
        half_expert(
            lax.all_to_all(outgoing, "expert", split_axis=0, concat_axis=0, tiled=True),
            gate_up,
            down_proj,
        ),
        "expert",
        split_axis=0,
        concat_axis=0,
        tiled=True,
    )
    columns = returned.shape[1]
    flat_table = returned.reshape(devices * columns, model_width)

    def expert_values(flattened, pick_rank, offset):
        first_half = flat_table[2 * flattened * columns + offset + pick_rank]
        other_half = flat_table[(2 * flattened + 1) * columns + offset + pick_rank]
        return (first_half.astype(jnp.float32) + other_half.astype(jnp.float32)).astype(
            jnp.bfloat16
        )

    prefill_values = expert_values(prefill_flat, prefill_rank, 0)
    decode_values = expert_values(decode_flat, decode_rank, prefill_count)
    prefill_out = weighted_rows(prefill_values, prefill_gates)
    decode_out = weighted_rows(decode_values, decode_gates)
    span_count = span_owner.shape[0]
    block_rows = latents.shape[1]
    latent_width = latents.shape[2]
    numbered = jnp.arange(span_count)
    earlier = (span_owner[None, :] == span_owner[:, None]) & (numbered[None, :] < numbered[:, None])
    span_rank = jnp.sum(earlier, axis=1)
    placed = (span_owner[None, None, :] == jnp.arange(devices)[:, None, None]) & (
        span_rank[None, None, :] == jnp.arange(CAPC)[None, :, None]
    )
    selector = placed.reshape(devices * CAPC, span_count).astype(jnp.bfloat16)
    shipped = jnp.dot(selector, latents.reshape(span_count, -1), preferred_element_type=jnp.float32)
    shipped = shipped.astype(jnp.bfloat16).reshape(devices, CAPC, block_rows, latent_width)
    ship_request = jnp.sum(jnp.where(placed, span_request[None, None, :], 0), axis=2)
    ship_length = jnp.sum(jnp.where(placed, span_length[None, None, :], 0), axis=2)
    block_latents = lax.all_to_all(shipped, "expert", split_axis=0, concat_axis=0, tiled=True)
    block_requests = lax.all_to_all(ship_request, "expert", split_axis=0, concat_axis=0, tiled=True)
    block_lengths = lax.all_to_all(ship_length, "expert", split_axis=0, concat_axis=0, tiled=True)
    asking = queries[block_requests]
    expert_scores = (
        jnp.einsum("nchl,nctl->ncht", asking, block_latents, preferred_element_type=jnp.float32)
        * softmax_scale
    )
    inside = (jnp.arange(block_latents.shape[2])[None, None, :] < block_lengths[:, :, None])[
        :, :, None, :
    ]
    highest = jnp.max(jnp.where(inside, expert_scores, -jnp.inf), axis=3)
    highest = jnp.where((block_lengths > 0)[:, :, None], highest, empty_score)
    weights = jnp.where(inside, jnp.exp(expert_scores - highest[:, :, :, None]), 0.0)
    totals = jnp.sum(weights, axis=3)
    values = jnp.einsum(
        "ncht,nctk->nchk",
        weights.astype(jnp.bfloat16),
        block_latents[:, :, :, :KV],
        preferred_element_type=jnp.float32,
    )
    span_max = highest
    span_total = totals
    span_value = values
    head_count = queries.shape[1]
    slot_count = span_max.shape[0] * span_max.shape[1]
    span_max = span_max.reshape(slot_count, head_count)
    span_total = span_total.reshape(slot_count, head_count)
    span_value = span_value.reshape(slot_count, head_count, KV)
    member = block_requests.reshape(slot_count)[:, None] == jnp.arange(decode_count)[None, :]
    own_score = (
        jnp.einsum("rhl,rl->rh", queries, own_latent, preferred_element_type=jnp.float32)
        * softmax_scale
    )
    row_max = jnp.maximum(
        own_score, jnp.max(jnp.where(member[:, :, None], span_max[:, None, :], -jnp.inf), axis=0)
    )
    slot_max = jnp.sum(jnp.where(member[:, :, None], row_max[None, :, :], 0.0), axis=1)
    factor = jnp.exp(span_max - slot_max)
    own_factor = jnp.exp(own_score - row_max)
    member_weight = member.astype(jnp.float32)
    totals = own_factor + jnp.einsum(
        "sr,sh->rh", member_weight, factor * span_total, precision=lax.Precision.HIGHEST
    )
    numerator = own_factor[:, :, None] * own_latent[:, None, :KV].astype(jnp.float32)
    numerator = numerator + jnp.einsum(
        "sr,shk->rhk",
        member_weight,
        factor[:, :, None] * span_value,
        precision=lax.Precision.HIGHEST,
    )
    context = (numerator / totals[:, :, None]).astype(jnp.bfloat16)
    return (prefill_out, decode_out, context)


def solution(mesh):
    return jax.shard_map(
        per_device,
        mesh=mesh,
        in_specs=(
            P(("groups", "expert"), None),
            P(("groups", "expert"), None),
            P(("groups", "expert"), None),
            P(("groups", "expert"), None),
            P(("groups", "expert"), None),
            P(("groups", "expert"), None),
            P("expert", None, None),
            P("expert", None, None),
            P(("groups", "expert"), None, None),
            P(("groups", "expert"), None),
            P(("groups", "expert"), None, None),
            P(("groups", "expert")),
            P(("groups", "expert")),
            P(("groups", "expert")),
        ),
        out_specs=(
            P(("groups", "expert"), None),
            P(("groups", "expert"), None),
            P(("groups", "expert"), None, None),
        ),
        check_vma=False,
    )
```

profile of v0, /device:TPU:20, one launch (start us, length us, event | category | flops | bytes accessed | tf_op | source)
XLA Modules:
  0.0 847.5 jit_solution(738595637424205755)
XLA Ops:
  0.6 1.0 convert_reduce_fusion.2
  1.6 0.7 iota_compare_fusion.8
  2.3 1.9 select_reduce_fusion.3
  4.2 6.1 all-to-all-start.3
  10.4 0.8 copy.71
  11.1 0.1 eq.178
  11.2 0.2 convert_reduce_fusion
  11.4 0.8 copy.70
  12.2 0.1 eq.168
  12.3 0.2 convert_reduce_fusion.1
  12.5 0.2 and_reduce_fusion
  12.7 0.2 and_reduce_fusion.1
  12.9 0.4 fusion.22
  13.6 14.9 %gather_fusion.1 = bf16[512,7168]{1,0:T(8,128)(2,1)} fusion(bf16[32,7168]{1,0:T(8,128)(2,1)} %param.17, s32[1024]{0:T(1024)S(1)} %pad_clamp_fusion.5), kind=kCustom, calls=%fused_computation.1 | custom fusion | bytes 14682112 | tf_op jit(solution)/shard_map/gather | solution.py:44
  28.4 6.6 broadcast_select_fusion
  35.1 7.0 gather_fusion
  42.1 6.6 broadcast_select_fusion.1
  48.7 6.0 all-to-all-start.2
  54.7 13.4 %pad_maximum_fusion = bf16[16,64,7168]{2,1,0:T(8,128)(2,1)} fusion(bf16[16,32,7168]{2,1,0:T(8,128)(2,1)} %broadcast_select_fusion, bf16[16,32,7168]{2,1,0:T(8,128)(2,1)} %broadcast_select_fusion.1), kind=kLoop, calls=%fused_computation.8 | loop fusion | flops 29360128 | bytes 29360128 | tf_op jit(solution)/shard_map/concatenate | solution.py:82
  68.2 6.4 all-to-all-start
  74.6 3.5 reshape.549
  78.1 3.4 convolution_convert_fusion
  81.5 5.6 reshape.550
  87.2 302.8 %all-to-all-done = bf16[16,64,7168]{2,1,0:T(8,128)(2,1)} async-done(((bf16[16,64,7168]{2,1,0:T(8,128)(2,1)}), bf16[16,64,7168]{2,1,0:T(8,128)(2,1)}, u32[]{:S(2)}, u32[]{:S(2)}) %all-to-all-start) | async-done | bytes 14680096 | tf_op jit(solution)/shard_map/all_to_all | solution.py:99
  390.0 6.5 all-to-all-start.4
  396.5 19.2 %fusion = f32[1024,1024]{1,0:T(8,128)S(1)} fusion(bf16[1024,7168]{1,0:T(8,128)(2,1)} %bitcast.5, bf16[1,7168,1024]{2,1,0:T(8,128)(2,1)} %param.20), kind=kOutput, calls=%fused_computation.9 | convolution fusion | flops 15032385536 | bytes 33554432 | tf_op jit(solution)/shard_map/dot_general | solution.py:18
  415.7 14.1 %convolution_convert_fusion.1 = bf16[1024,7168]{1,0:T(8,128)(2,1)} fusion(bf16[1,512,7168]{2,1,0:T(8,128)(2,1)} %param.21, f32[1024,1024]{1,0:T(8,128)S(1)} %fusion), kind=kOutput, calls=%fused_computation.11 | convolution fusion | flops 7526678528 | bytes 26214400 | tf_op jit(solution)/shard_map/dot_general | solution.py:23
  429.8 23.9 %all-to-all-done.4 = bf16[16,2,64,576]{3,2,1,0:T(8,128)(2,1)} async-done(((bf16[16,2,64,576]{3,2,1,0:T(8,128)(2,1)}), bf16[16,2,64,576]{3,2,1,0:T(8,128)(2,1)}, u32[]{:S(2)}, u32[]{:S(2)}) %all-to-all-start.4) | async-done | bytes 2359328 | tf_op jit(solution)/shard_map/all_to_all | solution.py:136
  453.7 6.7 all-to-all-start.1
  460.4 0.1 copy.92
  460.5 0.1 mul.121
  460.7 0.1 mul.124
  460.8 0.1 copy.94
  461.0 0.1 add.196
  461.2 0.1 add.201
  461.4 0.9 fusion.26
  462.4 0.1 copy.82
  462.6 0.1 reshape.603
  462.8 2.3 gather_fusion.6
  465.1 0.1 copy.87
  465.2 0.1 gt.14
  465.3 0.5 broadcast.478
  465.9 0.7 reduce.5
  466.6 0.1 copy.78
  466.7 0.1 iota_compare_fusion.3
  466.8 4.5 select_reduce_fusion
  471.4 0.2 select_reduce_fusion.2
  471.6 0.2 select_reduce_fusion.1
  472.1 0.1 broadcast_select_fusion.2
  472.2 1.6 fusion.16
  473.8 0.1 convolution_add_fusion
  473.9 0.1 copy.90
  474.0 3.0 fusion.10
  477.1 13.8 %divide_convert_fusion = bf16[32,64,512]{2,0,1:T(8,128)(2,1)S(1)} fusion(f32[32,64,512]{2,1,0:T(8,128)S(1)} %bitcast.72, f32[32,64]{0,1:T(8,128)S(1)} %copy.90, f32[32,64]{0,1:T(8,128)S(1)} %copy.86, f32[32,512]{1,0:T(8,128)S(1)} %slice_convert_fusion, f32[32,64]{0,1:T(8,128)S(1)} %copy.85, s32[32]{0:T(128)S(1)} %eq.196), kind=kOutput, calls=%fused_computation.19 | convolution fusion | flops 407897088 | bytes 6381696 | tf_op jit(solution)/shard_map/sr,shk->rhk/dot_general | solution.py:181
  490.8 2.5 copy.91
  493.3 282.6 %all-to-all-done.1 = bf16[16,64,7168]{2,1,0:T(8,128)(2,1)} async-done(((bf16[16,64,7168]{2,1,0:T(8,128)(2,1)}), bf16[16,64,7168]{2,1,0:T(8,128)(2,1)}, u32[]{:S(2)}, u32[]{:S(2)}) %all-to-all-start.1) | async-done | bytes 14680096 | tf_op jit(solution)/shard_map/all_to_all | solution.py:97
  775.9 15.0 %gather_fusion.3 = bf16[256,7168]{1,0:T(8,128)(2,1)} fusion(bf16[1024,7168]{1,0:T(8,128)(2,1)} %bitcast.9, s32[1024]{0:T(1024)S(1)} %pad_clamp_fusion.3), kind=kCustom, calls=%fused_computation.3 | custom fusion | bytes 7341056 | tf_op jit(solution)/shard_map/gather | solution.py:113
  791.0 15.3 %gather_fusion.2 = bf16[256,7168]{1,0:T(8,128)(2,1)} fusion(bf16[1024,7168]{1,0:T(8,128)(2,1)} %bitcast.9, s32[1024]{0:T(1024)S(1)} %pad_clamp_fusion.4), kind=kCustom, calls=%fused_computation.2 | custom fusion | bytes 7341056 | tf_op jit(solution)/shard_map/gather | solution.py:112
  806.3 4.3 fusion.8
  810.6 0.9 copy.112
  811.5 15.3 %gather_fusion.5 = bf16[256,7168]{1,0:T(8,128)(2,1)} fusion(bf16[1024,7168]{1,0:T(8,128)(2,1)} %bitcast.9, s32[1024]{0:T(1024)S(1)} %pad_clamp_fusion.1), kind=kCustom, calls=%fused_computation.5 | custom fusion | bytes 7341056 | tf_op jit(solution)/shard_map/gather | solution.py:113
  826.8 15.1 %gather_fusion.4 = bf16[256,7168]{1,0:T(8,128)(2,1)} fusion(bf16[1024,7168]{1,0:T(8,128)(2,1)} %bitcast.9, s32[1024]{0:T(1024)S(1)} %pad_clamp_fusion.2), kind=kCustom, calls=%fused_computation.4 | custom fusion | bytes 7341056 | tf_op jit(solution)/shard_map/gather | solution.py:112
  841.9 4.3 fusion.6
  846.2 0.9 copy.111
  (62 shorter events, 1.4 us)
Async XLA Ops:
  0.6 460.8 %copy-start = (bf16[32,64,576]{2,1,0:T(8,128)(2,1)S(1)}, bf16[32,64,576]{2,1,0:T(8,128)(2,1)}, u32[]{:S(2)}) copy-start(bf16[32,64,576]{2,1,0:T(8,128)(2,1)} %param.22) | copy-start | bytes 7077892
  4.2 44.5 %all-to-all-start.3 = ((s32[16,1,2]{2,1,0:T(1,128)}), s32[16,1,2]{2,1,0:T(1,128)S(1)}, u32[]{:S(2)}, u32[]{:S(2)}) async-start(s32[16,1,2]{2,1,0:T(1,128)} %bitcast.34), calls=%async_computation.3 | async-start | bytes 16384 | tf_op jit(solution)/shard_map/all_to_all | solution.py:138
  28.4 6.6 copy-start.1
  48.7 19.4 %all-to-all-start.2 = ((s32[16,1,2]{2,1,0:T(1,128)}), s32[16,1,2]{2,1,0:T(1,128)S(1)}, u32[]{:S(2)}, u32[]{:S(2)}) async-start(s32[16,1,2]{2,1,0:T(1,128)} %bitcast.33), calls=%async_computation.2 | async-start | bytes 16384 | tf_op jit(solution)/shard_map/all_to_all | solution.py:137
  68.2 321.9 %all-to-all-start = ((bf16[16,64,7168]{2,1,0:T(8,128)(2,1)}), bf16[16,64,7168]{2,1,0:T(8,128)(2,1)}, u32[]{:S(2)}, u32[]{:S(2)}) async-start(bf16[16,64,7168]{2,1,0:T(8,128)(2,1)} %pad_maximum_fusion), calls=%async_computation | async-start | bytes 29360128 | tf_op jit(solution)/shard_map/all_to_all | solution.py:99
  390.0 63.7 %all-to-all-start.4 = ((bf16[16,2,64,576]{3,2,1,0:T(8,128)(2,1)}), bf16[16,2,64,576]{3,2,1,0:T(8,128)(2,1)}, u32[]{:S(2)}, u32[]{:S(2)}) async-start(bf16[16,2,64,576]{3,2,1,0:T(8,128)(2,1)} %reshape.550), calls=%async_computation.4 | async-start | bytes 5242880 | tf_op jit(solution)/shard_map/all_to_all | solution.py:136
  453.7 6.7 copy-start.5
  453.7 6.8 copy-start.3
  453.7 7.1 copy-start.6
  453.7 7.2 copy-start.4
  453.7 7.7 copy-start.2
  453.7 322.2 %all-to-all-start.1 = ((bf16[16,64,7168]{2,1,0:T(8,128)(2,1)}), bf16[16,64,7168]{2,1,0:T(8,128)(2,1)}, u32[]{:S(2)}, u32[]{:S(2)}) async-start(bf16[16,64,7168]{2,1,0:T(8,128)(2,1)} %bitcast.71), calls=%async_computation.1 | async-start | bytes 29360128 | tf_op jit(solution)/shard_map/all_to_all | solution.py:97
where the time goes:
time: 859 us; the launch traced here: 848 us
  waiting for transfers between devices  609 us (71%)
  local copies, waits for them, and re-layouts  103 us (12%)
  matrix products  67.6 us (8%)
  other arithmetic  34.6 us (4%)
  starting transfers between devices  31.7 us (4%)
    all_to_all x1, waiting for transfers between devices, per_device(): lax.all_to_all(outgoing, 'expert', split_axis=0, concat_axis=0, tiled=True)  303 us
    all_to_all x1, waiting for transfers between devices, per_device(): lax.all_to_all(half_expert(lax.all_to_all(outgoing, 'expert', split_axis=...  283 us
    gather x2, local copies, waits for them, and re-layouts, expert_values(): first_half = flat_table[2 * flattened * columns + offset + pick_rank]  30.4 us
    gather x2, local copies, waits for them, and re-layouts, expert_values(): other_half = flat_table[(2 * flattened + 1) * columns + offset + pick_rank]  30.3 us
    all_to_all x1, waiting for transfers between devices, per_device(): lax.all_to_all(shipped, 'expert', split_axis=0, concat_axis=0, tiled=True)  23.9 us
    gather x2, local copies, waits for them, and re-layouts, fetch_rows(): source[tokens]  21.9 us
    dot_general x1, matrix products, half_expert(): jnp.dot(inputs.reshape(-1, inputs.shape[-1]), gate_up, preferred_element_...  19.2 us
  transfers between devices with their start and end apart: 5, of which 3 were waited for; matrix products, arithmetic and copies ran while one was open for 15% of the time, Pallas kernels for 0%

commit v1 on v0

v1 whole, which is shorter than its diff:
```python
import functools

import jax
import jax.numpy as jnp
import numpy as np
from jax import lax
from jax.experimental import pallas as pl
from jax.experimental.pallas import tpu as pltpu
from jax.sharding import PartitionSpec as P

KV = 512
CAPC = 2

softmax_scale = 192.0 ** (-0.5)
gate_unit = 65536.0
AXIS = "expert"
VMEM_LIMIT = 56 * 1024 * 1024


def mlp_kernel(sizes, steps, *refs):
    count = len(sizes)
    x_refs = refs[:count]
    gate_ref, up_ref, down_ref = refs[count : count + 3]
    out_refs = refs[count + 3 : 2 * count + 3]
    rows_ref, total_ref = refs[2 * count + 3 :]
    step = pl.program_id(0)

    @pl.when(step == 0)
    def _():
        at = 0
        for x_ref, size in zip(x_refs, sizes):
            rows_ref[at : at + size, :] = x_ref[...]
            at += size

    rows = rows_ref[...]
    gate = jnp.dot(rows, gate_ref[...], preferred_element_type=jnp.float32)
    up = jnp.dot(rows, up_ref[...], preferred_element_type=jnp.float32)
    hidden = (jax.nn.silu(gate) * up).astype(jnp.bfloat16)
    width = down_ref.shape[1]
    tile = 1024 if width % 1024 == 0 else width

    for j in range(width // tile):
        cols = slice(j * tile, (j + 1) * tile)
        part = jnp.dot(hidden, down_ref[:, cols], preferred_element_type=jnp.float32)

        @pl.when(step == 0)
        def _(part=part, cols=cols):
            total_ref[:, cols] = part

        @pl.when((step > 0) & (step < steps - 1))
        def _(part=part, cols=cols):
            total_ref[:, cols] += part

        @pl.when(step == steps - 1)
        def _(part=part, cols=cols):
            value = (total_ref[:, cols] + part).astype(jnp.bfloat16)
            at = 0
            for out_ref, size in zip(out_refs, sizes):
                out_ref[:, cols] = value[at : at + size, :]
                at += size


def mlp(chunks, gate_up, down_proj):
    width = chunks[0].shape[1]
    half = down_proj.shape[0]
    tile = 256
    steps = half // tile
    sizes = tuple(c.shape[0] for c in chunks)
    rows = sum(sizes)
    x_specs = [pl.BlockSpec((size, width), lambda i: (0, 0)) for size in sizes]
    return pl.pallas_call(
        functools.partial(mlp_kernel, sizes, steps),
        grid=(steps,),
        in_specs=x_specs
        + [
            pl.BlockSpec((width, tile), lambda i: (0, i)),
            pl.BlockSpec((width, tile), lambda i: (0, i + steps)),
            pl.BlockSpec((tile, width), lambda i: (i, 0)),
        ],
        out_specs=[pl.BlockSpec((size, width), lambda i: (0, 0)) for size in sizes],
        out_shape=[jax.ShapeDtypeStruct((size, width), jnp.bfloat16) for size in sizes],
        scratch_shapes=[
            pltpu.VMEM((rows, width), jnp.bfloat16),
            pltpu.VMEM((rows, width), jnp.float32),
        ],
        compiler_params=pltpu.CompilerParams(vmem_limit_bytes=VMEM_LIMIT),
        cost_estimate=pl.CostEstimate(
            flops=6 * rows * width * half,
            bytes_accessed=6 * width * half + 4 * rows * width,
            transcendentals=rows * half,
        ),
        name="mlp",
    )(*chunks, gate_up, gate_up, down_proj)


def ship_kernel(source_ref, block_ref, out_ref):
    out_ref[...] = block_ref[...]


def ship_blocks(latents, source):
    slots = source.shape[0]
    shape = (1,) + latents.shape[1:]
    return pl.pallas_call(
        ship_kernel,
        grid_spec=pltpu.PrefetchScalarGridSpec(
            num_scalar_prefetch=1,
            grid=(slots,),
            in_specs=[pl.BlockSpec(shape, lambda i, source: (source[i], 0, 0))],
            out_specs=pl.BlockSpec(shape, lambda i, source: (i, 0, 0)),
        ),
        out_shape=jax.ShapeDtypeStruct((slots,) + latents.shape[1:], latents.dtype),
        name="ship",
    )(source, latents)


def attend_kernel(order_ref, start_ref, length_ref, query_ref, own_ref, latent_ref, out_ref):
    row = pl.program_id(0)
    query = query_ref[0]
    own = own_ref[0].astype(jnp.float32)
    own_score = (
        jnp.sum(query.astype(jnp.float32) * own, axis=1, keepdims=True) * softmax_scale
    )
    heads = query.shape[0]
    block = latent_ref.shape[1]

    def step(j, state):
        top, total, value = state
        slot = order_ref[j]
        latent = latent_ref[slot]
        scores = (
            lax.dot_general(
                query, latent, (((1,), (1,)), ((), ())), preferred_element_type=jnp.float32
            )
            * softmax_scale
        )
        inside = lax.broadcasted_iota(jnp.int32, (heads, block), 1) < length_ref[slot]
        span_max = jnp.max(jnp.where(inside, scores, -jnp.inf), axis=1, keepdims=True)
        weights = jnp.where(inside, jnp.exp(scores - span_max), 0.0)
        span_total = jnp.sum(weights, axis=1, keepdims=True)
        span_value = jnp.dot(
            weights.astype(jnp.bfloat16), latent[:, :KV], preferred_element_type=jnp.float32
        )
        higher = jnp.maximum(top, span_max)
        old = jnp.exp(top - higher)
        new = jnp.exp(span_max - higher)
        return (higher, old * total + new * span_total, old * value + new * span_value)

    state = (
        own_score,
        jnp.ones((heads, 1), jnp.float32),
        jnp.broadcast_to(own[:, :KV], (heads, KV)),
    )
    top, total, value = lax.fori_loop(start_ref[row], start_ref[row + 1], step, state)
    out_ref[0] = (value / total).astype(jnp.bfloat16)


def attend(order, start, lengths, queries, own_latent, latents):
    rows, heads, width = queries.shape
    slots, block, _ = latents.shape
    return pl.pallas_call(
        attend_kernel,
        grid_spec=pltpu.PrefetchScalarGridSpec(
            num_scalar_prefetch=3,
            grid=(rows,),
            in_specs=[
                pl.BlockSpec((1, heads, width), lambda i, *_: (i, 0, 0)),
                pl.BlockSpec((1, 1, width), lambda i, *_: (i, 0, 0)),
                pl.BlockSpec((slots, block, width), lambda i, *_: (0, 0, 0)),
            ],
            out_specs=pl.BlockSpec((1, heads, KV), lambda i, *_: (i, 0, 0)),
        ),
        out_shape=jax.ShapeDtypeStruct((rows, heads, KV), jnp.bfloat16),
        compiler_params=pltpu.CompilerParams(vmem_limit_bytes=VMEM_LIMIT),
        cost_estimate=pl.CostEstimate(
            flops=4 * slots * heads * block * width,
            bytes_accessed=2 * (rows * heads * (width + KV) + slots * block * width),
            transcendentals=slots * heads * block,
        ),
        name="attend",
    )(order, start, lengths, queries, own_latent.reshape(rows, 1, width), latents)


def dense_gates(experts, gates, expert_count):
    named = experts[:, :, None] == jnp.arange(expert_count)[None, None, :]
    return jnp.sum(jnp.where(named, gates[:, :, None], 0), axis=1)


def per_device(
    prefill_tokens,
    prefill_experts,
    prefill_gates,
    decode_rows,
    decode_experts,
    decode_gates,
    w_gate_up,
    w_down,
    queries,
    own_latent,
    latents,
    span_owner,
    span_request,
    span_length,
):
    devices = lax.axis_size(AXIS)
    chips = devices // 2
    half = chips // 2
    gate_up = w_gate_up[0]
    down_proj = w_down[0]
    prefill_count = prefill_tokens.shape[0]
    decode_count = decode_rows.shape[0]
    row_count = prefill_count + decode_count
    split = prefill_count

    ring = list(range(0, chips, 2)) + list(range(1, chips, 2))[::-1]
    place_of = np.zeros(chips, np.int32)
    for i, chip in enumerate(ring):
        place_of[chip] = i
    ahead = [
        (2 * ring[i] + c, 2 * ring[(i + 1) % chips] + c) for i in range(chips) for c in range(2)
    ]
    back = [(b, a) for a, b in ahead]
    across = [(i, i ^ 1) for i in range(devices)]
    me = lax.axis_index(AXIS)
    my_chip = me // 2
    my_core = me % 2
    place = jnp.asarray(place_of)[my_chip]

    def device_at(shift):
        return 2 * jnp.asarray(np.array(ring, np.int32))[(place + shift + chips) % chips] + my_core

    gates = jnp.concatenate(
        [
            dense_gates(prefill_experts, prefill_gates, chips),
            dense_gates(decode_experts, decode_gates, chips),
        ],
        axis=0,
    )
    span_count = span_owner.shape[0]
    block_rows = latents.shape[1]
    codes = (span_owner * decode_count + span_request) * (block_rows + 1) + span_length
    small = jnp.concatenate([gates.T.reshape(-1), codes]).astype(jnp.int32)
    small = lax.all_gather(small, AXIS, tiled=False)
    gate_table = small[:, : chips * row_count].reshape(devices, chips, row_count)
    gate_table = (
        lax.dynamic_index_in_dim(gate_table, my_chip, 1, keepdims=False).astype(jnp.float32)
        / gate_unit
    )
    all_codes = small[:, chips * row_count :]

    numbered = jnp.arange(span_count)
    earlier = (span_owner[None, :] == span_owner[:, None]) & (numbered[None, :] < numbered[:, None])
    span_rank = jnp.sum(earlier, axis=1)
    slot_of = span_owner * CAPC + span_rank
    slots = devices * CAPC
    source = jnp.sum(
        jnp.where(slot_of[None, :] == jnp.arange(slots)[:, None], numbered[None, :], 0), axis=1
    ).astype(jnp.int32)
    shipped = ship_blocks(latents, source)

    own_rows = jnp.concatenate([prefill_tokens, decode_rows], axis=0)
    front = [own_rows]
    rear = [own_rows]
    for s in range(1, half):
        front.append(lax.ppermute(front[-1], AXIS, ahead))
        rear.append(lax.ppermute(rear[-1], AXIS, back))
    front.append(lax.ppermute(front[-1][:split], AXIS, ahead))
    rear.append(lax.ppermute(rear[-1][split:], AXIS, back))

    block_latents = lax.optimization_barrier((shipped, front[half - 1], rear[half - 1]))[0]
    block_latents = lax.all_to_all(block_latents, AXIS, split_axis=0, concat_axis=0, tiled=True)

    own_part = {}
    for s in range(half + 1):
        mine = [own_rows] if s == 0 else [front[s], rear[s]]
        other = [lax.ppermute(c, AXIS, across) for c in mine]
        parts = mlp(mine + other, gate_up, down_proj)
        count = len(mine)
        for k in range(count):
            own_part[(s, k)] = (parts[k], lax.ppermute(parts[count + k], AXIS, across))

    def contribution(s, k, lo, hi):
        part, from_other = own_part[(s, k)]
        both = (part.astype(jnp.float32) + from_other.astype(jnp.float32)).astype(jnp.bfloat16)
        shift = (-s, s)[k] if s else 0
        weight = lax.dynamic_index_in_dim(gate_table, device_at(shift), 0, keepdims=False)
        return weight[lo:hi, None] * both.astype(jnp.float32)

    up = contribution(half, 0, 0, split).astype(jnp.bfloat16)
    down = contribution(half, 1, split, row_count).astype(jnp.bfloat16)
    for s in range(half - 1, 0, -1):
        up = lax.ppermute(up, AXIS, ahead).astype(jnp.float32)
        down = lax.ppermute(down, AXIS, back).astype(jnp.float32)
        up_own = contribution(s, 1, 0, row_count)
        down_own = contribution(s, 0, 0, row_count)
        if s == half - 1:
            up = jnp.pad(up, ((0, row_count - split), (0, 0)))
            down = jnp.pad(down, ((split, 0), (0, 0)))
        up = (up + up_own).astype(jnp.bfloat16)
        down = (down + down_own).astype(jnp.bfloat16)
    up = lax.ppermute(up, AXIS, ahead).astype(jnp.float32)
    down = lax.ppermute(down, AXIS, back).astype(jnp.float32)
    out = (contribution(0, 0, 0, row_count) + up + down).astype(jnp.bfloat16)
    prefill_out = out[:split]
    decode_out = out[split:]

    lengths = all_codes % (block_rows + 1)
    targets = all_codes // (block_rows + 1)
    owners = targets // decode_count
    requests = targets % decode_count
    here = owners == me
    rank = jnp.cumsum(here.astype(jnp.int32), axis=1) - 1
    taken = here[:, None, :] & (rank[:, None, :] == jnp.arange(CAPC)[None, :, None])
    slot_length = jnp.sum(jnp.where(taken, lengths[:, None, :], 0), axis=2).reshape(-1)
    slot_request = jnp.sum(jnp.where(taken, requests[:, None, :], 0), axis=2).reshape(-1)
    key = jnp.where(slot_length > 0, slot_request, decode_count)
    index = jnp.arange(slots)
    before = (key[None, :] < key[:, None]) | (
        (key[None, :] == key[:, None]) & (index[None, :] < index[:, None])
    )
    position = jnp.sum(before, axis=1)
    order = jnp.sum(
        jnp.where(position[None, :] == index[:, None], index[None, :], 0), axis=1
    ).astype(jnp.int32)
    start = jnp.sum(key[None, :] < jnp.arange(decode_count + 1)[:, None], axis=1).astype(jnp.int32)
    context = attend(
        order, start, slot_length.astype(jnp.int32), queries, own_latent, block_latents
    )
    return (prefill_out, decode_out, context)


def solution(mesh):
    rows = P(("groups", "expert"), None)
    blocks = P(("groups", "expert"), None, None)
    line = P(("groups", "expert"))
    weights = P("expert", None, None)
    return jax.shard_map(
        per_device,
        mesh=mesh,
        in_specs=(rows,) * 6 + (weights, weights, blocks, rows, blocks, line, line, line),
        out_specs=(rows, rows, blocks),
        check_vma=False,
    )
```

time: 859 us -> 354 us (0.41)
  waiting for transfers between devices: 609 us -> 91.3 us
  Pallas kernels: 0 us -> 120 us
  local copies, waits for them, and re-layouts: 103 us -> 13.8 us
  matrix products: 67.6 us -> 0 us
  blocking collectives: 0 us -> 57.7 us
  other arithmetic: 34.6 us -> 10.8 us
  between operations: 1.42 us -> 13.6 us
  starting transfers between devices: 31.7 us -> 40.7 us
    all_to_all x5 -> x1, waiting for transfers between devices: 609 us -> 0.01 us  [per_device(): lax.all_to_all(block_latents, AXIS, split_axis=0, concat_axis=0, tiled=True)]
    pallas_call x0 -> x7, Pallas kernels: none -> 120 us  [the longest x5 78.5 us: mlp(): pl.pallas_call(functools.partial(mlp_kernel, sizes, steps), grid=(steps,)...]
    ppermute x0 -> x34, waiting for transfers between devices: none -> 91.3 us  [the longest x4 44.7 us: per_device(): down = lax.ppermute(down, AXIS, back).astype(jnp.float32)]
    gather x7 -> x0, local copies, waits for them, and re-layouts: 85 us -> none  [the longest x2 30.4 us: expert_values(): first_half = flat_table[2 * flattened * columns + offset + pick_rank]]
    dot_general x10 -> x0, matrix products: 67.6 us -> none  [the longest x1 19.2 us: half_expert(): jnp.dot(inputs.reshape(-1, inputs.shape[-1]), gate_up, preferred_element_...]
    unnamed x0 -> x1, blocking collectives: none -> 57.7 us
    ppermute x0 -> x34, starting transfers between devices: none -> 34.2 us  [the longest x3 11.9 us: per_device(): rear.append(lax.ppermute(rear[-1], AXIS, back))]
    all_to_all x5 -> x1, starting transfers between devices: 31.7 us -> 6.45 us  [per_device(): lax.all_to_all(block_latents, AXIS, split_axis=0, concat_axis=0, tiled=True)]
  transfers between devices with their start and end apart: 5 -> 35, of which waited for: 3 -> 8; matrix products, arithmetic and copies ran while one was open for 15% -> 5% of each run, Pallas kernels for 0% -> 34%
where the time goes in v1:
time: 354 us; the launch traced here: 348 us
  Pallas kernels  120 us (34%)
  waiting for transfers between devices  91.3 us (26%)
  blocking collectives  57.7 us (16%)
  starting transfers between devices  40.7 us (11%)
  local copies, waits for them, and re-layouts  13.8 us (4%)
  between operations  13.6 us (4%)
  other arithmetic  10.8 us (3%)
    pallas_call x5, Pallas kernels, mlp(): pl.pallas_call(functools.partial(mlp_kernel, sizes, steps), grid=(steps,)...  78.5 us
    unnamed x1, blocking collectives  57.7 us
    ppermute x4, waiting for transfers between devices, per_device(): down = lax.ppermute(down, AXIS, back).astype(jnp.float32)  44.7 us
    ppermute x4, waiting for transfers between devices, per_device(): up = lax.ppermute(up, AXIS, ahead).astype(jnp.float32)  32.2 us
    pallas_call x1, Pallas kernels, attend(): pl.pallas_call(attend_kernel, grid_spec=pltpu.PrefetchScalarGridSpec(num_...  24.5 us
    pallas_call x1, Pallas kernels, ship_blocks(): pl.pallas_call(ship_kernel, grid_spec=pltpu.PrefetchScalarGridSpec(num_sc...  16.8 us
    ppermute x3, starting transfers between devices, per_device(): rear.append(lax.ppermute(rear[-1], AXIS, back))  11.9 us
  transfers between devices with their start and end apart: 35, of which 8 were waited for; matrix products, arithmetic and copies ran while one was open for 5% of the time, Pallas kernels for 34%

profile of v1, /device:TPU:20, one launch (start us, length us, event | category | flops | bytes accessed | tf_op | source)
XLA Modules:
  0.0 347.5 jit_solution(7132471417335918909)
XLA Ops:
  0.7 1.1 constant_dynamic-update-slice_fusion.1
  1.8 1.1 constant_dynamic-update-slice_fusion.refs_0_
  2.9 0.5 collective-permute-start.2
  3.4 1.6 collective-permute-start.6
  5.0 0.6 dynamic_slice.67
  11.6 0.7 fusion.22
  18.0 7.0 %collective-permute-done.2.refs_0_ = bf16[64,7168]{1,0:T(8,128)(2,1)S(1)} collective-permute-done((bf16[64,7168]{1,0:T(8,128)(2,1)S(1)}, bf16[64,7168]{1,0:T(8,128)(2,1)S(1)}, u32[]{:S(2)}, u32[]{:S(2)}) %collective-permute-start.2) | collective-permute-done | bytes 917536 | tf_op jit(solution)/shard_map/ppermute | solution.py:264
  25.1 0.4 collective-permute-start.3
  25.9 1.6 collective-permute-start.7
  27.5 0.6 dynamic-slice.9
  28.9 57.7 %all-reduce.2 = s32[8448]{0:T(1024)S(1)} all-reduce(s32[8448]{0:T(1024)S(1)} %add_dynamic-update-slice_fusion), channel_id=2, replica_groups=mesh['groups'=2,'expert'=16] {'expert'}, use_global_device_ids=true, to_apply=%add.2 | all-reduce | flops 8448 | bytes 67584
  86.8 2.2 collective-permute-start.4
  89.0 0.6 fusion.19
  89.6 0.8 reduce_window_sum.11
  90.3 0.6 select_reduce_fusion.5.source_ref
  90.9 16.8 %ship.1 = bf16[32,64,576]{2,1,0:T(8,128)(2,1)} custom-call(s32[32]{0:T(128)} %select_reduce_fusion.5.source_ref, bf16[16,64,576]{2,1,0:T(8,128)(2,1)} %block_ref.1), custom_call_target="tpu_custom_call" | custom-call | tf_op jit(solution)/shard_map/ship/pallas_call | solution.py:103
  107.7 0.6 fusion.9
  108.4 0.4 collective-permute-start.22
  108.9 0.4 collective-permute-start.18
  109.3 8.7 %collective-permute-start.8 = (bf16[64,7168]{1,0:T(8,128)(2,1)}, bf16[64,7168]{1,0:T(8,128)(2,1)}, u32[]{:S(2)}, u32[]{:S(2)}) collective-permute-start(bf16[64,7168]{1,0:T(8,128)(2,1)} %collective-permute-done.7.refs_1_), channel_id=1, source_target_pairs={{4,0},{5,1},{8,4},{9,5},{12,8},{13,9},{14,12},{15,13},{10,14},{11,... | collective-permute-start | bytes 2752520 | tf_op jit(solution)/shard_map/ppermute | solution.py:265
  118.0 0.6 slice_bitcast_fusion.1
  118.7 0.8 slice_bitcast_fusion
  119.5 13.0 %mlp.5 = (bf16[64,7168]{1,0:T(8,128)(2,1)}, bf16[64,7168]{1,0:T(8,128)(2,1)}) custom-call(bf16[64,7168]{1,0:T(8,128)(2,1)} %copy-done.2, bf16[64,7168]{1,0:T(8,128)(2,1)} %collective-permute-done.refs_1_, bf16[7168,1024]{1,0:T(8,128)(2,1)} %bitcast.46, bf16[7168,1024]{1,0:T(8,128)(2,1)} %bitcast.47, bf16[512,7168]{1,0:T(8,128)(2,1)} %bitcast.56), custom_call_target="tpu_custom_call" | custom-call | flops 2818572288 | bytes 25690112 | tf_op jit(solution)/shard_map/mlp/pallas_call | solution.py:71
  132.5 0.8 slice.35
  133.3 4.9 %collective-permute-done.8.refs_1_ = bf16[64,7168]{1,0:T(8,128)(2,1)} collective-permute-done((bf16[64,7168]{1,0:T(8,128)(2,1)}, bf16[64,7168]{1,0:T(8,128)(2,1)}, u32[]{:S(2)}, u32[]{:S(2)}) %collective-permute-start.8) | collective-permute-done | bytes 917536 | tf_op jit(solution)/shard_map/ppermute | solution.py:265
  138.1 5.3 %collective-permute-start.5 = (bf16[32,7168]{1,0:T(8,128)(2,1)}, bf16[32,7168]{1,0:T(8,128)(2,1)}, u32[]{:S(2)}, u32[]{:S(2)}) collective-permute-start(bf16[32,7168]{1,0:T(8,128)(2,1)} %slice.35), channel_id=1, source_target_pairs={{0,4},{1,5},{4,8},{5,9},{8,12},{9,13},{12,14},{13,15},{14,10},{15,... | collective-permute-start | bytes 1376264 | tf_op jit(solution)/shard_map/ppermute | solution.py:266
  143.4 1.8 slice.36
  145.3 0.5 collective-permute-start.15
  145.8 0.3 copy-done.9
  146.4 17.5 %mlp.9 = (bf16[64,7168]{1,0:T(8,128)(2,1)}, bf16[64,7168]{1,0:T(8,128)(2,1)}, bf16[64,7168]{1,0:T(8,128)(2,1)}, bf16[64,7168]{1,0:T(8,128)(2,1)}) custom-call(bf16[64,7168]{1,0:T(8,128)(2,1)} %copy-done.4, bf16[64,7168]{1,0:T(8,128)(2,1)} %collective-permute-done.6.refs_1_, bf16[64,7168]{1,0:T(8,128)(2,1)} %copy-done.9, bf16[64,7168]{1,0:T(8,128)(2,1)} %copy-done.11, ...), custom_call_target="tpu_custom_call" | custom-call | flops 5637144576 | bytes 29360128 | tf_op jit(solution)/shard_map/mlp/pallas_call | solution.py:71
  163.9 6.5 %all-to-all-start = ((bf16[32,64,576]{2,1,0:T(8,128)(2,1)}), bf16[32,64,576]{2,1,0:T(8,128)(2,1)S(1)}, u32[]{:S(2)}, u32[]{:S(2)}) async-start(bf16[32,64,576]{2,1,0:T(8,128)(2,1)} %ship.1), calls=%async_computation | async-start | bytes 5242880 | tf_op jit(solution)/shard_map/all_to_all | solution.py:270
  170.6 0.4 collective-permute-start.10
  171.1 17.4 %mlp.8 = (bf16[64,7168]{1,0:T(8,128)(2,1)}, bf16[64,7168]{1,0:T(8,128)(2,1)}, bf16[64,7168]{1,0:T(8,128)(2,1)}, bf16[64,7168]{1,0:T(8,128)(2,1)}) custom-call(bf16[64,7168]{1,0:T(8,128)(2,1)} %collective-permute-done.3.refs_0_, bf16[64,7168]{1,0:T(8,128)(2,1)} %collective-permute-done.7.refs_1_, bf16[64,7168]{1,0:T(8,128)(2,1)} %collective-permute-done.18.refs_2_, ...), custom_call_target="tpu_custom_call" | custom-call | flops 5637144576 | bytes 29360128 | tf_op jit(solution)/shard_map/mlp/pallas_call | solution.py:71
  188.5 0.4 collective-permute-start.24
  189.3 0.4 copy-done.14
  189.7 12.9 %mlp.6 = (bf16[32,7168]{1,0:T(8,128)(2,1)}, bf16[32,7168]{1,0:T(8,128)(2,1)}, bf16[32,7168]{1,0:T(8,128)(2,1)}, bf16[32,7168]{1,0:T(8,128)(2,1)}) custom-call(bf16[32,7168]{1,0:T(8,128)(2,1)} %collective-permute-done.5.refs_0_, bf16[32,7168]{1,0:T(8,128)(2,1)} %collective-permute-done.9.refs_1_, bf16[32,7168]{1,0:T(8,128)(2,1)} %copy-done.13, ...), custom_call_target="tpu_custom_call" | custom-call | flops 2818572288 | bytes 25690112 | tf_op jit(solution)/shard_map/mlp/pallas_call | solution.py:71
  202.9 17.7 %mlp.7 = (bf16[64,7168]{1,0:T(8,128)(2,1)}, bf16[64,7168]{1,0:T(8,128)(2,1)}, bf16[64,7168]{1,0:T(8,128)(2,1)}, bf16[64,7168]{1,0:T(8,128)(2,1)}) custom-call(bf16[64,7168]{1,0:T(8,128)(2,1)} %copy-done.1, bf16[64,7168]{1,0:T(8,128)(2,1)} %collective-permute-done.8.refs_1_, bf16[64,7168]{1,0:T(8,128)(2,1)} %collective-permute-done.14.refs_2_, ...), custom_call_target="tpu_custom_call" | custom-call | flops 5637144576 | bytes 29360128 | tf_op jit(solution)/shard_map/mlp/pallas_call | solution.py:71
  220.6 0.4 collective-permute-start.16
  221.3 2.5 collective-permute-done.26
  223.8 0.5 collective-permute-start.13
  224.7 12.6 %collective-permute-done.13 = bf16[32,7168]{1,0:T(8,128)(2,1)S(1)} collective-permute-done((bf16[32,7168]{1,0:T(8,128)(2,1)S(1)}, bf16[32,7168]{1,0:T(8,128)(2,1)S(1)}, u32[]{:S(2)}, u32[]{:S(2)}) %collective-permute-start.13) | collective-permute-done | bytes 458784 | tf_op jit(solution)/shard_map/ppermute | solution.py:291
  237.2 2.4 collective-permute-start.27
  239.6 0.3 add_convert_fusion.11
  240.1 9.9 %collective-permute-done.27 = bf16[32,7168]{1,0:T(8,128)(2,1)S(1)} collective-permute-done((bf16[32,7168]{1,0:T(8,128)(2,1)S(1)}, bf16[32,7168]{1,0:T(8,128)(2,1)S(1)}, u32[]{:S(2)}, u32[]{:S(2)}) %collective-permute-start.27) | collective-permute-done | bytes 458784 | tf_op jit(solution)/shard_map/ppermute | solution.py:292
  250.0 1.7 collective-permute-start.17
  251.8 0.3 add_convert_fusion.5
  252.2 19.6 %collective-permute-done.17 = bf16[64,7168]{1,0:T(8,128)(2,1)S(1)} collective-permute-done((bf16[64,7168]{1,0:T(8,128)(2,1)S(1)}, bf16[64,7168]{1,0:T(8,128)(2,1)S(1)}, u32[]{:S(2)}, u32[]{:S(2)}) %collective-permute-start.17) | collective-permute-done | bytes 917536 | tf_op jit(solution)/shard_map/ppermute | solution.py:291
  271.8 1.7 collective-permute-start.29
  273.6 0.4 add_convert_fusion.9
  274.3 18.3 %collective-permute-done.29 = bf16[64,7168]{1,0:T(8,128)(2,1)S(1)} collective-permute-done((bf16[64,7168]{1,0:T(8,128)(2,1)S(1)}, bf16[64,7168]{1,0:T(8,128)(2,1)S(1)}, u32[]{:S(2)}, u32[]{:S(2)}) %collective-permute-start.29) | collective-permute-done | bytes 917536 | tf_op jit(solution)/shard_map/ppermute | solution.py:292
  292.7 0.4 add_convert_fusion.3
  293.1 1.5 collective-permute-start.31
  294.6 1.3 add_convert_fusion.7
  296.0 0.6 collective-permute-start.25
  296.6 16.5 %collective-permute-done.31 = bf16[64,7168]{1,0:T(8,128)(2,1)S(1)} collective-permute-done((bf16[64,7168]{1,0:T(8,128)(2,1)S(1)}, bf16[64,7168]{1,0:T(8,128)(2,1)S(1)}, u32[]{:S(2)}, u32[]{:S(2)}) %collective-permute-start.31) | collective-permute-done | bytes 917536 | tf_op jit(solution)/shard_map/ppermute | solution.py:292
  313.1 1.3 add_convert_fusion.1
  314.4 1.2 collective-permute-start.33
  316.1 0.7 copy.38.own_ref
  317.0 0.6 select_reduce_fusion.2.order_ref
  317.6 0.6 convert_reduce_fusion.start_ref
  318.3 1.5 copy-done
  319.7 24.5 %attend.1 = bf16[32,64,512]{2,1,0:T(8,128)(2,1)} custom-call(s32[32]{0:T(128)} %select_reduce_fusion.2.order_ref, s32[33]{0:T(128)} %convert_reduce_fusion.start_ref, s32[32]{0:T(128)} %copy-done.26, bf16[32,64,576]{2,1,0:T(8,128)(2,1)} %query_ref.1, bf16[32,1,576]{2,1,0:T(2,128)(2,1)} %copy.38.own_ref, bf16[32,64,576]{2,1,0:T(8,128)(2,1)} %copy-done), custom_call_target="tpu_custom_call" | custom-call | flops 301989888 | bytes 6815744 | tf_op jit(solution)/shard_map/attend/pallas_call | solution.py:160
  344.3 2.3 add_convert_fusion
  346.6 1.0 fusion.21
  (149 shorter events, 4.1 us)
Async XLA Ops:
  0.7 26.9 %copy-start.42 = (u32[32]{0:T(128)S(1)}, u32[32]{0:T(128)}, u32[]{:S(2)}) copy-start(u32[32]{0:T(128)} %constant.218) | copy-start | bytes 388
  0.7 24.8 %copy-start.24 = (s32[32,8]{0,1:T(8,128)S(1)}, s32[32,8]{0,1:T(8,128)}, u32[]{:S(2)}) copy-start(s32[32,8]{0,1:T(8,128)} %param.25) | copy-start | bytes 3076
  0.7 24.8 %copy-start.23 = (s32[32,8]{0,1:T(8,128)S(1)}, s32[32,8]{0,1:T(8,128)}, u32[]{:S(2)}) copy-start(s32[32,8]{0,1:T(8,128)} %param.26) | copy-start | bytes 3076
  0.7 24.8 %copy-start.22 = (s32[32,8]{0,1:T(8,128)S(1)}, s32[32,8]{0,1:T(8,128)}, u32[]{:S(2)}) copy-start(s32[32,8]{0,1:T(8,128)} %param.28) | copy-start | bytes 3076
  0.7 24.8 %copy-start.21 = (s32[32,8]{0,1:T(8,128)S(1)}, s32[32,8]{0,1:T(8,128)}, u32[]{:S(2)}) copy-start(s32[32,8]{0,1:T(8,128)} %param.29) | copy-start | bytes 3076
  0.7 25.0 %copy-start.35 = (s32[16]{0:T(128)S(1)}, s32[16]{0:T(128)}, u32[]{:S(2)}) copy-start(s32[16]{0:T(128)} %param.35) | copy-start | bytes 196
  0.7 25.2 %copy-start.37 = (s32[16]{0:T(128)S(1)}, s32[16]{0:T(128)}, u32[]{:S(2)}) copy-start(s32[16]{0:T(128)} %param.36) | copy-start | bytes 196
  0.7 25.2 %copy-start.36 = (s32[16]{0:T(128)S(1)}, s32[16]{0:T(128)}, u32[]{:S(2)}) copy-start(s32[16]{0:T(128)} %param.37) | copy-start | bytes 196
  2.9 104.8 %copy-start.2 = (bf16[64,7168]{1,0:T(8,128)(2,1)}, bf16[64,7168]{1,0:T(8,128)(2,1)S(1)}, u32[]{:S(2)}) copy-start(bf16[64,7168]{1,0:T(8,128)(2,1)S(1)} %constant_dynamic-update-slice_fusion.refs_0_) | copy-start | bytes 2752516
  2.9 22.1 %collective-permute-start.2 = (bf16[64,7168]{1,0:T(8,128)(2,1)S(1)}, bf16[64,7168]{1,0:T(8,128)(2,1)S(1)}, u32[]{:S(2)}, u32[]{:S(2)}) collective-permute-start(bf16[64,7168]{1,0:T(8,128)(2,1)S(1)} %constant_dynamic-update-slice_fusion.refs_0_), channel_id=1, source_target_pairs={{0,4},{1,5},{4,8},{5,9},{8,12},{9,13},{12,14},{13,15},{14,10},{15,... | collective-permute-start | bytes 2752520 | tf_op jit(solution)/shard_map/ppermute | solution.py:264
  3.4 22.5 %collective-permute-start.6 = (bf16[64,7168]{1,0:T(8,128)(2,1)S(1)}, bf16[64,7168]{1,0:T(8,128)(2,1)}, u32[]{:S(2)}, u32[]{:S(2)}) collective-permute-start(bf16[64,7168]{1,0:T(8,128)(2,1)S(1)} %constant_dynamic-update-slice_fusion.refs_0_), channel_id=1, source_target_pairs={{4,0},{5,1},{8,4},{9,5},{12,8},{13,9},{14,12},{15,13},{10,14},{11,... | collective-permute-start | bytes 2752520 | tf_op jit(solution)/shard_map/ppermute | solution.py:265
  5.0 103.9 %collective-permute-start = (bf16[64,7168]{1,0:T(8,128)(2,1)S(1)}, bf16[64,7168]{1,0:T(8,128)(2,1)}, u32[]{:S(2)}, u32[]{:S(2)}) collective-permute-start(bf16[64,7168]{1,0:T(8,128)(2,1)S(1)} %constant_dynamic-update-slice_fusion.refs_0_), channel_id=1, source_target_pairs={{0,1},{1,0},{2,3},{3,2},{4,5},{5,4},{6,7},{7,6},{8,9},{9,8},{10,11... | collective-permute-start | bytes 2752520 | tf_op jit(solution)/shard_map/ppermute | solution.py:275
  25.1 83.3 %copy-start.4 = (bf16[64,7168]{1,0:T(8,128)(2,1)}, bf16[64,7168]{1,0:T(8,128)(2,1)S(1)}, u32[]{:S(2)}) copy-start(bf16[64,7168]{1,0:T(8,128)(2,1)S(1)} %collective-permute-done.2.refs_0_) | copy-start | bytes 2752516
  25.1 61.7 %collective-permute-start.3 = (bf16[64,7168]{1,0:T(8,128)(2,1)S(1)}, bf16[64,7168]{1,0:T(8,128)(2,1)}, u32[]{:S(2)}, u32[]{:S(2)}) collective-permute-start(bf16[64,7168]{1,0:T(8,128)(2,1)S(1)} %collective-permute-done.2.refs_0_), channel_id=1, source_target_pairs={{0,4},{1,5},{4,8},{5,9},{8,12},{9,13},{12,14},{13,15},{14,10},{15,... | collective-permute-start | bytes 2752520 | tf_op jit(solution)/shard_map/ppermute | solution.py:264
  25.9 83.4 %collective-permute-start.7 = (bf16[64,7168]{1,0:T(8,128)(2,1)}, bf16[64,7168]{1,0:T(8,128)(2,1)}, u32[]{:S(2)}, u32[]{:S(2)}) collective-permute-start(bf16[64,7168]{1,0:T(8,128)(2,1)} %collective-permute-done.6.refs_1_), channel_id=1, source_target_pairs={{4,0},{5,1},{8,4},{9,5},{12,8},{13,9},{14,12},{15,13},{10,14},{11,... | collective-permute-start | bytes 2752520 | tf_op jit(solution)/shard_map/ppermute | solution.py:265
  86.8 31.8 %collective-permute-start.4 = (bf16[64,7168]{1,0:T(8,128)(2,1)}, bf16[64,7168]{1,0:T(8,128)(2,1)S(1)}, u32[]{:S(2)}, u32[]{:S(2)}) collective-permute-start(bf16[64,7168]{1,0:T(8,128)(2,1)} %collective-permute-done.3.refs_0_), channel_id=1, source_target_pairs={{0,4},{1,5},{4,8},{5,9},{8,12},{9,13},{12,14},{13,15},{14,10},{15,... | collective-permute-start | bytes 2752520 | tf_op jit(solution)/shard_map/ppermute | solution.py:264
  108.4 36.8 %collective-permute-start.22 = (bf16[64,7168]{1,0:T(8,128)(2,1)S(1)}, bf16[64,7168]{1,0:T(8,128)(2,1)S(1)}, u32[]{:S(2)}, u32[]{:S(2)}) collective-permute-start(bf16[64,7168]{1,0:T(8,128)(2,1)S(1)} %collective-permute-done.2.refs_0_), channel_id=1, source_target_pairs={{0,1},{1,0},{2,3},{3,2},{4,5},{5,4},{6,7},{7,6},{8,9},{9,8},{10,11... | collective-permute-start | bytes 2752520 | tf_op jit(solution)/shard_map/ppermute | solution.py:275
  108.8 36.5 %collective-permute-start.23 = (bf16[64,7168]{1,0:T(8,128)(2,1)}, bf16[64,7168]{1,0:T(8,128)(2,1)S(1)}, u32[]{:S(2)}, u32[]{:S(2)}) collective-permute-start(bf16[64,7168]{1,0:T(8,128)(2,1)} %collective-permute-done.6.refs_1_), channel_id=1, source_target_pairs={{0,1},{1,0},{2,3},{3,2},{4,5},{5,4},{6,7},{7,6},{8,9},{9,8},{10,11... | collective-permute-start | bytes 2752520 | tf_op jit(solution)/shard_map/ppermute | solution.py:275
  108.9 36.4 %collective-permute-start.18 = (bf16[64,7168]{1,0:T(8,128)(2,1)}, bf16[64,7168]{1,0:T(8,128)(2,1)}, u32[]{:S(2)}, u32[]{:S(2)}) collective-permute-start(bf16[64,7168]{1,0:T(8,128)(2,1)} %collective-permute-done.3.refs_0_), channel_id=1, source_target_pairs={{0,1},{1,0},{2,3},{3,2},{4,5},{5,4},{6,7},{7,6},{8,9},{9,8},{10,11... | collective-permute-start | bytes 2752520 | tf_op jit(solution)/shard_map/ppermute | solution.py:275
  109.3 28.8 %collective-permute-start.8 = (bf16[64,7168]{1,0:T(8,128)(2,1)}, bf16[64,7168]{1,0:T(8,128)(2,1)}, u32[]{:S(2)}, u32[]{:S(2)}) collective-permute-start(bf16[64,7168]{1,0:T(8,128)(2,1)} %collective-permute-done.7.refs_1_), channel_id=1, source_target_pairs={{4,0},{5,1},{8,4},{9,5},{12,8},{13,9},{14,12},{15,13},{10,14},{11,... | collective-permute-start | bytes 2752520 | tf_op jit(solution)/shard_map/ppermute | solution.py:265
  118.6 26.7 %copy-start.1 = (bf16[64,7168]{1,0:T(8,128)(2,1)}, bf16[64,7168]{1,0:T(8,128)(2,1)S(1)}, u32[]{:S(2)}) copy-start(bf16[64,7168]{1,0:T(8,128)(2,1)S(1)} %collective-permute-done.4.refs_0_) | copy-start | bytes 2752516
  118.6 51.8 %collective-permute-start.19 = (bf16[64,7168]{1,0:T(8,128)(2,1)}, bf16[64,7168]{1,0:T(8,128)(2,1)}, u32[]{:S(2)}, u32[]{:S(2)}) collective-permute-start(bf16[64,7168]{1,0:T(8,128)(2,1)} %collective-permute-done.7.refs_1_), channel_id=1, source_target_pairs={{0,1},{1,0},{2,3},{3,2},{4,5},{5,4},{6,7},{7,6},{8,9},{9,8},{10,11... | collective-permute-start | bytes 2752520 | tf_op jit(solution)/shard_map/ppermute | solution.py:275
  138.1 32.4 %collective-permute-start.5 = (bf16[32,7168]{1,0:T(8,128)(2,1)}, bf16[32,7168]{1,0:T(8,128)(2,1)}, u32[]{:S(2)}, u32[]{:S(2)}) collective-permute-start(bf16[32,7168]{1,0:T(8,128)(2,1)} %slice.35), channel_id=1, source_target_pairs={{0,4},{1,5},{4,8},{5,9},{8,12},{9,13},{12,14},{13,15},{14,10},{15,... | collective-permute-start | bytes 1376264 | tf_op jit(solution)/shard_map/ppermute | solution.py:266
  145.2 25.7 %collective-permute-start.9 = (bf16[32,7168]{1,0:T(8,128)(2,1)}, bf16[32,7168]{1,0:T(8,128)(2,1)}, u32[]{:S(2)}, u32[]{:S(2)}) collective-permute-start(bf16[32,7168]{1,0:T(8,128)(2,1)} %slice.36), channel_id=1, source_target_pairs={{4,0},{5,1},{8,4},{9,5},{12,8},{13,9},{14,12},{15,13},{10,14},{11,... | collective-permute-start | bytes 1376264 | tf_op jit(solution)/shard_map/ppermute | solution.py:267
  145.2 57.4 %collective-permute-start.14 = (bf16[64,7168]{1,0:T(8,128)(2,1)S(1)}, bf16[64,7168]{1,0:T(8,128)(2,1)}, u32[]{:S(2)}, u32[]{:S(2)}) collective-permute-start(bf16[64,7168]{1,0:T(8,128)(2,1)S(1)} %collective-permute-done.4.refs_0_), channel_id=1, source_target_pairs={{0,1},{1,0},{2,3},{3,2},{4,5},{5,4},{6,7},{7,6},{8,9},{9,8},{10,11... | collective-permute-start | bytes 2752520 | tf_op jit(solution)/shard_map/ppermute | solution.py:275
  145.3 57.6 %collective-permute-start.15 = (bf16[64,7168]{1,0:T(8,128)(2,1)}, bf16[64,7168]{1,0:T(8,128)(2,1)}, u32[]{:S(2)}, u32[]{:S(2)}) collective-permute-start(bf16[64,7168]{1,0:T(8,128)(2,1)} %collective-permute-done.8.refs_1_), channel_id=1, source_target_pairs={{0,1},{1,0},{2,3},{3,2},{4,5},{5,4},{6,7},{7,6},{8,9},{9,8},{10,11... | collective-permute-start | bytes 2752520 | tf_op jit(solution)/shard_map/ppermute | solution.py:275
  163.9 154.4 %all-to-all-start = ((bf16[32,64,576]{2,1,0:T(8,128)(2,1)}), bf16[32,64,576]{2,1,0:T(8,128)(2,1)S(1)}, u32[]{:S(2)}, u32[]{:S(2)}) async-start(bf16[32,64,576]{2,1,0:T(8,128)(2,1)} %ship.1), calls=%async_computation | async-start | bytes 5242880 | tf_op jit(solution)/shard_map/all_to_all | solution.py:270
  170.3 173.9 %collective-permute-start.1 = (bf16[64,7168]{1,0:T(8,128)(2,1)}, bf16[64,7168]{1,0:T(8,128)(2,1)}, u32[]{:S(2)}, u32[]{:S(2)}) collective-permute-start(bf16[64,7168]{1,0:T(8,128)(2,1)} %get-tuple-element.23), channel_id=1, source_target_pairs={{0,1},{1,0},{2,3},{3,2},{4,5},{5,4},{6,7},{7,6},{8,9},{9,8},{10,11... | collective-permute-start | bytes 2752520 | tf_op jit(solution)/shard_map/ppermute | solution.py:279
  170.6 18.0 %collective-permute-start.10 = (bf16[32,7168]{1,0:T(8,128)(2,1)}, bf16[32,7168]{1,0:T(8,128)(2,1)S(1)}, u32[]{:S(2)}, u32[]{:S(2)}) collective-permute-start(bf16[32,7168]{1,0:T(8,128)(2,1)} %collective-permute-done.5.refs_0_), channel_id=1, source_target_pairs={{0,1},{1,0},{2,3},{3,2},{4,5},{5,4},{6,7},{7,6},{8,9},{9,8},{10,11... | collective-permute-start | bytes 1376264 | tf_op jit(solution)/shard_map/ppermute | solution.py:275
  170.9 18.0 %collective-permute-start.11 = (bf16[32,7168]{1,0:T(8,128)(2,1)}, bf16[32,7168]{1,0:T(8,128)(2,1)S(1)}, u32[]{:S(2)}, u32[]{:S(2)}) collective-permute-start(bf16[32,7168]{1,0:T(8,128)(2,1)} %collective-permute-done.9.refs_1_), channel_id=1, source_target_pairs={{0,1},{1,0},{2,3},{3,2},{4,5},{5,4},{6,7},{7,6},{8,9},{9,8},{10,11... | collective-permute-start | bytes 1376264 | tf_op jit(solution)/shard_map/ppermute | solution.py:275
  188.5 106.1 %collective-permute-start.24 = (bf16[64,7168]{1,0:T(8,128)(2,1)}, bf16[64,7168]{1,0:T(8,128)(2,1)S(1)}, u32[]{:S(2)}, u32[]{:S(2)}) collective-permute-start(bf16[64,7168]{1,0:T(8,128)(2,1)} %get-tuple-element.31), channel_id=1, source_target_pairs={{0,1},{1,0},{2,3},{3,2},{4,5},{5,4},{6,7},{7,6},{8,9},{9,8},{10,11... | collective-permute-start | bytes 2752520 | tf_op jit(solution)/shard_map/ppermute | solution.py:279
  189.0 107.6 %collective-permute-start.32 = (bf16[64,7168]{1,0:T(8,128)(2,1)}, bf16[64,7168]{1,0:T(8,128)(2,1)S(1)}, u32[]{:S(2)}, u32[]{:S(2)}) collective-permute-start(bf16[64,7168]{1,0:T(8,128)(2,1)} %get-tuple-element.39), channel_id=1, source_target_pairs={{0,1},{1,0},{2,3},{3,2},{4,5},{5,4},{6,7},{7,6},{8,9},{9,8},{10,11... | collective-permute-start | bytes 2752520 | tf_op jit(solution)/shard_map/ppermute | solution.py:279
  202.6 18.4 %copy-start.41 = (bf16[32,7168]{1,0:T(8,128)(2,1)S(1)}, bf16[32,7168]{1,0:T(8,128)(2,1)}, u32[]{:S(2)}) copy-start(bf16[32,7168]{1,0:T(8,128)(2,1)} %get-tuple-element.33) | copy-start | bytes 1376260
  202.7 18.5 %copy-start.16 = (bf16[32,7168]{1,0:T(8,128)(2,1)S(1)}, bf16[32,7168]{1,0:T(8,128)(2,1)}, u32[]{:S(2)}) copy-start(bf16[32,7168]{1,0:T(8,128)(2,1)} %get-tuple-element.24) | copy-start | bytes 1376260
  202.7 18.5 %copy-start.34 = (f32[32]{0:T(128)S(1)}, f32[32]{0:T(128)}, u32[]{:S(2)}) copy-start(f32[32]{0:T(128)} %slice_bitcast_fusion.1) | copy-start | bytes 388
  202.7 21.6 %copy-start.15 = (bf16[32,7168]{1,0:T(8,128)(2,1)S(1)}, bf16[32,7168]{1,0:T(8,128)(2,1)}, u32[]{:S(2)}) copy-start(bf16[32,7168]{1,0:T(8,128)(2,1)} %get-tuple-element.32) | copy-start | bytes 1376260
  202.7 21.6 %copy-start.33 = (f32[32]{0:T(128)S(1)}, f32[32]{0:T(128)}, u32[]{:S(2)}) copy-start(f32[32]{0:T(128)} %slice_bitcast_fusion) | copy-start | bytes 388
  202.7 18.3 %collective-permute-start.12 = (bf16[32,7168]{1,0:T(8,128)(2,1)}, bf16[32,7168]{1,0:T(8,128)(2,1)S(1)}, u32[]{:S(2)}, u32[]{:S(2)}) collective-permute-start(bf16[32,7168]{1,0:T(8,128)(2,1)} %get-tuple-element.25), channel_id=1, source_target_pairs={{0,1},{1,0},{2,3},{3,2},{4,5},{5,4},{6,7},{7,6},{8,9},{9,8},{10,11... | collective-permute-start | bytes 1376264 | tf_op jit(solution)/shard_map/ppermute | solution.py:279
  220.6 19.1 %copy-start.12 = (bf16[64,7168]{1,0:T(8,128)(2,1)S(1)}, bf16[64,7168]{1,0:T(8,128)(2,1)}, u32[]{:S(2)}) copy-start(bf16[64,7168]{1,0:T(8,128)(2,1)} %get-tuple-element.26) | copy-start | bytes 2752516
  220.6 19.1 %copy-start.28 = (f32[64]{0:T(128)S(1)}, f32[64]{0:T(128)}, u32[]{:S(2)}) copy-start(f32[64]{0:T(128)} %get-tuple-element.56) | copy-start | bytes 772
  220.6 3.9 %collective-permute-start.16 = (bf16[64,7168]{1,0:T(8,128)(2,1)}, bf16[64,7168]{1,0:T(8,128)(2,1)S(1)}, u32[]{:S(2)}, u32[]{:S(2)}) collective-permute-start(bf16[64,7168]{1,0:T(8,128)(2,1)} %get-tuple-element.27), channel_id=1, source_target_pairs={{0,1},{1,0},{2,3},{3,2},{4,5},{5,4},{6,7},{7,6},{8,9},{9,8},{10,11... | collective-permute-start | bytes 2752520 | tf_op jit(solution)/shard_map/ppermute | solution.py:279
  221.0 2.8 collective-permute-start.26
  223.8 13.4 %collective-permute-start.13 = (bf16[32,7168]{1,0:T(8,128)(2,1)S(1)}, bf16[32,7168]{1,0:T(8,128)(2,1)S(1)}, u32[]{:S(2)}, u32[]{:S(2)}) collective-permute-start(bf16[32,7168]{1,0:T(8,128)(2,1)S(1)} %multiply_convert_fusion.1), channel_id=1, source_target_pairs={{0,4},{1,5},{4,8},{5,9},{8,12},{9,13},{12,14},{13,15},{14,10},{15,... | collective-permute-start | bytes 1376264 | tf_op jit(solution)/shard_map/ppermute | solution.py:291
  224.5 15.6 %copy-start.39 = (bf16[64,7168]{1,0:T(8,128)(2,1)S(1)}, bf16[64,7168]{1,0:T(8,128)(2,1)}, u32[]{:S(2)}) copy-start(bf16[64,7168]{1,0:T(8,128)(2,1)} %get-tuple-element.29) | copy-start | bytes 2752516
  224.5 27.3 %copy-start.10 = (bf16[64,7168]{1,0:T(8,128)(2,1)S(1)}, bf16[64,7168]{1,0:T(8,128)(2,1)}, u32[]{:S(2)}) copy-start(bf16[64,7168]{1,0:T(8,128)(2,1)} %get-tuple-element.34) | copy-start | bytes 2752516
  224.5 27.3 %copy-start.27 = (f32[64]{0:T(128)S(1)}, f32[64]{0:T(128)}, u32[]{:S(2)}) copy-start(f32[64]{0:T(128)} %get-tuple-element.52) | copy-start | bytes 772
  224.5 15.5 %collective-permute-start.28 = (bf16[64,7168]{1,0:T(8,128)(2,1)S(1)}, bf16[64,7168]{1,0:T(8,128)(2,1)S(1)}, u32[]{:S(2)}, u32[]{:S(2)}) collective-permute-start(bf16[64,7168]{1,0:T(8,128)(2,1)S(1)} %copy-done.40), channel_id=1, source_target_pairs={{0,1},{1,0},{2,3},{3,2},{4,5},{5,4},{6,7},{7,6},{8,9},{9,8},{10,11... | collective-permute-start | bytes 2752520 | tf_op jit(solution)/shard_map/ppermute | solution.py:279
  237.2 12.8 %collective-permute-start.27 = (bf16[32,7168]{1,0:T(8,128)(2,1)S(1)}, bf16[32,7168]{1,0:T(8,128)(2,1)S(1)}, u32[]{:S(2)}, u32[]{:S(2)}) collective-permute-start(bf16[32,7168]{1,0:T(8,128)(2,1)S(1)} %multiply_convert_fusion), channel_id=1, source_target_pairs={{4,0},{5,1},{8,4},{9,5},{12,8},{13,9},{14,12},{15,13},{10,14},{11,... | collective-permute-start | bytes 1376264 | tf_op jit(solution)/shard_map/ppermute | solution.py:292
  240.0 33.6 %copy-start.8 = (bf16[64,7168]{1,0:T(8,128)(2,1)S(1)}, bf16[64,7168]{1,0:T(8,128)(2,1)}, u32[]{:S(2)}) copy-start(bf16[64,7168]{1,0:T(8,128)(2,1)} %get-tuple-element.28) | copy-start | bytes 2752516
  240.0 33.6 %copy-start.32 = (f32[64]{0:T(128)S(1)}, f32[64]{0:T(128)}, u32[]{:S(2)}) copy-start(f32[64]{0:T(128)} %get-tuple-element.55) | copy-start | bytes 772
  240.0 12.1 %collective-permute-start.20 = (bf16[64,7168]{1,0:T(8,128)(2,1)S(1)}, bf16[64,7168]{1,0:T(8,128)(2,1)S(1)}, u32[]{:S(2)}, u32[]{:S(2)}) collective-permute-start(bf16[64,7168]{1,0:T(8,128)(2,1)S(1)} %copy-done.39), channel_id=1, source_target_pairs={{0,1},{1,0},{2,3},{3,2},{4,5},{5,4},{6,7},{7,6},{8,9},{9,8},{10,11... | collective-permute-start | bytes 2752520 | tf_op jit(solution)/shard_map/ppermute | solution.py:279
  250.0 21.8 %collective-permute-start.17 = (bf16[64,7168]{1,0:T(8,128)(2,1)S(1)}, bf16[64,7168]{1,0:T(8,128)(2,1)S(1)}, u32[]{:S(2)}, u32[]{:S(2)}) collective-permute-start(bf16[64,7168]{1,0:T(8,128)(2,1)S(1)} %add_convert_fusion.11), channel_id=1, source_target_pairs={{0,4},{1,5},{4,8},{5,9},{8,12},{9,13},{12,14},{13,15},{14,10},{15,... | collective-permute-start | bytes 2752520 | tf_op jit(solution)/shard_map/ppermute | solution.py:291
  252.1 21.9 %collective-permute-start.30 = (bf16[64,7168]{1,0:T(8,128)(2,1)S(1)}, bf16[64,7168]{1,0:T(8,128)(2,1)S(1)}, u32[]{:S(2)}, u32[]{:S(2)}) collective-permute-start(bf16[64,7168]{1,0:T(8,128)(2,1)S(1)} %copy-done.38), channel_id=1, source_target_pairs={{0,1},{1,0},{2,3},{3,2},{4,5},{5,4},{6,7},{7,6},{8,9},{9,8},{10,11... | collective-permute-start | bytes 2752520 | tf_op jit(solution)/shard_map/ppermute | solution.py:279
  271.8 20.8 %collective-permute-start.29 = (bf16[64,7168]{1,0:T(8,128)(2,1)S(1)}, bf16[64,7168]{1,0:T(8,128)(2,1)S(1)}, u32[]{:S(2)}, u32[]{:S(2)}) collective-permute-start(bf16[64,7168]{1,0:T(8,128)(2,1)S(1)} %add_convert_fusion.5), channel_id=1, source_target_pairs={{4,0},{5,1},{8,4},{9,5},{12,8},{13,9},{14,12},{15,13},{10,14},{11,... | collective-permute-start | bytes 2752520 | tf_op jit(solution)/shard_map/ppermute | solution.py:292
  273.6 19.1 %copy-start.7 = (bf16[64,7168]{1,0:T(8,128)(2,1)S(1)}, bf16[64,7168]{1,0:T(8,128)(2,1)}, u32[]{:S(2)}) copy-start(bf16[64,7168]{1,0:T(8,128)(2,1)} %get-tuple-element.36) | copy-start | bytes 2752516
  273.6 19.1 %copy-start.31 = (f32[64]{0:T(128)S(1)}, f32[64]{0:T(128)}, u32[]{:S(2)}) copy-start(f32[64]{0:T(128)} %get-tuple-element.51) | copy-start | bytes 772
  274.0 20.6 %collective-permute-start.21 = (bf16[64,7168]{1,0:T(8,128)(2,1)S(1)}, bf16[64,7168]{1,0:T(8,128)(2,1)S(1)}, u32[]{:S(2)}, u32[]{:S(2)}) collective-permute-start(bf16[64,7168]{1,0:T(8,128)(2,1)S(1)} %add_convert_fusion.9), channel_id=1, source_target_pairs={{0,4},{1,5},{4,8},{5,9},{8,12},{9,13},{12,14},{13,15},{14,10},{15,... | collective-permute-start | bytes 2752520 | tf_op jit(solution)/shard_map/ppermute | solution.py:291
  293.1 20.0 %collective-permute-start.31 = (bf16[64,7168]{1,0:T(8,128)(2,1)S(1)}, bf16[64,7168]{1,0:T(8,128)(2,1)S(1)}, u32[]{:S(2)}, u32[]{:S(2)}) collective-permute-start(bf16[64,7168]{1,0:T(8,128)(2,1)S(1)} %add_convert_fusion.3), channel_id=1, source_target_pairs={{4,0},{5,1},{8,4},{9,5},{12,8},{13,9},{14,12},{15,13},{10,14},{11,... | collective-permute-start | bytes 2752520 | tf_op jit(solution)/shard_map/ppermute | solution.py:292
  294.6 18.4 %copy-start.5 = (bf16[64,7168]{1,0:T(8,128)(2,1)S(1)}, bf16[64,7168]{1,0:T(8,128)(2,1)}, u32[]{:S(2)}) copy-start(bf16[64,7168]{1,0:T(8,128)(2,1)} %get-tuple-element.38) | copy-start | bytes 2752516
  294.6 18.4 %copy-start.29 = (f32[64]{0:T(128)S(1)}, f32[64]{0:T(128)}, u32[]{:S(2)}) copy-start(f32[64]{0:T(128)} %get-tuple-element.50) | copy-start | bytes 772
  296.0 48.3 %collective-permute-start.25 = (bf16[64,7168]{1,0:T(8,128)(2,1)}, bf16[64,7168]{1,0:T(8,128)(2,1)}, u32[]{:S(2)}, u32[]{:S(2)}) collective-permute-start(bf16[64,7168]{1,0:T(8,128)(2,1)} %add_convert_fusion.7), channel_id=1, source_target_pairs={{0,4},{1,5},{4,8},{5,9},{8,12},{9,13},{12,14},{13,15},{14,10},{15,... | collective-permute-start | bytes 2752520 | tf_op jit(solution)/shard_map/ppermute | solution.py:300
  314.4 29.8 %collective-permute-start.33 = (bf16[64,7168]{1,0:T(8,128)(2,1)}, bf16[64,7168]{1,0:T(8,128)(2,1)}, u32[]{:S(2)}, u32[]{:S(2)}) collective-permute-start(bf16[64,7168]{1,0:T(8,128)(2,1)} %add_convert_fusion.1), channel_id=1, source_target_pairs={{4,0},{5,1},{8,4},{9,5},{12,8},{13,9},{14,12},{15,13},{10,14},{11,... | collective-permute-start | bytes 2752520 | tf_op jit(solution)/shard_map/ppermute | solution.py:301
  318.2 26.0 %copy-start.3 = (bf16[64,7168]{1,0:T(8,128)(2,1)S(1)}, bf16[64,7168]{1,0:T(8,128)(2,1)}, u32[]{:S(2)}) copy-start(bf16[64,7168]{1,0:T(8,128)(2,1)} %get-tuple-element.22) | copy-start | bytes 2752516
  318.2 26.0 %copy-start.25 = (f32[64]{0:T(128)S(1)}, f32[64]{0:T(128)}, u32[]{:S(2)}) copy-start(f32[64]{0:T(128)} %get-tuple-element.49) | copy-start | bytes 772
  (15 other events, 50.9 us)

commit v2 on v1

v2 whole, which is shorter than its diff:
```python
import functools

import jax
import jax.numpy as jnp
import numpy as np
from jax import lax
from jax.experimental import pallas as pl
from jax.experimental.pallas import tpu as pltpu
from jax.sharding import PartitionSpec as P

KV = 512
CAPC = 2

softmax_scale = 192.0 ** (-0.5)
gate_unit = 65536.0
AXIS = "expert"
WAIT_STEP = 1
VMEM_LIMIT = 16 << 20


def mlp_kernel(sizes, tile, *refs):
    count = len(sizes)
    x_refs = refs[:count]
    up_hbm, down_hbm, mine_hbm, other_hbm = refs[count : count + 4]
    rows_ref, up_ref, down_ref, part_ref, x_sems, up_sems, down_sems, out_sems = refs[count + 4 :]
    width = up_hbm.shape[0]
    half = down_hbm.shape[0]
    tiles = width // tile
    size = mine_hbm.shape[0]
    spans = [pl.ds(k * tile, tile) for k in range(tiles)]
    starts = [sum(sizes[:c]) for c in range(count)]
    x_copies = [
        [
            pltpu.make_async_copy(
                x_refs[c].at[:, spans[k]],
                rows_ref.at[pl.ds(starts[c], sizes[c]), spans[k]],
                x_sems.at[c, k],
            )
            for c in range(count)
        ]
        for k in range(tiles)
    ]
    up_copies = [
        pltpu.make_async_copy(up_hbm.at[s], up_ref.at[s], up_sems.at[k])
        for k, s in enumerate(spans)
    ]
    down_copies = [
        pltpu.make_async_copy(down_hbm.at[:, s], down_ref.at[:, s], down_sems.at[k])
        for k, s in enumerate(spans)
    ]
    for k in range(tiles):
        for copy in x_copies[k]:
            copy.start()
        up_copies[k].start()
    for copy in down_copies:
        copy.start()
    merged = None
    for k in range(tiles):
        for copy in x_copies[k]:
            copy.wait()
        up_copies[k].wait()
        cols = slice(k * tile, (k + 1) * tile)
        part = jnp.dot(rows_ref[:, cols], up_ref[cols, :], preferred_element_type=jnp.float32)
        merged = part if merged is None else merged + part
    hidden = (jax.nn.silu(merged[:, :half]) * merged[:, half:]).astype(jnp.bfloat16)
    out_copies = []
    for n, s in enumerate(spans):
        down_copies[n].wait()
        cols = slice(n * tile, (n + 1) * tile)
        part = jnp.dot(hidden, down_ref[:, cols], preferred_element_type=jnp.float32)
        part_ref[:, cols] = part.astype(jnp.bfloat16)
        for c, target in enumerate((mine_hbm, other_hbm)):
            copy = pltpu.make_async_copy(
                part_ref.at[pl.ds(c * size, size), s], target.at[:, s], out_sems.at[c, n]
            )
            copy.start()
            out_copies.append(copy)
    for copy in out_copies:
        copy.wait()


def mlp(mine, other, gate_up, down_proj, tile=1024):
    chunks = mine + other
    width, both = gate_up.shape
    half = down_proj.shape[0]
    tile = tile if width % tile == 0 else width
    tiles = width // tile
    sizes = tuple(c.shape[0] for c in chunks)
    rows = sum(sizes)
    anywhere = pl.BlockSpec(memory_space=pltpu.HBM)
    dma = pltpu.SemaphoreType.DMA
    return pl.pallas_call(
        functools.partial(mlp_kernel, sizes, tile),
        in_specs=[anywhere] * (len(chunks) + 2),
        out_specs=[anywhere, anywhere],
        out_shape=[jax.ShapeDtypeStruct((rows // 2, width), jnp.bfloat16)] * 2,
        scratch_shapes=[
            pltpu.VMEM((rows, width), jnp.bfloat16),
            pltpu.VMEM((width, both), jnp.bfloat16),
            pltpu.VMEM((half, width), jnp.bfloat16),
            pltpu.VMEM((rows, width), jnp.bfloat16),
            dma((len(chunks), tiles)),
            dma((tiles,)),
            dma((tiles,)),
            dma((2, tiles)),
        ],
        compiler_params=pltpu.CompilerParams(vmem_limit_bytes=44 << 20),
        cost_estimate=pl.CostEstimate(
            flops=6 * rows * width * half,
            bytes_accessed=6 * width * half + 4 * rows * width,
            transcendentals=rows * half,
        ),
        name="mlp",
    )(*chunks, gate_up, down_proj)


def ship_kernel(source_ref, block_ref, out_ref):
    for i in range(out_ref.shape[0]):
        out_ref[i] = block_ref[source_ref[i]]


def ship_blocks(latents, source):
    slots = source.shape[0]
    resident = pl.BlockSpec(memory_space=pltpu.VMEM)
    return pl.pallas_call(
        ship_kernel,
        in_specs=[pl.BlockSpec(memory_space=pltpu.SMEM), resident],
        out_specs=resident,
        out_shape=jax.ShapeDtypeStruct((slots,) + latents.shape[1:], latents.dtype),
        compiler_params=pltpu.CompilerParams(vmem_limit_bytes=16 << 20),
        cost_estimate=pl.CostEstimate(
            flops=0, bytes_accessed=6 * latents.size, transcendentals=0
        ),
        name="ship",
    )(source, latents)


def attend_kernel(order_ref, start_ref, length_ref, query_ref, own_ref, latent_ref, out_ref):
    row = pl.program_id(0)
    query = query_ref[0]
    own = own_ref[0].astype(jnp.float32)
    own_score = (
        jnp.sum(query.astype(jnp.float32) * own, axis=1, keepdims=True) * softmax_scale
    )
    heads = query.shape[0]
    block = latent_ref.shape[1]

    def step(j, state):
        top, total, value = state
        slot = order_ref[j]
        latent = latent_ref[slot]
        scores = (
            lax.dot_general(
                query, latent, (((1,), (1,)), ((), ())), preferred_element_type=jnp.float32
            )
            * softmax_scale
        )
        inside = lax.broadcasted_iota(jnp.int32, (heads, block), 1) < length_ref[slot]
        span_max = jnp.max(jnp.where(inside, scores, -jnp.inf), axis=1, keepdims=True)
        weights = jnp.where(inside, jnp.exp(scores - span_max), 0.0)
        span_total = jnp.sum(weights, axis=1, keepdims=True)
        span_value = jnp.dot(
            weights.astype(jnp.bfloat16), latent[:, :KV], preferred_element_type=jnp.float32
        )
        higher = jnp.maximum(top, span_max)
        old = jnp.exp(top - higher)
        new = jnp.exp(span_max - higher)
        return (higher, old * total + new * span_total, old * value + new * span_value)

    state = (
        own_score,
        jnp.ones((heads, 1), jnp.float32),
        jnp.broadcast_to(own[:, :KV], (heads, KV)),
    )
    top, total, value = lax.fori_loop(start_ref[row], start_ref[row + 1], step, state)
    out_ref[0] = (value / total).astype(jnp.bfloat16)


def attend(order, start, lengths, queries, own_latent, latents, first, rows):
    _, heads, width = queries.shape
    slots, block, _ = latents.shape
    own_latent = own_latent.reshape(own_latent.shape[0], 1, width)
    return pl.pallas_call(
        attend_kernel,
        grid_spec=pltpu.PrefetchScalarGridSpec(
            num_scalar_prefetch=3,
            grid=(rows,),
            in_specs=[
                pl.BlockSpec((1, heads, width), lambda i, *_: (i + first, 0, 0)),
                pl.BlockSpec((1, 1, width), lambda i, *_: (i + first, 0, 0)),
                pl.BlockSpec((slots, block, width), lambda i, *_: (0, 0, 0)),
            ],
            out_specs=pl.BlockSpec((1, heads, KV), lambda i, *_: (i, 0, 0)),
        ),
        out_shape=jax.ShapeDtypeStruct((rows, heads, KV), jnp.bfloat16),
        compiler_params=pltpu.CompilerParams(vmem_limit_bytes=VMEM_LIMIT),
        cost_estimate=pl.CostEstimate(
            flops=2 * slots * heads * block * width,
            bytes_accessed=2 * (rows * heads * (width + KV) + slots * block * width),
            transcendentals=slots * heads * block,
        ),
        name="attend",
    )(order, start[first : first + rows + 1], lengths, queries, own_latent, latents)


def dense_gates(experts, gates, expert_count):
    named = experts[:, :, None] == jnp.arange(expert_count)[None, None, :]
    return jnp.sum(jnp.where(named, gates[:, :, None], 0), axis=1)


def per_device(
    prefill_tokens,
    prefill_experts,
    prefill_gates,
    decode_rows,
    decode_experts,
    decode_gates,
    w_gate_up,
    w_down,
    queries,
    own_latent,
    latents,
    span_owner,
    span_request,
    span_length,
):
    devices = lax.axis_size(AXIS)
    chips = devices // 2
    half = chips // 2
    gate_up = w_gate_up[0]
    down_proj = w_down[0]
    prefill_count = prefill_tokens.shape[0]
    decode_count = decode_rows.shape[0]
    row_count = prefill_count + decode_count
    split = prefill_count

    ring = list(range(0, chips, 2)) + list(range(1, chips, 2))[::-1]
    place_of = np.zeros(chips, np.int32)
    for i, chip in enumerate(ring):
        place_of[chip] = i
    ahead = [
        (2 * ring[i] + c, 2 * ring[(i + 1) % chips] + c) for i in range(chips) for c in range(2)
    ]
    back = [(b, a) for a, b in ahead]
    across = [(i, i ^ 1) for i in range(devices)]
    me = lax.axis_index(AXIS)
    my_chip = me // 2
    my_core = me % 2
    place = jnp.asarray(place_of)[my_chip]

    def device_at(shift):
        return 2 * jnp.asarray(np.array(ring, np.int32))[(place + shift + chips) % chips] + my_core

    span_count = span_owner.shape[0]
    block_rows = latents.shape[1]
    slots = devices * CAPC
    numbered = jnp.arange(span_count)
    earlier = (span_owner[None, :] == span_owner[:, None]) & (numbered[None, :] < numbered[:, None])
    span_rank = jnp.sum(earlier, axis=1)
    slot_of = span_owner * CAPC + span_rank
    placed = slot_of[None, :] == jnp.arange(slots)[:, None]
    source = jnp.sum(jnp.where(placed, numbered[None, :], 0), axis=1).astype(jnp.int32)
    codes = span_request * (block_rows + 1) + span_length
    slot_codes = jnp.sum(jnp.where(placed, codes[None, :], 0), axis=1).astype(jnp.int32)

    gates = jnp.concatenate(
        [
            dense_gates(prefill_experts, prefill_gates, chips),
            dense_gates(decode_experts, decode_gates, chips),
        ],
        axis=0,
    )
    small = jnp.concatenate(
        [jnp.repeat(gates.T, 2, axis=0), slot_codes.reshape(devices, CAPC)], axis=1
    ).astype(jnp.int32)
    small = lax.all_to_all(small, AXIS, split_axis=0, concat_axis=0, tiled=True)
    gate_table = small[:, :row_count].astype(jnp.float32) / gate_unit
    slot_codes = small[:, row_count:].reshape(-1)
    slot_length = slot_codes % (block_rows + 1)
    slot_request = slot_codes // (block_rows + 1)

    shipped = ship_blocks(latents, source)

    own_rows = jnp.concatenate([prefill_tokens, decode_rows], axis=0)
    own_other = lax.ppermute(own_rows, AXIS, across)
    a = lax.ppermute(own_rows, AXIS, ahead)
    b = lax.ppermute(own_rows, AXIS, back)
    a, b, shipped, gate_table = lax.optimization_barrier((a, b, shipped, gate_table))
    arrived = [(a, b)]
    parts = {}
    for s in range(1, half + 1):
        a, b = arrived[-1]
        if s < half:
            if s == half - 1:
                next_a = lax.ppermute(a[:split], AXIS, ahead)
                next_b = lax.ppermute(b[split:], AXIS, back)
                block_latents = lax.all_to_all(
                    shipped, AXIS, split_axis=0, concat_axis=0, tiled=True
                )
            else:
                next_a = lax.ppermute(a, AXIS, ahead)
                next_b = lax.ppermute(b, AXIS, back)
        mine = [a, b]
        other = [lax.ppermute(c, AXIS, across) for c in mine]
        if s == 1:
            mine = mine + [own_rows]
            other = other + [own_other]
        part, for_other = mlp(mine, other, gate_up, down_proj)
        if s < half:
            next_a, next_b, part, for_other, shipped = lax.optimization_barrier(
                (next_a, next_b, part, for_other, shipped)
            )
            arrived.append((next_a, next_b))
        parts[s] = (part, lax.ppermute(for_other, AXIS, across))

    def contribution(s, k):
        part, from_other = parts[max(s, 1)]
        size = split if s == half else row_count
        lo = 2 * size if s == 0 else k * size
        both = part[lo : lo + size].astype(jnp.float32) + from_other[lo : lo + size].astype(
            jnp.float32
        )
        both = both.astype(jnp.bfloat16).astype(jnp.float32)
        shift = (-s, s)[k] if s else 0
        weight = lax.dynamic_index_in_dim(gate_table, device_at(shift), 0, keepdims=False)
        if s == half:
            weight = (weight[:split], weight[split:])[k]
        return weight[:, None] * both

    key = jnp.where(slot_length > 0, slot_request, decode_count)
    index = jnp.arange(slots)
    before = (key[None, :] < key[:, None]) | (
        (key[None, :] == key[:, None]) & (index[None, :] < index[:, None])
    )
    position = jnp.sum(before, axis=1)
    order = jnp.sum(
        jnp.where(position[None, :] == index[:, None], index[None, :], 0), axis=1
    ).astype(jnp.int32)
    start = jnp.sum(key[None, :] < jnp.arange(decode_count + 1)[:, None], axis=1).astype(jnp.int32)
    first_rows = decode_count // 2

    up = contribution(half, 0).astype(jnp.bfloat16)
    down = contribution(half, 1).astype(jnp.bfloat16)
    for s in range(half - 1, -1, -1):
        up, down = lax.optimization_barrier((up, down))
        up = lax.ppermute(up, AXIS, ahead)
        down = lax.ppermute(down, AXIS, back)
        up, down = lax.optimization_barrier((up, down))
        if s == half - WAIT_STEP:
            up, down, block_latents = lax.optimization_barrier((up, down, block_latents))
        up = up.astype(jnp.float32)
        down = down.astype(jnp.float32)
        if s == half - 1:
            up = jnp.pad(up, ((0, row_count - split), (0, 0)))
            down = jnp.pad(down, ((split, 0), (0, 0)))
        if s:
            up = (up + contribution(s, 1)).astype(jnp.bfloat16)
            down = (down + contribution(s, 0)).astype(jnp.bfloat16)
        if s == 1:
            early = attend(
                order, start, slot_length, queries, own_latent, block_latents, 0, first_rows
            )
            up, down, early = lax.optimization_barrier((up, down, early))
            late = attend(
                order,
                start,
                slot_length,
                queries,
                own_latent,
                block_latents,
                first_rows,
                decode_count - first_rows,
            )
            context = jnp.concatenate([early, late], axis=0)
    out = (contribution(0, 0) + up + down).astype(jnp.bfloat16)
    prefill_out = out[:split]
    decode_out = out[split:]
    return (prefill_out, decode_out, context)


def solution(mesh):
    rows = P(("groups", "expert"), None)
    blocks = P(("groups", "expert"), None, None)
    line = P(("groups", "expert"))
    weights = P("expert", None, None)
    return jax.shard_map(
        per_device,
        mesh=mesh,
        in_specs=(rows,) * 6 + (weights, weights, blocks, rows, blocks, line, line, line),
        out_specs=(rows, rows, blocks),
        check_vma=False,
    )
```

time: 354 us -> 274 us (0.77)
  Pallas kernels: 120 us -> 58.1 us
  blocking collectives: 57.7 us -> 0 us
  waiting for transfers between devices: 91.3 us -> 134 us
  starting transfers between devices: 40.7 us -> 30.5 us
  other arithmetic: 10.8 us -> 18.9 us
    unnamed x1 -> x0, blocking collectives: 57.7 us -> none
    pallas_call x6 -> x5, Pallas kernels: 95.2 us -> 51.5 us  [the longest x4 50.8 us: mlp(): pl.pallas_call(functools.partial(mlp_kernel, sizes, tile), in_specs=[anyw...]
    ppermute x25 -> x21, waiting for transfers between devices: 91.3 us -> 119 us  [the longest x4 55 us: per_device(): up = lax.ppermute(up, AXIS, ahead)]
    pallas_call x1 -> x2, Pallas kernels: 24.5 us -> 6.55 us  [attend(): pl.pallas_call(attend_kernel, grid_spec=pltpu.PrefetchScalarGridSpec(num_...]
    ppermute x25 -> x21, starting transfers between devices: 32.2 us -> 17.2 us  [the longest x4 4.56 us: per_device(): down = lax.ppermute(down, AXIS, back)]
    all_to_all x1 -> x2, waiting for transfers between devices: 0.01 us -> 10.3 us  [the longest x1 10.3 us: per_device(): small = lax.all_to_all(small, AXIS, split_axis=0, concat_axis=0, tiled=True)]
    convert_element_type x10 -> x5, other arithmetic: 7.37 us -> 15.2 us  [the longest x3 12 us: per_device(): down = (down + contribution(s, 0)).astype(jnp.bfloat16)]
    unnamed x91 -> x41, local copies, waits for them, and re-layouts: 4.54 us -> 9.73 us
  transfers between devices with their start and end apart: 35 -> 31, of which waited for: 8 -> 20; matrix products, arithmetic and copies ran while one was open for 5% -> 7% of each run, Pallas kernels for 34% -> 21%
where the time goes in v2:
time: 274 us; the launch traced here: 270 us
  waiting for transfers between devices  134 us (49%)
  Pallas kernels  58.1 us (21%)
  starting transfers between devices  30.5 us (11%)
  other arithmetic  18.9 us (7%)
  local copies, waits for them, and re-layouts  16.1 us (6%)
  between operations  12.6 us (5%)
    ppermute x4, waiting for transfers between devices, per_device(): up = lax.ppermute(up, AXIS, ahead)  55 us
    pallas_call x4, Pallas kernels, mlp(): pl.pallas_call(functools.partial(mlp_kernel, sizes, tile), in_specs=[anyw...  50.8 us
    ppermute x1, waiting for transfers between devices, per_device(): next_a = lax.ppermute(a[:split], AXIS, ahead)  49.9 us
    convert_element_type x3, other arithmetic, per_device(): down = (down + contribution(s, 0)).astype(jnp.bfloat16)  12 us
    all_to_all x1, waiting for transfers between devices, per_device(): small = lax.all_to_all(small, AXIS, split_axis=0, concat_axis=0, tiled=True)  10.3 us
    unnamed x41, local copies, waits for them, and re-layouts  9.73 us
    ppermute x2, waiting for transfers between devices, per_device(): next_a = lax.ppermute(a, AXIS, ahead)  8.09 us
    pallas_call x2, Pallas kernels, attend(): pl.pallas_call(attend_kernel, grid_spec=pltpu.PrefetchScalarGridSpec(num_...  6.55 us
  transfers between devices with their start and end apart: 31, of which 20 were waited for; matrix products, arithmetic and copies ran while one was open for 7% of the time, Pallas kernels for 21%

profile of v2, /device:TPU:20, one launch (start us, length us, event | category | flops | bytes accessed | tf_op | source)
XLA Modules:
  0.0 270.2 jit_solution(14080580016753269452)
XLA Ops:
  0.7 1.1 constant_dynamic-update-slice_fusion.1
  1.8 1.1 constant_dynamic-update-slice_fusion.refs_2_
  3.4 1.6 collective-permute-start.1
  5.5 0.7 pad_add_fusion
  6.1 6.1 %all-to-all-start = ((s32[16,1,66]{2,1,0:T(1,128)}), s32[16,1,66]{2,1,0:T(1,128)S(1)}, u32[]{:S(2)}, u32[]{:S(2)}) async-start(s32[16,1,66]{2,1,0:T(1,128)} %bitcast.2), calls=%async_computation | async-start | bytes 16384 | tf_op jit(solution)/shard_map/all_to_all | solution.py:276
  12.4 1.3 copy-done.7
  13.7 0.7 ship.1
  14.5 1.5 copy-done.2
  16.0 10.3 %all-to-all-done = s32[16,1,66]{2,1,0:T(1,128)S(1)} async-done(((s32[16,1,66]{2,1,0:T(1,128)}), s32[16,1,66]{2,1,0:T(1,128)S(1)}, u32[]{:S(2)}, u32[]{:S(2)}) %all-to-all-start) | async-done | bytes 4256 | tf_op jit(solution)/shard_map/all_to_all | solution.py:276
  26.3 0.6 fusion.2
  26.9 0.5 collective-permute-start.5
  27.4 1.5 collective-permute-start.2
  28.9 0.6 collective-permute-start.3
  29.5 0.5 collective-permute-done.4.refs_3_
  30.0 0.9 collective-permute-done.5.refs_4_
  30.9 14.5 %mlp.4 = (bf16[192,7168]{1,0:T(8,128)(2,1)S(1)}, bf16[192,7168]{1,0:T(8,128)(2,1)}) custom-call(bf16[64,7168]{1,0:T(8,128)(2,1)S(1)} %collective-permute-done.refs_0_, bf16[64,7168]{1,0:T(8,128)(2,1)} %collective-permute-done.1.refs_1_, bf16[64,7168]{1,0:T(8,128)(2,1)S(1)} %constant_dynamic-update-slice_fusion.refs_2_, ...), custom_call_target="tpu_custom_call" | custom-call | flops 8455716864 | bytes 33030144 | tf_op jit(solution)/shard_map/mlp/pallas_call | solution.py:92
  45.4 1.5 copy-done.3
  46.9 2.8 %collective-permute-done.2.refs_0_ = bf16[64,7168]{1,0:T(8,128)(2,1)S(1)} collective-permute-done((bf16[64,7168]{1,0:T(8,128)(2,1)S(1)}, bf16[64,7168]{1,0:T(8,128)(2,1)S(1)}, u32[]{:S(2)}, u32[]{:S(2)}) %collective-permute-start.2) | collective-permute-done | bytes 917536 | tf_op jit(solution)/shard_map/ppermute | solution.py:301
  49.8 1.4 collective-permute-done.3.refs_1_
  51.1 0.5 collective-permute-start.11
  51.6 1.5 collective-permute-start.8
  53.1 0.6 collective-permute-start.9
  53.7 1.2 collective-permute-done.11.refs_3_
  54.9 12.4 %mlp.5 = (bf16[128,7168]{1,0:T(8,128)(2,1)S(1)}, bf16[128,7168]{1,0:T(8,128)(2,1)}) custom-call(bf16[64,7168]{1,0:T(8,128)(2,1)S(1)} %collective-permute-done.2.refs_0_, bf16[64,7168]{1,0:T(8,128)(2,1)S(1)} %collective-permute-done.3.refs_1_, bf16[64,7168]{1,0:T(8,128)(2,1)S(1)} %collective-permute-done.10.refs_2_, ...), custom_call_target="tpu_custom_call" | custom-call | flops 5637144576 | bytes 29360128 | tf_op jit(solution)/shard_map/mlp/pallas_call | solution.py:92
  67.4 1.2 copy-done.5
  68.6 5.3 %collective-permute-done.8.refs_0_ = bf16[64,7168]{1,0:T(8,128)(2,1)S(1)} collective-permute-done((bf16[64,7168]{1,0:T(8,128)(2,1)S(1)}, bf16[64,7168]{1,0:T(8,128)(2,1)S(1)}, u32[]{:S(2)}, u32[]{:S(2)}) %collective-permute-start.8) | collective-permute-done | bytes 917536 | tf_op jit(solution)/shard_map/ppermute | solution.py:301
  73.9 1.3 collective-permute-done.9.refs_1_
  75.2 0.5 collective-permute-start.15
  75.7 5.1 %all-to-all-start.1 = ((bf16[32,64,576]{2,1,0:T(8,128)(2,1)}), bf16[32,64,576]{2,1,0:T(8,128)(2,1)S(1)}, u32[]{:S(2)}, u32[]{:S(2)}) async-start(bf16[32,64,576]{2,1,0:T(8,128)(2,1)} %copy-done.2), calls=%async_computation.1 | async-start | bytes 5242880 | tf_op jit(solution)/shard_map/all_to_all | solution.py:297
  80.9 1.1 slice.91
  81.9 0.6 collective-permute-start.12
  82.5 1.5 collective-permute-start.13
  84.0 12.6 %mlp.6 = (bf16[128,7168]{1,0:T(8,128)(2,1)S(1)}, bf16[128,7168]{1,0:T(8,128)(2,1)S(1)}) custom-call(bf16[64,7168]{1,0:T(8,128)(2,1)S(1)} %collective-permute-done.8.refs_0_, bf16[64,7168]{1,0:T(8,128)(2,1)} %collective-permute-done.9.refs_1_, bf16[64,7168]{1,0:T(8,128)(2,1)} %collective-permute-done.14.refs_2_, ...), custom_call_target="tpu_custom_call" | custom-call | flops 5637144576 | bytes 29360128 | tf_op jit(solution)/shard_map/mlp/pallas_call | solution.py:92
  96.6 1.3 copy-done.6
  97.9 49.9 %collective-permute-done.12.refs_0_ = bf16[32,7168]{1,0:T(8,128)(2,1)S(1)} collective-permute-done((bf16[32,7168]{1,0:T(8,128)(2,1)S(1)}, bf16[32,7168]{1,0:T(8,128)(2,1)S(1)}, u32[]{:S(2)}, u32[]{:S(2)}) %collective-permute-start.12) | collective-permute-done | bytes 458784 | tf_op jit(solution)/shard_map/ppermute | solution.py:295
  147.8 0.8 collective-permute-done.13.refs_1_
  148.6 0.5 collective-permute-start.17
  149.1 1.3 collective-permute-done.16.refs_2_
  150.5 0.7 collective-permute-done.17.refs_3_
  151.1 11.3 %mlp.7 = (bf16[64,7168]{1,0:T(8,128)(2,1)S(1)}, bf16[64,7168]{1,0:T(8,128)(2,1)}) custom-call(bf16[32,7168]{1,0:T(8,128)(2,1)S(1)} %collective-permute-done.12.refs_0_, bf16[32,7168]{1,0:T(8,128)(2,1)S(1)} %collective-permute-done.13.refs_1_, bf16[32,7168]{1,0:T(8,128)(2,1)S(1)} %collective-permute-done.16.refs_2_, ...), custom_call_target="tpu_custom_call" | custom-call | flops 2818572288 | bytes 25690112 | tf_op jit(solution)/shard_map/mlp/pallas_call | solution.py:92
  162.6 0.6 dynamic_slice.58
  169.2 0.7 fusion.13
  175.5 1.5 fusion.4
  177.4 1.4 multiply_convert_fusion
  178.9 1.8 collective-permute-start.19
  180.9 10.5 %collective-permute-done.19 = bf16[32,7168]{1,0:T(8,128)(2,1)S(1)} collective-permute-done((bf16[32,7168]{1,0:T(8,128)(2,1)S(1)}, bf16[32,7168]{1,0:T(8,128)(2,1)S(1)}, u32[]{:S(2)}, u32[]{:S(2)}) %collective-permute-start.19) | collective-permute-done | bytes 458784 | tf_op jit(solution)/shard_map/ppermute | solution.py:346
  191.5 1.4 collective-permute-done.20
  192.9 4.0 %add_convert_fusion.9 = (bf16[64,7168]{1,0:T(8,128)(2,1)}, bf16[64,7168]{1,0:T(8,128)(2,1)}) fusion(bf16[128,7168]{1,0:T(8,128)(2,1)} %collective-permute-done.21, bf16[128,7168]{1,0:T(8,128)(2,1)} %copy-done.6, f32[64]{0:T(128)} %get-tuple-element.116, bf16[32,7168]{1,0:T(8,128)(2,1)S(1)} %collective-permute-done.20, f32[64]{0:T(128)} %get-tuple-element.117, ...), kind=kLoop, calls=%fused_computation.10 | loop fusion | flops 8257536 | bytes 6423040 | tf_op jit(solution)/shard_map/convert_element_type | solution.py:358
  197.3 1.7 collective-permute-start.23
  199.4 19.1 %collective-permute-done.22 = bf16[64,7168]{1,0:T(8,128)(2,1)} collective-permute-done((bf16[64,7168]{1,0:T(8,128)(2,1)}, bf16[64,7168]{1,0:T(8,128)(2,1)}, u32[]{:S(2)}, u32[]{:S(2)}) %collective-permute-start.22) | collective-permute-done | bytes 917536 | tf_op jit(solution)/shard_map/ppermute | solution.py:346
  218.9 4.8 %add_convert_fusion.5 = (bf16[64,7168]{1,0:T(8,128)(2,1)}, bf16[64,7168]{1,0:T(8,128)(2,1)}) fusion(bf16[64,7168]{1,0:T(8,128)(2,1)} %collective-permute-done.23, bf16[128,7168]{1,0:T(8,128)(2,1)} %collective-permute-done.24, bf16[128,7168]{1,0:T(8,128)(2,1)} %copy-done.5, f32[64]{0:T(128)} %get-tuple-element.114, f32[64]{0:T(128)} %get-tuple-element.115, ...), kind=kLoop, calls=%fused_computation.6 | loop fusion | flops 8257536 | bytes 7340544 | tf_op jit(solution)/shard_map/convert_element_type | solution.py:358
  223.7 0.6 collective-permute-start.25
  224.3 1.5 collective-permute-start.26
  226.4 1.7 copy-done
  228.1 3.3 %attend.2 = bf16[16,64,512]{2,1,0:T(8,128)(2,1)S(1)} custom-call(s32[32]{0:T(128)S(1)} %select_reduce_fusion.2.order_ref, s32[17]{0:T(128)S(1)} %get-tuple-element.123.start_ref, s32[32]{0:T(128)S(1)} %get-tuple-element.133.length_ref, bf16[32,64,576]{2,1,0:T(8,128)(2,1)S(1)} %copy-done, bf16[32,1,576]{2,1,0:T(2,128)(2,1)S(1)} %copy.43.own_ref, ...), custom_call_target="tpu_custom_call" | custom-call | flops 150994944 | bytes 4587520 | tf_op jit(solution)/shard_map/attend/pallas_call | solution.py:183
  231.4 12.9 %collective-permute-done.25 = bf16[64,7168]{1,0:T(8,128)(2,1)} collective-permute-done((bf16[64,7168]{1,0:T(8,128)(2,1)}, bf16[64,7168]{1,0:T(8,128)(2,1)}, u32[]{:S(2)}, u32[]{:S(2)}) %collective-permute-start.25) | collective-permute-done | bytes 917536 | tf_op jit(solution)/shard_map/ppermute | solution.py:346
  244.8 3.1 %add_convert_fusion.1 = (bf16[64,7168]{1,0:T(8,128)(2,1)S(1)}, bf16[64,7168]{1,0:T(8,128)(2,1)S(1)}) fusion(bf16[64,7168]{1,0:T(8,128)(2,1)} %collective-permute-done.26, bf16[192,7168]{1,0:T(8,128)(2,1)} %collective-permute-done.7, bf16[192,7168]{1,0:T(8,128)(2,1)S(1)} %copy-done.4, f32[64]{0:T(128)S(1)} %get-tuple-element.112, f32[64]{0:T(128)S(1)} %copy-done.15, ...), kind=kLoop, calls=%fused_computation.2 | loop fusion | flops 8257536 | bytes 7340544 | tf_op jit(solution)/shard_map/convert_element_type | solution.py:358
  247.9 1.0 collective-permute-start.27
  248.9 1.1 collective-permute-start.28
  250.0 3.3 %attend.3 = bf16[16,64,512]{2,1,0:T(8,128)(2,1)S(1)} custom-call(s32[32]{0:T(128)S(1)} %select_reduce_fusion.2.order_ref, s32[17]{0:T(128)S(1)} %get-tuple-element.122.start_ref, s32[32]{0:T(128)S(1)} %get-tuple-element.133.length_ref, bf16[32,64,576]{2,1,0:T(8,128)(2,1)S(1)} %copy-done.1, bf16[32,1,576]{2,1,0:T(2,128)(2,1)S(1)} %copy.43.own_ref, ...), custom_call_target="tpu_custom_call" | custom-call | flops 150994944 | bytes 4587520 | tf_op jit(solution)/shard_map/attend/pallas_call | solution.py:183
  253.3 1.5 pad_maximum_fusion
  254.8 12.4 %collective-permute-done.27 = bf16[64,7168]{1,0:T(8,128)(2,1)S(1)} collective-permute-done((bf16[64,7168]{1,0:T(8,128)(2,1)S(1)}, bf16[64,7168]{1,0:T(8,128)(2,1)S(1)}, u32[]{:S(2)}, u32[]{:S(2)}) %collective-permute-start.27) | collective-permute-done | bytes 917536 | tf_op jit(solution)/shard_map/ppermute | solution.py:346
  267.5 1.7 add_convert_fusion
  269.2 1.0 fusion.11
  (81 shorter events, 4.7 us)
Async XLA Ops:
  0.6 4.3 %copy-start.18 = (s32[16]{0:T(128)S(1)}, s32[16]{0:T(128)}, u32[]{:S(2)}) copy-start(s32[16]{0:T(128)} %param.35) | copy-start | bytes 196
  0.6 4.5 %copy-start.17 = (s32[16]{0:T(128)S(1)}, s32[16]{0:T(128)}, u32[]{:S(2)}) copy-start(s32[16]{0:T(128)} %param.36) | copy-start | bytes 196
  0.7 4.5 %copy-start.16 = (s32[16]{0:T(128)S(1)}, s32[16]{0:T(128)}, u32[]{:S(2)}) copy-start(s32[16]{0:T(128)} %param.37) | copy-start | bytes 196
  0.7 4.7 %copy-start.14 = (s32[32,8]{0,1:T(8,128)S(1)}, s32[32,8]{0,1:T(8,128)}, u32[]{:S(2)}) copy-start(s32[32,8]{0,1:T(8,128)} %param.25) | copy-start | bytes 3076
  0.7 4.7 %copy-start.13 = (s32[32,8]{0,1:T(8,128)S(1)}, s32[32,8]{0,1:T(8,128)}, u32[]{:S(2)}) copy-start(s32[32,8]{0,1:T(8,128)} %param.26) | copy-start | bytes 3076
  0.7 4.7 %copy-start.12 = (s32[32,8]{0,1:T(8,128)S(1)}, s32[32,8]{0,1:T(8,128)}, u32[]{:S(2)}) copy-start(s32[32,8]{0,1:T(8,128)} %param.28) | copy-start | bytes 3076
  0.7 4.7 %copy-start.11 = (s32[32,8]{0,1:T(8,128)S(1)}, s32[32,8]{0,1:T(8,128)}, u32[]{:S(2)}) copy-start(s32[32,8]{0,1:T(8,128)} %param.29) | copy-start | bytes 3076
  2.8 24.1 %collective-permute-start = (bf16[64,7168]{1,0:T(8,128)(2,1)S(1)}, bf16[64,7168]{1,0:T(8,128)(2,1)S(1)}, u32[]{:S(2)}, u32[]{:S(2)}) collective-permute-start(bf16[64,7168]{1,0:T(8,128)(2,1)S(1)} %constant_dynamic-update-slice_fusion.refs_2_), channel_id=1, source_target_pairs={{0,4},{1,5},{4,8},{5,9},{8,12},{9,13},{12,14},{13,15},{14,10},{15,... | collective-permute-start | bytes 2752520 | tf_op jit(solution)/shard_map/ppermute | solution.py:286
  3.4 23.6 %collective-permute-start.1 = (bf16[64,7168]{1,0:T(8,128)(2,1)S(1)}, bf16[64,7168]{1,0:T(8,128)(2,1)}, u32[]{:S(2)}, u32[]{:S(2)}) collective-permute-start(bf16[64,7168]{1,0:T(8,128)(2,1)S(1)} %constant_dynamic-update-slice_fusion.refs_2_), channel_id=1, source_target_pairs={{4,0},{5,1},{8,4},{9,5},{12,8},{13,9},{14,12},{15,13},{10,14},{11,... | collective-permute-start | bytes 2752520 | tf_op jit(solution)/shard_map/ppermute | solution.py:287
  6.1 20.2 %all-to-all-start = ((s32[16,1,66]{2,1,0:T(1,128)}), s32[16,1,66]{2,1,0:T(1,128)S(1)}, u32[]{:S(2)}, u32[]{:S(2)}) async-start(s32[16,1,66]{2,1,0:T(1,128)} %bitcast.2), calls=%async_computation | async-start | bytes 16384 | tf_op jit(solution)/shard_map/all_to_all | solution.py:276
  12.3 17.2 %collective-permute-start.6 = (bf16[64,7168]{1,0:T(8,128)(2,1)S(1)}, bf16[64,7168]{1,0:T(8,128)(2,1)}, u32[]{:S(2)}, u32[]{:S(2)}) collective-permute-start(bf16[64,7168]{1,0:T(8,128)(2,1)S(1)} %constant_dynamic-update-slice_fusion.refs_2_), channel_id=1, source_target_pairs={{0,1},{1,0},{2,3},{3,2},{4,5},{5,4},{6,7},{7,6},{8,9},{9,8},{10,11... | collective-permute-start | bytes 2752520 | tf_op jit(solution)/shard_map/ppermute | solution.py:285
  12.4 1.3 copy-start.7
  14.5 1.5 copy-start.2
  26.9 3.1 %collective-permute-start.4 = (bf16[64,7168]{1,0:T(8,128)(2,1)S(1)}, bf16[64,7168]{1,0:T(8,128)(2,1)S(1)}, u32[]{:S(2)}, u32[]{:S(2)}) collective-permute-start(bf16[64,7168]{1,0:T(8,128)(2,1)S(1)} %collective-permute-done.refs_0_), channel_id=1, source_target_pairs={{0,1},{1,0},{2,3},{3,2},{4,5},{5,4},{6,7},{7,6},{8,9},{9,8},{10,11... | collective-permute-start | bytes 2752520 | tf_op jit(solution)/shard_map/ppermute | solution.py:304
  26.9 4.0 %collective-permute-start.5 = (bf16[64,7168]{1,0:T(8,128)(2,1)}, bf16[64,7168]{1,0:T(8,128)(2,1)S(1)}, u32[]{:S(2)}, u32[]{:S(2)}) collective-permute-start(bf16[64,7168]{1,0:T(8,128)(2,1)} %collective-permute-done.1.refs_1_), channel_id=1, source_target_pairs={{0,1},{1,0},{2,3},{3,2},{4,5},{5,4},{6,7},{7,6},{8,9},{9,8},{10,11... | collective-permute-start | bytes 2752520 | tf_op jit(solution)/shard_map/ppermute | solution.py:304
  27.4 22.3 %collective-permute-start.2 = (bf16[64,7168]{1,0:T(8,128)(2,1)S(1)}, bf16[64,7168]{1,0:T(8,128)(2,1)S(1)}, u32[]{:S(2)}, u32[]{:S(2)}) collective-permute-start(bf16[64,7168]{1,0:T(8,128)(2,1)S(1)} %collective-permute-done.refs_0_), channel_id=1, source_target_pairs={{0,4},{1,5},{4,8},{5,9},{8,12},{9,13},{12,14},{13,15},{14,10},{15,... | collective-permute-start | bytes 2752520 | tf_op jit(solution)/shard_map/ppermute | solution.py:301
  28.9 22.3 %collective-permute-start.3 = (bf16[64,7168]{1,0:T(8,128)(2,1)}, bf16[64,7168]{1,0:T(8,128)(2,1)S(1)}, u32[]{:S(2)}, u32[]{:S(2)}) collective-permute-start(bf16[64,7168]{1,0:T(8,128)(2,1)} %collective-permute-done.1.refs_1_), channel_id=1, source_target_pairs={{4,0},{5,1},{8,4},{9,5},{12,8},{13,9},{14,12},{15,13},{10,14},{11,... | collective-permute-start | bytes 2752520 | tf_op jit(solution)/shard_map/ppermute | solution.py:302
  45.4 1.6 copy-start.3
  51.1 2.5 collective-permute-start.10
  51.1 3.8 %collective-permute-start.11 = (bf16[64,7168]{1,0:T(8,128)(2,1)S(1)}, bf16[64,7168]{1,0:T(8,128)(2,1)S(1)}, u32[]{:S(2)}, u32[]{:S(2)}) collective-permute-start(bf16[64,7168]{1,0:T(8,128)(2,1)S(1)} %collective-permute-done.3.refs_1_), channel_id=1, source_target_pairs={{0,1},{1,0},{2,3},{3,2},{4,5},{5,4},{6,7},{7,6},{8,9},{9,8},{10,11... | collective-permute-start | bytes 2752520 | tf_op jit(solution)/shard_map/ppermute | solution.py:304
  51.6 22.3 %collective-permute-start.8 = (bf16[64,7168]{1,0:T(8,128)(2,1)S(1)}, bf16[64,7168]{1,0:T(8,128)(2,1)S(1)}, u32[]{:S(2)}, u32[]{:S(2)}) collective-permute-start(bf16[64,7168]{1,0:T(8,128)(2,1)S(1)} %collective-permute-done.2.refs_0_), channel_id=1, source_target_pairs={{0,4},{1,5},{4,8},{5,9},{8,12},{9,13},{12,14},{13,15},{14,10},{15,... | collective-permute-start | bytes 2752520 | tf_op jit(solution)/shard_map/ppermute | solution.py:301
  53.1 22.1 %collective-permute-start.9 = (bf16[64,7168]{1,0:T(8,128)(2,1)S(1)}, bf16[64,7168]{1,0:T(8,128)(2,1)}, u32[]{:S(2)}, u32[]{:S(2)}) collective-permute-start(bf16[64,7168]{1,0:T(8,128)(2,1)S(1)} %collective-permute-done.3.refs_1_), channel_id=1, source_target_pairs={{4,0},{5,1},{8,4},{9,5},{12,8},{13,9},{14,12},{15,13},{10,14},{11,... | collective-permute-start | bytes 2752520 | tf_op jit(solution)/shard_map/ppermute | solution.py:302
  67.4 1.2 copy-start.5
  75.2 8.8 %collective-permute-start.14 = (bf16[64,7168]{1,0:T(8,128)(2,1)S(1)}, bf16[64,7168]{1,0:T(8,128)(2,1)}, u32[]{:S(2)}, u32[]{:S(2)}) collective-permute-start(bf16[64,7168]{1,0:T(8,128)(2,1)S(1)} %collective-permute-done.8.refs_0_), channel_id=1, source_target_pairs={{0,1},{1,0},{2,3},{3,2},{4,5},{5,4},{6,7},{7,6},{8,9},{9,8},{10,11... | collective-permute-start | bytes 2752520 | tf_op jit(solution)/shard_map/ppermute | solution.py:304
  75.2 8.8 %collective-permute-start.15 = (bf16[64,7168]{1,0:T(8,128)(2,1)}, bf16[64,7168]{1,0:T(8,128)(2,1)}, u32[]{:S(2)}, u32[]{:S(2)}) collective-permute-start(bf16[64,7168]{1,0:T(8,128)(2,1)} %collective-permute-done.9.refs_1_), channel_id=1, source_target_pairs={{0,1},{1,0},{2,3},{3,2},{4,5},{5,4},{6,7},{7,6},{8,9},{9,8},{10,11... | collective-permute-start | bytes 2752520 | tf_op jit(solution)/shard_map/ppermute | solution.py:304
  75.7 117.2 %all-to-all-start.1 = ((bf16[32,64,576]{2,1,0:T(8,128)(2,1)}), bf16[32,64,576]{2,1,0:T(8,128)(2,1)S(1)}, u32[]{:S(2)}, u32[]{:S(2)}) async-start(bf16[32,64,576]{2,1,0:T(8,128)(2,1)} %copy-done.2), calls=%async_computation.1 | async-start | bytes 5242880 | tf_op jit(solution)/shard_map/all_to_all | solution.py:297
  81.9 65.9 %collective-permute-start.12 = (bf16[32,7168]{1,0:T(8,128)(2,1)S(1)}, bf16[32,7168]{1,0:T(8,128)(2,1)S(1)}, u32[]{:S(2)}, u32[]{:S(2)}) collective-permute-start(bf16[32,7168]{1,0:T(8,128)(2,1)S(1)} %slice.90), channel_id=1, source_target_pairs={{0,4},{1,5},{4,8},{5,9},{8,12},{9,13},{12,14},{13,15},{14,10},{15,... | collective-permute-start | bytes 1376264 | tf_op jit(solution)/shard_map/ppermute | solution.py:295
  82.5 66.1 %collective-permute-start.13 = (bf16[32,7168]{1,0:T(8,128)(2,1)S(1)}, bf16[32,7168]{1,0:T(8,128)(2,1)S(1)}, u32[]{:S(2)}, u32[]{:S(2)}) collective-permute-start(bf16[32,7168]{1,0:T(8,128)(2,1)S(1)} %slice.91), channel_id=1, source_target_pairs={{4,0},{5,1},{8,4},{9,5},{12,8},{13,9},{14,12},{15,13},{10,14},{11,... | collective-permute-start | bytes 1376264 | tf_op jit(solution)/shard_map/ppermute | solution.py:296
  96.6 1.3 copy-start.6
  97.9 64.5 %copy-start.8 = (bf16[128,7168]{1,0:T(8,128)(2,1)}, bf16[128,7168]{1,0:T(8,128)(2,1)S(1)}, u32[]{:S(2)}) copy-start(bf16[128,7168]{1,0:T(8,128)(2,1)S(1)} %get-tuple-element.79) | copy-start | bytes 5505028
  148.6 14.0 %copy-start.19 = (s32[8]{0:T(128)S(1)}, s32[8]{0:T(128)}, u32[]{:S(2)}) copy-start(s32[8]{0:T(128)} %constant.167.clone) | copy-start | bytes 100
  148.6 20.6 %copy-start.9 = (s32[8]{0:T(128)S(1)}, s32[8]{0:T(128)}, u32[]{:S(2)}) copy-start(s32[8]{0:T(128)} %constant.168.clone) | copy-start | bytes 100
  148.6 1.8 collective-permute-start.16
  148.6 2.5 collective-permute-start.17
  162.4 15.0 %collective-permute-start.18 = (bf16[64,7168]{1,0:T(8,128)(2,1)}, bf16[64,7168]{1,0:T(8,128)(2,1)}, u32[]{:S(2)}, u32[]{:S(2)}) collective-permute-start(bf16[64,7168]{1,0:T(8,128)(2,1)} %get-tuple-element.72), channel_id=1, source_target_pairs={{0,1},{1,0},{2,3},{3,2},{4,5},{5,4},{6,7},{7,6},{8,9},{9,8},{10,11... | collective-permute-start | bytes 2752520 | tf_op jit(solution)/shard_map/ppermute | solution.py:314
  177.0 15.9 %collective-permute-start.21 = (bf16[128,7168]{1,0:T(8,128)(2,1)}, bf16[128,7168]{1,0:T(8,128)(2,1)}, u32[]{:S(2)}, u32[]{:S(2)}) collective-permute-start(bf16[128,7168]{1,0:T(8,128)(2,1)} %copy-done.8), channel_id=1, source_target_pairs={{0,1},{1,0},{2,3},{3,2},{4,5},{5,4},{6,7},{7,6},{8,9},{9,8},{10,11... | collective-permute-start | bytes 5505032 | tf_op jit(solution)/shard_map/ppermute | solution.py:314
  178.9 12.6 %collective-permute-start.19 = (bf16[32,7168]{1,0:T(8,128)(2,1)S(1)}, bf16[32,7168]{1,0:T(8,128)(2,1)S(1)}, u32[]{:S(2)}, u32[]{:S(2)}) collective-permute-start(bf16[32,7168]{1,0:T(8,128)(2,1)S(1)} %get-tuple-element.73), channel_id=1, source_target_pairs={{0,4},{1,5},{4,8},{5,9},{8,12},{9,13},{12,14},{13,15},{14,10},{15,... | collective-permute-start | bytes 1376264 | tf_op jit(solution)/shard_map/ppermute | solution.py:346
  180.6 12.3 %collective-permute-start.20 = (bf16[32,7168]{1,0:T(8,128)(2,1)S(1)}, bf16[32,7168]{1,0:T(8,128)(2,1)S(1)}, u32[]{:S(2)}, u32[]{:S(2)}) collective-permute-start(bf16[32,7168]{1,0:T(8,128)(2,1)S(1)} %get-tuple-element.74), channel_id=1, source_target_pairs={{4,0},{5,1},{8,4},{9,5},{12,8},{13,9},{14,12},{15,13},{10,14},{11,... | collective-permute-start | bytes 1376264 | tf_op jit(solution)/shard_map/ppermute | solution.py:347
  180.9 37.9 %collective-permute-start.24 = (bf16[128,7168]{1,0:T(8,128)(2,1)}, bf16[128,7168]{1,0:T(8,128)(2,1)}, u32[]{:S(2)}, u32[]{:S(2)}) collective-permute-start(bf16[128,7168]{1,0:T(8,128)(2,1)} %get-tuple-element.85), channel_id=1, source_target_pairs={{0,1},{1,0},{2,3},{3,2},{4,5},{5,4},{6,7},{7,6},{8,9},{9,8},{10,11... | collective-permute-start | bytes 5505032 | tf_op jit(solution)/shard_map/ppermute | solution.py:314
  192.9 6.1 %copy-start.10 = (bf16[32,576]{1,0:T(8,128)(2,1)S(1)}, bf16[32,576]{1,0:T(8,128)(2,1)}, u32[]{:S(2)}) copy-start(bf16[32,576]{1,0:T(8,128)(2,1)} %param.33) | copy-start | bytes 110596
  196.9 21.5 %collective-permute-start.22 = (bf16[64,7168]{1,0:T(8,128)(2,1)}, bf16[64,7168]{1,0:T(8,128)(2,1)}, u32[]{:S(2)}, u32[]{:S(2)}) collective-permute-start(bf16[64,7168]{1,0:T(8,128)(2,1)} %get-tuple-element.81), channel_id=1, source_target_pairs={{0,4},{1,5},{4,8},{5,9},{8,12},{9,13},{12,14},{13,15},{14,10},{15,... | collective-permute-start | bytes 2752520 | tf_op jit(solution)/shard_map/ppermute | solution.py:346
  197.3 21.6 %collective-permute-start.23 = (bf16[64,7168]{1,0:T(8,128)(2,1)}, bf16[64,7168]{1,0:T(8,128)(2,1)}, u32[]{:S(2)}, u32[]{:S(2)}) collective-permute-start(bf16[64,7168]{1,0:T(8,128)(2,1)} %get-tuple-element.82), channel_id=1, source_target_pairs={{4,0},{5,1},{8,4},{9,5},{12,8},{13,9},{14,12},{15,13},{10,14},{11,... | collective-permute-start | bytes 2752520 | tf_op jit(solution)/shard_map/ppermute | solution.py:347
  199.0 45.7 %collective-permute-start.7 = (bf16[192,7168]{1,0:T(8,128)(2,1)}, bf16[192,7168]{1,0:T(8,128)(2,1)}, u32[]{:S(2)}, u32[]{:S(2)}) collective-permute-start(bf16[192,7168]{1,0:T(8,128)(2,1)} %get-tuple-element.58), channel_id=1, source_target_pairs={{0,1},{1,0},{2,3},{3,2},{4,5},{5,4},{6,7},{7,6},{8,9},{9,8},{10,11... | collective-permute-start | bytes 8257544 | tf_op jit(solution)/shard_map/ppermute | solution.py:314
  223.7 20.7 %collective-permute-start.25 = (bf16[64,7168]{1,0:T(8,128)(2,1)}, bf16[64,7168]{1,0:T(8,128)(2,1)}, u32[]{:S(2)}, u32[]{:S(2)}) collective-permute-start(bf16[64,7168]{1,0:T(8,128)(2,1)} %get-tuple-element.87), channel_id=1, source_target_pairs={{0,4},{1,5},{4,8},{5,9},{8,12},{9,13},{12,14},{13,15},{14,10},{15,... | collective-permute-start | bytes 2752520 | tf_op jit(solution)/shard_map/ppermute | solution.py:346
  224.3 20.5 %collective-permute-start.26 = (bf16[64,7168]{1,0:T(8,128)(2,1)}, bf16[64,7168]{1,0:T(8,128)(2,1)}, u32[]{:S(2)}, u32[]{:S(2)}) collective-permute-start(bf16[64,7168]{1,0:T(8,128)(2,1)} %get-tuple-element.88), channel_id=1, source_target_pairs={{4,0},{5,1},{8,4},{9,5},{12,8},{13,9},{14,12},{15,13},{10,14},{11,... | collective-permute-start | bytes 2752520 | tf_op jit(solution)/shard_map/ppermute | solution.py:347
  226.4 1.7 copy-start
  228.1 16.6 %copy-start.4 = (bf16[192,7168]{1,0:T(8,128)(2,1)S(1)}, bf16[192,7168]{1,0:T(8,128)(2,1)}, u32[]{:S(2)}) copy-start(bf16[192,7168]{1,0:T(8,128)(2,1)} %copy-done.3) | copy-start | bytes 8257540
  228.1 16.6 %copy-start.15 = (f32[64]{0:T(128)S(1)}, f32[64]{0:T(128)}, u32[]{:S(2)}) copy-start(f32[64]{0:T(128)} %get-tuple-element.113) | copy-start | bytes 772
  244.8 5.2 %copy-start.1 = (bf16[32,64,576]{2,1,0:T(8,128)(2,1)S(1)}, bf16[32,64,576]{2,1,0:T(8,128)(2,1)}, u32[]{:S(2)}) copy-start(bf16[32,64,576]{2,1,0:T(8,128)(2,1)} %query_ref.3) | copy-start | bytes 7077892
  247.9 19.3 %collective-permute-start.27 = (bf16[64,7168]{1,0:T(8,128)(2,1)S(1)}, bf16[64,7168]{1,0:T(8,128)(2,1)S(1)}, u32[]{:S(2)}, u32[]{:S(2)}) collective-permute-start(bf16[64,7168]{1,0:T(8,128)(2,1)S(1)} %get-tuple-element.94), channel_id=1, source_target_pairs={{0,4},{1,5},{4,8},{5,9},{8,12},{9,13},{12,14},{13,15},{14,10},{15,... | collective-permute-start | bytes 2752520 | tf_op jit(solution)/shard_map/ppermute | solution.py:346
  248.9 18.6 %collective-permute-start.28 = (bf16[64,7168]{1,0:T(8,128)(2,1)S(1)}, bf16[64,7168]{1,0:T(8,128)(2,1)S(1)}, u32[]{:S(2)}, u32[]{:S(2)}) collective-permute-start(bf16[64,7168]{1,0:T(8,128)(2,1)S(1)} %get-tuple-element.95), channel_id=1, source_target_pairs={{4,0},{5,1},{8,4},{9,5},{12,8},{13,9},{14,12},{15,13},{10,14},{11,... | collective-permute-start | bytes 2752520 | tf_op jit(solution)/shard_map/ppermute | solution.py:347

commit v3 on v2

--- a/solution.py
+++ b/solution.py
@@ -14,7 +14,6 @@
 softmax_scale = 192.0 ** (-0.5)
 gate_unit = 65536.0
 AXIS = "expert"
-WAIT_STEP = 1
 VMEM_LIMIT = 16 << 20
 
 
@@ -244,12 +243,11 @@
     back = [(b, a) for a, b in ahead]
     across = [(i, i ^ 1) for i in range(devices)]
     me = lax.axis_index(AXIS)
-    my_chip = me // 2
-    my_core = me % 2
-    place = jnp.asarray(place_of)[my_chip]
-
-    def device_at(shift):
-        return 2 * jnp.asarray(np.array(ring, np.int32))[(place + shift + chips) % chips] + my_core
+    neighbours = np.zeros((devices, chips), np.int32)
+    for device in range(devices):
+        for shift in range(chips):
+            chip = ring[(place_of[device // 2] + shift) % chips]
+            neighbours[device, shift] = 2 * chip + device % 2
 
     span_count = span_owner.shape[0]
     block_rows = latents.shape[1]
@@ -274,58 +272,53 @@
         [jnp.repeat(gates.T, 2, axis=0), slot_codes.reshape(devices, CAPC)], axis=1
     ).astype(jnp.int32)
     small = lax.all_to_all(small, AXIS, split_axis=0, concat_axis=0, tiled=True)
-    gate_table = small[:, :row_count].astype(jnp.float32) / gate_unit
+    at_shift = lax.dynamic_index_in_dim(jnp.asarray(neighbours), me, 0, keepdims=False)
+    picked = at_shift[:, None] == jnp.arange(devices)[None, :]
+    shift_gates = jnp.sum(jnp.where(picked[:, :, None], small[None, :, :row_count], 0), axis=1)
+    shift_gates = shift_gates.astype(jnp.float32) / gate_unit
     slot_codes = small[:, row_count:].reshape(-1)
     slot_length = slot_codes % (block_rows + 1)
     slot_request = slot_codes // (block_rows + 1)
 
     shipped = ship_blocks(latents, source)
 
-    own_rows = jnp.concatenate([prefill_tokens, decode_rows], axis=0)
-    own_other = lax.ppermute(own_rows, AXIS, across)
-    a = lax.ppermute(own_rows, AXIS, ahead)
-    b = lax.ppermute(own_rows, AXIS, back)
-    a, b, shipped, gate_table = lax.optimization_barrier((a, b, shipped, gate_table))
-    arrived = [(a, b)]
+    own = [prefill_tokens, decode_rows]
+    own_other = [lax.ppermute(c, AXIS, across) for c in own]
+    front = [lax.ppermute(c, AXIS, ahead) for c in own]
+    rear = [lax.ppermute(c, AXIS, back) for c in own]
+    front, rear, shipped = lax.optimization_barrier((front, rear, shipped))
     parts = {}
     for s in range(1, half + 1):
-        a, b = arrived[-1]
-        if s < half:
-            if s == half - 1:
-                next_a = lax.ppermute(a[:split], AXIS, ahead)
-                next_b = lax.ppermute(b[split:], AXIS, back)
-                block_latents = lax.all_to_all(
-                    shipped, AXIS, split_axis=0, concat_axis=0, tiled=True
-                )
-            else:
-                next_a = lax.ppermute(a, AXIS, ahead)
-                next_b = lax.ppermute(b, AXIS, back)
-        mine = [a, b]
+        if s == half - 1:
+            next_front = [lax.ppermute(front[0], AXIS, ahead)]
+            next_rear = [lax.ppermute(rear[1], AXIS, back)]
+        elif s < half:
+            next_front = [lax.ppermute(c, AXIS, ahead) for c in front]
+            next_rear = [lax.ppermute(c, AXIS, back) for c in rear]
+        mine = front + rear
         other = [lax.ppermute(c, AXIS, across) for c in mine]
         if s == 1:
-            mine = mine + [own_rows]
-            other = other + [own_other]
+            mine = mine + own
+            other = other + own_other
         part, for_other = mlp(mine, other, gate_up, down_proj)
         if s < half:
-            next_a, next_b, part, for_other, shipped = lax.optimization_barrier(
-                (next_a, next_b, part, for_other, shipped)
-            )
-            arrived.append((next_a, next_b))
+            front, rear, part, for_other, shipped, shift_gates = lax.optimization_barrier(
+                (next_front, next_rear, part, for_other, shipped, shift_gates)
+            )
         parts[s] = (part, lax.ppermute(for_other, AXIS, across))
+    block_latents = lax.all_to_all(shipped, AXIS, split_axis=0, concat_axis=0, tiled=True)
 
     def contribution(s, k):
         part, from_other = parts[max(s, 1)]
         size = split if s == half else row_count
-        lo = 2 * size if s == 0 else k * size
+        lo = 2 * row_count if s == 0 else k * size
         both = part[lo : lo + size].astype(jnp.float32) + from_other[lo : lo + size].astype(
             jnp.float32
         )
-        both = both.astype(jnp.bfloat16).astype(jnp.float32)
-        shift = (-s, s)[k] if s else 0
-        weight = lax.dynamic_index_in_dim(gate_table, device_at(shift), 0, keepdims=False)
+        weight = shift_gates[((-s, s)[k] + chips) % chips]
         if s == half:
             weight = (weight[:split], weight[split:])[k]
-        return weight[:, None] * both
+        return (weight[:, None] * both).astype(jnp.bfloat16)
 
     key = jnp.where(slot_length > 0, slot_request, decode_count)
     index = jnp.arange(slots)
@@ -339,23 +332,28 @@
     start = jnp.sum(key[None, :] < jnp.arange(decode_count + 1)[:, None], axis=1).astype(jnp.int32)
     first_rows = decode_count // 2
 
-    up = contribution(half, 0).astype(jnp.bfloat16)
-    down = contribution(half, 1).astype(jnp.bfloat16)
+    up = contribution(half, 0)
+    down = contribution(half, 1)
+    up, down, block_latents = lax.optimization_barrier((up, down, block_latents))
+    to_up = {s: contribution(s, 1) for s in range(half)}
+    to_down = {s: contribution(s, 0) for s in range(1, half)}
     for s in range(half - 1, -1, -1):
         up, down = lax.optimization_barrier((up, down))
         up = lax.ppermute(up, AXIS, ahead)
         down = lax.ppermute(down, AXIS, back)
-        up, down = lax.optimization_barrier((up, down))
-        if s == half - WAIT_STEP:
-            up, down, block_latents = lax.optimization_barrier((up, down, block_latents))
+        if s == half - 1:
+            up, down, to_up, to_down = lax.optimization_barrier((up, down, to_up, to_down))
+        else:
+            up, down = lax.optimization_barrier((up, down))
+        if s == 0:
+            break
         up = up.astype(jnp.float32)
         down = down.astype(jnp.float32)
         if s == half - 1:
             up = jnp.pad(up, ((0, row_count - split), (0, 0)))
             down = jnp.pad(down, ((split, 0), (0, 0)))
-        if s:
-            up = (up + contribution(s, 1)).astype(jnp.bfloat16)
-            down = (down + contribution(s, 0)).astype(jnp.bfloat16)
+        up = (up + to_up[s].astype(jnp.float32)).astype(jnp.bfloat16)
+        down = (down + to_down[s].astype(jnp.float32)).astype(jnp.bfloat16)
         if s == 1:
             early = attend(
                 order, start, slot_length, queries, own_latent, block_latents, 0, first_rows
@@ -372,10 +370,12 @@
                 decode_count - first_rows,
             )
             context = jnp.concatenate([early, late], axis=0)
-    out = (contribution(0, 0) + up + down).astype(jnp.bfloat16)
-    prefill_out = out[:split]
-    decode_out = out[split:]
-    return (prefill_out, decode_out, context)
+
+    def finish(lo, hi):
+        total = up[lo:hi].astype(jnp.float32) + down[lo:hi].astype(jnp.float32)
+        return (total + to_up[0][lo:hi].astype(jnp.float32)).astype(jnp.bfloat16)
+
+    return (finish(0, split), finish(split, row_count), context)
 
 
 def solution(mesh):

time: 274 us -> 251 us (0.916)
  waiting for transfers between devices: 134 us -> 107 us
  between operations: 12.6 us -> 0.91 us
  starting transfers between devices: 30.5 us -> 39.3 us
  other arithmetic: 18.9 us -> 26.8 us
  Pallas kernels: 58.1 us -> 62.5 us
  local copies, waits for them, and re-layouts: 16.1 us -> 11.8 us
    ppermute x9 -> x16, waiting for transfers between devices: 61.5 us -> 13.5 us  [the longest x4 5.23 us: per_device(): next_front = [lax.ppermute(c, AXIS, ahead) for c in front]]
    all_to_all x1, waiting for transfers between devices: 0.01 us -> 36.3 us  [per_device(): lax.all_to_all(shipped, AXIS, split_axis=0, concat_axis=0, tiled=True)]
    all_to_all x1, waiting for transfers between devices: 10.3 us -> 0.01 us  [per_device(): small = lax.all_to_all(small, AXIS, split_axis=0, concat_axis=0, tiled=True)]
    ppermute x9 -> x16, starting transfers between devices: 8.36 us -> 14.6 us  [the longest x4 4.22 us: per_device(): next_rear = [lax.ppermute(c, AXIS, back) for c in rear]]
    convert_element_type x5 -> x11, other arithmetic: 15.2 us -> 21.4 us  [the longest x4 10.1 us: contribution(): return (weight[:, None] * both).astype(jnp.bfloat16)]
    ppermute x4, waiting for transfers between devices: 55 us -> 50.2 us  [per_device(): up = lax.ppermute(up, AXIS, ahead)]
    pallas_call x2, Pallas kernels: 6.55 us -> 9.85 us  [attend(): pl.pallas_call(attend_kernel, grid_spec=pltpu.PrefetchScalarGridSpec(num_...]
    unnamed x41 -> x34, local copies, waits for them, and re-layouts: 9.73 us -> 9.99 us
  transfers between devices with their start and end apart: 31 -> 44, of which waited for: 20 -> 18; matrix products, arithmetic and copies ran while one was open for 7% -> 7% of each run, Pallas kernels for 21% -> 25%
where the time goes in v3:
time: 251 us; the launch traced here: 248 us
  waiting for transfers between devices  107 us (43%)
  Pallas kernels  62.5 us (25%)
  starting transfers between devices  39.3 us (16%)
  other arithmetic  26.8 us (11%)
  local copies, waits for them, and re-layouts  11.8 us (5%)
    pallas_call x4, Pallas kernels, mlp(): pl.pallas_call(functools.partial(mlp_kernel, sizes, tile), in_specs=[anyw...  51.9 us
    ppermute x4, waiting for transfers between devices, per_device(): up = lax.ppermute(up, AXIS, ahead)  50.2 us
    all_to_all x1, waiting for transfers between devices, per_device(): lax.all_to_all(shipped, AXIS, split_axis=0, concat_axis=0, tiled=True)  36.3 us
    convert_element_type x4, other arithmetic, contribution(): return (weight[:, None] * both).astype(jnp.bfloat16)  10.1 us
    unnamed x34, local copies, waits for them, and re-layouts  9.99 us
    pallas_call x2, Pallas kernels, attend(): pl.pallas_call(attend_kernel, grid_spec=pltpu.PrefetchScalarGridSpec(num_...  9.85 us
    all_to_all x1, starting transfers between devices, per_device(): small = lax.all_to_all(small, AXIS, split_axis=0, concat_axis=0, tiled=True)  6.24 us
    all_to_all x1, starting transfers between devices, per_device(): lax.all_to_all(shipped, AXIS, split_axis=0, concat_axis=0, tiled=True)  6.01 us
  transfers between devices with their start and end apart: 44, of which 18 were waited for; matrix products, arithmetic and copies ran while one was open for 7% of the time, Pallas kernels for 25%

profile of v3, /device:TPU:20, one launch (start us, length us, event | category | flops | bytes accessed | tf_op | source)
XLA Modules:
  0.0 247.9 jit_solution(14137689380157734415)
XLA Ops:
  1.1 1.6 collective-permute-start.2
  3.2 1.6 collective-permute-start.3
  4.7 0.9 convert_reduce_fusion.2
  5.7 0.7 multiply_add_fusion
  6.5 0.8 select_reduce_fusion.1
  7.4 0.7 pad_add_fusion
  8.0 6.2 %all-to-all-start = ((s32[16,1,66]{2,1,0:T(1,128)}), s32[16,1,66]{2,1,0:T(1,128)S(1)}, u32[]{:S(2)}, u32[]{:S(2)}) async-start(s32[16,1,66]{2,1,0:T(1,128)} %bitcast.5), calls=%async_computation | async-start | bytes 16384 | tf_op jit(solution)/shard_map/all_to_all | solution.py:274
  14.3 1.3 copy-done.8
  15.6 0.7 ship.1
  16.4 1.5 copy-done.2
  17.8 0.7 dynamic-slice_bitcast_fusion
  18.8 4.3 %collective-permute-done.1.refs_1_ = bf16[32,7168]{1,0:T(8,128)(2,1)S(1)} collective-permute-done((bf16[32,7168]{1,0:T(8,128)(2,1)}, bf16[32,7168]{1,0:T(8,128)(2,1)S(1)}, u32[]{:S(2)}, u32[]{:S(2)}) %collective-permute-start.1) | collective-permute-done | bytes 458784 | tf_op jit(solution)/shard_map/ppermute | solution.py:287
  24.5 1.4 collective-permute-start.4
  25.9 1.5 collective-permute-start.5
  27.4 0.6 collective-permute-start.6
  28.0 1.0 collective-permute-start.7
  29.0 15.2 %mlp.4 = (bf16[192,7168]{1,0:T(8,128)(2,1)S(1)}, bf16[192,7168]{1,0:T(8,128)(2,1)}) custom-call(bf16[32,7168]{1,0:T(8,128)(2,1)S(1)} %collective-permute-done.refs_0_, bf16[32,7168]{1,0:T(8,128)(2,1)S(1)} %collective-permute-done.1.refs_1_, bf16[32,7168]{1,0:T(8,128)(2,1)S(1)} %collective-permute-done.2.refs_2_, ...), custom_call_target="tpu_custom_call" | custom-call | flops 8455716864 | bytes 33030144 | tf_op jit(solution)/shard_map/mlp/pallas_call | solution.py:91
  44.2 1.5 copy-done.3
  45.7 1.1 collective-permute-done.5.refs_1_
  46.8 2.1 collective-permute-done.7.refs_3_
  50.0 0.6 collective-permute-start.14
  50.7 0.6 collective-permute-start.15
  51.4 1.4 collective-permute-start.16
  52.8 1.2 collective-permute-start.17
  54.0 12.8 %mlp.5 = (bf16[128,7168]{1,0:T(8,128)(2,1)S(1)}, bf16[128,7168]{1,0:T(8,128)(2,1)}) custom-call(bf16[32,7168]{1,0:T(8,128)(2,1)S(1)} %collective-permute-done.4.refs_0_, bf16[32,7168]{1,0:T(8,128)(2,1)S(1)} %collective-permute-done.5.refs_1_, bf16[32,7168]{1,0:T(8,128)(2,1)S(1)} %collective-permute-done.6.refs_2_, ...), custom_call_target="tpu_custom_call" | custom-call | flops 5637144576 | bytes 29360128 | tf_op jit(solution)/shard_map/mlp/pallas_call | solution.py:91
  66.9 1.2 copy-done.5
  68.1 4.1 %collective-permute-done.15.refs_1_ = bf16[32,7168]{1,0:T(8,128)(2,1)S(1)} collective-permute-done((bf16[32,7168]{1,0:T(8,128)(2,1)S(1)}, bf16[32,7168]{1,0:T(8,128)(2,1)S(1)}, u32[]{:S(2)}, u32[]{:S(2)}) %collective-permute-start.15) | collective-permute-done | bytes 458784 | tf_op jit(solution)/shard_map/ppermute | solution.py:296
  72.2 1.6 collective-permute-done.17.refs_3_
  74.8 3.0 %collective-permute-done.24.refs_4_ = bf16[32,7168]{1,0:T(8,128)(2,1)S(1)} collective-permute-done((bf16[32,7168]{1,0:T(8,128)(2,1)S(1)}, bf16[32,7168]{1,0:T(8,128)(2,1)S(1)}, u32[]{:S(2)}, u32[]{:S(2)}) %collective-permute-start.24) | collective-permute-done | bytes 458784 | tf_op jit(solution)/shard_map/ppermute | solution.py:299
  77.9 0.8 collective-permute-start.22
  78.7 1.2 collective-permute-start.23
  80.2 12.8 %mlp.6 = (bf16[128,7168]{1,0:T(8,128)(2,1)S(1)}, bf16[128,7168]{1,0:T(8,128)(2,1)}) custom-call(bf16[32,7168]{1,0:T(8,128)(2,1)S(1)} %collective-permute-done.14.refs_0_, bf16[32,7168]{1,0:T(8,128)(2,1)S(1)} %collective-permute-done.15.refs_1_, bf16[32,7168]{1,0:T(8,128)(2,1)S(1)} %collective-permute-done.16.refs_2_, ...), custom_call_target="tpu_custom_call" | custom-call | flops 5637144576 | bytes 29360128 | tf_op jit(solution)/shard_map/mlp/pallas_call | solution.py:91
  93.1 1.2 copy-done.7
  95.3 6.0 %all-to-all-start.1 = ((bf16[32,64,576]{2,1,0:T(8,128)(2,1)}), bf16[32,64,576]{2,1,0:T(8,128)(2,1)S(1)}, u32[]{:S(2)}, u32[]{:S(2)}) async-start(bf16[32,64,576]{2,1,0:T(8,128)(2,1)} %copy-done.2), calls=%async_computation.1 | async-start | bytes 5242880 | tf_op jit(solution)/shard_map/all_to_all | solution.py:309
  101.9 11.1 %mlp.7 = (bf16[64,7168]{1,0:T(8,128)(2,1)S(1)}, bf16[64,7168]{1,0:T(8,128)(2,1)S(1)}) custom-call(bf16[32,7168]{1,0:T(8,128)(2,1)S(1)} %collective-permute-done.22.refs_0_, bf16[32,7168]{1,0:T(8,128)(2,1)S(1)} %collective-permute-done.23.refs_1_, bf16[32,7168]{1,0:T(8,128)(2,1)} %collective-permute-done.28.refs_2_, ...), custom_call_target="tpu_custom_call" | custom-call | flops 2818572288 | bytes 25690112 | tf_op jit(solution)/shard_map/mlp/pallas_call | solution.py:91
  113.2 3.3 %multiply_convert_fusion.1 = (bf16[64,7168]{1,0:T(8,128)(2,1)}, bf16[64,7168]{1,0:T(8,128)(2,1)}) fusion(bf16[128,7168]{1,0:T(8,128)(2,1)} %collective-permute-done.34, bf16[128,7168]{1,0:T(8,128)(2,1)S(1)} %copy-done.6, f32[64]{0:T(128)S(1)} %get-tuple-element.147, f32[64]{0:T(128)S(1)} %get-tuple-element.150), kind=kLoop, calls=%fused_computation.8 | loop fusion | flops 4587520 | bytes 5505536 | tf_op jit(solution)/shard_map/convert_element_type | solution.py:321
  116.8 1.5 copy-done.4
  118.3 3.9 %multiply_convert_fusion.2 = (bf16[64,7168]{1,0:T(8,128)(2,1)}, bf16[64,7168]{1,0:T(8,128)(2,1)}, bf16[64,7168]{1,0:T(8,128)(2,1)}) fusion(bf16[192,7168]{1,0:T(8,128)(2,1)} %collective-permute-done.33, bf16[192,7168]{1,0:T(8,128)(2,1)S(1)} %copy-done.4, f32[64]{0:T(128)S(1)} %get-tuple-element.148, f32[64]{0:T(128)S(1)} %get-tuple-element.151, ...), kind=kLoop, calls=%fused_computation.9 | loop fusion | flops 6881280 | bytes 8258304 | tf_op jit(solution)/shard_map/convert_element_type | solution.py:321
  122.2 36.3 %all-to-all-done.1.latent_ref = bf16[32,64,576]{2,1,0:T(8,128)(2,1)S(1)} async-done(((bf16[32,64,576]{2,1,0:T(8,128)(2,1)}), bf16[32,64,576]{2,1,0:T(8,128)(2,1)S(1)}, u32[]{:S(2)}, u32[]{:S(2)}) %all-to-all-start.1) | async-done | bytes 2359328 | tf_op jit(solution)/shard_map/all_to_all | solution.py:309
  158.5 1.9 collective-permute-start.31
  160.5 2.6 %multiply_convert_fusion = (bf16[64,7168]{1,0:T(8,128)(2,1)S(1)}, bf16[64,7168]{1,0:T(8,128)(2,1)S(1)}) fusion(bf16[128,7168]{1,0:T(8,128)(2,1)} %collective-permute-done.35, bf16[128,7168]{1,0:T(8,128)(2,1)} %copy-done.7, f32[64]{0:T(128)S(1)} %get-tuple-element.146, f32[64]{0:T(128)S(1)} %copy-done.16), kind=kLoop, calls=%fused_computation.7 | loop fusion | flops 4587520 | bytes 5505536 | tf_op jit(solution)/shard_map/convert_element_type | solution.py:321
  163.2 8.1 %collective-permute-done.31 = bf16[32,7168]{1,0:T(8,128)(2,1)S(1)} collective-permute-done((bf16[32,7168]{1,0:T(8,128)(2,1)S(1)}, bf16[32,7168]{1,0:T(8,128)(2,1)S(1)}, u32[]{:S(2)}, u32[]{:S(2)}) %collective-permute-start.31) | collective-permute-done | bytes 458784 | tf_op jit(solution)/shard_map/ppermute | solution.py:342
  171.3 1.5 collective-permute-done.32
  172.8 1.0 add_convert_fusion.4
  173.9 1.1 add_convert_fusion.5
  175.2 1.7 collective-permute-start.37
  177.3 19.4 %collective-permute-done.36 = bf16[64,7168]{1,0:T(8,128)(2,1)} collective-permute-done((bf16[64,7168]{1,0:T(8,128)(2,1)}, bf16[64,7168]{1,0:T(8,128)(2,1)}, u32[]{:S(2)}, u32[]{:S(2)}) %collective-permute-start.36) | collective-permute-done | bytes 917536 | tf_op jit(solution)/shard_map/ppermute | solution.py:342
  197.0 2.6 %add_convert_fusion.2 = bf16[64,7168]{1,0:T(8,128)(2,1)} fusion(bf16[64,7168]{1,0:T(8,128)(2,1)} %get-tuple-element.115, bf16[64,7168]{1,0:T(8,128)(2,1)} %collective-permute-done.37), kind=kLoop, calls=%fused_computation.3 | loop fusion | flops 1835008 | bytes 2752512 | tf_op jit(solution)/shard_map/convert_element_type | solution.py:356
  199.6 2.3 add_convert_fusion.3
  201.9 0.6 collective-permute-start.38
  202.5 1.4 collective-permute-start.39
  204.6 1.7 copy-done
  206.4 3.7 %attend.2 = bf16[16,64,512]{2,1,0:T(8,128)(2,1)S(1)} custom-call(s32[32]{0:T(128)S(1)} %select_reduce_fusion.3.order_ref, s32[17]{0:T(128)S(1)} %get-tuple-element.156.start_ref, s32[32]{0:T(128)S(1)} %get-tuple-element.157.length_ref, bf16[32,64,576]{2,1,0:T(8,128)(2,1)S(1)} %copy-done, bf16[32,1,576]{2,1,0:T(2,128)(2,1)S(1)} %copy.34.own_ref, ...), custom_call_target="tpu_custom_call" | custom-call | flops 150994944 | bytes 4587520 | tf_op jit(solution)/shard_map/attend/pallas_call | solution.py:182
  210.1 12.7 %collective-permute-done.38 = bf16[64,7168]{1,0:T(8,128)(2,1)} collective-permute-done((bf16[64,7168]{1,0:T(8,128)(2,1)}, bf16[64,7168]{1,0:T(8,128)(2,1)}, u32[]{:S(2)}, u32[]{:S(2)}) %collective-permute-start.38) | collective-permute-done | bytes 917536 | tf_op jit(solution)/shard_map/ppermute | solution.py:342
  222.8 0.6 collective-permute-done.39
  223.4 1.4 add_convert_fusion
  224.9 1.5 add_convert_fusion.1
  226.4 0.7 collective-permute-start.40
  227.1 1.4 collective-permute-start.41
  228.5 6.2 %attend.3 = bf16[16,64,512]{2,1,0:T(8,128)(2,1)S(1)} custom-call(s32[32]{0:T(128)S(1)} %select_reduce_fusion.3.order_ref, s32[17]{0:T(128)S(1)} %get-tuple-element.155.start_ref, s32[32]{0:T(128)S(1)} %get-tuple-element.157.length_ref, bf16[32,64,576]{2,1,0:T(8,128)(2,1)S(1)} %copy-done.1, bf16[32,1,576]{2,1,0:T(2,128)(2,1)S(1)} %copy.34.own_ref, ...), custom_call_target="tpu_custom_call" | custom-call | flops 150994944 | bytes 4587520 | tf_op jit(solution)/shard_map/attend/pallas_call | solution.py:182
  234.7 1.5 pad_maximum_fusion
  236.2 10.0 %collective-permute-done.40 = bf16[64,7168]{1,0:T(8,128)(2,1)S(1)} collective-permute-done((bf16[64,7168]{1,0:T(8,128)(2,1)S(1)}, bf16[64,7168]{1,0:T(8,128)(2,1)S(1)}, u32[]{:S(2)}, u32[]{:S(2)}) %collective-permute-start.40) | collective-permute-done | bytes 917536 | tf_op jit(solution)/shard_map/ppermute | solution.py:342
  246.1 0.5 collective-permute-done.41
  246.7 1.2 add_convert_fusion.6
  (102 shorter events, 9.4 us)
Async XLA Ops:
  0.6 17.9 %collective-permute-start = (bf16[32,7168]{1,0:T(8,128)(2,1)}, bf16[32,7168]{1,0:T(8,128)(2,1)S(1)}, u32[]{:S(2)}, u32[]{:S(2)}) collective-permute-start(bf16[32,7168]{1,0:T(8,128)(2,1)} %refs_4_.1), channel_id=1, source_target_pairs={{0,4},{1,5},{4,8},{5,9},{8,12},{9,13},{12,14},{13,15},{14,10},{15,... | collective-permute-start | bytes 1376264 | tf_op jit(solution)/shard_map/ppermute | solution.py:287
  1.1 21.9 %collective-permute-start.2 = (bf16[32,7168]{1,0:T(8,128)(2,1)}, bf16[32,7168]{1,0:T(8,128)(2,1)S(1)}, u32[]{:S(2)}, u32[]{:S(2)}) collective-permute-start(bf16[32,7168]{1,0:T(8,128)(2,1)} %refs_4_.1), channel_id=1, source_target_pairs={{4,0},{5,1},{8,4},{9,5},{12,8},{13,9},{14,12},{15,13},{10,14},{11,... | collective-permute-start | bytes 1376264 | tf_op jit(solution)/shard_map/ppermute | solution.py:288
  2.7 20.3 %collective-permute-start.1 = (bf16[32,7168]{1,0:T(8,128)(2,1)}, bf16[32,7168]{1,0:T(8,128)(2,1)S(1)}, u32[]{:S(2)}, u32[]{:S(2)}) collective-permute-start(bf16[32,7168]{1,0:T(8,128)(2,1)} %refs_5_.1), channel_id=1, source_target_pairs={{0,4},{1,5},{4,8},{5,9},{8,12},{9,13},{12,14},{13,15},{14,10},{15,... | collective-permute-start | bytes 1376264 | tf_op jit(solution)/shard_map/ppermute | solution.py:287
  3.2 20.1 %collective-permute-start.3 = (bf16[32,7168]{1,0:T(8,128)(2,1)}, bf16[32,7168]{1,0:T(8,128)(2,1)S(1)}, u32[]{:S(2)}, u32[]{:S(2)}) collective-permute-start(bf16[32,7168]{1,0:T(8,128)(2,1)} %refs_5_.1), channel_id=1, source_target_pairs={{4,0},{5,1},{8,4},{9,5},{12,8},{13,9},{14,12},{15,13},{10,14},{11,... | collective-permute-start | bytes 1376264 | tf_op jit(solution)/shard_map/ppermute | solution.py:288
  4.7 19.1 %collective-permute-start.12 = (bf16[32,7168]{1,0:T(8,128)(2,1)}, bf16[32,7168]{1,0:T(8,128)(2,1)S(1)}, u32[]{:S(2)}, u32[]{:S(2)}) collective-permute-start(bf16[32,7168]{1,0:T(8,128)(2,1)} %refs_4_.1), channel_id=1, source_target_pairs={{0,1},{1,0},{2,3},{3,2},{4,5},{5,4},{6,7},{7,6},{8,9},{9,8},{10,11... | collective-permute-start | bytes 1376264 | tf_op jit(solution)/shard_map/ppermute | solution.py:286
  8.0 16.3 %all-to-all-start = ((s32[16,1,66]{2,1,0:T(1,128)}), s32[16,1,66]{2,1,0:T(1,128)S(1)}, u32[]{:S(2)}, u32[]{:S(2)}) async-start(s32[16,1,66]{2,1,0:T(1,128)} %bitcast.5), calls=%async_computation | async-start | bytes 16384 | tf_op jit(solution)/shard_map/all_to_all | solution.py:274
  14.3 1.3 copy-start.8
  15.6 2.9 %copy-start.10 = (bf16[32,7168]{1,0:T(8,128)(2,1)S(1)}, bf16[32,7168]{1,0:T(8,128)(2,1)}, u32[]{:S(2)}) copy-start(bf16[32,7168]{1,0:T(8,128)(2,1)} %refs_5_.1) | copy-start | bytes 1376260
  15.6 13.4 %copy-start.9 = (bf16[32,7168]{1,0:T(8,128)(2,1)S(1)}, bf16[32,7168]{1,0:T(8,128)(2,1)}, u32[]{:S(2)}) copy-start(bf16[32,7168]{1,0:T(8,128)(2,1)} %refs_4_.1) | copy-start | bytes 1376260
  16.4 1.5 copy-start.2
  18.5 6.0 %collective-permute-start.13 = (bf16[32,7168]{1,0:T(8,128)(2,1)S(1)}, bf16[32,7168]{1,0:T(8,128)(2,1)}, u32[]{:S(2)}, u32[]{:S(2)}) collective-permute-start(bf16[32,7168]{1,0:T(8,128)(2,1)S(1)} %copy-done.10), channel_id=1, source_target_pairs={{0,1},{1,0},{2,3},{3,2},{4,5},{5,4},{6,7},{7,6},{8,9},{9,8},{10,11... | collective-permute-start | bytes 1376264 | tf_op jit(solution)/shard_map/ppermute | solution.py:286
  23.3 2.6 %collective-permute-start.10 = (bf16[32,7168]{1,0:T(8,128)(2,1)S(1)}, bf16[32,7168]{1,0:T(8,128)(2,1)}, u32[]{:S(2)}, u32[]{:S(2)}) collective-permute-start(bf16[32,7168]{1,0:T(8,128)(2,1)S(1)} %collective-permute-done.2.refs_2_), channel_id=1, source_target_pairs={{0,1},{1,0},{2,3},{3,2},{4,5},{5,4},{6,7},{7,6},{8,9},{9,8},{10,11... | collective-permute-start | bytes 1376264 | tf_op jit(solution)/shard_map/ppermute | solution.py:299
  23.3 4.1 %collective-permute-start.11 = (bf16[32,7168]{1,0:T(8,128)(2,1)S(1)}, bf16[32,7168]{1,0:T(8,128)(2,1)}, u32[]{:S(2)}, u32[]{:S(2)}) collective-permute-start(bf16[32,7168]{1,0:T(8,128)(2,1)S(1)} %collective-permute-done.3.refs_3_), channel_id=1, source_target_pairs={{0,1},{1,0},{2,3},{3,2},{4,5},{5,4},{6,7},{7,6},{8,9},{9,8},{10,11... | collective-permute-start | bytes 1376264 | tf_op jit(solution)/shard_map/ppermute | solution.py:299
  23.8 4.2 %collective-permute-start.8 = (bf16[32,7168]{1,0:T(8,128)(2,1)S(1)}, bf16[32,7168]{1,0:T(8,128)(2,1)}, u32[]{:S(2)}, u32[]{:S(2)}) collective-permute-start(bf16[32,7168]{1,0:T(8,128)(2,1)S(1)} %collective-permute-done.refs_0_), channel_id=1, source_target_pairs={{0,1},{1,0},{2,3},{3,2},{4,5},{5,4},{6,7},{7,6},{8,9},{9,8},{10,11... | collective-permute-start | bytes 1376264 | tf_op jit(solution)/shard_map/ppermute | solution.py:299
  23.8 5.2 %collective-permute-start.9 = (bf16[32,7168]{1,0:T(8,128)(2,1)S(1)}, bf16[32,7168]{1,0:T(8,128)(2,1)}, u32[]{:S(2)}, u32[]{:S(2)}) collective-permute-start(bf16[32,7168]{1,0:T(8,128)(2,1)S(1)} %collective-permute-done.1.refs_1_), channel_id=1, source_target_pairs={{0,1},{1,0},{2,3},{3,2},{4,5},{5,4},{6,7},{7,6},{8,9},{9,8},{10,11... | collective-permute-start | bytes 1376264 | tf_op jit(solution)/shard_map/ppermute | solution.py:299
  24.5 21.2 %collective-permute-start.4 = (bf16[32,7168]{1,0:T(8,128)(2,1)S(1)}, bf16[32,7168]{1,0:T(8,128)(2,1)S(1)}, u32[]{:S(2)}, u32[]{:S(2)}) collective-permute-start(bf16[32,7168]{1,0:T(8,128)(2,1)S(1)} %collective-permute-done.refs_0_), channel_id=1, source_target_pairs={{0,4},{1,5},{4,8},{5,9},{8,12},{9,13},{12,14},{13,15},{14,10},{15,... | collective-permute-start | bytes 1376264 | tf_op jit(solution)/shard_map/ppermute | solution.py:296
  25.9 20.9 %collective-permute-start.5 = (bf16[32,7168]{1,0:T(8,128)(2,1)S(1)}, bf16[32,7168]{1,0:T(8,128)(2,1)S(1)}, u32[]{:S(2)}, u32[]{:S(2)}) collective-permute-start(bf16[32,7168]{1,0:T(8,128)(2,1)S(1)} %collective-permute-done.1.refs_1_), channel_id=1, source_target_pairs={{0,4},{1,5},{4,8},{5,9},{8,12},{9,13},{12,14},{13,15},{14,10},{15,... | collective-permute-start | bytes 1376264 | tf_op jit(solution)/shard_map/ppermute | solution.py:296
  27.4 19.4 %collective-permute-start.6 = (bf16[32,7168]{1,0:T(8,128)(2,1)S(1)}, bf16[32,7168]{1,0:T(8,128)(2,1)S(1)}, u32[]{:S(2)}, u32[]{:S(2)}) collective-permute-start(bf16[32,7168]{1,0:T(8,128)(2,1)S(1)} %collective-permute-done.2.refs_2_), channel_id=1, source_target_pairs={{4,0},{5,1},{8,4},{9,5},{12,8},{13,9},{14,12},{15,13},{10,14},{11,... | collective-permute-start | bytes 1376264 | tf_op jit(solution)/shard_map/ppermute | solution.py:297
  28.0 21.0 %collective-permute-start.7 = (bf16[32,7168]{1,0:T(8,128)(2,1)S(1)}, bf16[32,7168]{1,0:T(8,128)(2,1)S(1)}, u32[]{:S(2)}, u32[]{:S(2)}) collective-permute-start(bf16[32,7168]{1,0:T(8,128)(2,1)S(1)} %collective-permute-done.3.refs_3_), channel_id=1, source_target_pairs={{4,0},{5,1},{8,4},{9,5},{12,8},{13,9},{14,12},{15,13},{10,14},{11,... | collective-permute-start | bytes 1376264 | tf_op jit(solution)/shard_map/ppermute | solution.py:297
  44.2 1.5 copy-start.3
  48.9 1.8 collective-permute-start.18
  48.9 2.5 collective-permute-start.19
  49.4 3.3 %collective-permute-start.20 = (bf16[32,7168]{1,0:T(8,128)(2,1)S(1)}, bf16[32,7168]{1,0:T(8,128)(2,1)S(1)}, u32[]{:S(2)}, u32[]{:S(2)}) collective-permute-start(bf16[32,7168]{1,0:T(8,128)(2,1)S(1)} %collective-permute-done.6.refs_2_), channel_id=1, source_target_pairs={{0,1},{1,0},{2,3},{3,2},{4,5},{5,4},{6,7},{7,6},{8,9},{9,8},{10,11... | collective-permute-start | bytes 1376264 | tf_op jit(solution)/shard_map/ppermute | solution.py:299
  49.4 4.6 %collective-permute-start.21 = (bf16[32,7168]{1,0:T(8,128)(2,1)S(1)}, bf16[32,7168]{1,0:T(8,128)(2,1)S(1)}, u32[]{:S(2)}, u32[]{:S(2)}) collective-permute-start(bf16[32,7168]{1,0:T(8,128)(2,1)S(1)} %collective-permute-done.7.refs_3_), channel_id=1, source_target_pairs={{0,1},{1,0},{2,3},{3,2},{4,5},{5,4},{6,7},{7,6},{8,9},{9,8},{10,11... | collective-permute-start | bytes 1376264 | tf_op jit(solution)/shard_map/ppermute | solution.py:299
  50.0 18.1 %collective-permute-start.14 = (bf16[32,7168]{1,0:T(8,128)(2,1)S(1)}, bf16[32,7168]{1,0:T(8,128)(2,1)S(1)}, u32[]{:S(2)}, u32[]{:S(2)}) collective-permute-start(bf16[32,7168]{1,0:T(8,128)(2,1)S(1)} %collective-permute-done.4.refs_0_), channel_id=1, source_target_pairs={{0,4},{1,5},{4,8},{5,9},{8,12},{9,13},{12,14},{13,15},{14,10},{15,... | collective-permute-start | bytes 1376264 | tf_op jit(solution)/shard_map/ppermute | solution.py:296
  50.7 21.5 %collective-permute-start.15 = (bf16[32,7168]{1,0:T(8,128)(2,1)S(1)}, bf16[32,7168]{1,0:T(8,128)(2,1)S(1)}, u32[]{:S(2)}, u32[]{:S(2)}) collective-permute-start(bf16[32,7168]{1,0:T(8,128)(2,1)S(1)} %collective-permute-done.5.refs_1_), channel_id=1, source_target_pairs={{0,4},{1,5},{4,8},{5,9},{8,12},{9,13},{12,14},{13,15},{14,10},{15,... | collective-permute-start | bytes 1376264 | tf_op jit(solution)/shard_map/ppermute | solution.py:296
  51.4 20.8 %collective-permute-start.16 = (bf16[32,7168]{1,0:T(8,128)(2,1)S(1)}, bf16[32,7168]{1,0:T(8,128)(2,1)S(1)}, u32[]{:S(2)}, u32[]{:S(2)}) collective-permute-start(bf16[32,7168]{1,0:T(8,128)(2,1)S(1)} %collective-permute-done.6.refs_2_), channel_id=1, source_target_pairs={{4,0},{5,1},{8,4},{9,5},{12,8},{13,9},{14,12},{15,13},{10,14},{11,... | collective-permute-start | bytes 1376264 | tf_op jit(solution)/shard_map/ppermute | solution.py:297
  52.8 21.0 %collective-permute-start.17 = (bf16[32,7168]{1,0:T(8,128)(2,1)S(1)}, bf16[32,7168]{1,0:T(8,128)(2,1)S(1)}, u32[]{:S(2)}, u32[]{:S(2)}) collective-permute-start(bf16[32,7168]{1,0:T(8,128)(2,1)S(1)} %collective-permute-done.7.refs_3_), channel_id=1, source_target_pairs={{4,0},{5,1},{8,4},{9,5},{12,8},{13,9},{14,12},{15,13},{10,14},{11,... | collective-permute-start | bytes 1376264 | tf_op jit(solution)/shard_map/ppermute | solution.py:297
  66.9 1.2 copy-start.5
  73.8 39.4 %collective-permute-start.34 = (bf16[128,7168]{1,0:T(8,128)(2,1)}, bf16[128,7168]{1,0:T(8,128)(2,1)}, u32[]{:S(2)}, u32[]{:S(2)}) collective-permute-start(bf16[128,7168]{1,0:T(8,128)(2,1)} %get-tuple-element.103), channel_id=1, source_target_pairs={{0,1},{1,0},{2,3},{3,2},{4,5},{5,4},{6,7},{7,6},{8,9},{9,8},{10,11... | collective-permute-start | bytes 5505032 | tf_op jit(solution)/shard_map/ppermute | solution.py:308
  73.8 4.1 %collective-permute-start.24 = (bf16[32,7168]{1,0:T(8,128)(2,1)S(1)}, bf16[32,7168]{1,0:T(8,128)(2,1)S(1)}, u32[]{:S(2)}, u32[]{:S(2)}) collective-permute-start(bf16[32,7168]{1,0:T(8,128)(2,1)S(1)} %collective-permute-done.14.refs_0_), channel_id=1, source_target_pairs={{0,1},{1,0},{2,3},{3,2},{4,5},{5,4},{6,7},{7,6},{8,9},{9,8},{10,11... | collective-permute-start | bytes 1376264 | tf_op jit(solution)/shard_map/ppermute | solution.py:299
  74.3 4.4 %collective-permute-start.25 = (bf16[32,7168]{1,0:T(8,128)(2,1)S(1)}, bf16[32,7168]{1,0:T(8,128)(2,1)S(1)}, u32[]{:S(2)}, u32[]{:S(2)}) collective-permute-start(bf16[32,7168]{1,0:T(8,128)(2,1)S(1)} %collective-permute-done.15.refs_1_), channel_id=1, source_target_pairs={{0,1},{1,0},{2,3},{3,2},{4,5},{5,4},{6,7},{7,6},{8,9},{9,8},{10,11... | collective-permute-start | bytes 1376264 | tf_op jit(solution)/shard_map/ppermute | solution.py:299
  74.3 5.6 %collective-permute-start.26 = (bf16[32,7168]{1,0:T(8,128)(2,1)S(1)}, bf16[32,7168]{1,0:T(8,128)(2,1)S(1)}, u32[]{:S(2)}, u32[]{:S(2)}) collective-permute-start(bf16[32,7168]{1,0:T(8,128)(2,1)S(1)} %collective-permute-done.16.refs_2_), channel_id=1, source_target_pairs={{0,1},{1,0},{2,3},{3,2},{4,5},{5,4},{6,7},{7,6},{8,9},{9,8},{10,11... | collective-permute-start | bytes 1376264 | tf_op jit(solution)/shard_map/ppermute | solution.py:299
  74.8 5.4 %collective-permute-start.27 = (bf16[32,7168]{1,0:T(8,128)(2,1)S(1)}, bf16[32,7168]{1,0:T(8,128)(2,1)S(1)}, u32[]{:S(2)}, u32[]{:S(2)}) collective-permute-start(bf16[32,7168]{1,0:T(8,128)(2,1)S(1)} %collective-permute-done.17.refs_3_), channel_id=1, source_target_pairs={{0,1},{1,0},{2,3},{3,2},{4,5},{5,4},{6,7},{7,6},{8,9},{9,8},{10,11... | collective-permute-start | bytes 1376264 | tf_op jit(solution)/shard_map/ppermute | solution.py:299
  77.9 16.4 %collective-permute-start.22 = (bf16[32,7168]{1,0:T(8,128)(2,1)S(1)}, bf16[32,7168]{1,0:T(8,128)(2,1)S(1)}, u32[]{:S(2)}, u32[]{:S(2)}) collective-permute-start(bf16[32,7168]{1,0:T(8,128)(2,1)S(1)} %collective-permute-done.14.refs_0_), channel_id=1, source_target_pairs={{0,4},{1,5},{4,8},{5,9},{8,12},{9,13},{12,14},{13,15},{14,10},{15,... | collective-permute-start | bytes 1376264 | tf_op jit(solution)/shard_map/ppermute | solution.py:293
  78.7 15.6 %collective-permute-start.23 = (bf16[32,7168]{1,0:T(8,128)(2,1)S(1)}, bf16[32,7168]{1,0:T(8,128)(2,1)S(1)}, u32[]{:S(2)}, u32[]{:S(2)}) collective-permute-start(bf16[32,7168]{1,0:T(8,128)(2,1)S(1)} %collective-permute-done.17.refs_3_), channel_id=1, source_target_pairs={{4,0},{5,1},{8,4},{9,5},{12,8},{13,9},{14,12},{15,13},{10,14},{11,... | collective-permute-start | bytes 1376264 | tf_op jit(solution)/shard_map/ppermute | solution.py:294
  93.1 1.2 copy-start.7
  94.3 7.6 %collective-permute-start.28 = (bf16[32,7168]{1,0:T(8,128)(2,1)S(1)}, bf16[32,7168]{1,0:T(8,128)(2,1)}, u32[]{:S(2)}, u32[]{:S(2)}) collective-permute-start(bf16[32,7168]{1,0:T(8,128)(2,1)S(1)} %collective-permute-done.22.refs_0_), channel_id=1, source_target_pairs={{0,1},{1,0},{2,3},{3,2},{4,5},{5,4},{6,7},{7,6},{8,9},{9,8},{10,11... | collective-permute-start | bytes 1376264 | tf_op jit(solution)/shard_map/ppermute | solution.py:299
  94.4 7.5 %collective-permute-start.29 = (bf16[32,7168]{1,0:T(8,128)(2,1)S(1)}, bf16[32,7168]{1,0:T(8,128)(2,1)}, u32[]{:S(2)}, u32[]{:S(2)}) collective-permute-start(bf16[32,7168]{1,0:T(8,128)(2,1)S(1)} %collective-permute-done.23.refs_1_), channel_id=1, source_target_pairs={{0,1},{1,0},{2,3},{3,2},{4,5},{5,4},{6,7},{7,6},{8,9},{9,8},{10,11... | collective-permute-start | bytes 1376264 | tf_op jit(solution)/shard_map/ppermute | solution.py:299
  94.8 22.0 %collective-permute-start.33 = (bf16[192,7168]{1,0:T(8,128)(2,1)}, bf16[192,7168]{1,0:T(8,128)(2,1)}, u32[]{:S(2)}, u32[]{:S(2)}) collective-permute-start(bf16[192,7168]{1,0:T(8,128)(2,1)} %get-tuple-element.101), channel_id=1, source_target_pairs={{0,1},{1,0},{2,3},{3,2},{4,5},{5,4},{6,7},{7,6},{8,9},{9,8},{10,11... | collective-permute-start | bytes 8257544 | tf_op jit(solution)/shard_map/ppermute | solution.py:308
  94.9 65.6 %collective-permute-start.35 = (bf16[128,7168]{1,0:T(8,128)(2,1)}, bf16[128,7168]{1,0:T(8,128)(2,1)}, u32[]{:S(2)}, u32[]{:S(2)}) collective-permute-start(bf16[128,7168]{1,0:T(8,128)(2,1)} %get-tuple-element.105), channel_id=1, source_target_pairs={{0,1},{1,0},{2,3},{3,2},{4,5},{5,4},{6,7},{7,6},{8,9},{9,8},{10,11... | collective-permute-start | bytes 5505032 | tf_op jit(solution)/shard_map/ppermute | solution.py:308
  95.3 63.2 %all-to-all-start.1 = ((bf16[32,64,576]{2,1,0:T(8,128)(2,1)}), bf16[32,64,576]{2,1,0:T(8,128)(2,1)S(1)}, u32[]{:S(2)}, u32[]{:S(2)}) async-start(bf16[32,64,576]{2,1,0:T(8,128)(2,1)} %copy-done.2), calls=%async_computation.1 | async-start | bytes 5242880 | tf_op jit(solution)/shard_map/all_to_all | solution.py:309
  101.9 11.3 %copy-start.6 = (bf16[128,7168]{1,0:T(8,128)(2,1)S(1)}, bf16[128,7168]{1,0:T(8,128)(2,1)}, u32[]{:S(2)}) copy-start(bf16[128,7168]{1,0:T(8,128)(2,1)} %copy-done.5) | copy-start | bytes 5505028
  113.0 3.5 %collective-permute-start.30 = (bf16[64,7168]{1,0:T(8,128)(2,1)S(1)}, bf16[64,7168]{1,0:T(8,128)(2,1)S(1)}, u32[]{:S(2)}, u32[]{:S(2)}) collective-permute-start(bf16[64,7168]{1,0:T(8,128)(2,1)S(1)} %get-tuple-element.94), channel_id=1, source_target_pairs={{0,1},{1,0},{2,3},{3,2},{4,5},{5,4},{6,7},{7,6},{8,9},{9,8},{10,11... | collective-permute-start | bytes 2752520 | tf_op jit(solution)/shard_map/ppermute | solution.py:308
  116.5 1.8 copy-start.4
  118.3 42.2 %copy-start.16 = (f32[64]{0:T(128)S(1)}, f32[64]{0:T(128)}, u32[]{:S(2)}) copy-start(f32[64]{0:T(128)} %get-tuple-element.149) | copy-start | bytes 772
  158.5 12.8 %collective-permute-start.31 = (bf16[32,7168]{1,0:T(8,128)(2,1)S(1)}, bf16[32,7168]{1,0:T(8,128)(2,1)S(1)}, u32[]{:S(2)}, u32[]{:S(2)}) collective-permute-start(bf16[32,7168]{1,0:T(8,128)(2,1)S(1)} %get-tuple-element.98), channel_id=1, source_target_pairs={{0,4},{1,5},{4,8},{5,9},{8,12},{9,13},{12,14},{13,15},{14,10},{15,... | collective-permute-start | bytes 1376264 | tf_op jit(solution)/shard_map/ppermute | solution.py:342
  160.4 12.4 %collective-permute-start.32 = (bf16[32,7168]{1,0:T(8,128)(2,1)S(1)}, bf16[32,7168]{1,0:T(8,128)(2,1)S(1)}, u32[]{:S(2)}, u32[]{:S(2)}) collective-permute-start(bf16[32,7168]{1,0:T(8,128)(2,1)S(1)} %get-tuple-element.99), channel_id=1, source_target_pairs={{4,0},{5,1},{8,4},{9,5},{12,8},{13,9},{14,12},{15,13},{10,14},{11,... | collective-permute-start | bytes 1376264 | tf_op jit(solution)/shard_map/ppermute | solution.py:343
  172.8 4.2 %copy-start.15 = (bf16[32,576]{1,0:T(8,128)(2,1)S(1)}, bf16[32,576]{1,0:T(8,128)(2,1)}, u32[]{:S(2)}) copy-start(bf16[32,576]{1,0:T(8,128)(2,1)} %param.24) | copy-start | bytes 110596
  174.9 21.7 %collective-permute-start.36 = (bf16[64,7168]{1,0:T(8,128)(2,1)}, bf16[64,7168]{1,0:T(8,128)(2,1)}, u32[]{:S(2)}, u32[]{:S(2)}) collective-permute-start(bf16[64,7168]{1,0:T(8,128)(2,1)} %add_convert_fusion.5), channel_id=1, source_target_pairs={{0,4},{1,5},{4,8},{5,9},{8,12},{9,13},{12,14},{13,15},{14,10},{15,... | collective-permute-start | bytes 2752520 | tf_op jit(solution)/shard_map/ppermute | solution.py:342
  175.2 21.8 %collective-permute-start.37 = (bf16[64,7168]{1,0:T(8,128)(2,1)}, bf16[64,7168]{1,0:T(8,128)(2,1)}, u32[]{:S(2)}, u32[]{:S(2)}) collective-permute-start(bf16[64,7168]{1,0:T(8,128)(2,1)} %add_convert_fusion.4), channel_id=1, source_target_pairs={{4,0},{5,1},{8,4},{9,5},{12,8},{13,9},{14,12},{15,13},{10,14},{11,... | collective-permute-start | bytes 2752520 | tf_op jit(solution)/shard_map/ppermute | solution.py:343
  177.3 22.3 %copy-start.14 = (bf16[64,7168]{1,0:T(8,128)(2,1)S(1)}, bf16[64,7168]{1,0:T(8,128)(2,1)}, u32[]{:S(2)}) copy-start(bf16[64,7168]{1,0:T(8,128)(2,1)} %get-tuple-element.113) | copy-start | bytes 2752516
  201.9 20.9 %collective-permute-start.38 = (bf16[64,7168]{1,0:T(8,128)(2,1)}, bf16[64,7168]{1,0:T(8,128)(2,1)}, u32[]{:S(2)}, u32[]{:S(2)}) collective-permute-start(bf16[64,7168]{1,0:T(8,128)(2,1)} %add_convert_fusion.3), channel_id=1, source_target_pairs={{0,4},{1,5},{4,8},{5,9},{8,12},{9,13},{12,14},{13,15},{14,10},{15,... | collective-permute-start | bytes 2752520 | tf_op jit(solution)/shard_map/ppermute | solution.py:342
  202.5 20.9 %collective-permute-start.39 = (bf16[64,7168]{1,0:T(8,128)(2,1)}, bf16[64,7168]{1,0:T(8,128)(2,1)}, u32[]{:S(2)}, u32[]{:S(2)}) collective-permute-start(bf16[64,7168]{1,0:T(8,128)(2,1)} %add_convert_fusion.2), channel_id=1, source_target_pairs={{4,0},{5,1},{8,4},{9,5},{12,8},{13,9},{14,12},{15,13},{10,14},{11,... | collective-permute-start | bytes 2752520 | tf_op jit(solution)/shard_map/ppermute | solution.py:343
  204.6 1.7 copy-start
  206.4 17.1 %copy-start.13 = (bf16[64,7168]{1,0:T(8,128)(2,1)S(1)}, bf16[64,7168]{1,0:T(8,128)(2,1)}, u32[]{:S(2)}) copy-start(bf16[64,7168]{1,0:T(8,128)(2,1)} %get-tuple-element.121) | copy-start | bytes 2752516
  210.1 14.8 %copy-start.12 = (bf16[64,7168]{1,0:T(8,128)(2,1)S(1)}, bf16[64,7168]{1,0:T(8,128)(2,1)}, u32[]{:S(2)}) copy-start(bf16[64,7168]{1,0:T(8,128)(2,1)} %get-tuple-element.119) | copy-start | bytes 2752516
  224.8 3.6 %copy-start.1 = (bf16[32,64,576]{2,1,0:T(8,128)(2,1)S(1)}, bf16[32,64,576]{2,1,0:T(8,128)(2,1)}, u32[]{:S(2)}) copy-start(bf16[32,64,576]{2,1,0:T(8,128)(2,1)} %query_ref.3) | copy-start | bytes 7077892
  226.4 19.7 %collective-permute-start.40 = (bf16[64,7168]{1,0:T(8,128)(2,1)S(1)}, bf16[64,7168]{1,0:T(8,128)(2,1)S(1)}, u32[]{:S(2)}, u32[]{:S(2)}) collective-permute-start(bf16[64,7168]{1,0:T(8,128)(2,1)S(1)} %add_convert_fusion.1), channel_id=1, source_target_pairs={{0,4},{1,5},{4,8},{5,9},{8,12},{9,13},{12,14},{13,15},{14,10},{15,... | collective-permute-start | bytes 2752520 | tf_op jit(solution)/shard_map/ppermute | solution.py:342
  227.1 19.6 %collective-permute-start.41 = (bf16[64,7168]{1,0:T(8,128)(2,1)S(1)}, bf16[64,7168]{1,0:T(8,128)(2,1)S(1)}, u32[]{:S(2)}, u32[]{:S(2)}) collective-permute-start(bf16[64,7168]{1,0:T(8,128)(2,1)S(1)} %add_convert_fusion), channel_id=1, source_target_pairs={{4,0},{5,1},{8,4},{9,5},{12,8},{13,9},{14,12},{15,13},{10,14},{11,... | collective-permute-start | bytes 2752520 | tf_op jit(solution)/shard_map/ppermute | solution.py:343
  234.7 12.0 %copy-start.11 = (bf16[64,7168]{1,0:T(8,128)(2,1)S(1)}, bf16[64,7168]{1,0:T(8,128)(2,1)}, u32[]{:S(2)}) copy-start(bf16[64,7168]{1,0:T(8,128)(2,1)} %get-tuple-element.129) | copy-start | bytes 2752516

commit v4 on v3

--- a/solution.py
+++ b/solution.py
@@ -272,6 +272,15 @@
         [jnp.repeat(gates.T, 2, axis=0), slot_codes.reshape(devices, CAPC)], axis=1
     ).astype(jnp.int32)
     small = lax.all_to_all(small, AXIS, split_axis=0, concat_axis=0, tiled=True)
+    shipped = ship_blocks(latents, source)
+
+    own = [prefill_tokens, decode_rows]
+    sizes = [prefill_count, decode_count]
+    front = {1: [lax.ppermute(c, AXIS, ahead) for c in own]}
+    rear = {1: [lax.ppermute(c, AXIS, back) for c in own]}
+    front[1][0], rear[1][0], shipped, small = lax.optimization_barrier(
+        (front[1][0], rear[1][0], shipped, small)
+    )
     at_shift = lax.dynamic_index_in_dim(jnp.asarray(neighbours), me, 0, keepdims=False)
     picked = at_shift[:, None] == jnp.arange(devices)[None, :]
     shift_gates = jnp.sum(jnp.where(picked[:, :, None], small[None, :, :row_count], 0), axis=1)
@@ -280,44 +289,42 @@
     slot_length = slot_codes % (block_rows + 1)
     slot_request = slot_codes // (block_rows + 1)
 
-    shipped = ship_blocks(latents, source)
-
-    own = [prefill_tokens, decode_rows]
-    own_other = [lax.ppermute(c, AXIS, across) for c in own]
-    front = [lax.ppermute(c, AXIS, ahead) for c in own]
-    rear = [lax.ppermute(c, AXIS, back) for c in own]
-    front, rear, shipped = lax.optimization_barrier((front, rear, shipped))
-    parts = {}
-    for s in range(1, half + 1):
-        if s == half - 1:
-            next_front = [lax.ppermute(front[0], AXIS, ahead)]
-            next_rear = [lax.ppermute(rear[1], AXIS, back)]
-        elif s < half:
-            next_front = [lax.ppermute(c, AXIS, ahead) for c in front]
-            next_rear = [lax.ppermute(c, AXIS, back) for c in rear]
-        mine = front + rear
+    for s in range(2, half):
+        front[s] = [lax.ppermute(c, AXIS, ahead) for c in front[s - 1]]
+        rear[s] = [lax.ppermute(c, AXIS, back) for c in rear[s - 1]]
+
+    def work(s, mine):
         other = [lax.ppermute(c, AXIS, across) for c in mine]
-        if s == 1:
-            mine = mine + own
-            other = other + own_other
-        part, for_other = mlp(mine, other, gate_up, down_proj)
-        if s < half:
-            front, rear, part, for_other, shipped, shift_gates = lax.optimization_barrier(
-                (next_front, next_rear, part, for_other, shipped, shift_gates)
-            )
-        parts[s] = (part, lax.ppermute(for_other, AXIS, across))
+        return mlp(mine, other, gate_up, down_proj)
+
+    first = min(2, half - 1)
+    near, _ = lax.optimization_barrier((front[1] + rear[1] + own, front[first][:1]))
+    results = {1: work(1, near)}
+    last_rear, results[1] = lax.optimization_barrier((rear[half - 1][1], results[1]))
+    front[half] = [lax.ppermute(front[half - 1][0], AXIS, ahead)]
+    rear[half] = [lax.ppermute(last_rear, AXIS, back)]
+    front, rear, shipped, shift_gates, results = lax.optimization_barrier(
+        (front, rear, shipped, shift_gates, results)
+    )
     block_latents = lax.all_to_all(shipped, AXIS, split_axis=0, concat_axis=0, tiled=True)
-
-    def contribution(s, k):
+    for s in [half] + list(range(half - 1, 1, -1)):
+        results[s] = work(s, front[s] + rear[s])
+    parts = {s: (part, lax.ppermute(rest, AXIS, across)) for s, (part, rest) in results.items()}
+
+    def contribution(s, k, flow):
         part, from_other = parts[max(s, 1)]
-        size = split if s == half else row_count
-        lo = 2 * row_count if s == 0 else k * size
+        size = sizes[flow]
+        lo = flow * split
+        if s == half:
+            lo = k * split
+        elif s == 0:
+            lo = lo + 2 * row_count
+        else:
+            lo = lo + k * row_count
         both = part[lo : lo + size].astype(jnp.float32) + from_other[lo : lo + size].astype(
             jnp.float32
         )
-        weight = shift_gates[((-s, s)[k] + chips) % chips]
-        if s == half:
-            weight = (weight[:split], weight[split:])[k]
+        weight = shift_gates[((-s, s)[k] + chips) % chips, flow * split : flow * split + size]
         return (weight[:, None] * both).astype(jnp.bfloat16)
 
     key = jnp.where(slot_length > 0, slot_request, decode_count)
@@ -332,50 +339,59 @@
     start = jnp.sum(key[None, :] < jnp.arange(decode_count + 1)[:, None], axis=1).astype(jnp.int32)
     first_rows = decode_count // 2
 
-    up = contribution(half, 0)
-    down = contribution(half, 1)
-    up, down, block_latents = lax.optimization_barrier((up, down, block_latents))
-    to_up = {s: contribution(s, 1) for s in range(half)}
-    to_down = {s: contribution(s, 0) for s in range(1, half)}
+    sums = [{"up": contribution(half, 0, 0)}, {"down": contribution(half, 1, 1)}]
+    sums, block_latents = lax.optimization_barrier((sums, block_latents))
+    terms = {
+        (s, flow): {"up": contribution(s, 1, flow), "down": contribution(s, 0, flow)}
+        for s in range(1, half)
+        for flow in range(2)
+    }
+    last = [contribution(0, 0, flow) for flow in range(2)]
+    course = {"up": ahead, "down": back}
+
+    def add(a, b):
+        return (a.astype(jnp.float32) + b.astype(jnp.float32)).astype(jnp.bfloat16)
+
     for s in range(half - 1, -1, -1):
-        up, down = lax.optimization_barrier((up, down))
-        up = lax.ppermute(up, AXIS, ahead)
-        down = lax.ppermute(down, AXIS, back)
-        if s == half - 1:
-            up, down, to_up, to_down = lax.optimization_barrier((up, down, to_up, to_down))
-        else:
-            up, down = lax.optimization_barrier((up, down))
-        if s == 0:
-            break
-        up = up.astype(jnp.float32)
-        down = down.astype(jnp.float32)
-        if s == half - 1:
-            up = jnp.pad(up, ((0, row_count - split), (0, 0)))
-            down = jnp.pad(down, ((split, 0), (0, 0)))
-        up = (up + to_up[s].astype(jnp.float32)).astype(jnp.bfloat16)
-        down = (down + to_down[s].astype(jnp.float32)).astype(jnp.bfloat16)
-        if s == 1:
-            early = attend(
-                order, start, slot_length, queries, own_latent, block_latents, 0, first_rows
-            )
-            up, down, early = lax.optimization_barrier((up, down, early))
-            late = attend(
-                order,
-                start,
-                slot_length,
-                queries,
-                own_latent,
-                block_latents,
-                first_rows,
-                decode_count - first_rows,
-            )
-            context = jnp.concatenate([early, late], axis=0)
-
-    def finish(lo, hi):
-        total = up[lo:hi].astype(jnp.float32) + down[lo:hi].astype(jnp.float32)
-        return (total + to_up[0][lo:hi].astype(jnp.float32)).astype(jnp.bfloat16)
-
-    return (finish(0, split), finish(split, row_count), context)
+        for flow in range(2):
+            moved = {
+                way: lax.ppermute(value, AXIS, course[way]) for way, value in sums[flow].items()
+            }
+            if s == half - 1:
+                moved, terms, last = lax.optimization_barrier((moved, terms, last))
+            else:
+                moved = lax.optimization_barrier(moved)
+            if s == 0:
+                sums[flow] = moved
+                continue
+            added = {
+                way: add(moved[way], term) if way in moved else term
+                for way, term in terms[(s, flow)].items()
+            }
+            if s == 1 and flow == 0:
+                early = attend(
+                    order, start, slot_length, queries, own_latent, block_latents, 0, first_rows
+                )
+            if s == 1 and flow == 1:
+                added, early = lax.optimization_barrier((added, early))
+                late = attend(
+                    order,
+                    start,
+                    slot_length,
+                    queries,
+                    own_latent,
+                    block_latents,
+                    first_rows,
+                    decode_count - first_rows,
+                )
+                context = jnp.concatenate([early, late], axis=0)
+            sums[flow] = lax.optimization_barrier(added)
+
+    def finish(flow):
+        total = sums[flow]["up"].astype(jnp.float32) + sums[flow]["down"].astype(jnp.float32)
+        return (total + last[flow].astype(jnp.float32)).astype(jnp.bfloat16)
+
+    return (finish(0), finish(1), context)
 
 
 def solution(mesh):

time: 251 us -> 232 us (0.924)
  waiting for transfers between devices: 107 us -> 87.5 us
  starting transfers between devices: 39.3 us -> 50 us
  other arithmetic: 26.8 us -> 17.7 us
    all_to_all x1, waiting for transfers between devices: 36.3 us -> 11.7 us  [per_device(): lax.all_to_all(shipped, AXIS, split_axis=0, concat_axis=0, tiled=True)]
    ppermute x42 -> x48, starting transfers between devices: 27.1 us -> 37.9 us  [the longest x14 18.2 us: per_device(): lax.ppermute(value, AXIS, course[way])]
    convert_element_type x7 -> x12, other arithmetic: 11.2 us -> 2.97 us  [the longest x2 1.87 us: finish(): return (total + last[flow].astype(jnp.float32)).astype(jnp.bfloat16)]
    ppermute x42 -> x48, waiting for transfers between devices: 70.3 us -> 75.8 us  [the longest x14 43.3 us: per_device(): lax.ppermute(value, AXIS, course[way])]
    unnamed x34 -> x44, local copies, waits for them, and re-layouts: 9.99 us -> 9.99 us
  transfers between devices with their start and end apart: 44 -> 50, of which waited for: 18 -> 18; matrix products, arithmetic and copies ran while one was open for 7% -> 7% of each run, Pallas kernels for 25% -> 27%
where the time goes in v4:
time: 232 us; the launch traced here: 228 us
  waiting for transfers between devices  87.5 us (38%)
  Pallas kernels  61 us (26%)
  starting transfers between devices  50 us (22%)
  other arithmetic  17.7 us (8%)
  local copies, waits for them, and re-layouts  11.3 us (5%)
    pallas_call x4, Pallas kernels, mlp(): pl.pallas_call(functools.partial(mlp_kernel, sizes, tile), in_specs=[anyw...  51.3 us
    ppermute x14, waiting for transfers between devices, per_device(): lax.ppermute(value, AXIS, course[way])  43.3 us
    ppermute x14, starting transfers between devices, per_device(): lax.ppermute(value, AXIS, course[way])  18.2 us
    ppermute x4, waiting for transfers between devices, per_device(): front[s] = [lax.ppermute(c, AXIS, ahead) for c in front[s - 1]]  13.4 us
    all_to_all x1, waiting for transfers between devices, per_device(): lax.all_to_all(shipped, AXIS, split_axis=0, concat_axis=0, tiled=True)  11.7 us
    ppermute x1, waiting for transfers between devices, per_device(): front[half] = [lax.ppermute(front[half - 1][0], AXIS, ahead)]  10.3 us
    unnamed x44, local copies, waits for them, and re-layouts  9.99 us
    convert_element_type x4, other arithmetic, contribution(): return (weight[:, None] * both).astype(jnp.bfloat16)  9.29 us
  transfers between devices with their start and end apart: 50, of which 18 were waited for; matrix products, arithmetic and copies ran while one was open for 7% of the time, Pallas kernels for 27%

profile of v4, /device:TPU:20, one launch (start us, length us, event | category | flops | bytes accessed | tf_op | source)
XLA Modules:
  0.0 228.4 jit_solution(7765626857423558782)
XLA Ops:
  1.1 1.6 collective-permute-start.1
  2.7 0.9 convert_reduce_fusion.2
  3.6 0.7 multiply_add_fusion
  4.5 0.8 select_reduce_fusion.1
  5.3 0.7 pad_add_fusion
  6.0 6.1 %all-to-all-start = ((s32[16,1,66]{2,1,0:T(1,128)}), s32[16,1,66]{2,1,0:T(1,128)S(1)}, u32[]{:S(2)}, u32[]{:S(2)}) async-start(s32[16,1,66]{2,1,0:T(1,128)} %bitcast.2), calls=%async_computation | async-start | bytes 16384 | tf_op jit(solution)/shard_map/all_to_all | solution.py:274
  12.7 1.5 collective-permute-start.8
  14.2 1.3 copy-done.3
  15.5 0.7 ship.1
  16.3 1.4 copy-done.1
  17.7 0.6 collective-permute-start.3
  18.3 7.5 %collective-permute-done.2.refs_1_ = bf16[32,7168]{1,0:T(8,128)(2,1)} collective-permute-done((bf16[32,7168]{1,0:T(8,128)(2,1)}, bf16[32,7168]{1,0:T(8,128)(2,1)}, u32[]{:S(2)}, u32[]{:S(2)}) %collective-permute-start.2) | collective-permute-done | bytes 458784 | tf_op jit(solution)/shard_map/ppermute | solution.py:279
  25.8 0.6 collective-permute-start.4
  26.4 1.4 collective-permute-start.9
  27.9 1.5 collective-permute-start.10
  29.3 6.2 %collective-permute-done.3.refs_0_ = bf16[32,7168]{1,0:T(8,128)(2,1)S(1)} collective-permute-done((bf16[32,7168]{1,0:T(8,128)(2,1)S(1)}, bf16[32,7168]{1,0:T(8,128)(2,1)S(1)}, u32[]{:S(2)}, u32[]{:S(2)}) %collective-permute-start.3) | collective-permute-done | bytes 458784 | tf_op jit(solution)/shard_map/ppermute | solution.py:293
  35.6 0.8 copy-done.10
  36.3 0.7 dynamic-slice_bitcast_fusion
  37.5 7.1 %collective-permute-done.4.refs_1_ = bf16[32,7168]{1,0:T(8,128)(2,1)S(1)} collective-permute-done((bf16[32,7168]{1,0:T(8,128)(2,1)}, bf16[32,7168]{1,0:T(8,128)(2,1)S(1)}, u32[]{:S(2)}, u32[]{:S(2)}) %collective-permute-start.4) | collective-permute-done | bytes 458784 | tf_op jit(solution)/shard_map/ppermute | solution.py:293
  44.7 0.8 copy-done.12
  45.9 1.3 collective-permute-done.10.refs_3_
  49.1 1.5 collective-permute-start.11
  50.6 1.5 collective-permute-start.12
  52.2 1.0 copy-done.7
  53.2 1.0 copy-done.9
  54.2 1.0 copy-done.11
  55.2 1.0 copy-done.13
  56.3 14.9 %mlp.4 = (bf16[192,7168]{1,0:T(8,128)(2,1)S(1)}, bf16[192,7168]{1,0:T(8,128)(2,1)}) custom-call(bf16[32,7168]{1,0:T(8,128)(2,1)S(1)} %copy-done.11, bf16[32,7168]{1,0:T(8,128)(2,1)} %collective-permute-done.2.refs_1_, bf16[32,7168]{1,0:T(8,128)(2,1)S(1)} %copy-done.13, bf16[32,7168]{1,0:T(8,128)(2,1)} %collective-permute-done.8.refs_3_, ...), custom_call_target="tpu_custom_call" | custom-call | flops 8455716864 | bytes 33030144 | tf_op jit(solution)/shard_map/mlp/pallas_call | solution.py:91
  71.1 1.5 copy-done.2
  72.7 1.4 collective-permute-start.19
  74.0 0.6 collective-permute-start.7
  75.1 10.3 %collective-permute-done.7.refs_0_ = bf16[32,7168]{1,0:T(8,128)(2,1)} collective-permute-done((bf16[32,7168]{1,0:T(8,128)(2,1)}, bf16[32,7168]{1,0:T(8,128)(2,1)}, u32[]{:S(2)}, u32[]{:S(2)}) %collective-permute-start.7) | collective-permute-done | bytes 458784 | tf_op jit(solution)/shard_map/ppermute | solution.py:304
  86.5 5.9 %all-to-all-start.1 = ((bf16[32,64,576]{2,1,0:T(8,128)(2,1)}), bf16[32,64,576]{2,1,0:T(8,128)(2,1)S(1)}, u32[]{:S(2)}, u32[]{:S(2)}) async-start(bf16[32,64,576]{2,1,0:T(8,128)(2,1)} %copy-done.1), calls=%async_computation.1 | async-start | bytes 5242880 | tf_op jit(solution)/shard_map/all_to_all | solution.py:309
  93.8 11.2 %mlp.5 = (bf16[64,7168]{1,0:T(8,128)(2,1)S(1)}, bf16[64,7168]{1,0:T(8,128)(2,1)S(1)}) custom-call(bf16[32,7168]{1,0:T(8,128)(2,1)} %collective-permute-done.7.refs_0_, bf16[32,7168]{1,0:T(8,128)(2,1)} %collective-permute-done.19.refs_1_, bf16[32,7168]{1,0:T(8,128)(2,1)} %collective-permute-done.20.refs_2_, bf16[32,7168]{1,0:T(8,128)(2,1)} %collective-permute-done.21.refs_3_, ...), custom_call_target="tpu_custom_call" | custom-call | flops 2818572288 | bytes 25690112 | tf_op jit(solution)/shard_map/mlp/pallas_call | solution.py:91
  106.1 12.4 %mlp.6 = (bf16[128,7168]{1,0:T(8,128)(2,1)S(1)}, bf16[128,7168]{1,0:T(8,128)(2,1)S(1)}) custom-call(bf16[32,7168]{1,0:T(8,128)(2,1)S(1)} %collective-permute-done.3.refs_0_, bf16[32,7168]{1,0:T(8,128)(2,1)S(1)} %copy-done.5, bf16[32,7168]{1,0:T(8,128)(2,1)} %collective-permute-done.9.refs_2_, bf16[32,7168]{1,0:T(8,128)(2,1)} %collective-permute-done.10.refs_3_, ...), custom_call_target="tpu_custom_call" | custom-call | flops 5637144576 | bytes 29360128 | tf_op jit(solution)/shard_map/mlp/pallas_call | solution.py:91
  119.2 12.7 %mlp.7 = (bf16[128,7168]{1,0:T(8,128)(2,1)S(1)}, bf16[128,7168]{1,0:T(8,128)(2,1)S(1)}) custom-call(bf16[32,7168]{1,0:T(8,128)(2,1)} %collective-permute-done.5.refs_0_, bf16[32,7168]{1,0:T(8,128)(2,1)} %collective-permute-done.6.refs_1_, bf16[32,7168]{1,0:T(8,128)(2,1)} %collective-permute-done.11.refs_2_, ...), custom_call_target="tpu_custom_call" | custom-call | flops 5637144576 | bytes 29360128 | tf_op jit(solution)/shard_map/mlp/pallas_call | solution.py:91
  132.3 2.4 %multiply_convert_fusion.14 = (bf16[32,7168]{1,0:T(8,128)(2,1)}, bf16[32,7168]{1,0:T(8,128)(2,1)}) fusion(bf16[64,7168]{1,0:T(8,128)(2,1)} %collective-permute-done.22, bf16[64,7168]{1,0:T(8,128)(2,1)S(1)} %get-tuple-element.114, f32[32]{0:T(128)S(1)} %get-tuple-element.223, f32[32]{0:T(128)S(1)} %get-tuple-element.224), kind=kLoop, calls=%fused_computation.27 | loop fusion | flops 2293760 | bytes 2752768 | tf_op jit(solution)/shard_map/convert_element_type | solution.py:328
  134.8 1.5 multiply_convert_fusion.6
  136.2 1.6 multiply_convert_fusion.2
  137.9 11.7 %all-to-all-done.1.latent_ref = bf16[32,64,576]{2,1,0:T(8,128)(2,1)S(1)} async-done(((bf16[32,64,576]{2,1,0:T(8,128)(2,1)}), bf16[32,64,576]{2,1,0:T(8,128)(2,1)S(1)}, u32[]{:S(2)}, u32[]{:S(2)}) %all-to-all-start.1) | async-done | bytes 2359328 | tf_op jit(solution)/shard_map/all_to_all | solution.py:309
  149.6 1.8 collective-permute-start.37
  151.6 3.8 %multiply_convert_fusion = (bf16[32,7168]{1,0:T(8,128)(2,1)S(1)}, bf16[32,7168]{1,0:T(8,128)(2,1)S(1)}, bf16[32,7168]{1,0:T(8,128)(2,1)S(1)}, bf16[32,7168]{1,0:...) fusion(bf16[192,7168]{1,0:T(8,128)(2,1)} %collective-permute-done.24, ...), kind=kLoop, calls=%fused_computation.13 | loop fusion | flops 6881280 | bytes 8258304 | tf_op jit(solution)/shard_map/convert_element_type | solution.py:328
  155.4 5.3 %attend.2 = bf16[16,64,512]{2,1,0:T(8,128)(2,1)S(1)} custom-call(s32[32]{0:T(128)S(1)} %select_reduce_fusion.3.order_ref, s32[17]{0:T(128)S(1)} %get-tuple-element.226.start_ref, s32[32]{0:T(128)S(1)} %get-tuple-element.227.length_ref, bf16[32,64,576]{2,1,0:T(8,128)(2,1)S(1)} %copy-done, bf16[32,1,576]{2,1,0:T(2,128)(2,1)S(1)} %copy.34.own_ref, ...), custom_call_target="tpu_custom_call" | custom-call | flops 150994944 | bytes 4587520 | tf_op jit(solution)/shard_map/attend/pallas_call | solution.py:182
  160.8 3.3 %collective-permute-done.23 = bf16[32,7168]{1,0:T(8,128)(2,1)S(1)} collective-permute-done((bf16[32,7168]{1,0:T(8,128)(2,1)}, bf16[32,7168]{1,0:T(8,128)(2,1)S(1)}, u32[]{:S(2)}, u32[]{:S(2)}) %collective-permute-start.23) | collective-permute-done | bytes 458784 | tf_op jit(solution)/shard_map/ppermute | solution.py:358
  164.5 3.7 %collective-permute-start.36 = (bf16[32,7168]{1,0:T(8,128)(2,1)S(1)}, bf16[32,7168]{1,0:T(8,128)(2,1)S(1)}, u32[]{:S(2)}, u32[]{:S(2)}) collective-permute-start(bf16[32,7168]{1,0:T(8,128)(2,1)S(1)} %add_convert_fusion.11), channel_id=1, source_target_pairs={{0,4},{1,5},{4,8},{5,9},{8,12},{9,13},{12,14},{13,15},{14,10},{15,... | collective-permute-start | bytes 1376264 | tf_op jit(solution)/shard_map/ppermute | solution.py:358
  168.4 2.0 collective-permute-start.43
  170.5 9.2 %collective-permute-done.35 = bf16[32,7168]{1,0:T(8,128)(2,1)S(1)} collective-permute-done((bf16[32,7168]{1,0:T(8,128)(2,1)S(1)}, bf16[32,7168]{1,0:T(8,128)(2,1)S(1)}, u32[]{:S(2)}, u32[]{:S(2)}) %collective-permute-start.35) | collective-permute-done | bytes 458784 | tf_op jit(solution)/shard_map/ppermute | solution.py:358
  180.2 1.9 collective-permute-start.39
  182.1 6.5 %collective-permute-done.42 = bf16[32,7168]{1,0:T(8,128)(2,1)S(1)} collective-permute-done((bf16[32,7168]{1,0:T(8,128)(2,1)S(1)}, bf16[32,7168]{1,0:T(8,128)(2,1)S(1)}, u32[]{:S(2)}, u32[]{:S(2)}) %collective-permute-start.42) | collective-permute-done | bytes 458784 | tf_op jit(solution)/shard_map/ppermute | solution.py:358
  189.3 0.7 collective-permute-start.44
  190.0 1.9 collective-permute-start.45
  191.9 6.5 %collective-permute-done.38 = bf16[32,7168]{1,0:T(8,128)(2,1)S(1)} collective-permute-done((bf16[32,7168]{1,0:T(8,128)(2,1)S(1)}, bf16[32,7168]{1,0:T(8,128)(2,1)S(1)}, u32[]{:S(2)}, u32[]{:S(2)}) %collective-permute-start.38) | collective-permute-done | bytes 458784 | tf_op jit(solution)/shard_map/ppermute | solution.py:358
  199.1 0.7 collective-permute-start.40
  199.9 1.9 collective-permute-start.41
  201.7 6.5 %collective-permute-done.44 = bf16[32,7168]{1,0:T(8,128)(2,1)S(1)} collective-permute-done((bf16[32,7168]{1,0:T(8,128)(2,1)S(1)}, bf16[32,7168]{1,0:T(8,128)(2,1)S(1)}, u32[]{:S(2)}, u32[]{:S(2)}) %collective-permute-start.44) | collective-permute-done | bytes 458784 | tf_op jit(solution)/shard_map/ppermute | solution.py:358
  209.0 0.7 collective-permute-start.46
  209.7 1.9 collective-permute-start.47
  211.6 3.7 %attend.3 = bf16[16,64,512]{2,1,0:T(8,128)(2,1)S(1)} custom-call(s32[32]{0:T(128)S(1)} %select_reduce_fusion.3.order_ref, s32[17]{0:T(128)S(1)} %get-tuple-element.225.start_ref, s32[32]{0:T(128)S(1)} %get-tuple-element.227.length_ref, bf16[32,64,576]{2,1,0:T(8,128)(2,1)S(1)} %copy-done, bf16[32,1,576]{2,1,0:T(2,128)(2,1)S(1)} %copy.34.own_ref, ...), custom_call_target="tpu_custom_call" | custom-call | flops 150994944 | bytes 4587520 | tf_op jit(solution)/shard_map/attend/pallas_call | solution.py:182
  215.3 1.5 pad_maximum_fusion
  216.8 1.3 collective-permute-done.40
  218.6 6.4 %collective-permute-done.46 = bf16[32,7168]{1,0:T(8,128)(2,1)S(1)} collective-permute-done((bf16[32,7168]{1,0:T(8,128)(2,1)S(1)}, bf16[32,7168]{1,0:T(8,128)(2,1)S(1)}, u32[]{:S(2)}, u32[]{:S(2)}) %collective-permute-start.46) | collective-permute-done | bytes 458784 | tf_op jit(solution)/shard_map/ppermute | solution.py:358
  225.0 1.6 collective-permute-done.47
  226.6 0.9 add_convert_fusion.6
  227.5 0.9 add_convert_fusion
  (128 shorter events, 13.1 us)
Async XLA Ops:
  0.6 47.2 %copy-start.21 = (bf16[32,576]{1,0:T(8,128)(2,1)S(1)}, bf16[32,576]{1,0:T(8,128)(2,1)}, u32[]{:S(2)}) copy-start(bf16[32,576]{1,0:T(8,128)(2,1)} %param.24) | copy-start | bytes 110596
  0.6 17.1 %collective-permute-start = (bf16[32,7168]{1,0:T(8,128)(2,1)}, bf16[32,7168]{1,0:T(8,128)(2,1)S(1)}, u32[]{:S(2)}, u32[]{:S(2)}) collective-permute-start(bf16[32,7168]{1,0:T(8,128)(2,1)} %refs_4_), channel_id=1, source_target_pairs={{0,4},{1,5},{4,8},{5,9},{8,12},{9,13},{12,14},{13,15},{14,10},{15,... | collective-permute-start | bytes 1376264 | tf_op jit(solution)/shard_map/ppermute | solution.py:279
  1.1 16.6 %collective-permute-start.1 = (bf16[32,7168]{1,0:T(8,128)(2,1)}, bf16[32,7168]{1,0:T(8,128)(2,1)S(1)}, u32[]{:S(2)}, u32[]{:S(2)}) collective-permute-start(bf16[32,7168]{1,0:T(8,128)(2,1)} %refs_4_), channel_id=1, source_target_pairs={{4,0},{5,1},{8,4},{9,5},{12,8},{13,9},{14,12},{15,13},{10,14},{11,... | collective-permute-start | bytes 1376264 | tf_op jit(solution)/shard_map/ppermute | solution.py:280
  6.0 11.7 %all-to-all-start = ((s32[16,1,66]{2,1,0:T(1,128)}), s32[16,1,66]{2,1,0:T(1,128)S(1)}, u32[]{:S(2)}, u32[]{:S(2)}) async-start(s32[16,1,66]{2,1,0:T(1,128)} %bitcast.2), calls=%async_computation | async-start | bytes 16384 | tf_op jit(solution)/shard_map/all_to_all | solution.py:274
  12.2 13.7 %collective-permute-start.2 = (bf16[32,7168]{1,0:T(8,128)(2,1)}, bf16[32,7168]{1,0:T(8,128)(2,1)}, u32[]{:S(2)}, u32[]{:S(2)}) collective-permute-start(bf16[32,7168]{1,0:T(8,128)(2,1)} %refs_5_), channel_id=1, source_target_pairs={{0,4},{1,5},{4,8},{5,9},{8,12},{9,13},{12,14},{13,15},{14,10},{15,... | collective-permute-start | bytes 1376264 | tf_op jit(solution)/shard_map/ppermute | solution.py:279
  12.7 15.1 %collective-permute-start.8 = (bf16[32,7168]{1,0:T(8,128)(2,1)}, bf16[32,7168]{1,0:T(8,128)(2,1)}, u32[]{:S(2)}, u32[]{:S(2)}) collective-permute-start(bf16[32,7168]{1,0:T(8,128)(2,1)} %refs_5_), channel_id=1, source_target_pairs={{4,0},{5,1},{8,4},{9,5},{12,8},{13,9},{14,12},{15,13},{10,14},{11,... | collective-permute-start | bytes 1376264 | tf_op jit(solution)/shard_map/ppermute | solution.py:280
  15.5 31.7 %copy-start.6 = (bf16[32,7168]{1,0:T(8,128)(2,1)S(1)}, bf16[32,7168]{1,0:T(8,128)(2,1)}, u32[]{:S(2)}) copy-start(bf16[32,7168]{1,0:T(8,128)(2,1)} %refs_4_) | copy-start | bytes 1376260
  15.5 31.7 %copy-start.8 = (bf16[32,7168]{1,0:T(8,128)(2,1)S(1)}, bf16[32,7168]{1,0:T(8,128)(2,1)}, u32[]{:S(2)}) copy-start(bf16[32,7168]{1,0:T(8,128)(2,1)} %refs_5_) | copy-start | bytes 1376260
  17.7 17.8 %collective-permute-start.3 = (bf16[32,7168]{1,0:T(8,128)(2,1)S(1)}, bf16[32,7168]{1,0:T(8,128)(2,1)S(1)}, u32[]{:S(2)}, u32[]{:S(2)}) collective-permute-start(bf16[32,7168]{1,0:T(8,128)(2,1)S(1)} %collective-permute-done.refs_0_), channel_id=1, source_target_pairs={{0,4},{1,5},{4,8},{5,9},{8,12},{9,13},{12,14},{13,15},{14,10},{15,... | collective-permute-start | bytes 1376264 | tf_op jit(solution)/shard_map/ppermute | solution.py:293
  25.8 18.8 %collective-permute-start.4 = (bf16[32,7168]{1,0:T(8,128)(2,1)}, bf16[32,7168]{1,0:T(8,128)(2,1)S(1)}, u32[]{:S(2)}, u32[]{:S(2)}) collective-permute-start(bf16[32,7168]{1,0:T(8,128)(2,1)} %collective-permute-done.2.refs_1_), channel_id=1, source_target_pairs={{0,4},{1,5},{4,8},{5,9},{8,12},{9,13},{12,14},{13,15},{14,10},{15,... | collective-permute-start | bytes 1376264 | tf_op jit(solution)/shard_map/ppermute | solution.py:293
  26.4 19.0 %collective-permute-start.9 = (bf16[32,7168]{1,0:T(8,128)(2,1)S(1)}, bf16[32,7168]{1,0:T(8,128)(2,1)}, u32[]{:S(2)}, u32[]{:S(2)}) collective-permute-start(bf16[32,7168]{1,0:T(8,128)(2,1)S(1)} %collective-permute-done.1.refs_2_), channel_id=1, source_target_pairs={{4,0},{5,1},{8,4},{9,5},{12,8},{13,9},{14,12},{15,13},{10,14},{11,... | collective-permute-start | bytes 1376264 | tf_op jit(solution)/shard_map/ppermute | solution.py:294
  27.9 19.4 %collective-permute-start.10 = (bf16[32,7168]{1,0:T(8,128)(2,1)}, bf16[32,7168]{1,0:T(8,128)(2,1)}, u32[]{:S(2)}, u32[]{:S(2)}) collective-permute-start(bf16[32,7168]{1,0:T(8,128)(2,1)} %collective-permute-done.8.refs_3_), channel_id=1, source_target_pairs={{4,0},{5,1},{8,4},{9,5},{12,8},{13,9},{14,12},{15,13},{10,14},{11,... | collective-permute-start | bytes 1376264 | tf_op jit(solution)/shard_map/ppermute | solution.py:294
  35.6 11.7 %collective-permute-start.13 = (bf16[32,7168]{1,0:T(8,128)(2,1)S(1)}, bf16[32,7168]{1,0:T(8,128)(2,1)}, u32[]{:S(2)}, u32[]{:S(2)}) collective-permute-start(bf16[32,7168]{1,0:T(8,128)(2,1)S(1)} %collective-permute-done.refs_0_), channel_id=1, source_target_pairs={{0,1},{1,0},{2,3},{3,2},{4,5},{5,4},{6,7},{7,6},{8,9},{9,8},{10,11... | collective-permute-start | bytes 1376264 | tf_op jit(solution)/shard_map/ppermute | solution.py:297
  37.0 11.0 %collective-permute-start.14 = (bf16[32,7168]{1,0:T(8,128)(2,1)}, bf16[32,7168]{1,0:T(8,128)(2,1)S(1)}, u32[]{:S(2)}, u32[]{:S(2)}) collective-permute-start(bf16[32,7168]{1,0:T(8,128)(2,1)} %collective-permute-done.2.refs_1_), channel_id=1, source_target_pairs={{0,1},{1,0},{2,3},{3,2},{4,5},{5,4},{6,7},{7,6},{8,9},{9,8},{10,11... | collective-permute-start | bytes 1376264 | tf_op jit(solution)/shard_map/ppermute | solution.py:297
  44.7 26.5 %copy-start.4 = (bf16[32,7168]{1,0:T(8,128)(2,1)}, bf16[32,7168]{1,0:T(8,128)(2,1)S(1)}, u32[]{:S(2)}) copy-start(bf16[32,7168]{1,0:T(8,128)(2,1)S(1)} %collective-permute-done.4.refs_1_) | copy-start | bytes 1376260
  44.7 3.9 %collective-permute-start.15 = (bf16[32,7168]{1,0:T(8,128)(2,1)S(1)}, bf16[32,7168]{1,0:T(8,128)(2,1)S(1)}, u32[]{:S(2)}, u32[]{:S(2)}) collective-permute-start(bf16[32,7168]{1,0:T(8,128)(2,1)S(1)} %collective-permute-done.1.refs_2_), channel_id=1, source_target_pairs={{0,1},{1,0},{2,3},{3,2},{4,5},{5,4},{6,7},{7,6},{8,9},{9,8},{10,11... | collective-permute-start | bytes 1376264 | tf_op jit(solution)/shard_map/ppermute | solution.py:297
  45.5 3.6 %collective-permute-start.16 = (bf16[32,7168]{1,0:T(8,128)(2,1)}, bf16[32,7168]{1,0:T(8,128)(2,1)S(1)}, u32[]{:S(2)}, u32[]{:S(2)}) collective-permute-start(bf16[32,7168]{1,0:T(8,128)(2,1)} %collective-permute-done.8.refs_3_), channel_id=1, source_target_pairs={{0,1},{1,0},{2,3},{3,2},{4,5},{5,4},{6,7},{7,6},{8,9},{9,8},{10,11... | collective-permute-start | bytes 1376264 | tf_op jit(solution)/shard_map/ppermute | solution.py:297
  47.2 3.4 %collective-permute-start.17 = (bf16[32,7168]{1,0:T(8,128)(2,1)S(1)}, bf16[32,7168]{1,0:T(8,128)(2,1)S(1)}, u32[]{:S(2)}, u32[]{:S(2)}) collective-permute-start(bf16[32,7168]{1,0:T(8,128)(2,1)S(1)} %copy-done.6), channel_id=1, source_target_pairs={{0,1},{1,0},{2,3},{3,2},{4,5},{5,4},{6,7},{7,6},{8,9},{9,8},{10,11... | collective-permute-start | bytes 1376264 | tf_op jit(solution)/shard_map/ppermute | solution.py:297
  47.2 4.9 %collective-permute-start.18 = (bf16[32,7168]{1,0:T(8,128)(2,1)S(1)}, bf16[32,7168]{1,0:T(8,128)(2,1)S(1)}, u32[]{:S(2)}, u32[]{:S(2)}) collective-permute-start(bf16[32,7168]{1,0:T(8,128)(2,1)S(1)} %copy-done.8), channel_id=1, source_target_pairs={{0,1},{1,0},{2,3},{3,2},{4,5},{5,4},{6,7},{7,6},{8,9},{9,8},{10,11... | collective-permute-start | bytes 1376264 | tf_op jit(solution)/shard_map/ppermute | solution.py:297
  48.1 26.0 %collective-permute-start.5 = (bf16[32,7168]{1,0:T(8,128)(2,1)S(1)}, bf16[32,7168]{1,0:T(8,128)(2,1)}, u32[]{:S(2)}, u32[]{:S(2)}) collective-permute-start(bf16[32,7168]{1,0:T(8,128)(2,1)S(1)} %collective-permute-done.3.refs_0_), channel_id=1, source_target_pairs={{0,4},{1,5},{4,8},{5,9},{8,12},{9,13},{12,14},{13,15},{14,10},{15,... | collective-permute-start | bytes 1376264 | tf_op jit(solution)/shard_map/ppermute | solution.py:293
  48.6 26.5 %collective-permute-start.6 = (bf16[32,7168]{1,0:T(8,128)(2,1)S(1)}, bf16[32,7168]{1,0:T(8,128)(2,1)}, u32[]{:S(2)}, u32[]{:S(2)}) collective-permute-start(bf16[32,7168]{1,0:T(8,128)(2,1)S(1)} %collective-permute-done.4.refs_1_), channel_id=1, source_target_pairs={{0,4},{1,5},{4,8},{5,9},{8,12},{9,13},{12,14},{13,15},{14,10},{15,... | collective-permute-start | bytes 1376264 | tf_op jit(solution)/shard_map/ppermute | solution.py:293
  49.1 26.0 %collective-permute-start.11 = (bf16[32,7168]{1,0:T(8,128)(2,1)}, bf16[32,7168]{1,0:T(8,128)(2,1)}, u32[]{:S(2)}, u32[]{:S(2)}) collective-permute-start(bf16[32,7168]{1,0:T(8,128)(2,1)} %collective-permute-done.9.refs_2_), channel_id=1, source_target_pairs={{4,0},{5,1},{8,4},{9,5},{12,8},{13,9},{14,12},{15,13},{10,14},{11,... | collective-permute-start | bytes 1376264 | tf_op jit(solution)/shard_map/ppermute | solution.py:294
  50.6 22.0 %collective-permute-start.12 = (bf16[32,7168]{1,0:T(8,128)(2,1)}, bf16[32,7168]{1,0:T(8,128)(2,1)}, u32[]{:S(2)}, u32[]{:S(2)}) collective-permute-start(bf16[32,7168]{1,0:T(8,128)(2,1)} %collective-permute-done.10.refs_3_), channel_id=1, source_target_pairs={{4,0},{5,1},{8,4},{9,5},{12,8},{13,9},{14,12},{15,13},{10,14},{11,... | collective-permute-start | bytes 1376264 | tf_op jit(solution)/shard_map/ppermute | solution.py:294
  71.1 1.5 copy-start.2
  72.7 12.8 %collective-permute-start.19 = (bf16[32,7168]{1,0:T(8,128)(2,1)}, bf16[32,7168]{1,0:T(8,128)(2,1)}, u32[]{:S(2)}, u32[]{:S(2)}) collective-permute-start(bf16[32,7168]{1,0:T(8,128)(2,1)} %collective-permute-done.12.refs_3_), channel_id=1, source_target_pairs={{4,0},{5,1},{8,4},{9,5},{12,8},{13,9},{14,12},{15,13},{10,14},{11,... | collective-permute-start | bytes 1376264 | tf_op jit(solution)/shard_map/ppermute | solution.py:305
  74.0 11.4 %collective-permute-start.7 = (bf16[32,7168]{1,0:T(8,128)(2,1)}, bf16[32,7168]{1,0:T(8,128)(2,1)}, u32[]{:S(2)}, u32[]{:S(2)}) collective-permute-start(bf16[32,7168]{1,0:T(8,128)(2,1)} %collective-permute-done.5.refs_0_), channel_id=1, source_target_pairs={{0,4},{1,5},{4,8},{5,9},{8,12},{9,13},{12,14},{13,15},{14,10},{15,... | collective-permute-start | bytes 1376264 | tf_op jit(solution)/shard_map/ppermute | solution.py:304
  85.5 7.6 %collective-permute-start.20 = (bf16[32,7168]{1,0:T(8,128)(2,1)}, bf16[32,7168]{1,0:T(8,128)(2,1)}, u32[]{:S(2)}, u32[]{:S(2)}) collective-permute-start(bf16[32,7168]{1,0:T(8,128)(2,1)} %collective-permute-done.7.refs_0_), channel_id=1, source_target_pairs={{0,1},{1,0},{2,3},{3,2},{4,5},{5,4},{6,7},{7,6},{8,9},{9,8},{10,11... | collective-permute-start | bytes 1376264 | tf_op jit(solution)/shard_map/ppermute | solution.py:297
  85.7 7.8 %collective-permute-start.21 = (bf16[32,7168]{1,0:T(8,128)(2,1)}, bf16[32,7168]{1,0:T(8,128)(2,1)}, u32[]{:S(2)}, u32[]{:S(2)}) collective-permute-start(bf16[32,7168]{1,0:T(8,128)(2,1)} %collective-permute-done.19.refs_1_), channel_id=1, source_target_pairs={{0,1},{1,0},{2,3},{3,2},{4,5},{5,4},{6,7},{7,6},{8,9},{9,8},{10,11... | collective-permute-start | bytes 1376264 | tf_op jit(solution)/shard_map/ppermute | solution.py:297
  86.5 63.1 %all-to-all-start.1 = ((bf16[32,64,576]{2,1,0:T(8,128)(2,1)}), bf16[32,64,576]{2,1,0:T(8,128)(2,1)S(1)}, u32[]{:S(2)}, u32[]{:S(2)}) async-start(bf16[32,64,576]{2,1,0:T(8,128)(2,1)} %copy-done.1), calls=%async_computation.1 | async-start | bytes 5242880 | tf_op jit(solution)/shard_map/all_to_all | solution.py:309
  92.4 12.6 %collective-permute-start.25 = (bf16[32,7168]{1,0:T(8,128)(2,1)S(1)}, bf16[32,7168]{1,0:T(8,128)(2,1)S(1)}, u32[]{:S(2)}, u32[]{:S(2)}) collective-permute-start(bf16[32,7168]{1,0:T(8,128)(2,1)S(1)} %collective-permute-done.3.refs_0_), channel_id=1, source_target_pairs={{0,1},{1,0},{2,3},{3,2},{4,5},{5,4},{6,7},{7,6},{8,9},{9,8},{10,11... | collective-permute-start | bytes 1376264 | tf_op jit(solution)/shard_map/ppermute | solution.py:297
  92.6 12.9 %collective-permute-start.26 = (bf16[32,7168]{1,0:T(8,128)(2,1)}, bf16[32,7168]{1,0:T(8,128)(2,1)S(1)}, u32[]{:S(2)}, u32[]{:S(2)}) collective-permute-start(bf16[32,7168]{1,0:T(8,128)(2,1)} %copy-done.4), channel_id=1, source_target_pairs={{0,1},{1,0},{2,3},{3,2},{4,5},{5,4},{6,7},{7,6},{8,9},{9,8},{10,11... | collective-permute-start | bytes 1376264 | tf_op jit(solution)/shard_map/ppermute | solution.py:297
  93.0 12.7 %collective-permute-start.27 = (bf16[32,7168]{1,0:T(8,128)(2,1)}, bf16[32,7168]{1,0:T(8,128)(2,1)S(1)}, u32[]{:S(2)}, u32[]{:S(2)}) collective-permute-start(bf16[32,7168]{1,0:T(8,128)(2,1)} %collective-permute-done.9.refs_2_), channel_id=1, source_target_pairs={{0,1},{1,0},{2,3},{3,2},{4,5},{5,4},{6,7},{7,6},{8,9},{9,8},{10,11... | collective-permute-start | bytes 1376264 | tf_op jit(solution)/shard_map/ppermute | solution.py:297
  93.1 12.9 %collective-permute-start.28 = (bf16[32,7168]{1,0:T(8,128)(2,1)}, bf16[32,7168]{1,0:T(8,128)(2,1)S(1)}, u32[]{:S(2)}, u32[]{:S(2)}) collective-permute-start(bf16[32,7168]{1,0:T(8,128)(2,1)} %collective-permute-done.10.refs_3_), channel_id=1, source_target_pairs={{0,1},{1,0},{2,3},{3,2},{4,5},{5,4},{6,7},{7,6},{8,9},{9,8},{10,11... | collective-permute-start | bytes 1376264 | tf_op jit(solution)/shard_map/ppermute | solution.py:297
  93.5 12.6 %copy-start.5 = (bf16[32,7168]{1,0:T(8,128)(2,1)S(1)}, bf16[32,7168]{1,0:T(8,128)(2,1)}, u32[]{:S(2)}) copy-start(bf16[32,7168]{1,0:T(8,128)(2,1)} %copy-done.4) | copy-start | bytes 1376260
  93.5 25.0 %collective-permute-start.30 = (bf16[32,7168]{1,0:T(8,128)(2,1)}, bf16[32,7168]{1,0:T(8,128)(2,1)S(1)}, u32[]{:S(2)}, u32[]{:S(2)}) collective-permute-start(bf16[32,7168]{1,0:T(8,128)(2,1)} %collective-permute-done.5.refs_0_), channel_id=1, source_target_pairs={{0,1},{1,0},{2,3},{3,2},{4,5},{5,4},{6,7},{7,6},{8,9},{9,8},{10,11... | collective-permute-start | bytes 1376264 | tf_op jit(solution)/shard_map/ppermute | solution.py:297
  105.0 14.0 %collective-permute-start.31 = (bf16[32,7168]{1,0:T(8,128)(2,1)}, bf16[32,7168]{1,0:T(8,128)(2,1)S(1)}, u32[]{:S(2)}, u32[]{:S(2)}) collective-permute-start(bf16[32,7168]{1,0:T(8,128)(2,1)} %collective-permute-done.6.refs_1_), channel_id=1, source_target_pairs={{0,1},{1,0},{2,3},{3,2},{4,5},{5,4},{6,7},{7,6},{8,9},{9,8},{10,11... | collective-permute-start | bytes 1376264 | tf_op jit(solution)/shard_map/ppermute | solution.py:297
  105.5 13.7 %collective-permute-start.32 = (bf16[32,7168]{1,0:T(8,128)(2,1)}, bf16[32,7168]{1,0:T(8,128)(2,1)S(1)}, u32[]{:S(2)}, u32[]{:S(2)}) collective-permute-start(bf16[32,7168]{1,0:T(8,128)(2,1)} %collective-permute-done.11.refs_2_), channel_id=1, source_target_pairs={{0,1},{1,0},{2,3},{3,2},{4,5},{5,4},{6,7},{7,6},{8,9},{9,8},{10,11... | collective-permute-start | bytes 1376264 | tf_op jit(solution)/shard_map/ppermute | solution.py:297
  105.6 13.6 %collective-permute-start.33 = (bf16[32,7168]{1,0:T(8,128)(2,1)}, bf16[32,7168]{1,0:T(8,128)(2,1)S(1)}, u32[]{:S(2)}, u32[]{:S(2)}) collective-permute-start(bf16[32,7168]{1,0:T(8,128)(2,1)} %collective-permute-done.12.refs_3_), channel_id=1, source_target_pairs={{0,1},{1,0},{2,3},{3,2},{4,5},{5,4},{6,7},{7,6},{8,9},{9,8},{10,11... | collective-permute-start | bytes 1376264 | tf_op jit(solution)/shard_map/ppermute | solution.py:297
  106.0 26.4 %collective-permute-start.22 = (bf16[64,7168]{1,0:T(8,128)(2,1)S(1)}, bf16[64,7168]{1,0:T(8,128)(2,1)}, u32[]{:S(2)}, u32[]{:S(2)}) collective-permute-start(bf16[64,7168]{1,0:T(8,128)(2,1)S(1)} %get-tuple-element.115), channel_id=1, source_target_pairs={{0,1},{1,0},{2,3},{3,2},{4,5},{5,4},{6,7},{7,6},{8,9},{9,8},{10,11... | collective-permute-start | bytes 2752520 | tf_op jit(solution)/shard_map/ppermute | solution.py:312
  118.6 33.0 %collective-permute-start.24 = (bf16[192,7168]{1,0:T(8,128)(2,1)}, bf16[192,7168]{1,0:T(8,128)(2,1)}, u32[]{:S(2)}, u32[]{:S(2)}) collective-permute-start(bf16[192,7168]{1,0:T(8,128)(2,1)} %get-tuple-element.119), channel_id=1, source_target_pairs={{0,1},{1,0},{2,3},{3,2},{4,5},{5,4},{6,7},{7,6},{8,9},{9,8},{10,11... | collective-permute-start | bytes 8257544 | tf_op jit(solution)/shard_map/ppermute | solution.py:312
  119.0 15.8 %collective-permute-start.29 = (bf16[128,7168]{1,0:T(8,128)(2,1)S(1)}, bf16[128,7168]{1,0:T(8,128)(2,1)S(1)}, u32[]{:S(2)}, u32[]{:S(2)}) collective-permute-start(bf16[128,7168]{1,0:T(8,128)(2,1)S(1)} %get-tuple-element.125), channel_id=1, source_target_pairs={{0,1},{1,0},{2,3},{3,2},{4,5},{5,4},{6,7},{7,6},{8,9},{9,8},{10,11... | collective-permute-start | bytes 5505032 | tf_op jit(solution)/shard_map/ppermute | solution.py:312
  131.9 4.3 %collective-permute-start.34 = (bf16[128,7168]{1,0:T(8,128)(2,1)S(1)}, bf16[128,7168]{1,0:T(8,128)(2,1)S(1)}, u32[]{:S(2)}, u32[]{:S(2)}) collective-permute-start(bf16[128,7168]{1,0:T(8,128)(2,1)S(1)} %get-tuple-element.131), channel_id=1, source_target_pairs={{0,1},{1,0},{2,3},{3,2},{4,5},{5,4},{6,7},{7,6},{8,9},{9,8},{10,11... | collective-permute-start | bytes 5505032 | tf_op jit(solution)/shard_map/ppermute | solution.py:312
  149.6 14.5 %collective-permute-start.37 = (bf16[32,7168]{1,0:T(8,128)(2,1)}, bf16[32,7168]{1,0:T(8,128)(2,1)S(1)}, u32[]{:S(2)}, u32[]{:S(2)}) collective-permute-start(bf16[32,7168]{1,0:T(8,128)(2,1)} %get-tuple-element.138), channel_id=1, source_target_pairs={{4,0},{5,1},{8,4},{9,5},{12,8},{13,9},{14,12},{15,13},{10,14},{11,... | collective-permute-start | bytes 1376264 | tf_op jit(solution)/shard_map/ppermute | solution.py:358
  151.4 12.7 %collective-permute-start.23 = (bf16[32,7168]{1,0:T(8,128)(2,1)}, bf16[32,7168]{1,0:T(8,128)(2,1)S(1)}, u32[]{:S(2)}, u32[]{:S(2)}) collective-permute-start(bf16[32,7168]{1,0:T(8,128)(2,1)} %get-tuple-element.117), channel_id=1, source_target_pairs={{0,4},{1,5},{4,8},{5,9},{8,12},{9,13},{12,14},{13,15},{14,10},{15,... | collective-permute-start | bytes 1376264 | tf_op jit(solution)/shard_map/ppermute | solution.py:358
  151.6 3.8 %copy-start = (bf16[32,64,576]{2,1,0:T(8,128)(2,1)S(1)}, bf16[32,64,576]{2,1,0:T(8,128)(2,1)}, u32[]{:S(2)}) copy-start(bf16[32,64,576]{2,1,0:T(8,128)(2,1)} %query_ref.3) | copy-start | bytes 7077892
  155.4 8.7 %copy-start.18 = (bf16[32,7168]{1,0:T(8,128)(2,1)S(1)}, bf16[32,7168]{1,0:T(8,128)(2,1)}, u32[]{:S(2)}) copy-start(bf16[32,7168]{1,0:T(8,128)(2,1)} %get-tuple-element.134) | copy-start | bytes 1376260
  155.4 8.8 %copy-start.20 = (bf16[32,7168]{1,0:T(8,128)(2,1)S(1)}, bf16[32,7168]{1,0:T(8,128)(2,1)}, u32[]{:S(2)}) copy-start(bf16[32,7168]{1,0:T(8,128)(2,1)} %get-tuple-element.135) | copy-start | bytes 1376260
  155.4 12.9 %copy-start.17 = (bf16[32,7168]{1,0:T(8,128)(2,1)S(1)}, bf16[32,7168]{1,0:T(8,128)(2,1)}, u32[]{:S(2)}) copy-start(bf16[32,7168]{1,0:T(8,128)(2,1)} %get-tuple-element.166) | copy-start | bytes 1376260
  160.7 7.7 %copy-start.19 = (bf16[32,7168]{1,0:T(8,128)(2,1)S(1)}, bf16[32,7168]{1,0:T(8,128)(2,1)}, u32[]{:S(2)}) copy-start(bf16[32,7168]{1,0:T(8,128)(2,1)} %get-tuple-element.169) | copy-start | bytes 1376260
  160.7 18.9 %copy-start.16 = (bf16[32,7168]{1,0:T(8,128)(2,1)S(1)}, bf16[32,7168]{1,0:T(8,128)(2,1)}, u32[]{:S(2)}) copy-start(bf16[32,7168]{1,0:T(8,128)(2,1)} %get-tuple-element.151) | copy-start | bytes 1376260
  160.7 19.0 %copy-start.15 = (bf16[32,7168]{1,0:T(8,128)(2,1)S(1)}, bf16[32,7168]{1,0:T(8,128)(2,1)}, u32[]{:S(2)}) copy-start(bf16[32,7168]{1,0:T(8,128)(2,1)} %get-tuple-element.153) | copy-start | bytes 1376260
  164.2 24.9 %copy-start.14 = (bf16[32,7168]{1,0:T(8,128)(2,1)S(1)}, bf16[32,7168]{1,0:T(8,128)(2,1)}, u32[]{:S(2)}) copy-start(bf16[32,7168]{1,0:T(8,128)(2,1)} %get-tuple-element.171) | copy-start | bytes 1376260
  164.2 15.4 %collective-permute-start.35 = (bf16[32,7168]{1,0:T(8,128)(2,1)S(1)}, bf16[32,7168]{1,0:T(8,128)(2,1)S(1)}, u32[]{:S(2)}, u32[]{:S(2)}) collective-permute-start(bf16[32,7168]{1,0:T(8,128)(2,1)S(1)} %copy-done.20), channel_id=1, source_target_pairs={{4,0},{5,1},{8,4},{9,5},{12,8},{13,9},{14,12},{15,13},{10,14},{11,... | collective-permute-start | bytes 1376264 | tf_op jit(solution)/shard_map/ppermute | solution.py:358
  164.5 15.1 %collective-permute-start.36 = (bf16[32,7168]{1,0:T(8,128)(2,1)S(1)}, bf16[32,7168]{1,0:T(8,128)(2,1)S(1)}, u32[]{:S(2)}, u32[]{:S(2)}) collective-permute-start(bf16[32,7168]{1,0:T(8,128)(2,1)S(1)} %add_convert_fusion.11), channel_id=1, source_target_pairs={{0,4},{1,5},{4,8},{5,9},{8,12},{9,13},{12,14},{13,15},{14,10},{15,... | collective-permute-start | bytes 1376264 | tf_op jit(solution)/shard_map/ppermute | solution.py:358
  168.4 20.2 %collective-permute-start.42 = (bf16[32,7168]{1,0:T(8,128)(2,1)S(1)}, bf16[32,7168]{1,0:T(8,128)(2,1)S(1)}, u32[]{:S(2)}, u32[]{:S(2)}) collective-permute-start(bf16[32,7168]{1,0:T(8,128)(2,1)S(1)} %add_convert_fusion.5), channel_id=1, source_target_pairs={{4,0},{5,1},{8,4},{9,5},{12,8},{13,9},{14,12},{15,13},{10,14},{11,... | collective-permute-start | bytes 1376264 | tf_op jit(solution)/shard_map/ppermute | solution.py:358
  168.4 20.6 %collective-permute-start.43 = (bf16[32,7168]{1,0:T(8,128)(2,1)S(1)}, bf16[32,7168]{1,0:T(8,128)(2,1)S(1)}, u32[]{:S(2)}, u32[]{:S(2)}) collective-permute-start(bf16[32,7168]{1,0:T(8,128)(2,1)S(1)} %copy-done.19), channel_id=1, source_target_pairs={{0,4},{1,5},{4,8},{5,9},{8,12},{9,13},{12,14},{13,15},{14,10},{15,... | collective-permute-start | bytes 1376264 | tf_op jit(solution)/shard_map/ppermute | solution.py:358
  179.9 18.6 %collective-permute-start.38 = (bf16[32,7168]{1,0:T(8,128)(2,1)S(1)}, bf16[32,7168]{1,0:T(8,128)(2,1)S(1)}, u32[]{:S(2)}, u32[]{:S(2)}) collective-permute-start(bf16[32,7168]{1,0:T(8,128)(2,1)S(1)} %add_convert_fusion.10), channel_id=1, source_target_pairs={{4,0},{5,1},{8,4},{9,5},{12,8},{13,9},{14,12},{15,13},{10,14},{11,... | collective-permute-start | bytes 1376264 | tf_op jit(solution)/shard_map/ppermute | solution.py:358
  180.2 18.7 %collective-permute-start.39 = (bf16[32,7168]{1,0:T(8,128)(2,1)S(1)}, bf16[32,7168]{1,0:T(8,128)(2,1)S(1)}, u32[]{:S(2)}, u32[]{:S(2)}) collective-permute-start(bf16[32,7168]{1,0:T(8,128)(2,1)S(1)} %add_convert_fusion.9), channel_id=1, source_target_pairs={{0,4},{1,5},{4,8},{5,9},{8,12},{9,13},{12,14},{13,15},{14,10},{15,... | collective-permute-start | bytes 1376264 | tf_op jit(solution)/shard_map/ppermute | solution.py:358
  189.3 19.0 %collective-permute-start.44 = (bf16[32,7168]{1,0:T(8,128)(2,1)S(1)}, bf16[32,7168]{1,0:T(8,128)(2,1)S(1)}, u32[]{:S(2)}, u32[]{:S(2)}) collective-permute-start(bf16[32,7168]{1,0:T(8,128)(2,1)S(1)} %add_convert_fusion.4), channel_id=1, source_target_pairs={{4,0},{5,1},{8,4},{9,5},{12,8},{13,9},{14,12},{15,13},{10,14},{11,... | collective-permute-start | bytes 1376264 | tf_op jit(solution)/shard_map/ppermute | solution.py:358
  190.0 18.7 %collective-permute-start.45 = (bf16[32,7168]{1,0:T(8,128)(2,1)S(1)}, bf16[32,7168]{1,0:T(8,128)(2,1)S(1)}, u32[]{:S(2)}, u32[]{:S(2)}) collective-permute-start(bf16[32,7168]{1,0:T(8,128)(2,1)S(1)} %add_convert_fusion.3), channel_id=1, source_target_pairs={{0,4},{1,5},{4,8},{5,9},{8,12},{9,13},{12,14},{13,15},{14,10},{15,... | collective-permute-start | bytes 1376264 | tf_op jit(solution)/shard_map/ppermute | solution.py:358
  199.1 19.0 %collective-permute-start.40 = (bf16[32,7168]{1,0:T(8,128)(2,1)S(1)}, bf16[32,7168]{1,0:T(8,128)(2,1)S(1)}, u32[]{:S(2)}, u32[]{:S(2)}) collective-permute-start(bf16[32,7168]{1,0:T(8,128)(2,1)S(1)} %add_convert_fusion.8), channel_id=1, source_target_pairs={{4,0},{5,1},{8,4},{9,5},{12,8},{13,9},{14,12},{15,13},{10,14},{11,... | collective-permute-start | bytes 1376264 | tf_op jit(solution)/shard_map/ppermute | solution.py:358
  199.9 18.7 %collective-permute-start.41 = (bf16[32,7168]{1,0:T(8,128)(2,1)S(1)}, bf16[32,7168]{1,0:T(8,128)(2,1)S(1)}, u32[]{:S(2)}, u32[]{:S(2)}) collective-permute-start(bf16[32,7168]{1,0:T(8,128)(2,1)S(1)} %add_convert_fusion.7), channel_id=1, source_target_pairs={{0,4},{1,5},{4,8},{5,9},{8,12},{9,13},{12,14},{13,15},{14,10},{15,... | collective-permute-start | bytes 1376264 | tf_op jit(solution)/shard_map/ppermute | solution.py:358
  209.0 16.0 %collective-permute-start.46 = (bf16[32,7168]{1,0:T(8,128)(2,1)S(1)}, bf16[32,7168]{1,0:T(8,128)(2,1)S(1)}, u32[]{:S(2)}, u32[]{:S(2)}) collective-permute-start(bf16[32,7168]{1,0:T(8,128)(2,1)S(1)} %add_convert_fusion.2), channel_id=1, source_target_pairs={{4,0},{5,1},{8,4},{9,5},{12,8},{13,9},{14,12},{15,13},{10,14},{11,... | collective-permute-start | bytes 1376264 | tf_op jit(solution)/shard_map/ppermute | solution.py:358
  209.7 16.9 %collective-permute-start.47 = (bf16[32,7168]{1,0:T(8,128)(2,1)S(1)}, bf16[32,7168]{1,0:T(8,128)(2,1)S(1)}, u32[]{:S(2)}, u32[]{:S(2)}) collective-permute-start(bf16[32,7168]{1,0:T(8,128)(2,1)S(1)} %add_convert_fusion.1), channel_id=1, source_target_pairs={{0,4},{1,5},{4,8},{5,9},{8,12},{9,13},{12,14},{13,15},{14,10},{15,... | collective-permute-start | bytes 1376264 | tf_op jit(solution)/shard_map/ppermute | solution.py:358
  (8 other events, 8.4 us)

commit v5 on v4

--- a/solution.py
+++ b/solution.py
@@ -86,11 +86,11 @@
     tiles = width // tile
     sizes = tuple(c.shape[0] for c in chunks)
     rows = sum(sizes)
-    anywhere = pl.BlockSpec(memory_space=pltpu.HBM)
+    anywhere = pl.BlockSpec(memory_space=pl.ANY)
     dma = pltpu.SemaphoreType.DMA
     return pl.pallas_call(
         functools.partial(mlp_kernel, sizes, tile),
-        in_specs=[anywhere] * (len(chunks) + 2),
+        in_specs=[anywhere] * len(chunks) + [pl.BlockSpec(memory_space=pltpu.HBM)] * 2,
         out_specs=[anywhere, anywhere],
         out_shape=[jax.ShapeDtypeStruct((rows // 2, width), jnp.bfloat16)] * 2,
         scratch_shapes=[
@@ -297,18 +297,15 @@
         other = [lax.ppermute(c, AXIS, across) for c in mine]
         return mlp(mine, other, gate_up, down_proj)
 
-    first = min(2, half - 1)
-    near, _ = lax.optimization_barrier((front[1] + rear[1] + own, front[first][:1]))
-    results = {1: work(1, near)}
-    last_rear, results[1] = lax.optimization_barrier((rear[half - 1][1], results[1]))
     front[half] = [lax.ppermute(front[half - 1][0], AXIS, ahead)]
-    rear[half] = [lax.ppermute(last_rear, AXIS, back)]
-    front, rear, shipped, shift_gates, results = lax.optimization_barrier(
-        (front, rear, shipped, shift_gates, results)
+    rear[half] = [lax.ppermute(rear[half - 1][1], AXIS, back)]
+    front, rear, shipped, shift_gates = lax.optimization_barrier(
+        (front, rear, shipped, shift_gates)
     )
     block_latents = lax.all_to_all(shipped, AXIS, split_axis=0, concat_axis=0, tiled=True)
-    for s in [half] + list(range(half - 1, 1, -1)):
-        results[s] = work(s, front[s] + rear[s])
+    results = {}
+    for s in range(half, 0, -1):
+        results[s] = work(s, front[s] + rear[s] + (own if s == 1 else []))
     parts = {s: (part, lax.ppermute(rest, AXIS, across)) for s, (part, rest) in results.items()}
 
     def contribution(s, k, flow):
@@ -340,7 +337,6 @@
     first_rows = decode_count // 2
 
     sums = [{"up": contribution(half, 0, 0)}, {"down": contribution(half, 1, 1)}]
-    sums, block_latents = lax.optimization_barrier((sums, block_latents))
     terms = {
         (s, flow): {"up": contribution(s, 1, flow), "down": contribution(s, 0, flow)}
         for s in range(1, half)
@@ -358,7 +354,9 @@
                 way: lax.ppermute(value, AXIS, course[way]) for way, value in sums[flow].items()
             }
             if s == half - 1:
-                moved, terms, last = lax.optimization_barrier((moved, terms, last))
+                moved, terms, last, block_latents = lax.optimization_barrier(
+                    (moved, terms, last, block_latents)
+                )
             else:
                 moved = lax.optimization_barrier(moved)
             if s == 0:

time: 232 us -> 227 us (0.978)
  starting transfers between devices: 50 us -> 44.1 us
  other arithmetic: 17.7 us -> 21.6 us
  local copies, waits for them, and re-layouts: 11.3 us -> 7.47 us
    ppermute x4, waiting for transfers between devices: 1.28 us -> 17.8 us  [per_device(): rear[s] = [lax.ppermute(c, AXIS, back) for c in rear[s - 1]]]
    all_to_all x1, waiting for transfers between devices: 11.7 us -> 0.01 us  [per_device(): lax.all_to_all(shipped, AXIS, split_axis=0, concat_axis=0, tiled=True)]
    ppermute x2, waiting for transfers between devices: 7.49 us -> 0.01 us  [per_device(): front = {1: [lax.ppermute(c, AXIS, ahead) for c in own]}]
    all_to_all x1, waiting for transfers between devices: 0.01 us -> 7.45 us  [per_device(): small = lax.all_to_all(small, AXIS, split_axis=0, concat_axis=0, tiled=True)]
    unnamed x44 -> x62, local copies, waits for them, and re-layouts: 9.99 us -> 6.21 us
    ppermute x14, starting transfers between devices: 18.2 us -> 14.5 us  [per_device(): lax.ppermute(value, AXIS, course[way])]
    ppermute x4, starting transfers between devices: 5.93 us -> 2.38 us  [per_device(): rear[s] = [lax.ppermute(c, AXIS, back) for c in rear[s - 1]]]
    ppermute x4, starting transfers between devices: 2.28 us -> 5.73 us  [per_device(): front[s] = [lax.ppermute(c, AXIS, ahead) for c in front[s - 1]]]
  transfers between devices with their start and end apart: 50 -> 50, of which waited for: 18 -> 21; matrix products, arithmetic and copies ran while one was open for 7% -> 9% of each run, Pallas kernels for 27% -> 27%
where the time goes in v5:
time: 227 us; the launch traced here: 225 us
  waiting for transfers between devices  89.6 us (39%)
  Pallas kernels  61 us (27%)
  starting transfers between devices  44.1 us (19%)
  other arithmetic  21.6 us (10%)
  local copies, waits for them, and re-layouts  7.47 us (3%)
    pallas_call x4, Pallas kernels, mlp(): pl.pallas_call(functools.partial(mlp_kernel, sizes, tile), in_specs=[anyw...  52 us
    ppermute x14, waiting for transfers between devices, per_device(): lax.ppermute(value, AXIS, course[way])  40.5 us
    ppermute x4, waiting for transfers between devices, per_device(): rear[s] = [lax.ppermute(c, AXIS, back) for c in rear[s - 1]]  17.8 us
    ppermute x4, waiting for transfers between devices, per_device(): front[s] = [lax.ppermute(c, AXIS, ahead) for c in front[s - 1]]  15.3 us
    ppermute x14, starting transfers between devices, per_device(): lax.ppermute(value, AXIS, course[way])  14.5 us
    convert_element_type x4, other arithmetic, contribution(): return (weight[:, None] * both).astype(jnp.bfloat16)  10.7 us
    pallas_call x2, Pallas kernels, attend(): pl.pallas_call(attend_kernel, grid_spec=pltpu.PrefetchScalarGridSpec(num_...  8.2 us
    all_to_all x1, waiting for transfers between devices, per_device(): small = lax.all_to_all(small, AXIS, split_axis=0, concat_axis=0, tiled=True)  7.45 us
  transfers between devices with their start and end apart: 50, of which 21 were waited for; matrix products, arithmetic and copies ran while one was open for 9% of the time, Pallas kernels for 27%

profile of v5, /device:TPU:20, one launch (start us, length us, event | category | flops | bytes accessed | tf_op | source)
XLA Modules:
  0.0 224.8 jit_solution(1664724909824426914)
XLA Ops:
  1.1 1.6 collective-permute-start.1
  2.7 1.6 collective-permute-start.8
  4.3 0.9 convert_reduce_fusion.2
  5.2 0.7 multiply_add_fusion
  6.1 0.8 select_reduce_fusion.1
  7.6 5.1 %all-to-all-start = ((s32[16,1,66]{2,1,0:T(1,128)}), s32[16,1,66]{2,1,0:T(1,128)S(1)}, u32[]{:S(2)}, u32[]{:S(2)}) async-start(s32[16,1,66]{2,1,0:T(1,128)} %bitcast.2), calls=%async_computation | async-start | bytes 16384 | tf_op jit(solution)/shard_map/all_to_all | solution.py:274
  13.3 1.3 copy-done.2
  14.6 0.7 ship.1
  15.4 1.5 copy-done.1
  16.8 7.5 %all-to-all-done = s32[16,1,66]{2,1,0:T(1,128)S(1)} async-done(((s32[16,1,66]{2,1,0:T(1,128)}), s32[16,1,66]{2,1,0:T(1,128)S(1)}, u32[]{:S(2)}, u32[]{:S(2)}) %all-to-all-start) | async-done | bytes 4256 | tf_op jit(solution)/shard_map/all_to_all | solution.py:274
  24.3 0.8 copy-done.15
  25.1 1.5 collective-permute-start.3
  28.5 1.4 collective-permute-start.4
  29.8 8.9 %collective-permute-done.3.refs_0_ = bf16[32,7168]{1,0:T(8,128)(2,1)S(1)} collective-permute-done((bf16[32,7168]{1,0:T(8,128)(2,1)}, bf16[32,7168]{1,0:T(8,128)(2,1)S(1)}, u32[]{:S(2)}, u32[]{:S(2)}) %collective-permute-start.3) | collective-permute-done | bytes 458784 | tf_op jit(solution)/shard_map/ppermute | solution.py:293
  38.7 1.5 collective-permute-start.5
  41.1 9.0 %collective-permute-done.9.refs_2_ = bf16[32,7168]{1,0:T(8,128)(2,1)S(1)} collective-permute-done((bf16[32,7168]{1,0:T(8,128)(2,1)}, bf16[32,7168]{1,0:T(8,128)(2,1)S(1)}, u32[]{:S(2)}, u32[]{:S(2)}) %collective-permute-start.9) | collective-permute-done | bytes 458784 | tf_op jit(solution)/shard_map/ppermute | solution.py:294
  50.6 1.5 collective-permute-start.6
  52.1 6.4 %collective-permute-done.5.refs_0_ = bf16[32,7168]{1,0:T(8,128)(2,1)} collective-permute-done((bf16[32,7168]{1,0:T(8,128)(2,1)S(1)}, bf16[32,7168]{1,0:T(8,128)(2,1)}, u32[]{:S(2)}, u32[]{:S(2)}) %collective-permute-start.5) | collective-permute-done | bytes 458784 | tf_op jit(solution)/shard_map/ppermute | solution.py:293
  58.5 1.5 collective-permute-start.7
  60.9 8.8 %collective-permute-done.11.refs_2_ = bf16[32,7168]{1,0:T(8,128)(2,1)S(1)} collective-permute-done((bf16[32,7168]{1,0:T(8,128)(2,1)S(1)}, bf16[32,7168]{1,0:T(8,128)(2,1)S(1)}, u32[]{:S(2)}, u32[]{:S(2)}) %collective-permute-start.11) | collective-permute-done | bytes 458784 | tf_op jit(solution)/shard_map/ppermute | solution.py:294
  69.7 7.3 %collective-permute-done.7.refs_0_ = bf16[32,7168]{1,0:T(8,128)(2,1)} collective-permute-done((bf16[32,7168]{1,0:T(8,128)(2,1)}, bf16[32,7168]{1,0:T(8,128)(2,1)}, u32[]{:S(2)}, u32[]{:S(2)}) %collective-permute-start.7) | collective-permute-done | bytes 458784 | tf_op jit(solution)/shard_map/ppermute | solution.py:300
  77.0 1.2 collective-permute-done.13.refs_1_
  79.7 5.1 %all-to-all-start.1 = ((bf16[32,64,576]{2,1,0:T(8,128)(2,1)}), bf16[32,64,576]{2,1,0:T(8,128)(2,1)S(1)}, u32[]{:S(2)}, u32[]{:S(2)}) async-start(bf16[32,64,576]{2,1,0:T(8,128)(2,1)} %copy-done.1), calls=%async_computation.1 | async-start | bytes 5242880 | tf_op jit(solution)/shard_map/all_to_all | solution.py:305
  85.5 11.8 %mlp.4 = (bf16[64,7168]{1,0:T(8,128)(2,1)S(1)}, bf16[64,7168]{1,0:T(8,128)(2,1)}) custom-call(bf16[32,7168]{1,0:T(8,128)(2,1)} %collective-permute-done.7.refs_0_, bf16[32,7168]{1,0:T(8,128)(2,1)} %collective-permute-done.13.refs_1_, bf16[32,7168]{1,0:T(8,128)(2,1)} %collective-permute-done.14.refs_2_, bf16[32,7168]{1,0:T(8,128)(2,1)} %collective-permute-done.15.refs_3_, ...), custom_call_target="tpu_custom_call" | custom-call | flops 2818572288 | bytes 25690112 | tf_op jit(solution)/shard_map/mlp/pallas_call | solution.py:91
  98.7 12.6 %mlp.7 = (bf16[128,7168]{1,0:T(8,128)(2,1)S(1)}, bf16[128,7168]{1,0:T(8,128)(2,1)S(1)}) custom-call(bf16[32,7168]{1,0:T(8,128)(2,1)} %collective-permute-done.5.refs_0_, bf16[32,7168]{1,0:T(8,128)(2,1)} %collective-permute-done.6.refs_1_, bf16[32,7168]{1,0:T(8,128)(2,1)S(1)} %copy-done.12, bf16[32,7168]{1,0:T(8,128)(2,1)S(1)} %copy-done.10, ...), custom_call_target="tpu_custom_call" | custom-call | flops 5637144576 | bytes 29360128 | tf_op jit(solution)/shard_map/mlp/pallas_call | solution.py:91
  111.4 0.8 copy-done.17
  113.5 12.3 %mlp.6 = (bf16[128,7168]{1,0:T(8,128)(2,1)S(1)}, bf16[128,7168]{1,0:T(8,128)(2,1)S(1)}) custom-call(bf16[32,7168]{1,0:T(8,128)(2,1)S(1)} %collective-permute-done.3.refs_0_, bf16[32,7168]{1,0:T(8,128)(2,1)S(1)} %copy-done.8, bf16[32,7168]{1,0:T(8,128)(2,1)S(1)} %copy-done.6, bf16[32,7168]{1,0:T(8,128)(2,1)S(1)} %copy-done.4, ...), custom_call_target="tpu_custom_call" | custom-call | flops 5637144576 | bytes 29360128 | tf_op jit(solution)/shard_map/mlp/pallas_call | solution.py:91
  125.8 0.8 copy-done.19
  127.1 1.0 copy-done.20
  128.2 15.2 %mlp.5 = (bf16[192,7168]{1,0:T(8,128)(2,1)S(1)}, bf16[192,7168]{1,0:T(8,128)(2,1)}) custom-call(bf16[32,7168]{1,0:T(8,128)(2,1)S(1)} %copy-done.16, bf16[32,7168]{1,0:T(8,128)(2,1)} %collective-permute-done.2.refs_1_, bf16[32,7168]{1,0:T(8,128)(2,1)} %collective-permute-done.1.refs_2_, bf16[32,7168]{1,0:T(8,128)(2,1)} %collective-permute-done.8.refs_3_, ...), custom_call_target="tpu_custom_call" | custom-call | flops 8455716864 | bytes 33030144 | tf_op jit(solution)/shard_map/mlp/pallas_call | solution.py:91
  143.6 2.3 %multiply_convert_fusion.15 = (bf16[32,7168]{1,0:T(8,128)(2,1)S(1)}, bf16[32,7168]{1,0:T(8,128)(2,1)}) fusion(bf16[64,7168]{1,0:T(8,128)(2,1)} %collective-permute-done.16, bf16[64,7168]{1,0:T(8,128)(2,1)S(1)} %get-tuple-element.95, f32[32]{0:T(128)S(1)} %get-tuple-element.208, f32[32]{0:T(128)S(1)} %get-tuple-element.194), kind=kLoop, calls=%fused_computation.28 | loop fusion | flops 2293760 | bytes 2752768 | tf_op jit(solution)/shard_map/convert_element_type | solution.py:325
  146.5 1.5 collective-permute-start.37
  147.9 3.2 %multiply_convert_fusion.3 = (bf16[32,7168]{1,0:T(8,128)(2,1)}, bf16[32,7168]{1,0:T(8,128)(2,1)}, bf16[32,7168]{1,0:T(8,128)(2,1)}, bf16[32,7168]{1,0:T(8,128)(2,1)}) fusion(bf16[128,7168]{1,0:T(8,128)(2,1)} %collective-permute-done.34, bf16[128,7168]{1,0:T(8,128)(2,1)S(1)} %get-tuple-element.113, f32[32]{0:T(128)S(1)} %get-tuple-element.196, ...), kind=kLoop, calls=%fused_computation.16 | loop fusion | flops 4587520 | bytes 5505536 | tf_op jit(solution)/shard_map/convert_element_type | solution.py:325
  151.1 3.1 %multiply_convert_fusion.7 = (bf16[32,7168]{1,0:T(8,128)(2,1)}, bf16[32,7168]{1,0:T(8,128)(2,1)}, bf16[32,7168]{1,0:T(8,128)(2,1)}, bf16[32,7168]{1,0:T(8,128)(2,1)S(1)}) fusion(bf16[128,7168]{1,0:T(8,128)(2,1)} %collective-permute-done.29, bf16[128,7168]{1,0:T(8,128)(2,1)S(1)} %get-tuple-element.107, f32[32]{0:T(128)S(1)} %get-tuple-element.200, ...), kind=kLoop, calls=%fused_computation.20 | loop fusion | flops 4587520 | bytes 5505536 | tf_op jit(solution)/shard_map/convert_element_type | solution.py:325
  154.3 2.1 multiply_convert_fusion.1
  156.4 2.4 %collective-permute-done.17 = bf16[32,7168]{1,0:T(8,128)(2,1)} collective-permute-done((bf16[32,7168]{1,0:T(8,128)(2,1)S(1)}, bf16[32,7168]{1,0:T(8,128)(2,1)}, u32[]{:S(2)}, u32[]{:S(2)}) %collective-permute-start.17) | collective-permute-done | bytes 458784 | tf_op jit(solution)/shard_map/ppermute | solution.py:354
  159.3 1.5 add_convert_fusion.5
  160.8 1.5 collective-permute-start.42
  162.9 1.3 add_convert_fusion.11
  164.1 1.5 collective-permute-start.35
  166.2 4.1 %attend.2 = bf16[16,64,512]{2,1,0:T(8,128)(2,1)S(1)} custom-call(s32[32]{0:T(128)S(1)} %select_reduce_fusion.3.order_ref, s32[17]{0:T(128)S(1)} %get-tuple-element.210.start_ref, s32[32]{0:T(128)S(1)} %get-tuple-element.211.length_ref, bf16[32,64,576]{2,1,0:T(8,128)(2,1)S(1)} %copy-done, bf16[32,1,576]{2,1,0:T(2,128)(2,1)S(1)} %copy.34.own_ref, ...), custom_call_target="tpu_custom_call" | custom-call | flops 150994944 | bytes 4587520 | tf_op jit(solution)/shard_map/attend/pallas_call | solution.py:182
  170.3 4.0 %collective-permute-done.42 = bf16[32,7168]{1,0:T(8,128)(2,1)S(1)} collective-permute-done((bf16[32,7168]{1,0:T(8,128)(2,1)S(1)}, bf16[32,7168]{1,0:T(8,128)(2,1)S(1)}, u32[]{:S(2)}, u32[]{:S(2)}) %collective-permute-start.42) | collective-permute-done | bytes 458784 | tf_op jit(solution)/shard_map/ppermute | solution.py:354
  174.3 1.7 collective-permute-done.43
  176.2 1.3 collective-permute-start.44
  177.5 0.8 collective-permute-start.45
  178.3 5.8 %collective-permute-done.35 = bf16[32,7168]{1,0:T(8,128)(2,1)S(1)} collective-permute-done((bf16[32,7168]{1,0:T(8,128)(2,1)}, bf16[32,7168]{1,0:T(8,128)(2,1)S(1)}, u32[]{:S(2)}, u32[]{:S(2)}) %collective-permute-start.35) | collective-permute-done | bytes 458784 | tf_op jit(solution)/shard_map/ppermute | solution.py:354
  184.1 1.7 collective-permute-done.36
  186.1 1.3 collective-permute-start.38
  187.3 0.8 collective-permute-start.39
  188.1 5.8 %collective-permute-done.44 = bf16[32,7168]{1,0:T(8,128)(2,1)S(1)} collective-permute-done((bf16[32,7168]{1,0:T(8,128)(2,1)S(1)}, bf16[32,7168]{1,0:T(8,128)(2,1)S(1)}, u32[]{:S(2)}, u32[]{:S(2)}) %collective-permute-start.44) | collective-permute-done | bytes 458784 | tf_op jit(solution)/shard_map/ppermute | solution.py:354
  194.0 1.7 collective-permute-done.45
  195.9 1.3 collective-permute-start.46
  197.2 0.8 collective-permute-start.47
  198.0 5.8 %collective-permute-done.38 = bf16[32,7168]{1,0:T(8,128)(2,1)S(1)} collective-permute-done((bf16[32,7168]{1,0:T(8,128)(2,1)S(1)}, bf16[32,7168]{1,0:T(8,128)(2,1)S(1)}, u32[]{:S(2)}, u32[]{:S(2)}) %collective-permute-start.38) | collective-permute-done | bytes 458784 | tf_op jit(solution)/shard_map/ppermute | solution.py:354
  203.8 1.7 collective-permute-done.39
  205.7 1.3 collective-permute-start.40
  207.0 0.8 collective-permute-start.41
  207.8 4.1 %attend.3 = bf16[16,64,512]{2,1,0:T(8,128)(2,1)S(1)} custom-call(s32[32]{0:T(128)S(1)} %select_reduce_fusion.3.order_ref, s32[17]{0:T(128)S(1)} %get-tuple-element.209.start_ref, s32[32]{0:T(128)S(1)} %get-tuple-element.211.length_ref, bf16[32,64,576]{2,1,0:T(8,128)(2,1)S(1)} %copy-done, bf16[32,1,576]{2,1,0:T(2,128)(2,1)S(1)} %copy.34.own_ref, ...), custom_call_target="tpu_custom_call" | custom-call | flops 150994944 | bytes 4587520 | tf_op jit(solution)/shard_map/attend/pallas_call | solution.py:182
  211.9 1.5 pad_maximum_fusion
  213.6 1.7 collective-permute-done.47
  215.3 6.2 %collective-permute-done.40 = bf16[32,7168]{1,0:T(8,128)(2,1)S(1)} collective-permute-done((bf16[32,7168]{1,0:T(8,128)(2,1)S(1)}, bf16[32,7168]{1,0:T(8,128)(2,1)S(1)}, u32[]{:S(2)}, u32[]{:S(2)}) %collective-permute-start.40) | collective-permute-done | bytes 458784 | tf_op jit(solution)/shard_map/ppermute | solution.py:354
  221.5 1.4 collective-permute-done.41
  222.9 0.9 add_convert_fusion
  223.9 0.9 add_convert_fusion.6
  (146 shorter events, 15.3 us)
Async XLA Ops:
  0.6 40.2 %copy-start.30 = (bf16[32,576]{1,0:T(8,128)(2,1)S(1)}, bf16[32,576]{1,0:T(8,128)(2,1)}, u32[]{:S(2)}) copy-start(bf16[32,576]{1,0:T(8,128)(2,1)} %param.24) | copy-start | bytes 110596
  0.6 23.7 %collective-permute-start = (bf16[32,7168]{1,0:T(8,128)(2,1)}, bf16[32,7168]{1,0:T(8,128)(2,1)S(1)}, u32[]{:S(2)}, u32[]{:S(2)}) collective-permute-start(bf16[32,7168]{1,0:T(8,128)(2,1)} %refs_4_.1), channel_id=1, source_target_pairs={{0,4},{1,5},{4,8},{5,9},{8,12},{9,13},{12,14},{13,15},{14,10},{15,... | collective-permute-start | bytes 1376264 | tf_op jit(solution)/shard_map/ppermute | solution.py:279
  1.1 23.2 %collective-permute-start.1 = (bf16[32,7168]{1,0:T(8,128)(2,1)}, bf16[32,7168]{1,0:T(8,128)(2,1)}, u32[]{:S(2)}, u32[]{:S(2)}) collective-permute-start(bf16[32,7168]{1,0:T(8,128)(2,1)} %refs_4_.1), channel_id=1, source_target_pairs={{4,0},{5,1},{8,4},{9,5},{12,8},{13,9},{14,12},{15,13},{10,14},{11,... | collective-permute-start | bytes 1376264 | tf_op jit(solution)/shard_map/ppermute | solution.py:280
  2.7 23.8 %collective-permute-start.8 = (bf16[32,7168]{1,0:T(8,128)(2,1)}, bf16[32,7168]{1,0:T(8,128)(2,1)}, u32[]{:S(2)}, u32[]{:S(2)}) collective-permute-start(bf16[32,7168]{1,0:T(8,128)(2,1)} %refs_5_.1), channel_id=1, source_target_pairs={{4,0},{5,1},{8,4},{9,5},{12,8},{13,9},{14,12},{15,13},{10,14},{11,... | collective-permute-start | bytes 1376264 | tf_op jit(solution)/shard_map/ppermute | solution.py:280
  7.6 16.7 %all-to-all-start = ((s32[16,1,66]{2,1,0:T(1,128)}), s32[16,1,66]{2,1,0:T(1,128)S(1)}, u32[]{:S(2)}, u32[]{:S(2)}) async-start(s32[16,1,66]{2,1,0:T(1,128)} %bitcast.2), calls=%async_computation | async-start | bytes 16384 | tf_op jit(solution)/shard_map/all_to_all | solution.py:274
  12.7 15.7 %collective-permute-start.2 = (bf16[32,7168]{1,0:T(8,128)(2,1)}, bf16[32,7168]{1,0:T(8,128)(2,1)}, u32[]{:S(2)}, u32[]{:S(2)}) collective-permute-start(bf16[32,7168]{1,0:T(8,128)(2,1)} %refs_5_.1), channel_id=1, source_target_pairs={{0,4},{1,5},{4,8},{5,9},{8,12},{9,13},{12,14},{13,15},{14,10},{15,... | collective-permute-start | bytes 1376264 | tf_op jit(solution)/shard_map/ppermute | solution.py:279
  25.1 13.6 %collective-permute-start.3 = (bf16[32,7168]{1,0:T(8,128)(2,1)}, bf16[32,7168]{1,0:T(8,128)(2,1)S(1)}, u32[]{:S(2)}, u32[]{:S(2)}) collective-permute-start(bf16[32,7168]{1,0:T(8,128)(2,1)} %copy-done.15), channel_id=1, source_target_pairs={{0,4},{1,5},{4,8},{5,9},{8,12},{9,13},{12,14},{13,15},{14,10},{15,... | collective-permute-start | bytes 1376264 | tf_op jit(solution)/shard_map/ppermute | solution.py:293
  26.5 13.7 %collective-permute-start.10 = (bf16[32,7168]{1,0:T(8,128)(2,1)}, bf16[32,7168]{1,0:T(8,128)(2,1)S(1)}, u32[]{:S(2)}, u32[]{:S(2)}) collective-permute-start(bf16[32,7168]{1,0:T(8,128)(2,1)} %collective-permute-done.8.refs_3_), channel_id=1, source_target_pairs={{4,0},{5,1},{8,4},{9,5},{12,8},{13,9},{14,12},{15,13},{10,14},{11,... | collective-permute-start | bytes 1376264 | tf_op jit(solution)/shard_map/ppermute | solution.py:294
  27.1 70.3 %collective-permute-start.22 = (bf16[32,7168]{1,0:T(8,128)(2,1)}, bf16[32,7168]{1,0:T(8,128)(2,1)}, u32[]{:S(2)}, u32[]{:S(2)}) collective-permute-start(bf16[32,7168]{1,0:T(8,128)(2,1)} %refs_4_.1), channel_id=1, source_target_pairs={{0,1},{1,0},{2,3},{3,2},{4,5},{5,4},{6,7},{7,6},{8,9},{9,8},{10,11... | collective-permute-start | bytes 1376264 | tf_op jit(solution)/shard_map/ppermute | solution.py:297
  27.8 22.2 %collective-permute-start.9 = (bf16[32,7168]{1,0:T(8,128)(2,1)}, bf16[32,7168]{1,0:T(8,128)(2,1)S(1)}, u32[]{:S(2)}, u32[]{:S(2)}) collective-permute-start(bf16[32,7168]{1,0:T(8,128)(2,1)} %collective-permute-done.1.refs_2_), channel_id=1, source_target_pairs={{4,0},{5,1},{8,4},{9,5},{12,8},{13,9},{14,12},{15,13},{10,14},{11,... | collective-permute-start | bytes 1376264 | tf_op jit(solution)/shard_map/ppermute | solution.py:294
  28.5 22.1 %collective-permute-start.4 = (bf16[32,7168]{1,0:T(8,128)(2,1)}, bf16[32,7168]{1,0:T(8,128)(2,1)S(1)}, u32[]{:S(2)}, u32[]{:S(2)}) collective-permute-start(bf16[32,7168]{1,0:T(8,128)(2,1)} %collective-permute-done.2.refs_1_), channel_id=1, source_target_pairs={{0,4},{1,5},{4,8},{5,9},{8,12},{9,13},{12,14},{13,15},{14,10},{15,... | collective-permute-start | bytes 1376264 | tf_op jit(solution)/shard_map/ppermute | solution.py:293
  38.7 19.8 %collective-permute-start.5 = (bf16[32,7168]{1,0:T(8,128)(2,1)S(1)}, bf16[32,7168]{1,0:T(8,128)(2,1)}, u32[]{:S(2)}, u32[]{:S(2)}) collective-permute-start(bf16[32,7168]{1,0:T(8,128)(2,1)S(1)} %collective-permute-done.3.refs_0_), channel_id=1, source_target_pairs={{0,4},{1,5},{4,8},{5,9},{8,12},{9,13},{12,14},{13,15},{14,10},{15,... | collective-permute-start | bytes 1376264 | tf_op jit(solution)/shard_map/ppermute | solution.py:293
  40.2 39.5 %copy-start.3 = (bf16[32,7168]{1,0:T(8,128)(2,1)}, bf16[32,7168]{1,0:T(8,128)(2,1)S(1)}, u32[]{:S(2)}) copy-start(bf16[32,7168]{1,0:T(8,128)(2,1)S(1)} %collective-permute-done.10.refs_3_) | copy-start | bytes 1376260
  40.2 19.7 %collective-permute-start.12 = (bf16[32,7168]{1,0:T(8,128)(2,1)S(1)}, bf16[32,7168]{1,0:T(8,128)(2,1)S(1)}, u32[]{:S(2)}, u32[]{:S(2)}) collective-permute-start(bf16[32,7168]{1,0:T(8,128)(2,1)S(1)} %collective-permute-done.10.refs_3_), channel_id=1, source_target_pairs={{4,0},{5,1},{8,4},{9,5},{12,8},{13,9},{14,12},{15,13},{10,14},{11,... | collective-permute-start | bytes 1376264 | tf_op jit(solution)/shard_map/ppermute | solution.py:294
  50.0 29.6 %copy-start.5 = (bf16[32,7168]{1,0:T(8,128)(2,1)}, bf16[32,7168]{1,0:T(8,128)(2,1)S(1)}, u32[]{:S(2)}) copy-start(bf16[32,7168]{1,0:T(8,128)(2,1)S(1)} %collective-permute-done.9.refs_2_) | copy-start | bytes 1376260
  50.0 19.7 %collective-permute-start.11 = (bf16[32,7168]{1,0:T(8,128)(2,1)S(1)}, bf16[32,7168]{1,0:T(8,128)(2,1)S(1)}, u32[]{:S(2)}, u32[]{:S(2)}) collective-permute-start(bf16[32,7168]{1,0:T(8,128)(2,1)S(1)} %collective-permute-done.9.refs_2_), channel_id=1, source_target_pairs={{4,0},{5,1},{8,4},{9,5},{12,8},{13,9},{14,12},{15,13},{10,14},{11,... | collective-permute-start | bytes 1376264 | tf_op jit(solution)/shard_map/ppermute | solution.py:294
  50.6 29.1 %copy-start.7 = (bf16[32,7168]{1,0:T(8,128)(2,1)}, bf16[32,7168]{1,0:T(8,128)(2,1)S(1)}, u32[]{:S(2)}) copy-start(bf16[32,7168]{1,0:T(8,128)(2,1)S(1)} %collective-permute-done.4.refs_1_) | copy-start | bytes 1376260
  50.6 19.1 %collective-permute-start.6 = (bf16[32,7168]{1,0:T(8,128)(2,1)S(1)}, bf16[32,7168]{1,0:T(8,128)(2,1)}, u32[]{:S(2)}, u32[]{:S(2)}) collective-permute-start(bf16[32,7168]{1,0:T(8,128)(2,1)S(1)} %collective-permute-done.4.refs_1_), channel_id=1, source_target_pairs={{0,4},{1,5},{4,8},{5,9},{8,12},{9,13},{12,14},{13,15},{14,10},{15,... | collective-permute-start | bytes 1376264 | tf_op jit(solution)/shard_map/ppermute | solution.py:293
  58.5 18.5 %collective-permute-start.7 = (bf16[32,7168]{1,0:T(8,128)(2,1)}, bf16[32,7168]{1,0:T(8,128)(2,1)}, u32[]{:S(2)}, u32[]{:S(2)}) collective-permute-start(bf16[32,7168]{1,0:T(8,128)(2,1)} %collective-permute-done.5.refs_0_), channel_id=1, source_target_pairs={{0,4},{1,5},{4,8},{5,9},{8,12},{9,13},{12,14},{13,15},{14,10},{15,... | collective-permute-start | bytes 1376264 | tf_op jit(solution)/shard_map/ppermute | solution.py:300
  59.9 19.8 %copy-start.9 = (bf16[32,7168]{1,0:T(8,128)(2,1)}, bf16[32,7168]{1,0:T(8,128)(2,1)S(1)}, u32[]{:S(2)}) copy-start(bf16[32,7168]{1,0:T(8,128)(2,1)S(1)} %collective-permute-done.12.refs_3_) | copy-start | bytes 1376260
  59.9 18.2 %collective-permute-start.13 = (bf16[32,7168]{1,0:T(8,128)(2,1)S(1)}, bf16[32,7168]{1,0:T(8,128)(2,1)}, u32[]{:S(2)}, u32[]{:S(2)}) collective-permute-start(bf16[32,7168]{1,0:T(8,128)(2,1)S(1)} %collective-permute-done.12.refs_3_), channel_id=1, source_target_pairs={{4,0},{5,1},{8,4},{9,5},{12,8},{13,9},{14,12},{15,13},{10,14},{11,... | collective-permute-start | bytes 1376264 | tf_op jit(solution)/shard_map/ppermute | solution.py:301
  78.2 6.7 %collective-permute-start.14 = (bf16[32,7168]{1,0:T(8,128)(2,1)}, bf16[32,7168]{1,0:T(8,128)(2,1)}, u32[]{:S(2)}, u32[]{:S(2)}) collective-permute-start(bf16[32,7168]{1,0:T(8,128)(2,1)} %collective-permute-done.7.refs_0_), channel_id=1, source_target_pairs={{0,1},{1,0},{2,3},{3,2},{4,5},{5,4},{6,7},{7,6},{8,9},{9,8},{10,11... | collective-permute-start | bytes 1376264 | tf_op jit(solution)/shard_map/ppermute | solution.py:297
  78.2 6.9 %collective-permute-start.15 = (bf16[32,7168]{1,0:T(8,128)(2,1)}, bf16[32,7168]{1,0:T(8,128)(2,1)}, u32[]{:S(2)}, u32[]{:S(2)}) collective-permute-start(bf16[32,7168]{1,0:T(8,128)(2,1)} %collective-permute-done.13.refs_1_), channel_id=1, source_target_pairs={{0,1},{1,0},{2,3},{3,2},{4,5},{5,4},{6,7},{7,6},{8,9},{9,8},{10,11... | collective-permute-start | bytes 1376264 | tf_op jit(solution)/shard_map/ppermute | solution.py:297
  79.1 18.5 %collective-permute-start.30 = (bf16[32,7168]{1,0:T(8,128)(2,1)}, bf16[32,7168]{1,0:T(8,128)(2,1)}, u32[]{:S(2)}, u32[]{:S(2)}) collective-permute-start(bf16[32,7168]{1,0:T(8,128)(2,1)} %collective-permute-done.5.refs_0_), channel_id=1, source_target_pairs={{0,1},{1,0},{2,3},{3,2},{4,5},{5,4},{6,7},{7,6},{8,9},{9,8},{10,11... | collective-permute-start | bytes 1376264 | tf_op jit(solution)/shard_map/ppermute | solution.py:297
  79.2 18.8 %collective-permute-start.31 = (bf16[32,7168]{1,0:T(8,128)(2,1)}, bf16[32,7168]{1,0:T(8,128)(2,1)}, u32[]{:S(2)}, u32[]{:S(2)}) collective-permute-start(bf16[32,7168]{1,0:T(8,128)(2,1)} %collective-permute-done.6.refs_1_), channel_id=1, source_target_pairs={{0,1},{1,0},{2,3},{3,2},{4,5},{5,4},{6,7},{7,6},{8,9},{9,8},{10,11... | collective-permute-start | bytes 1376264 | tf_op jit(solution)/shard_map/ppermute | solution.py:297
  79.7 79.1 %all-to-all-start.1 = ((bf16[32,64,576]{2,1,0:T(8,128)(2,1)}), bf16[32,64,576]{2,1,0:T(8,128)(2,1)S(1)}, u32[]{:S(2)}, u32[]{:S(2)}) async-start(bf16[32,64,576]{2,1,0:T(8,128)(2,1)} %copy-done.1), calls=%async_computation.1 | async-start | bytes 5242880 | tf_op jit(solution)/shard_map/all_to_all | solution.py:305
  84.8 13.3 %collective-permute-start.32 = (bf16[32,7168]{1,0:T(8,128)(2,1)}, bf16[32,7168]{1,0:T(8,128)(2,1)S(1)}, u32[]{:S(2)}, u32[]{:S(2)}) collective-permute-start(bf16[32,7168]{1,0:T(8,128)(2,1)} %copy-done.11), channel_id=1, source_target_pairs={{0,1},{1,0},{2,3},{3,2},{4,5},{5,4},{6,7},{7,6},{8,9},{9,8},{10,11... | collective-permute-start | bytes 1376264 | tf_op jit(solution)/shard_map/ppermute | solution.py:297
  85.0 13.5 %collective-permute-start.33 = (bf16[32,7168]{1,0:T(8,128)(2,1)}, bf16[32,7168]{1,0:T(8,128)(2,1)S(1)}, u32[]{:S(2)}, u32[]{:S(2)}) collective-permute-start(bf16[32,7168]{1,0:T(8,128)(2,1)} %copy-done.9), channel_id=1, source_target_pairs={{0,1},{1,0},{2,3},{3,2},{4,5},{5,4},{6,7},{7,6},{8,9},{9,8},{10,11... | collective-permute-start | bytes 1376264 | tf_op jit(solution)/shard_map/ppermute | solution.py:297
  85.5 13.2 %copy-start.10 = (bf16[32,7168]{1,0:T(8,128)(2,1)S(1)}, bf16[32,7168]{1,0:T(8,128)(2,1)}, u32[]{:S(2)}) copy-start(bf16[32,7168]{1,0:T(8,128)(2,1)} %copy-done.9) | copy-start | bytes 1376260
  97.4 14.7 %copy-start.16 = (bf16[32,7168]{1,0:T(8,128)(2,1)S(1)}, bf16[32,7168]{1,0:T(8,128)(2,1)}, u32[]{:S(2)}) copy-start(bf16[32,7168]{1,0:T(8,128)(2,1)} %copy-done.15) | copy-start | bytes 1376260
  97.4 13.9 %collective-permute-start.23 = (bf16[32,7168]{1,0:T(8,128)(2,1)S(1)}, bf16[32,7168]{1,0:T(8,128)(2,1)S(1)}, u32[]{:S(2)}, u32[]{:S(2)}) collective-permute-start(bf16[32,7168]{1,0:T(8,128)(2,1)S(1)} %copy-done.14), channel_id=1, source_target_pairs={{0,1},{1,0},{2,3},{3,2},{4,5},{5,4},{6,7},{7,6},{8,9},{9,8},{10,11... | collective-permute-start | bytes 1376264 | tf_op jit(solution)/shard_map/ppermute | solution.py:297
  97.6 14.9 %collective-permute-start.25 = (bf16[32,7168]{1,0:T(8,128)(2,1)S(1)}, bf16[32,7168]{1,0:T(8,128)(2,1)S(1)}, u32[]{:S(2)}, u32[]{:S(2)}) collective-permute-start(bf16[32,7168]{1,0:T(8,128)(2,1)S(1)} %collective-permute-done.3.refs_0_), channel_id=1, source_target_pairs={{0,1},{1,0},{2,3},{3,2},{4,5},{5,4},{6,7},{7,6},{8,9},{9,8},{10,11... | collective-permute-start | bytes 1376264 | tf_op jit(solution)/shard_map/ppermute | solution.py:297
  98.0 14.6 %collective-permute-start.26 = (bf16[32,7168]{1,0:T(8,128)(2,1)S(1)}, bf16[32,7168]{1,0:T(8,128)(2,1)S(1)}, u32[]{:S(2)}, u32[]{:S(2)}) collective-permute-start(bf16[32,7168]{1,0:T(8,128)(2,1)S(1)} %copy-done.8), channel_id=1, source_target_pairs={{0,1},{1,0},{2,3},{3,2},{4,5},{5,4},{6,7},{7,6},{8,9},{9,8},{10,11... | collective-permute-start | bytes 1376264 | tf_op jit(solution)/shard_map/ppermute | solution.py:297
  98.2 14.8 %collective-permute-start.27 = (bf16[32,7168]{1,0:T(8,128)(2,1)S(1)}, bf16[32,7168]{1,0:T(8,128)(2,1)S(1)}, u32[]{:S(2)}, u32[]{:S(2)}) collective-permute-start(bf16[32,7168]{1,0:T(8,128)(2,1)S(1)} %copy-done.6), channel_id=1, source_target_pairs={{0,1},{1,0},{2,3},{3,2},{4,5},{5,4},{6,7},{7,6},{8,9},{9,8},{10,11... | collective-permute-start | bytes 1376264 | tf_op jit(solution)/shard_map/ppermute | solution.py:297
  98.5 14.6 %collective-permute-start.28 = (bf16[32,7168]{1,0:T(8,128)(2,1)S(1)}, bf16[32,7168]{1,0:T(8,128)(2,1)S(1)}, u32[]{:S(2)}, u32[]{:S(2)}) collective-permute-start(bf16[32,7168]{1,0:T(8,128)(2,1)S(1)} %copy-done.4), channel_id=1, source_target_pairs={{0,1},{1,0},{2,3},{3,2},{4,5},{5,4},{6,7},{7,6},{8,9},{9,8},{10,11... | collective-permute-start | bytes 1376264 | tf_op jit(solution)/shard_map/ppermute | solution.py:297
  112.1 13.7 %collective-permute-start.18 = (bf16[32,7168]{1,0:T(8,128)(2,1)S(1)}, bf16[32,7168]{1,0:T(8,128)(2,1)S(1)}, u32[]{:S(2)}, u32[]{:S(2)}) collective-permute-start(bf16[32,7168]{1,0:T(8,128)(2,1)S(1)} %copy-done.16), channel_id=1, source_target_pairs={{0,1},{1,0},{2,3},{3,2},{4,5},{5,4},{6,7},{7,6},{8,9},{9,8},{10,11... | collective-permute-start | bytes 1376264 | tf_op jit(solution)/shard_map/ppermute | solution.py:297
  112.5 14.3 %collective-permute-start.19 = (bf16[32,7168]{1,0:T(8,128)(2,1)}, bf16[32,7168]{1,0:T(8,128)(2,1)S(1)}, u32[]{:S(2)}, u32[]{:S(2)}) collective-permute-start(bf16[32,7168]{1,0:T(8,128)(2,1)} %collective-permute-done.2.refs_1_), channel_id=1, source_target_pairs={{0,1},{1,0},{2,3},{3,2},{4,5},{5,4},{6,7},{7,6},{8,9},{9,8},{10,11... | collective-permute-start | bytes 1376264 | tf_op jit(solution)/shard_map/ppermute | solution.py:297
  112.6 14.5 %collective-permute-start.20 = (bf16[32,7168]{1,0:T(8,128)(2,1)}, bf16[32,7168]{1,0:T(8,128)(2,1)S(1)}, u32[]{:S(2)}, u32[]{:S(2)}) collective-permute-start(bf16[32,7168]{1,0:T(8,128)(2,1)} %collective-permute-done.1.refs_2_), channel_id=1, source_target_pairs={{0,1},{1,0},{2,3},{3,2},{4,5},{5,4},{6,7},{7,6},{8,9},{9,8},{10,11... | collective-permute-start | bytes 1376264 | tf_op jit(solution)/shard_map/ppermute | solution.py:297
  113.0 14.1 %collective-permute-start.21 = (bf16[32,7168]{1,0:T(8,128)(2,1)}, bf16[32,7168]{1,0:T(8,128)(2,1)S(1)}, u32[]{:S(2)}, u32[]{:S(2)}) collective-permute-start(bf16[32,7168]{1,0:T(8,128)(2,1)} %collective-permute-done.8.refs_3_), channel_id=1, source_target_pairs={{0,1},{1,0},{2,3},{3,2},{4,5},{5,4},{6,7},{7,6},{8,9},{9,8},{10,11... | collective-permute-start | bytes 1376264 | tf_op jit(solution)/shard_map/ppermute | solution.py:297
  113.2 14.0 %copy-start.13 = (bf16[32,7168]{1,0:T(8,128)(2,1)S(1)}, bf16[32,7168]{1,0:T(8,128)(2,1)}, u32[]{:S(2)}) copy-start(bf16[32,7168]{1,0:T(8,128)(2,1)} %refs_4_.1) | copy-start | bytes 1376260
  113.2 14.0 %copy-start.18 = (bf16[32,7168]{1,0:T(8,128)(2,1)S(1)}, bf16[32,7168]{1,0:T(8,128)(2,1)}, u32[]{:S(2)}) copy-start(bf16[32,7168]{1,0:T(8,128)(2,1)} %copy-done.17) | copy-start | bytes 1376260
  113.2 30.5 %collective-permute-start.16 = (bf16[64,7168]{1,0:T(8,128)(2,1)}, bf16[64,7168]{1,0:T(8,128)(2,1)}, u32[]{:S(2)}, u32[]{:S(2)}) collective-permute-start(bf16[64,7168]{1,0:T(8,128)(2,1)} %get-tuple-element.96), channel_id=1, source_target_pairs={{0,1},{1,0},{2,3},{3,2},{4,5},{5,4},{6,7},{7,6},{8,9},{9,8},{10,11... | collective-permute-start | bytes 2752520 | tf_op jit(solution)/shard_map/ppermute | solution.py:309
  126.6 21.3 %collective-permute-start.34 = (bf16[128,7168]{1,0:T(8,128)(2,1)S(1)}, bf16[128,7168]{1,0:T(8,128)(2,1)}, u32[]{:S(2)}, u32[]{:S(2)}) collective-permute-start(bf16[128,7168]{1,0:T(8,128)(2,1)S(1)} %get-tuple-element.114), channel_id=1, source_target_pairs={{0,1},{1,0},{2,3},{3,2},{4,5},{5,4},{6,7},{7,6},{8,9},{9,8},{10,11... | collective-permute-start | bytes 5505032 | tf_op jit(solution)/shard_map/ppermute | solution.py:309
  126.8 24.3 %collective-permute-start.29 = (bf16[128,7168]{1,0:T(8,128)(2,1)S(1)}, bf16[128,7168]{1,0:T(8,128)(2,1)}, u32[]{:S(2)}, u32[]{:S(2)}) collective-permute-start(bf16[128,7168]{1,0:T(8,128)(2,1)S(1)} %get-tuple-element.108), channel_id=1, source_target_pairs={{0,1},{1,0},{2,3},{3,2},{4,5},{5,4},{6,7},{7,6},{8,9},{9,8},{10,11... | collective-permute-start | bytes 5505032 | tf_op jit(solution)/shard_map/ppermute | solution.py:309
  143.4 10.9 %collective-permute-start.24 = (bf16[192,7168]{1,0:T(8,128)(2,1)}, bf16[192,7168]{1,0:T(8,128)(2,1)S(1)}, u32[]{:S(2)}, u32[]{:S(2)}) collective-permute-start(bf16[192,7168]{1,0:T(8,128)(2,1)} %get-tuple-element.102), channel_id=1, source_target_pairs={{0,1},{1,0},{2,3},{3,2},{4,5},{5,4},{6,7},{7,6},{8,9},{9,8},{10,11... | collective-permute-start | bytes 8257544 | tf_op jit(solution)/shard_map/ppermute | solution.py:309
  145.9 12.9 %collective-permute-start.17 = (bf16[32,7168]{1,0:T(8,128)(2,1)S(1)}, bf16[32,7168]{1,0:T(8,128)(2,1)}, u32[]{:S(2)}, u32[]{:S(2)}) collective-permute-start(bf16[32,7168]{1,0:T(8,128)(2,1)S(1)} %get-tuple-element.189), channel_id=1, source_target_pairs={{0,4},{1,5},{4,8},{5,9},{8,12},{9,13},{12,14},{13,15},{14,10},{15,... | collective-permute-start | bytes 1376264 | tf_op jit(solution)/shard_map/ppermute | solution.py:354
  146.5 12.8 %collective-permute-start.37 = (bf16[32,7168]{1,0:T(8,128)(2,1)}, bf16[32,7168]{1,0:T(8,128)(2,1)}, u32[]{:S(2)}, u32[]{:S(2)}) collective-permute-start(bf16[32,7168]{1,0:T(8,128)(2,1)} %get-tuple-element.190), channel_id=1, source_target_pairs={{4,0},{5,1},{8,4},{9,5},{12,8},{13,9},{14,12},{15,13},{10,14},{11,... | collective-permute-start | bytes 1376264 | tf_op jit(solution)/shard_map/ppermute | solution.py:354
  160.8 13.5 %collective-permute-start.42 = (bf16[32,7168]{1,0:T(8,128)(2,1)S(1)}, bf16[32,7168]{1,0:T(8,128)(2,1)S(1)}, u32[]{:S(2)}, u32[]{:S(2)}) collective-permute-start(bf16[32,7168]{1,0:T(8,128)(2,1)S(1)} %add_convert_fusion.5), channel_id=1, source_target_pairs={{4,0},{5,1},{8,4},{9,5},{12,8},{13,9},{14,12},{15,13},{10,14},{11,... | collective-permute-start | bytes 1376264 | tf_op jit(solution)/shard_map/ppermute | solution.py:354
  162.3 13.7 %collective-permute-start.43 = (bf16[32,7168]{1,0:T(8,128)(2,1)}, bf16[32,7168]{1,0:T(8,128)(2,1)S(1)}, u32[]{:S(2)}, u32[]{:S(2)}) collective-permute-start(bf16[32,7168]{1,0:T(8,128)(2,1)} %get-tuple-element.153), channel_id=1, source_target_pairs={{0,4},{1,5},{4,8},{5,9},{8,12},{9,13},{12,14},{13,15},{14,10},{15,... | collective-permute-start | bytes 1376264 | tf_op jit(solution)/shard_map/ppermute | solution.py:354
  164.1 20.0 %collective-permute-start.35 = (bf16[32,7168]{1,0:T(8,128)(2,1)}, bf16[32,7168]{1,0:T(8,128)(2,1)S(1)}, u32[]{:S(2)}, u32[]{:S(2)}) collective-permute-start(bf16[32,7168]{1,0:T(8,128)(2,1)} %get-tuple-element.119), channel_id=1, source_target_pairs={{4,0},{5,1},{8,4},{9,5},{12,8},{13,9},{14,12},{15,13},{10,14},{11,... | collective-permute-start | bytes 1376264 | tf_op jit(solution)/shard_map/ppermute | solution.py:354
  165.6 20.2 %collective-permute-start.36 = (bf16[32,7168]{1,0:T(8,128)(2,1)S(1)}, bf16[32,7168]{1,0:T(8,128)(2,1)S(1)}, u32[]{:S(2)}, u32[]{:S(2)}) collective-permute-start(bf16[32,7168]{1,0:T(8,128)(2,1)S(1)} %add_convert_fusion.11), channel_id=1, source_target_pairs={{0,4},{1,5},{4,8},{5,9},{8,12},{9,13},{12,14},{13,15},{14,10},{15,... | collective-permute-start | bytes 1376264 | tf_op jit(solution)/shard_map/ppermute | solution.py:354
  170.3 15.5 %copy-start.21 = (bf16[32,7168]{1,0:T(8,128)(2,1)S(1)}, bf16[32,7168]{1,0:T(8,128)(2,1)}, u32[]{:S(2)}) copy-start(bf16[32,7168]{1,0:T(8,128)(2,1)} %get-tuple-element.137) | copy-start | bytes 1376260
  176.1 19.5 %copy-start.29 = (bf16[32,7168]{1,0:T(8,128)(2,1)S(1)}, bf16[32,7168]{1,0:T(8,128)(2,1)}, u32[]{:S(2)}) copy-start(bf16[32,7168]{1,0:T(8,128)(2,1)} %get-tuple-element.163) | copy-start | bytes 1376260
  176.2 19.5 %copy-start.28 = (bf16[32,7168]{1,0:T(8,128)(2,1)S(1)}, bf16[32,7168]{1,0:T(8,128)(2,1)}, u32[]{:S(2)}) copy-start(bf16[32,7168]{1,0:T(8,128)(2,1)} %get-tuple-element.161) | copy-start | bytes 1376260
  176.2 17.7 %collective-permute-start.44 = (bf16[32,7168]{1,0:T(8,128)(2,1)S(1)}, bf16[32,7168]{1,0:T(8,128)(2,1)S(1)}, u32[]{:S(2)}, u32[]{:S(2)}) collective-permute-start(bf16[32,7168]{1,0:T(8,128)(2,1)S(1)} %add_convert_fusion.4), channel_id=1, source_target_pairs={{4,0},{5,1},{8,4},{9,5},{12,8},{13,9},{14,12},{15,13},{10,14},{11,... | collective-permute-start | bytes 1376264 | tf_op jit(solution)/shard_map/ppermute | solution.py:354
  177.5 18.1 %collective-permute-start.45 = (bf16[32,7168]{1,0:T(8,128)(2,1)S(1)}, bf16[32,7168]{1,0:T(8,128)(2,1)S(1)}, u32[]{:S(2)}, u32[]{:S(2)}) collective-permute-start(bf16[32,7168]{1,0:T(8,128)(2,1)S(1)} %add_convert_fusion.3), channel_id=1, source_target_pairs={{0,4},{1,5},{4,8},{5,9},{8,12},{9,13},{12,14},{13,15},{14,10},{15,... | collective-permute-start | bytes 1376264 | tf_op jit(solution)/shard_map/ppermute | solution.py:354
  185.9 19.6 %copy-start.27 = (bf16[32,7168]{1,0:T(8,128)(2,1)S(1)}, bf16[32,7168]{1,0:T(8,128)(2,1)}, u32[]{:S(2)}) copy-start(bf16[32,7168]{1,0:T(8,128)(2,1)} %get-tuple-element.143) | copy-start | bytes 1376260
  186.0 19.5 %copy-start.26 = (bf16[32,7168]{1,0:T(8,128)(2,1)S(1)}, bf16[32,7168]{1,0:T(8,128)(2,1)}, u32[]{:S(2)}) copy-start(bf16[32,7168]{1,0:T(8,128)(2,1)} %get-tuple-element.141) | copy-start | bytes 1376260
  186.1 17.7 %collective-permute-start.38 = (bf16[32,7168]{1,0:T(8,128)(2,1)S(1)}, bf16[32,7168]{1,0:T(8,128)(2,1)S(1)}, u32[]{:S(2)}, u32[]{:S(2)}) collective-permute-start(bf16[32,7168]{1,0:T(8,128)(2,1)S(1)} %add_convert_fusion.10), channel_id=1, source_target_pairs={{4,0},{5,1},{8,4},{9,5},{12,8},{13,9},{14,12},{15,13},{10,14},{11,... | collective-permute-start | bytes 1376264 | tf_op jit(solution)/shard_map/ppermute | solution.py:354
  187.3 18.1 %collective-permute-start.39 = (bf16[32,7168]{1,0:T(8,128)(2,1)S(1)}, bf16[32,7168]{1,0:T(8,128)(2,1)S(1)}, u32[]{:S(2)}, u32[]{:S(2)}) collective-permute-start(bf16[32,7168]{1,0:T(8,128)(2,1)S(1)} %add_convert_fusion.9), channel_id=1, source_target_pairs={{0,4},{1,5},{4,8},{5,9},{8,12},{9,13},{12,14},{13,15},{14,10},{15,... | collective-permute-start | bytes 1376264 | tf_op jit(solution)/shard_map/ppermute | solution.py:354
  195.9 17.7 %collective-permute-start.46 = (bf16[32,7168]{1,0:T(8,128)(2,1)S(1)}, bf16[32,7168]{1,0:T(8,128)(2,1)S(1)}, u32[]{:S(2)}, u32[]{:S(2)}) collective-permute-start(bf16[32,7168]{1,0:T(8,128)(2,1)S(1)} %add_convert_fusion.2), channel_id=1, source_target_pairs={{4,0},{5,1},{8,4},{9,5},{12,8},{13,9},{14,12},{15,13},{10,14},{11,... | collective-permute-start | bytes 1376264 | tf_op jit(solution)/shard_map/ppermute | solution.py:354
  197.2 18.1 %collective-permute-start.47 = (bf16[32,7168]{1,0:T(8,128)(2,1)S(1)}, bf16[32,7168]{1,0:T(8,128)(2,1)S(1)}, u32[]{:S(2)}, u32[]{:S(2)}) collective-permute-start(bf16[32,7168]{1,0:T(8,128)(2,1)S(1)} %add_convert_fusion.1), channel_id=1, source_target_pairs={{0,4},{1,5},{4,8},{5,9},{8,12},{9,13},{12,14},{13,15},{14,10},{15,... | collective-permute-start | bytes 1376264 | tf_op jit(solution)/shard_map/ppermute | solution.py:354
  205.7 15.8 %collective-permute-start.40 = (bf16[32,7168]{1,0:T(8,128)(2,1)S(1)}, bf16[32,7168]{1,0:T(8,128)(2,1)S(1)}, u32[]{:S(2)}, u32[]{:S(2)}) collective-permute-start(bf16[32,7168]{1,0:T(8,128)(2,1)S(1)} %add_convert_fusion.8), channel_id=1, source_target_pairs={{4,0},{5,1},{8,4},{9,5},{12,8},{13,9},{14,12},{15,13},{10,14},{11,... | collective-permute-start | bytes 1376264 | tf_op jit(solution)/shard_map/ppermute | solution.py:354
  207.0 15.9 %collective-permute-start.41 = (bf16[32,7168]{1,0:T(8,128)(2,1)S(1)}, bf16[32,7168]{1,0:T(8,128)(2,1)S(1)}, u32[]{:S(2)}, u32[]{:S(2)}) collective-permute-start(bf16[32,7168]{1,0:T(8,128)(2,1)S(1)} %add_convert_fusion.7), channel_id=1, source_target_pairs={{0,4},{1,5},{4,8},{5,9},{8,12},{9,13},{12,14},{13,15},{14,10},{15,... | collective-permute-start | bytes 1376264 | tf_op jit(solution)/shard_map/ppermute | solution.py:354
  (17 other events, 129.5 us)

commit v6 on v5

--- a/solution.py
+++ b/solution.py
@@ -17,93 +17,130 @@
 VMEM_LIMIT = 16 << 20
 
 
-def mlp_kernel(sizes, tile, *refs):
-    count = len(sizes)
+def mlp_kernel(blocks, tile, *refs):
+    count = sum(len(sizes) for sizes in blocks)
+    total = len(blocks)
     x_refs = refs[:count]
-    up_hbm, down_hbm, mine_hbm, other_hbm = refs[count : count + 4]
-    rows_ref, up_ref, down_ref, part_ref, x_sems, up_sems, down_sems, out_sems = refs[count + 4 :]
+    up_hbm, down_hbm = refs[count : count + 2]
+    out_refs = refs[count + 2 : count + 2 + 2 * total]
+    rows_ref, up_ref, down_ref, part_ref, merged_ref, hidden_ref = refs[
+        count + 2 + 2 * total : count + 8 + 2 * total
+    ]
+    x_sems, up_sems, down_sems, out_sems = refs[count + 8 + 2 * total :]
     width = up_hbm.shape[0]
     half = down_hbm.shape[0]
     tiles = width // tile
-    size = mine_hbm.shape[0]
-    spans = [pl.ds(k * tile, tile) for k in range(tiles)]
-    starts = [sum(sizes[:c]) for c in range(count)]
-    x_copies = [
-        [
-            pltpu.make_async_copy(
-                x_refs[c].at[:, spans[k]],
-                rows_ref.at[pl.ds(starts[c], sizes[c]), spans[k]],
-                x_sems.at[c, k],
-            )
-            for c in range(count)
-        ]
-        for k in range(tiles)
-    ]
-    up_copies = [
-        pltpu.make_async_copy(up_hbm.at[s], up_ref.at[s], up_sems.at[k])
-        for k, s in enumerate(spans)
-    ]
-    down_copies = [
-        pltpu.make_async_copy(down_hbm.at[:, s], down_ref.at[:, s], down_sems.at[k])
-        for k, s in enumerate(spans)
-    ]
+    x_copies = []
+    at = 0
+    for b, sizes in enumerate(blocks):
+        copies = []
+        row = 0
+        for size in sizes:
+            copies.append(
+                pltpu.make_async_copy(
+                    x_refs[at], rows_ref.at[b % 2, pl.ds(row, size)], x_sems.at[at]
+                )
+            )
+            row += size
+            at += 1
+        x_copies.append(copies)
+    def up_copy(k):
+        span = pl.ds(pl.multiple_of(k * tile, tile), tile)
+        return pltpu.make_async_copy(up_hbm.at[span], up_ref.at[span], up_sems.at[k])
+
+    def down_copy(k):
+        span = pl.ds(pl.multiple_of(k * tile, tile), tile)
+        return pltpu.make_async_copy(down_hbm.at[:, span], down_ref.at[:, span], down_sems.at[k])
+
+    for copy in x_copies[0]:
+        copy.start()
     for k in range(tiles):
-        for copy in x_copies[k]:
+        up_copy(k).start()
+    for k in range(tiles):
+        down_copy(k).start()
+    out_copies = []
+    for b, sizes in enumerate(blocks):
+        slot = b % 2
+        rows = sum(sizes)
+        if b + 1 < total:
+            for copy in x_copies[b + 1]:
+                copy.start()
+        for copy in x_copies[b]:
+            copy.wait()
+        merged_ref[:rows] = jnp.zeros((rows, 2 * half), jnp.float32)
+
+        def up_step(k, _, b=b, slot=slot, rows=rows):
+            if b == 0:
+                up_copy(k).wait()
+            span = pl.ds(pl.multiple_of(k * tile, tile), tile)
+            merged_ref[:rows] += jnp.dot(
+                rows_ref[slot, :rows, span], up_ref[span, :], preferred_element_type=jnp.float32
+            )
+            return 0
+
+        lax.fori_loop(0, tiles, up_step, 0)
+        merged = merged_ref[:rows]
+        hidden_ref[:rows] = (jax.nn.silu(merged[:, :half]) * merged[:, half:]).astype(jnp.bfloat16)
+        if b >= 2:
+            for copy in out_copies[b - 2]:
+                copy.wait()
+
+        def down_step(k, _, b=b, slot=slot, rows=rows):
+            if b == 0:
+                down_copy(k).wait()
+            span = pl.ds(pl.multiple_of(k * tile, tile), tile)
+            part = jnp.dot(
+                hidden_ref[:rows], down_ref[:, span], preferred_element_type=jnp.float32
+            )
+            part_ref[slot, :rows, span] = part.astype(jnp.bfloat16)
+            return 0
+
+        lax.fori_loop(0, tiles, down_step, 0)
+        size = rows // 2
+        copies = []
+        for c in range(2):
+            copy = pltpu.make_async_copy(
+                part_ref.at[slot, pl.ds(c * size, size)], out_refs[2 * b + c], out_sems.at[b, c]
+            )
             copy.start()
-        up_copies[k].start()
-    for copy in down_copies:
-        copy.start()
-    merged = None
-    for k in range(tiles):
-        for copy in x_copies[k]:
+            copies.append(copy)
+        out_copies.append(copies)
+    for copies in out_copies[-2:]:
+        for copy in copies:
             copy.wait()
-        up_copies[k].wait()
-        cols = slice(k * tile, (k + 1) * tile)
-        part = jnp.dot(rows_ref[:, cols], up_ref[cols, :], preferred_element_type=jnp.float32)
-        merged = part if merged is None else merged + part
-    hidden = (jax.nn.silu(merged[:, :half]) * merged[:, half:]).astype(jnp.bfloat16)
-    out_copies = []
-    for n, s in enumerate(spans):
-        down_copies[n].wait()
-        cols = slice(n * tile, (n + 1) * tile)
-        part = jnp.dot(hidden, down_ref[:, cols], preferred_element_type=jnp.float32)
-        part_ref[:, cols] = part.astype(jnp.bfloat16)
-        for c, target in enumerate((mine_hbm, other_hbm)):
-            copy = pltpu.make_async_copy(
-                part_ref.at[pl.ds(c * size, size), s], target.at[:, s], out_sems.at[c, n]
-            )
-            copy.start()
-            out_copies.append(copy)
-    for copy in out_copies:
-        copy.wait()
-
-
-def mlp(mine, other, gate_up, down_proj, tile=1024):
-    chunks = mine + other
+
+
+def mlp(blocks, gate_up, down_proj):
     width, both = gate_up.shape
     half = down_proj.shape[0]
-    tile = tile if width % tile == 0 else width
+    tile = width // 4 if width % 512 == 0 else width
     tiles = width // tile
-    sizes = tuple(c.shape[0] for c in chunks)
-    rows = sum(sizes)
+    sizes = tuple(tuple(c.shape[0] for c in chunks) for chunks in blocks)
+    counts = [sum(block) for block in sizes]
+    chunks = [c for block in blocks for c in block]
+    rows = sum(counts)
     anywhere = pl.BlockSpec(memory_space=pl.ANY)
     dma = pltpu.SemaphoreType.DMA
-    return pl.pallas_call(
+    results = pl.pallas_call(
         functools.partial(mlp_kernel, sizes, tile),
         in_specs=[anywhere] * len(chunks) + [pl.BlockSpec(memory_space=pltpu.HBM)] * 2,
-        out_specs=[anywhere, anywhere],
-        out_shape=[jax.ShapeDtypeStruct((rows // 2, width), jnp.bfloat16)] * 2,
+        out_specs=[anywhere] * (2 * len(blocks)),
+        out_shape=[
+            jax.ShapeDtypeStruct((n // 2, width), jnp.bfloat16) for n in counts for _ in range(2)
+        ],
         scratch_shapes=[
-            pltpu.VMEM((rows, width), jnp.bfloat16),
+            pltpu.VMEM((2, max(counts), width), jnp.bfloat16),
             pltpu.VMEM((width, both), jnp.bfloat16),
             pltpu.VMEM((half, width), jnp.bfloat16),
-            pltpu.VMEM((rows, width), jnp.bfloat16),
-            dma((len(chunks), tiles)),
+            pltpu.VMEM((2, max(counts), width), jnp.bfloat16),
+            pltpu.VMEM((max(counts), both), jnp.float32),
+            pltpu.VMEM((max(counts), half), jnp.bfloat16),
+            dma((len(chunks),)),
             dma((tiles,)),
             dma((tiles,)),
-            dma((2, tiles)),
+            dma((len(blocks), 2)),
         ],
-        compiler_params=pltpu.CompilerParams(vmem_limit_bytes=44 << 20),
+        compiler_params=pltpu.CompilerParams(vmem_limit_bytes=46 << 20),
         cost_estimate=pl.CostEstimate(
             flops=6 * rows * width * half,
             bytes_accessed=6 * width * half + 4 * rows * width,
@@ -111,6 +148,7 @@
         ),
         name="mlp",
     )(*chunks, gate_up, down_proj)
+    return [(results[2 * b], results[2 * b + 1]) for b in range(len(blocks))]
 
 
 def ship_kernel(source_ref, block_ref, out_ref):
@@ -276,11 +314,18 @@
 
     own = [prefill_tokens, decode_rows]
     sizes = [prefill_count, decode_count]
-    front = {1: [lax.ppermute(c, AXIS, ahead) for c in own]}
-    rear = {1: [lax.ppermute(c, AXIS, back) for c in own]}
-    front[1][0], rear[1][0], shipped, small = lax.optimization_barrier(
-        (front[1][0], rear[1][0], shipped, small)
-    )
+    mine = {0: own}
+    front = [lax.ppermute(c, AXIS, ahead) for c in own]
+    rear = [lax.ppermute(c, AXIS, back) for c in own]
+    mine[1] = front + rear
+    for s in range(2, half):
+        front = [lax.ppermute(c, AXIS, ahead) for c in front]
+        rear = [lax.ppermute(c, AXIS, back) for c in rear]
+        if s == 2:
+            front[0], rear[0], shipped, small = lax.optimization_barrier(
+                (front[0], rear[0], shipped, small)
+            )
+        mine[s] = front + rear
     at_shift = lax.dynamic_index_in_dim(jnp.asarray(neighbours), me, 0, keepdims=False)
     picked = at_shift[:, None] == jnp.arange(devices)[None, :]
     shift_gates = jnp.sum(jnp.where(picked[:, :, None], small[None, :, :row_count], 0), axis=1)
@@ -289,35 +334,21 @@
     slot_length = slot_codes % (block_rows + 1)
     slot_request = slot_codes // (block_rows + 1)
 
-    for s in range(2, half):
-        front[s] = [lax.ppermute(c, AXIS, ahead) for c in front[s - 1]]
-        rear[s] = [lax.ppermute(c, AXIS, back) for c in rear[s - 1]]
-
-    def work(s, mine):
-        other = [lax.ppermute(c, AXIS, across) for c in mine]
-        return mlp(mine, other, gate_up, down_proj)
-
-    front[half] = [lax.ppermute(front[half - 1][0], AXIS, ahead)]
-    rear[half] = [lax.ppermute(rear[half - 1][1], AXIS, back)]
-    front, rear, shipped, shift_gates = lax.optimization_barrier(
-        (front, rear, shipped, shift_gates)
-    )
+
+    mine[half] = [lax.ppermute(front[0], AXIS, ahead), lax.ppermute(rear[1], AXIS, back)]
+    mine, shipped, shift_gates = lax.optimization_barrier((mine, shipped, shift_gates))
     block_latents = lax.all_to_all(shipped, AXIS, split_axis=0, concat_axis=0, tiled=True)
-    results = {}
-    for s in range(half, 0, -1):
-        results[s] = work(s, front[s] + rear[s] + (own if s == 1 else []))
-    parts = {s: (part, lax.ppermute(rest, AXIS, across)) for s, (part, rest) in results.items()}
+
+    parts = {}
+    for steps in ([half], list(range(half - 1, -1, -1))):
+        both = [mine[s] + [lax.ppermute(c, AXIS, across) for c in mine[s]] for s in steps]
+        for s, (part, rest) in zip(steps, mlp(both, gate_up, down_proj)):
+            parts[s] = (part, lax.ppermute(rest, AXIS, across))
 
     def contribution(s, k, flow):
-        part, from_other = parts[max(s, 1)]
+        part, from_other = parts[s]
         size = sizes[flow]
-        lo = flow * split
-        if s == half:
-            lo = k * split
-        elif s == 0:
-            lo = lo + 2 * row_count
-        else:
-            lo = lo + k * row_count
+        lo = k * split if s == half else flow * split + (k * row_count if s else 0)
         both = part[lo : lo + size].astype(jnp.float32) + from_other[lo : lo + size].astype(
             jnp.float32
         )

time: 227 us -> 231 us (1.018)
  other arithmetic: 21.6 us -> 17.8 us
  waiting for transfers between devices: 89.6 us -> 93.1 us
  local copies, waits for them, and re-layouts: 7.47 us -> 10.7 us
    ppermute x34 -> x35, waiting for transfers between devices: 41.6 us -> 47.9 us  [the longest x4 14.6 us: per_device(): front = [lax.ppermute(c, AXIS, ahead) for c in front]]
    pallas_call x4 -> x2, Pallas kernels: 52 us -> 47 us  [mlp(): pl.pallas_call(functools.partial(mlp_kernel, sizes, tile), in_specs=[anyw...]
    pallas_call x2, Pallas kernels: 8.2 us -> 12.3 us  [attend(): pl.pallas_call(attend_kernel, grid_spec=pltpu.PrefetchScalarGridSpec(num_...]
    convert_element_type x4 -> x5, other arithmetic: 10.7 us -> 7.11 us  [contribution(): return (weight[:, None] * both).astype(jnp.bfloat16)]
    unnamed x62 -> x76, local copies, waits for them, and re-layouts: 6.21 us -> 9.41 us
    ppermute x34 -> x35, starting transfers between devices: 19.3 us -> 19 us  [the longest x4 4.38 us: per_device(): rear = [lax.ppermute(c, AXIS, back) for c in rear]]
  transfers between devices with their start and end apart: 50 -> 51, of which waited for: 21 -> 23; matrix products, arithmetic and copies ran while one was open for 9% -> 7% of each run, Pallas kernels for 27% -> 26%
where the time goes in v6:
time: 231 us; the launch traced here: 229 us
  waiting for transfers between devices  93.1 us (40%)
  Pallas kernels  60.1 us (26%)
  starting transfers between devices  45.7 us (20%)
  other arithmetic  17.8 us (8%)
  local copies, waits for them, and re-layouts  10.7 us (5%)
    pallas_call x2, Pallas kernels, mlp(): pl.pallas_call(functools.partial(mlp_kernel, sizes, tile), in_specs=[anyw...  47 us
    ppermute x14, waiting for transfers between devices, per_device(): lax.ppermute(value, AXIS, course[way])  39.4 us
    ppermute x4, waiting for transfers between devices, per_device(): front = [lax.ppermute(c, AXIS, ahead) for c in front]  14.6 us
    ppermute x14, starting transfers between devices, per_device(): lax.ppermute(value, AXIS, course[way])  14.5 us
    pallas_call x2, Pallas kernels, attend(): pl.pallas_call(attend_kernel, grid_spec=pltpu.PrefetchScalarGridSpec(num_...  12.3 us
    unnamed x76, local copies, waits for them, and re-layouts  9.41 us
    ppermute x1, waiting for transfers between devices, per_device(): lax.ppermute(front[0], AXIS, ahead)  8.94 us
    ppermute x2, waiting for transfers between devices, per_device(): rear = [lax.ppermute(c, AXIS, back) for c in own]  8.18 us
  transfers between devices with their start and end apart: 51, of which 23 were waited for; matrix products, arithmetic and copies ran while one was open for 7% of the time, Pallas kernels for 26%

profile of v6, /device:TPU:20, one launch (start us, length us, event | category | flops | bytes accessed | tf_op | source)
XLA Modules:
  0.0 228.5 jit_solution(14301442953634614560)
XLA Ops:
  1.1 1.6 collective-permute-start.2
  2.7 1.6 collective-permute-start.3
  4.7 0.9 convert_reduce_fusion.2
  5.6 0.7 multiply_add_fusion
  6.3 8.1 %collective-permute-done.refs_16_ = bf16[32,7168]{1,0:T(8,128)(2,1)} collective-permute-done((bf16[32,7168]{1,0:T(8,128)(2,1)}, bf16[32,7168]{1,0:T(8,128)(2,1)}, u32[]{:S(2)}, u32[]{:S(2)}) %collective-permute-start) | collective-permute-done | bytes 458784 | tf_op jit(solution)/shard_map/ppermute | solution.py:318
  14.9 1.6 collective-permute-start.5
  16.4 8.2 %collective-permute-done.3.refs_19_ = bf16[32,7168]{1,0:T(8,128)(2,1)S(1)} collective-permute-done((bf16[32,7168]{1,0:T(8,128)(2,1)}, bf16[32,7168]{1,0:T(8,128)(2,1)S(1)}, u32[]{:S(2)}, u32[]{:S(2)}) %collective-permute-start.3) | collective-permute-done | bytes 458784 | tf_op jit(solution)/shard_map/ppermute | solution.py:319
  24.6 1.6 collective-permute-start.7
  26.4 0.8 select_reduce_fusion.1
  27.9 6.1 %all-to-all-start = ((s32[16,1,66]{2,1,0:T(1,128)}), s32[16,1,66]{2,1,0:T(1,128)S(1)}, u32[]{:S(2)}, u32[]{:S(2)}) async-start(s32[16,1,66]{2,1,0:T(1,128)} %bitcast.2), calls=%async_computation | async-start | bytes 16384 | tf_op jit(solution)/shard_map/all_to_all | solution.py:312
  34.0 1.3 copy-done.2
  35.3 0.7 ship.1
  36.1 1.5 copy-done.1
  38.2 5.8 %all-to-all-done = s32[16,1,66]{2,1,0:T(1,128)S(1)} async-done(((s32[16,1,66]{2,1,0:T(1,128)}), s32[16,1,66]{2,1,0:T(1,128)S(1)}, u32[]{:S(2)}, u32[]{:S(2)}) %all-to-all-start) | async-done | bytes 4256 | tf_op jit(solution)/shard_map/all_to_all | solution.py:312
  44.0 1.5 collective-permute-start.8
  47.3 3.6 %collective-permute-done.6.refs_9_ = bf16[32,7168]{1,0:T(8,128)(2,1)S(1)} collective-permute-done((bf16[32,7168]{1,0:T(8,128)(2,1)S(1)}, bf16[32,7168]{1,0:T(8,128)(2,1)S(1)}, u32[]{:S(2)}, u32[]{:S(2)}) %collective-permute-start.6) | collective-permute-done | bytes 458784 | tf_op jit(solution)/shard_map/ppermute | solution.py:322
  51.5 9.3 %collective-permute-done.8.refs_0_ = bf16[32,7168]{1,0:T(8,128)(2,1)S(1)} collective-permute-done((bf16[32,7168]{1,0:T(8,128)(2,1)S(1)}, bf16[32,7168]{1,0:T(8,128)(2,1)S(1)}, u32[]{:S(2)}, u32[]{:S(2)}) %collective-permute-start.8) | collective-permute-done | bytes 458784 | tf_op jit(solution)/shard_map/ppermute | solution.py:322
  61.4 1.5 collective-permute-start.13
  63.0 6.0 %collective-permute-done.10.refs_2_ = bf16[32,7168]{1,0:T(8,128)(2,1)} collective-permute-done((bf16[32,7168]{1,0:T(8,128)(2,1)}, bf16[32,7168]{1,0:T(8,128)(2,1)}, u32[]{:S(2)}, u32[]{:S(2)}) %collective-permute-start.10) | collective-permute-done | bytes 458784 | tf_op jit(solution)/shard_map/ppermute | solution.py:323
  69.0 1.7 collective-permute-done.9.refs_1_
  70.7 8.9 %collective-permute-done.12.refs_0_ = bf16[32,7168]{1,0:T(8,128)(2,1)S(1)} collective-permute-done((bf16[32,7168]{1,0:T(8,128)(2,1)S(1)}, bf16[32,7168]{1,0:T(8,128)(2,1)S(1)}, u32[]{:S(2)}, u32[]{:S(2)}) %collective-permute-start.12) | collective-permute-done | bytes 458784 | tf_op jit(solution)/shard_map/ppermute | solution.py:338
  79.7 0.8 copy-done.9
  81.6 0.8 copy-done.11
  82.4 0.8 copy-done.5
  83.2 0.8 copy-done.13
  84.4 0.8 copy-done.7
  86.8 0.8 copy-done.15
  88.1 6.1 %all-to-all-start.1 = ((bf16[32,64,576]{2,1,0:T(8,128)(2,1)}), bf16[32,64,576]{2,1,0:T(8,128)(2,1)S(1)}, u32[]{:S(2)}, u32[]{:S(2)}) async-start(bf16[32,64,576]{2,1,0:T(8,128)(2,1)} %copy-done.1), calls=%async_computation.1 | async-start | bytes 5242880 | tf_op jit(solution)/shard_map/all_to_all | solution.py:340
  95.6 11.6 %mlp.2 = (bf16[64,7168]{1,0:T(8,128)(2,1)S(1)}, bf16[64,7168]{1,0:T(8,128)(2,1)S(1)}) custom-call(bf16[32,7168]{1,0:T(8,128)(2,1)S(1)} %collective-permute-done.12.refs_0_, bf16[32,7168]{1,0:T(8,128)(2,1)} %collective-permute-done.13.refs_1_, bf16[32,7168]{1,0:T(8,128)(2,1)} %collective-permute-done.14.refs_2_, ...), custom_call_target="tpu_custom_call" | custom-call | flops 2818572288 | bytes 25690112 | tf_op jit(solution)/shard_map/mlp/pallas_call | solution.py:124
  108.7 0.8 copy-done.37
  109.6 35.5 %mlp.3 = (bf16[128,7168]{1,0:T(8,128)(2,1)}, bf16[128,7168]{1,0:T(8,128)(2,1)}, bf16[128,7168]{1,0:T(8,128)(2,1)}, bf16[128,7168]{1,0:T(8,128)(2,1)}, bf16[128,7...) custom-call(bf16[32,7168]{1,0:T(8,128)(2,1)S(1)} %copy-done.10, ...), custom_call_target="tpu_custom_call" | custom-call | flops 19730006016 | bytes 47710208 | tf_op jit(solution)/shard_map/mlp/pallas_call | solution.py:124
  146.1 1.1 multiply_convert_fusion.15
  147.8 1.5 collective-permute-start.38
  149.3 1.0 multiply_convert_fusion.1
  150.4 1.6 multiply_convert_fusion.3
  152.1 1.0 collective-permute-done.33
  153.0 1.7 multiply_convert_fusion.7
  154.7 0.9 collective-permute-done.32
  155.7 1.7 multiply_convert_fusion.11
  157.3 3.8 %collective-permute-done.17 = bf16[32,7168]{1,0:T(8,128)(2,1)} collective-permute-done((bf16[32,7168]{1,0:T(8,128)(2,1)S(1)}, bf16[32,7168]{1,0:T(8,128)(2,1)}, u32[]{:S(2)}, u32[]{:S(2)}) %collective-permute-start.17) | collective-permute-done | bytes 458784 | tf_op jit(solution)/shard_map/ppermute | solution.py:385
  161.1 1.0 collective-permute-done.38
  162.1 1.3 add_convert_fusion.5
  163.4 1.7 collective-permute-start.43
  165.5 1.3 add_convert_fusion.11
  166.7 1.7 collective-permute-start.36
  168.8 5.8 %attend.2 = bf16[16,64,512]{2,1,0:T(8,128)(2,1)S(1)} custom-call(s32[32]{0:T(128)S(1)} %select_reduce_fusion.3.order_ref, s32[17]{0:T(128)S(1)} %get-tuple-element.218.start_ref, s32[32]{0:T(128)S(1)} %get-tuple-element.219.length_ref, bf16[32,64,576]{2,1,0:T(8,128)(2,1)S(1)} %copy-done, bf16[32,1,576]{2,1,0:T(2,128)(2,1)S(1)} %copy.34.own_ref, ...), custom_call_target="tpu_custom_call" | custom-call | flops 150994944 | bytes 4587520 | tf_op jit(solution)/shard_map/attend/pallas_call | solution.py:220
  174.6 2.3 collective-permute-done.43
  176.9 1.9 collective-permute-done.44
  179.6 1.5 collective-permute-start.46
  181.1 5.6 %collective-permute-done.36 = bf16[32,7168]{1,0:T(8,128)(2,1)S(1)} collective-permute-done((bf16[32,7168]{1,0:T(8,128)(2,1)}, bf16[32,7168]{1,0:T(8,128)(2,1)S(1)}, u32[]{:S(2)}, u32[]{:S(2)}) %collective-permute-start.36) | collective-permute-done | bytes 458784 | tf_op jit(solution)/shard_map/ppermute | solution.py:385
  186.7 1.9 collective-permute-done.37
  189.5 1.5 collective-permute-start.40
  190.9 5.6 %collective-permute-done.45 = bf16[32,7168]{1,0:T(8,128)(2,1)S(1)} collective-permute-done((bf16[32,7168]{1,0:T(8,128)(2,1)S(1)}, bf16[32,7168]{1,0:T(8,128)(2,1)S(1)}, u32[]{:S(2)}, u32[]{:S(2)}) %collective-permute-start.45) | collective-permute-done | bytes 458784 | tf_op jit(solution)/shard_map/ppermute | solution.py:385
  196.6 1.9 collective-permute-done.46
  199.3 1.5 collective-permute-start.48
  200.7 5.6 %collective-permute-done.39 = bf16[32,7168]{1,0:T(8,128)(2,1)S(1)} collective-permute-done((bf16[32,7168]{1,0:T(8,128)(2,1)S(1)}, bf16[32,7168]{1,0:T(8,128)(2,1)S(1)}, u32[]{:S(2)}, u32[]{:S(2)}) %collective-permute-start.39) | collective-permute-done | bytes 458784 | tf_op jit(solution)/shard_map/ppermute | solution.py:385
  206.4 1.9 collective-permute-done.40
  209.1 1.5 collective-permute-start.42
  210.6 6.5 %attend.3 = bf16[16,64,512]{2,1,0:T(8,128)(2,1)S(1)} custom-call(s32[32]{0:T(128)S(1)} %select_reduce_fusion.3.order_ref, s32[17]{0:T(128)S(1)} %get-tuple-element.217.start_ref, s32[32]{0:T(128)S(1)} %get-tuple-element.219.length_ref, bf16[32,64,576]{2,1,0:T(8,128)(2,1)S(1)} %copy-done, bf16[32,1,576]{2,1,0:T(2,128)(2,1)S(1)} %copy.34.own_ref, ...), custom_call_target="tpu_custom_call" | custom-call | flops 150994944 | bytes 4587520 | tf_op jit(solution)/shard_map/attend/pallas_call | solution.py:220
  217.2 1.5 pad_maximum_fusion
  218.7 6.0 %collective-permute-done.41 = bf16[32,7168]{1,0:T(8,128)(2,1)S(1)} collective-permute-done((bf16[32,7168]{1,0:T(8,128)(2,1)S(1)}, bf16[32,7168]{1,0:T(8,128)(2,1)S(1)}, u32[]{:S(2)}, u32[]{:S(2)}) %collective-permute-start.41) | collective-permute-done | bytes 458784 | tf_op jit(solution)/shard_map/ppermute | solution.py:385
  224.7 2.0 collective-permute-done.42
  226.7 0.9 add_convert_fusion
  227.6 0.9 add_convert_fusion.6
  (161 shorter events, 18.7 us)
Async XLA Ops:
  0.6 13.8 %collective-permute-start = (bf16[32,7168]{1,0:T(8,128)(2,1)}, bf16[32,7168]{1,0:T(8,128)(2,1)}, u32[]{:S(2)}, u32[]{:S(2)}) collective-permute-start(bf16[32,7168]{1,0:T(8,128)(2,1)} %refs_24_), channel_id=1, source_target_pairs={{0,4},{1,5},{4,8},{5,9},{8,12},{9,13},{12,14},{13,15},{14,10},{15,... | collective-permute-start | bytes 1376264 | tf_op jit(solution)/shard_map/ppermute | solution.py:318
  1.1 13.7 %collective-permute-start.2 = (bf16[32,7168]{1,0:T(8,128)(2,1)}, bf16[32,7168]{1,0:T(8,128)(2,1)S(1)}, u32[]{:S(2)}, u32[]{:S(2)}) collective-permute-start(bf16[32,7168]{1,0:T(8,128)(2,1)} %refs_24_), channel_id=1, source_target_pairs={{4,0},{5,1},{8,4},{9,5},{12,8},{13,9},{14,12},{15,13},{10,14},{11,... | collective-permute-start | bytes 1376264 | tf_op jit(solution)/shard_map/ppermute | solution.py:319
  2.7 21.9 %collective-permute-start.3 = (bf16[32,7168]{1,0:T(8,128)(2,1)}, bf16[32,7168]{1,0:T(8,128)(2,1)S(1)}, u32[]{:S(2)}, u32[]{:S(2)}) collective-permute-start(bf16[32,7168]{1,0:T(8,128)(2,1)} %refs_25_), channel_id=1, source_target_pairs={{4,0},{5,1},{8,4},{9,5},{12,8},{13,9},{14,12},{15,13},{10,14},{11,... | collective-permute-start | bytes 1376264 | tf_op jit(solution)/shard_map/ppermute | solution.py:319
  4.3 33.3 %collective-permute-start.1 = (bf16[32,7168]{1,0:T(8,128)(2,1)}, bf16[32,7168]{1,0:T(8,128)(2,1)S(1)}, u32[]{:S(2)}, u32[]{:S(2)}) collective-permute-start(bf16[32,7168]{1,0:T(8,128)(2,1)} %refs_25_), channel_id=1, source_target_pairs={{0,4},{1,5},{4,8},{5,9},{8,12},{9,13},{12,14},{13,15},{14,10},{15,... | collective-permute-start | bytes 1376264 | tf_op jit(solution)/shard_map/ppermute | solution.py:318
  14.4 29.6 %collective-permute-start.4 = (bf16[32,7168]{1,0:T(8,128)(2,1)}, bf16[32,7168]{1,0:T(8,128)(2,1)S(1)}, u32[]{:S(2)}, u32[]{:S(2)}) collective-permute-start(bf16[32,7168]{1,0:T(8,128)(2,1)} %collective-permute-done.refs_16_), channel_id=1, source_target_pairs={{0,4},{1,5},{4,8},{5,9},{8,12},{9,13},{12,14},{13,15},{14,10},{15,... | collective-permute-start | bytes 1376264 | tf_op jit(solution)/shard_map/ppermute | solution.py:322
  14.9 21.2 %copy-start.31 = (bf16[32,7168]{1,0:T(8,128)(2,1)}, bf16[32,7168]{1,0:T(8,128)(2,1)S(1)}, u32[]{:S(2)}) copy-start(bf16[32,7168]{1,0:T(8,128)(2,1)S(1)} %collective-permute-done.2.refs_18_) | copy-start | bytes 1376260
  14.9 29.1 %collective-permute-start.5 = (bf16[32,7168]{1,0:T(8,128)(2,1)S(1)}, bf16[32,7168]{1,0:T(8,128)(2,1)}, u32[]{:S(2)}, u32[]{:S(2)}) collective-permute-start(bf16[32,7168]{1,0:T(8,128)(2,1)S(1)} %collective-permute-done.2.refs_18_), channel_id=1, source_target_pairs={{4,0},{5,1},{8,4},{9,5},{12,8},{13,9},{14,12},{15,13},{10,14},{11,... | collective-permute-start | bytes 1376264 | tf_op jit(solution)/shard_map/ppermute | solution.py:323
  24.6 20.8 %collective-permute-start.7 = (bf16[32,7168]{1,0:T(8,128)(2,1)S(1)}, bf16[32,7168]{1,0:T(8,128)(2,1)}, u32[]{:S(2)}, u32[]{:S(2)}) collective-permute-start(bf16[32,7168]{1,0:T(8,128)(2,1)S(1)} %collective-permute-done.3.refs_19_), channel_id=1, source_target_pairs={{4,0},{5,1},{8,4},{9,5},{12,8},{13,9},{14,12},{15,13},{10,14},{11,... | collective-permute-start | bytes 1376264 | tf_op jit(solution)/shard_map/ppermute | solution.py:323
  27.9 16.1 %all-to-all-start = ((s32[16,1,66]{2,1,0:T(1,128)}), s32[16,1,66]{2,1,0:T(1,128)S(1)}, u32[]{:S(2)}, u32[]{:S(2)}) async-start(s32[16,1,66]{2,1,0:T(1,128)} %bitcast.2), calls=%async_computation | async-start | bytes 16384 | tf_op jit(solution)/shard_map/all_to_all | solution.py:312
  35.3 45.1 %copy-start.30 = (bf16[32,576]{1,0:T(8,128)(2,1)S(1)}, bf16[32,576]{1,0:T(8,128)(2,1)}, u32[]{:S(2)}) copy-start(bf16[32,576]{1,0:T(8,128)(2,1)} %param.24) | copy-start | bytes 110596
  37.6 50.5 %copy-start.3 = (bf16[32,7168]{1,0:T(8,128)(2,1)}, bf16[32,7168]{1,0:T(8,128)(2,1)S(1)}, u32[]{:S(2)}) copy-start(bf16[32,7168]{1,0:T(8,128)(2,1)S(1)} %collective-permute-done.1.refs_17_) | copy-start | bytes 1376260
  37.6 13.4 %collective-permute-start.6 = (bf16[32,7168]{1,0:T(8,128)(2,1)S(1)}, bf16[32,7168]{1,0:T(8,128)(2,1)S(1)}, u32[]{:S(2)}, u32[]{:S(2)}) collective-permute-start(bf16[32,7168]{1,0:T(8,128)(2,1)S(1)} %collective-permute-done.1.refs_17_), channel_id=1, source_target_pairs={{0,4},{1,5},{4,8},{5,9},{8,12},{9,13},{12,14},{13,15},{14,10},{15,... | collective-permute-start | bytes 1376264 | tf_op jit(solution)/shard_map/ppermute | solution.py:322
  44.0 16.8 %collective-permute-start.8 = (bf16[32,7168]{1,0:T(8,128)(2,1)S(1)}, bf16[32,7168]{1,0:T(8,128)(2,1)S(1)}, u32[]{:S(2)}, u32[]{:S(2)}) collective-permute-start(bf16[32,7168]{1,0:T(8,128)(2,1)S(1)} %collective-permute-done.4.refs_8_), channel_id=1, source_target_pairs={{0,4},{1,5},{4,8},{5,9},{8,12},{9,13},{12,14},{13,15},{14,10},{15,... | collective-permute-start | bytes 1376264 | tf_op jit(solution)/shard_map/ppermute | solution.py:322
  45.4 15.9 %collective-permute-start.11 = (bf16[32,7168]{1,0:T(8,128)(2,1)}, bf16[32,7168]{1,0:T(8,128)(2,1)S(1)}, u32[]{:S(2)}, u32[]{:S(2)}) collective-permute-start(bf16[32,7168]{1,0:T(8,128)(2,1)} %collective-permute-done.7.refs_11_), channel_id=1, source_target_pairs={{4,0},{5,1},{8,4},{9,5},{12,8},{13,9},{14,12},{15,13},{10,14},{11,... | collective-permute-start | bytes 1376264 | tf_op jit(solution)/shard_map/ppermute | solution.py:323
  46.7 22.3 %collective-permute-start.10 = (bf16[32,7168]{1,0:T(8,128)(2,1)}, bf16[32,7168]{1,0:T(8,128)(2,1)}, u32[]{:S(2)}, u32[]{:S(2)}) collective-permute-start(bf16[32,7168]{1,0:T(8,128)(2,1)} %collective-permute-done.5.refs_10_), channel_id=1, source_target_pairs={{4,0},{5,1},{8,4},{9,5},{12,8},{13,9},{14,12},{15,13},{10,14},{11,... | collective-permute-start | bytes 1376264 | tf_op jit(solution)/shard_map/ppermute | solution.py:323
  51.0 19.8 %collective-permute-start.9 = (bf16[32,7168]{1,0:T(8,128)(2,1)S(1)}, bf16[32,7168]{1,0:T(8,128)(2,1)}, u32[]{:S(2)}, u32[]{:S(2)}) collective-permute-start(bf16[32,7168]{1,0:T(8,128)(2,1)S(1)} %collective-permute-done.6.refs_9_), channel_id=1, source_target_pairs={{0,4},{1,5},{4,8},{5,9},{8,12},{9,13},{12,14},{13,15},{14,10},{15,... | collective-permute-start | bytes 1376264 | tf_op jit(solution)/shard_map/ppermute | solution.py:322
  60.8 18.9 %collective-permute-start.12 = (bf16[32,7168]{1,0:T(8,128)(2,1)S(1)}, bf16[32,7168]{1,0:T(8,128)(2,1)S(1)}, u32[]{:S(2)}, u32[]{:S(2)}) collective-permute-start(bf16[32,7168]{1,0:T(8,128)(2,1)S(1)} %collective-permute-done.8.refs_0_), channel_id=1, source_target_pairs={{0,4},{1,5},{4,8},{5,9},{8,12},{9,13},{12,14},{13,15},{14,10},{15,... | collective-permute-start | bytes 1376264 | tf_op jit(solution)/shard_map/ppermute | solution.py:338
  61.4 18.3 %collective-permute-start.13 = (bf16[32,7168]{1,0:T(8,128)(2,1)S(1)}, bf16[32,7168]{1,0:T(8,128)(2,1)}, u32[]{:S(2)}, u32[]{:S(2)}) collective-permute-start(bf16[32,7168]{1,0:T(8,128)(2,1)S(1)} %collective-permute-done.11.refs_3_), channel_id=1, source_target_pairs={{4,0},{5,1},{8,4},{9,5},{12,8},{13,9},{14,12},{15,13},{10,14},{11,... | collective-permute-start | bytes 1376264 | tf_op jit(solution)/shard_map/ppermute | solution.py:338
  79.7 3.6 %collective-permute-start.18 = (bf16[32,7168]{1,0:T(8,128)(2,1)S(1)}, bf16[32,7168]{1,0:T(8,128)(2,1)S(1)}, u32[]{:S(2)}, u32[]{:S(2)}) collective-permute-start(bf16[32,7168]{1,0:T(8,128)(2,1)S(1)} %collective-permute-done.8.refs_0_), channel_id=1, source_target_pairs={{0,1},{1,0},{2,3},{3,2},{4,5},{5,4},{6,7},{7,6},{8,9},{9,8},{10,11... | collective-permute-start | bytes 1376264 | tf_op jit(solution)/shard_map/ppermute | solution.py:344
  80.5 5.2 %collective-permute-start.19 = (bf16[32,7168]{1,0:T(8,128)(2,1)}, bf16[32,7168]{1,0:T(8,128)(2,1)}, u32[]{:S(2)}, u32[]{:S(2)}) collective-permute-start(bf16[32,7168]{1,0:T(8,128)(2,1)} %collective-permute-done.9.refs_1_), channel_id=1, source_target_pairs={{0,1},{1,0},{2,3},{3,2},{4,5},{5,4},{6,7},{7,6},{8,9},{9,8},{10,11... | collective-permute-start | bytes 1376264 | tf_op jit(solution)/shard_map/ppermute | solution.py:344
  81.1 4.8 %collective-permute-start.20 = (bf16[32,7168]{1,0:T(8,128)(2,1)}, bf16[32,7168]{1,0:T(8,128)(2,1)}, u32[]{:S(2)}, u32[]{:S(2)}) collective-permute-start(bf16[32,7168]{1,0:T(8,128)(2,1)} %collective-permute-done.10.refs_2_), channel_id=1, source_target_pairs={{0,1},{1,0},{2,3},{3,2},{4,5},{5,4},{6,7},{7,6},{8,9},{9,8},{10,11... | collective-permute-start | bytes 1376264 | tf_op jit(solution)/shard_map/ppermute | solution.py:344
  81.2 5.1 %collective-permute-start.21 = (bf16[32,7168]{1,0:T(8,128)(2,1)S(1)}, bf16[32,7168]{1,0:T(8,128)(2,1)}, u32[]{:S(2)}, u32[]{:S(2)}) collective-permute-start(bf16[32,7168]{1,0:T(8,128)(2,1)S(1)} %collective-permute-done.11.refs_3_), channel_id=1, source_target_pairs={{0,1},{1,0},{2,3},{3,2},{4,5},{5,4},{6,7},{7,6},{8,9},{9,8},{10,11... | collective-permute-start | bytes 1376264 | tf_op jit(solution)/shard_map/ppermute | solution.py:344
  82.4 4.0 %collective-permute-start.22 = (bf16[32,7168]{1,0:T(8,128)(2,1)S(1)}, bf16[32,7168]{1,0:T(8,128)(2,1)}, u32[]{:S(2)}, u32[]{:S(2)}) collective-permute-start(bf16[32,7168]{1,0:T(8,128)(2,1)S(1)} %collective-permute-done.4.refs_8_), channel_id=1, source_target_pairs={{0,1},{1,0},{2,3},{3,2},{4,5},{5,4},{6,7},{7,6},{8,9},{9,8},{10,11... | collective-permute-start | bytes 1376264 | tf_op jit(solution)/shard_map/ppermute | solution.py:344
  84.0 2.8 %collective-permute-start.23 = (bf16[32,7168]{1,0:T(8,128)(2,1)S(1)}, bf16[32,7168]{1,0:T(8,128)(2,1)S(1)}, u32[]{:S(2)}, u32[]{:S(2)}) collective-permute-start(bf16[32,7168]{1,0:T(8,128)(2,1)S(1)} %collective-permute-done.6.refs_9_), channel_id=1, source_target_pairs={{0,1},{1,0},{2,3},{3,2},{4,5},{5,4},{6,7},{7,6},{8,9},{9,8},{10,11... | collective-permute-start | bytes 1376264 | tf_op jit(solution)/shard_map/ppermute | solution.py:344
  85.7 8.5 %collective-permute-start.24 = (bf16[32,7168]{1,0:T(8,128)(2,1)}, bf16[32,7168]{1,0:T(8,128)(2,1)}, u32[]{:S(2)}, u32[]{:S(2)}) collective-permute-start(bf16[32,7168]{1,0:T(8,128)(2,1)} %collective-permute-done.5.refs_10_), channel_id=1, source_target_pairs={{0,1},{1,0},{2,3},{3,2},{4,5},{5,4},{6,7},{7,6},{8,9},{9,8},{10,11... | collective-permute-start | bytes 1376264 | tf_op jit(solution)/shard_map/ppermute | solution.py:344
  85.8 8.6 %collective-permute-start.25 = (bf16[32,7168]{1,0:T(8,128)(2,1)}, bf16[32,7168]{1,0:T(8,128)(2,1)}, u32[]{:S(2)}, u32[]{:S(2)}) collective-permute-start(bf16[32,7168]{1,0:T(8,128)(2,1)} %collective-permute-done.7.refs_11_), channel_id=1, source_target_pairs={{0,1},{1,0},{2,3},{3,2},{4,5},{5,4},{6,7},{7,6},{8,9},{9,8},{10,11... | collective-permute-start | bytes 1376264 | tf_op jit(solution)/shard_map/ppermute | solution.py:344
  86.3 8.5 %collective-permute-start.26 = (bf16[32,7168]{1,0:T(8,128)(2,1)}, bf16[32,7168]{1,0:T(8,128)(2,1)}, u32[]{:S(2)}, u32[]{:S(2)}) collective-permute-start(bf16[32,7168]{1,0:T(8,128)(2,1)} %collective-permute-done.refs_16_), channel_id=1, source_target_pairs={{0,1},{1,0},{2,3},{3,2},{4,5},{5,4},{6,7},{7,6},{8,9},{9,8},{10,11... | collective-permute-start | bytes 1376264 | tf_op jit(solution)/shard_map/ppermute | solution.py:344
  86.4 8.6 %collective-permute-start.14 = (bf16[32,7168]{1,0:T(8,128)(2,1)S(1)}, bf16[32,7168]{1,0:T(8,128)(2,1)}, u32[]{:S(2)}, u32[]{:S(2)}) collective-permute-start(bf16[32,7168]{1,0:T(8,128)(2,1)S(1)} %collective-permute-done.12.refs_0_), channel_id=1, source_target_pairs={{0,1},{1,0},{2,3},{3,2},{4,5},{5,4},{6,7},{7,6},{8,9},{9,8},{10,11... | collective-permute-start | bytes 1376264 | tf_op jit(solution)/shard_map/ppermute | solution.py:344
  87.6 7.7 %collective-permute-start.15 = (bf16[32,7168]{1,0:T(8,128)(2,1)}, bf16[32,7168]{1,0:T(8,128)(2,1)}, u32[]{:S(2)}, u32[]{:S(2)}) collective-permute-start(bf16[32,7168]{1,0:T(8,128)(2,1)} %collective-permute-done.13.refs_1_), channel_id=1, source_target_pairs={{0,1},{1,0},{2,3},{3,2},{4,5},{5,4},{6,7},{7,6},{8,9},{9,8},{10,11... | collective-permute-start | bytes 1376264 | tf_op jit(solution)/shard_map/ppermute | solution.py:344
  88.1 73.0 %all-to-all-start.1 = ((bf16[32,64,576]{2,1,0:T(8,128)(2,1)}), bf16[32,64,576]{2,1,0:T(8,128)(2,1)S(1)}, u32[]{:S(2)}, u32[]{:S(2)}) async-start(bf16[32,64,576]{2,1,0:T(8,128)(2,1)} %copy-done.1), calls=%async_computation.1 | async-start | bytes 5242880 | tf_op jit(solution)/shard_map/all_to_all | solution.py:340
  94.2 13.0 %collective-permute-start.27 = (bf16[32,7168]{1,0:T(8,128)(2,1)}, bf16[32,7168]{1,0:T(8,128)(2,1)S(1)}, u32[]{:S(2)}, u32[]{:S(2)}) collective-permute-start(bf16[32,7168]{1,0:T(8,128)(2,1)} %copy-done.3), channel_id=1, source_target_pairs={{0,1},{1,0},{2,3},{3,2},{4,5},{5,4},{6,7},{7,6},{8,9},{9,8},{10,11... | collective-permute-start | bytes 1376264 | tf_op jit(solution)/shard_map/ppermute | solution.py:344
  94.4 13.2 %collective-permute-start.28 = (bf16[32,7168]{1,0:T(8,128)(2,1)}, bf16[32,7168]{1,0:T(8,128)(2,1)S(1)}, u32[]{:S(2)}, u32[]{:S(2)}) collective-permute-start(bf16[32,7168]{1,0:T(8,128)(2,1)} %copy-done.31), channel_id=1, source_target_pairs={{0,1},{1,0},{2,3},{3,2},{4,5},{5,4},{6,7},{7,6},{8,9},{9,8},{10,11... | collective-permute-start | bytes 1376264 | tf_op jit(solution)/shard_map/ppermute | solution.py:344
  94.8 12.8 %collective-permute-start.29 = (bf16[32,7168]{1,0:T(8,128)(2,1)}, bf16[32,7168]{1,0:T(8,128)(2,1)S(1)}, u32[]{:S(2)}, u32[]{:S(2)}) collective-permute-start(bf16[32,7168]{1,0:T(8,128)(2,1)} %copy-done.32), channel_id=1, source_target_pairs={{0,1},{1,0},{2,3},{3,2},{4,5},{5,4},{6,7},{7,6},{8,9},{9,8},{10,11... | collective-permute-start | bytes 1376264 | tf_op jit(solution)/shard_map/ppermute | solution.py:344
  95.0 12.7 %collective-permute-start.30 = (bf16[32,7168]{1,0:T(8,128)(2,1)}, bf16[32,7168]{1,0:T(8,128)(2,1)S(1)}, u32[]{:S(2)}, u32[]{:S(2)}) collective-permute-start(bf16[32,7168]{1,0:T(8,128)(2,1)} %refs_24_), channel_id=1, source_target_pairs={{0,1},{1,0},{2,3},{3,2},{4,5},{5,4},{6,7},{7,6},{8,9},{9,8},{10,11... | collective-permute-start | bytes 1376264 | tf_op jit(solution)/shard_map/ppermute | solution.py:344
  95.3 12.4 %collective-permute-start.31 = (bf16[32,7168]{1,0:T(8,128)(2,1)}, bf16[32,7168]{1,0:T(8,128)(2,1)S(1)}, u32[]{:S(2)}, u32[]{:S(2)}) collective-permute-start(bf16[32,7168]{1,0:T(8,128)(2,1)} %refs_25_), channel_id=1, source_target_pairs={{0,1},{1,0},{2,3},{3,2},{4,5},{5,4},{6,7},{7,6},{8,9},{9,8},{10,11... | collective-permute-start | bytes 1376264 | tf_op jit(solution)/shard_map/ppermute | solution.py:344
  95.5 14.0 %copy-start.4 = (bf16[32,7168]{1,0:T(8,128)(2,1)S(1)}, bf16[32,7168]{1,0:T(8,128)(2,1)}, u32[]{:S(2)}) copy-start(bf16[32,7168]{1,0:T(8,128)(2,1)} %copy-done.3) | copy-start | bytes 1376260
  95.6 14.0 %copy-start.6 = (bf16[32,7168]{1,0:T(8,128)(2,1)S(1)}, bf16[32,7168]{1,0:T(8,128)(2,1)}, u32[]{:S(2)}) copy-start(bf16[32,7168]{1,0:T(8,128)(2,1)} %copy-done.5) | copy-start | bytes 1376260
  95.6 14.0 %copy-start.8 = (bf16[32,7168]{1,0:T(8,128)(2,1)S(1)}, bf16[32,7168]{1,0:T(8,128)(2,1)}, u32[]{:S(2)}) copy-start(bf16[32,7168]{1,0:T(8,128)(2,1)} %copy-done.7) | copy-start | bytes 1376260
  95.6 14.0 %copy-start.10 = (bf16[32,7168]{1,0:T(8,128)(2,1)S(1)}, bf16[32,7168]{1,0:T(8,128)(2,1)}, u32[]{:S(2)}) copy-start(bf16[32,7168]{1,0:T(8,128)(2,1)} %copy-done.9) | copy-start | bytes 1376260
  107.2 38.9 %collective-permute-start.16 = (bf16[64,7168]{1,0:T(8,128)(2,1)S(1)}, bf16[64,7168]{1,0:T(8,128)(2,1)S(1)}, u32[]{:S(2)}, u32[]{:S(2)}) collective-permute-start(bf16[64,7168]{1,0:T(8,128)(2,1)S(1)} %get-tuple-element.100), channel_id=1, source_target_pairs={{0,1},{1,0},{2,3},{3,2},{4,5},{5,4},{6,7},{7,6},{8,9},{9,8},{10,11... | collective-permute-start | bytes 2752520 | tf_op jit(solution)/shard_map/ppermute | solution.py:346
  145.0 2.7 %collective-permute-start.35 = (bf16[64,7168]{1,0:T(8,128)(2,1)}, bf16[64,7168]{1,0:T(8,128)(2,1)S(1)}, u32[]{:S(2)}, u32[]{:S(2)}) collective-permute-start(bf16[64,7168]{1,0:T(8,128)(2,1)} %get-tuple-element.122), channel_id=1, source_target_pairs={{0,1},{1,0},{2,3},{3,2},{4,5},{5,4},{6,7},{7,6},{8,9},{9,8},{10,11... | collective-permute-start | bytes 2752520 | tf_op jit(solution)/shard_map/ppermute | solution.py:346
  145.3 5.2 %collective-permute-start.34 = (bf16[128,7168]{1,0:T(8,128)(2,1)}, bf16[128,7168]{1,0:T(8,128)(2,1)S(1)}, u32[]{:S(2)}, u32[]{:S(2)}) collective-permute-start(bf16[128,7168]{1,0:T(8,128)(2,1)} %get-tuple-element.120), channel_id=1, source_target_pairs={{0,1},{1,0},{2,3},{3,2},{4,5},{5,4},{6,7},{7,6},{8,9},{9,8},{10,11... | collective-permute-start | bytes 5505032 | tf_op jit(solution)/shard_map/ppermute | solution.py:346
  145.6 7.4 %collective-permute-start.33 = (bf16[128,7168]{1,0:T(8,128)(2,1)}, bf16[128,7168]{1,0:T(8,128)(2,1)S(1)}, u32[]{:S(2)}, u32[]{:S(2)}) collective-permute-start(bf16[128,7168]{1,0:T(8,128)(2,1)} %get-tuple-element.118), channel_id=1, source_target_pairs={{0,1},{1,0},{2,3},{3,2},{4,5},{5,4},{6,7},{7,6},{8,9},{9,8},{10,11... | collective-permute-start | bytes 5505032 | tf_op jit(solution)/shard_map/ppermute | solution.py:346
  145.8 9.9 %collective-permute-start.32 = (bf16[128,7168]{1,0:T(8,128)(2,1)}, bf16[128,7168]{1,0:T(8,128)(2,1)S(1)}, u32[]{:S(2)}, u32[]{:S(2)}) collective-permute-start(bf16[128,7168]{1,0:T(8,128)(2,1)} %get-tuple-element.116), channel_id=1, source_target_pairs={{0,1},{1,0},{2,3},{3,2},{4,5},{5,4},{6,7},{7,6},{8,9},{9,8},{10,11... | collective-permute-start | bytes 5505032 | tf_op jit(solution)/shard_map/ppermute | solution.py:346
  147.2 13.9 %collective-permute-start.17 = (bf16[32,7168]{1,0:T(8,128)(2,1)S(1)}, bf16[32,7168]{1,0:T(8,128)(2,1)}, u32[]{:S(2)}, u32[]{:S(2)}) collective-permute-start(bf16[32,7168]{1,0:T(8,128)(2,1)S(1)} %get-tuple-element.197), channel_id=1, source_target_pairs={{0,4},{1,5},{4,8},{5,9},{8,12},{9,13},{12,14},{13,15},{14,10},{15,... | collective-permute-start | bytes 1376264 | tf_op jit(solution)/shard_map/ppermute | solution.py:385
  147.8 14.3 %collective-permute-start.38 = (bf16[32,7168]{1,0:T(8,128)(2,1)}, bf16[32,7168]{1,0:T(8,128)(2,1)}, u32[]{:S(2)}, u32[]{:S(2)}) collective-permute-start(bf16[32,7168]{1,0:T(8,128)(2,1)} %get-tuple-element.198), channel_id=1, source_target_pairs={{4,0},{5,1},{8,4},{9,5},{12,8},{13,9},{14,12},{15,13},{10,14},{11,... | collective-permute-start | bytes 1376264 | tf_op jit(solution)/shard_map/ppermute | solution.py:385
  163.4 13.5 %collective-permute-start.43 = (bf16[32,7168]{1,0:T(8,128)(2,1)S(1)}, bf16[32,7168]{1,0:T(8,128)(2,1)S(1)}, u32[]{:S(2)}, u32[]{:S(2)}) collective-permute-start(bf16[32,7168]{1,0:T(8,128)(2,1)S(1)} %add_convert_fusion.5), channel_id=1, source_target_pairs={{4,0},{5,1},{8,4},{9,5},{12,8},{13,9},{14,12},{15,13},{10,14},{11,... | collective-permute-start | bytes 1376264 | tf_op jit(solution)/shard_map/ppermute | solution.py:385
  165.1 13.6 %collective-permute-start.44 = (bf16[32,7168]{1,0:T(8,128)(2,1)}, bf16[32,7168]{1,0:T(8,128)(2,1)S(1)}, u32[]{:S(2)}, u32[]{:S(2)}) collective-permute-start(bf16[32,7168]{1,0:T(8,128)(2,1)} %get-tuple-element.161), channel_id=1, source_target_pairs={{0,4},{1,5},{4,8},{5,9},{8,12},{9,13},{12,14},{13,15},{14,10},{15,... | collective-permute-start | bytes 1376264 | tf_op jit(solution)/shard_map/ppermute | solution.py:385
  166.7 20.0 %collective-permute-start.36 = (bf16[32,7168]{1,0:T(8,128)(2,1)}, bf16[32,7168]{1,0:T(8,128)(2,1)S(1)}, u32[]{:S(2)}, u32[]{:S(2)}) collective-permute-start(bf16[32,7168]{1,0:T(8,128)(2,1)} %get-tuple-element.127), channel_id=1, source_target_pairs={{4,0},{5,1},{8,4},{9,5},{12,8},{13,9},{14,12},{15,13},{10,14},{11,... | collective-permute-start | bytes 1376264 | tf_op jit(solution)/shard_map/ppermute | solution.py:385
  168.5 20.1 %collective-permute-start.37 = (bf16[32,7168]{1,0:T(8,128)(2,1)S(1)}, bf16[32,7168]{1,0:T(8,128)(2,1)S(1)}, u32[]{:S(2)}, u32[]{:S(2)}) collective-permute-start(bf16[32,7168]{1,0:T(8,128)(2,1)S(1)} %add_convert_fusion.11), channel_id=1, source_target_pairs={{0,4},{1,5},{4,8},{5,9},{8,12},{9,13},{12,14},{13,15},{14,10},{15,... | collective-permute-start | bytes 1376264 | tf_op jit(solution)/shard_map/ppermute | solution.py:385
  174.6 14.0 %copy-start.23 = (bf16[32,7168]{1,0:T(8,128)(2,1)S(1)}, bf16[32,7168]{1,0:T(8,128)(2,1)}, u32[]{:S(2)}) copy-start(bf16[32,7168]{1,0:T(8,128)(2,1)} %get-tuple-element.145) | copy-start | bytes 1376260
  174.6 14.1 %copy-start.22 = (bf16[32,7168]{1,0:T(8,128)(2,1)S(1)}, bf16[32,7168]{1,0:T(8,128)(2,1)}, u32[]{:S(2)}) copy-start(bf16[32,7168]{1,0:T(8,128)(2,1)} %get-tuple-element.143) | copy-start | bytes 1376260
  178.9 19.5 %copy-start.21 = (bf16[32,7168]{1,0:T(8,128)(2,1)S(1)}, bf16[32,7168]{1,0:T(8,128)(2,1)}, u32[]{:S(2)}) copy-start(bf16[32,7168]{1,0:T(8,128)(2,1)} %get-tuple-element.171) | copy-start | bytes 1376260
  179.0 19.5 %copy-start.20 = (bf16[32,7168]{1,0:T(8,128)(2,1)S(1)}, bf16[32,7168]{1,0:T(8,128)(2,1)}, u32[]{:S(2)}) copy-start(bf16[32,7168]{1,0:T(8,128)(2,1)} %get-tuple-element.169) | copy-start | bytes 1376260
  179.0 17.5 %collective-permute-start.45 = (bf16[32,7168]{1,0:T(8,128)(2,1)S(1)}, bf16[32,7168]{1,0:T(8,128)(2,1)S(1)}, u32[]{:S(2)}, u32[]{:S(2)}) collective-permute-start(bf16[32,7168]{1,0:T(8,128)(2,1)S(1)} %add_convert_fusion.4), channel_id=1, source_target_pairs={{4,0},{5,1},{8,4},{9,5},{12,8},{13,9},{14,12},{15,13},{10,14},{11,... | collective-permute-start | bytes 1376264 | tf_op jit(solution)/shard_map/ppermute | solution.py:385
  179.6 18.8 %collective-permute-start.46 = (bf16[32,7168]{1,0:T(8,128)(2,1)S(1)}, bf16[32,7168]{1,0:T(8,128)(2,1)S(1)}, u32[]{:S(2)}, u32[]{:S(2)}) collective-permute-start(bf16[32,7168]{1,0:T(8,128)(2,1)S(1)} %add_convert_fusion.3), channel_id=1, source_target_pairs={{0,4},{1,5},{4,8},{5,9},{8,12},{9,13},{12,14},{13,15},{14,10},{15,... | collective-permute-start | bytes 1376264 | tf_op jit(solution)/shard_map/ppermute | solution.py:385
  188.7 19.5 %copy-start.19 = (bf16[32,7168]{1,0:T(8,128)(2,1)S(1)}, bf16[32,7168]{1,0:T(8,128)(2,1)}, u32[]{:S(2)}) copy-start(bf16[32,7168]{1,0:T(8,128)(2,1)} %get-tuple-element.151) | copy-start | bytes 1376260
  188.8 19.5 %copy-start.18 = (bf16[32,7168]{1,0:T(8,128)(2,1)S(1)}, bf16[32,7168]{1,0:T(8,128)(2,1)}, u32[]{:S(2)}) copy-start(bf16[32,7168]{1,0:T(8,128)(2,1)} %get-tuple-element.149) | copy-start | bytes 1376260
  188.8 17.5 %collective-permute-start.39 = (bf16[32,7168]{1,0:T(8,128)(2,1)S(1)}, bf16[32,7168]{1,0:T(8,128)(2,1)S(1)}, u32[]{:S(2)}, u32[]{:S(2)}) collective-permute-start(bf16[32,7168]{1,0:T(8,128)(2,1)S(1)} %add_convert_fusion.10), channel_id=1, source_target_pairs={{4,0},{5,1},{8,4},{9,5},{12,8},{13,9},{14,12},{15,13},{10,14},{11,... | collective-permute-start | bytes 1376264 | tf_op jit(solution)/shard_map/ppermute | solution.py:385
  189.5 18.8 %collective-permute-start.40 = (bf16[32,7168]{1,0:T(8,128)(2,1)S(1)}, bf16[32,7168]{1,0:T(8,128)(2,1)S(1)}, u32[]{:S(2)}, u32[]{:S(2)}) collective-permute-start(bf16[32,7168]{1,0:T(8,128)(2,1)S(1)} %add_convert_fusion.9), channel_id=1, source_target_pairs={{0,4},{1,5},{4,8},{5,9},{8,12},{9,13},{12,14},{13,15},{14,10},{15,... | collective-permute-start | bytes 1376264 | tf_op jit(solution)/shard_map/ppermute | solution.py:385
  198.7 20.0 %collective-permute-start.47 = (bf16[32,7168]{1,0:T(8,128)(2,1)S(1)}, bf16[32,7168]{1,0:T(8,128)(2,1)S(1)}, u32[]{:S(2)}, u32[]{:S(2)}) collective-permute-start(bf16[32,7168]{1,0:T(8,128)(2,1)S(1)} %add_convert_fusion.2), channel_id=1, source_target_pairs={{4,0},{5,1},{8,4},{9,5},{12,8},{13,9},{14,12},{15,13},{10,14},{11,... | collective-permute-start | bytes 1376264 | tf_op jit(solution)/shard_map/ppermute | solution.py:385
  199.3 19.4 %collective-permute-start.48 = (bf16[32,7168]{1,0:T(8,128)(2,1)S(1)}, bf16[32,7168]{1,0:T(8,128)(2,1)S(1)}, u32[]{:S(2)}, u32[]{:S(2)}) collective-permute-start(bf16[32,7168]{1,0:T(8,128)(2,1)S(1)} %add_convert_fusion.1), channel_id=1, source_target_pairs={{0,4},{1,5},{4,8},{5,9},{8,12},{9,13},{12,14},{13,15},{14,10},{15,... | collective-permute-start | bytes 1376264 | tf_op jit(solution)/shard_map/ppermute | solution.py:385
  208.5 16.2 %collective-permute-start.41 = (bf16[32,7168]{1,0:T(8,128)(2,1)S(1)}, bf16[32,7168]{1,0:T(8,128)(2,1)S(1)}, u32[]{:S(2)}, u32[]{:S(2)}) collective-permute-start(bf16[32,7168]{1,0:T(8,128)(2,1)S(1)} %add_convert_fusion.8), channel_id=1, source_target_pairs={{4,0},{5,1},{8,4},{9,5},{12,8},{13,9},{14,12},{15,13},{10,14},{11,... | collective-permute-start | bytes 1376264 | tf_op jit(solution)/shard_map/ppermute | solution.py:385
  209.1 17.5 %collective-permute-start.42 = (bf16[32,7168]{1,0:T(8,128)(2,1)S(1)}, bf16[32,7168]{1,0:T(8,128)(2,1)S(1)}, u32[]{:S(2)}, u32[]{:S(2)}) collective-permute-start(bf16[32,7168]{1,0:T(8,128)(2,1)S(1)} %add_convert_fusion.7), channel_id=1, source_target_pairs={{0,4},{1,5},{4,8},{5,9},{8,12},{9,13},{12,14},{13,15},{14,10},{15,... | collective-permute-start | bytes 1376264 | tf_op jit(solution)/shard_map/ppermute | solution.py:385
  (25 other events, 115.1 us)

commit v7 on v6

--- a/solution.py
+++ b/solution.py
@@ -23,13 +23,14 @@
     x_refs = refs[:count]
     up_hbm, down_hbm = refs[count : count + 2]
     out_refs = refs[count + 2 : count + 2 + 2 * total]
-    rows_ref, up_ref, down_ref, part_ref, merged_ref, hidden_ref = refs[
-        count + 2 + 2 * total : count + 8 + 2 * total
+    rows_ref, up_ref, down_ref, part_ref, hidden_ref = refs[
+        count + 2 + 2 * total : count + 7 + 2 * total
     ]
-    x_sems, up_sems, down_sems, out_sems = refs[count + 8 + 2 * total :]
+    x_sems, up_sems, down_sems, out_sems = refs[count + 7 + 2 * total :]
     width = up_hbm.shape[0]
     half = down_hbm.shape[0]
     tiles = width // tile
+    piece = 256 if half % 256 == 0 else half
     x_copies = []
     at = 0
     for b, sizes in enumerate(blocks):
@@ -67,20 +68,33 @@
                 copy.start()
         for copy in x_copies[b]:
             copy.wait()
-        merged_ref[:rows] = jnp.zeros((rows, 2 * half), jnp.float32)
-
-        def up_step(k, _, b=b, slot=slot, rows=rows):
-            if b == 0:
+        if b == 0:
+            merged = None
+            for k in range(tiles):
                 up_copy(k).wait()
-            span = pl.ds(pl.multiple_of(k * tile, tile), tile)
-            merged_ref[:rows] += jnp.dot(
-                rows_ref[slot, :rows, span], up_ref[span, :], preferred_element_type=jnp.float32
-            )
-            return 0
-
-        lax.fori_loop(0, tiles, up_step, 0)
-        merged = merged_ref[:rows]
-        hidden_ref[:rows] = (jax.nn.silu(merged[:, :half]) * merged[:, half:]).astype(jnp.bfloat16)
+                span = slice(k * tile, (k + 1) * tile)
+                part = jnp.dot(
+                    rows_ref[0, :rows, span], up_ref[span, :], preferred_element_type=jnp.float32
+                )
+                merged = part if merged is None else merged + part
+            value = jax.nn.silu(merged[:, :half]) * merged[:, half:]
+            hidden_ref[:rows] = value.astype(jnp.bfloat16)
+        else:
+
+            def up_step(j, _, slot=slot, rows=rows):
+                at = pl.multiple_of(j * piece, piece)
+                here = rows_ref[slot, :rows]
+                gate = jnp.dot(
+                    here, up_ref[:, pl.ds(at, piece)], preferred_element_type=jnp.float32
+                )
+                up = jnp.dot(
+                    here, up_ref[:, pl.ds(half + at, piece)], preferred_element_type=jnp.float32
+                )
+                value = jax.nn.silu(gate) * up
+                hidden_ref[:rows, pl.ds(at, piece)] = value.astype(jnp.bfloat16)
+                return 0
+
+            lax.fori_loop(0, half // piece, up_step, 0)
         if b >= 2:
             for copy in out_copies[b - 2]:
                 copy.wait()
@@ -133,7 +147,6 @@
             pltpu.VMEM((width, both), jnp.bfloat16),
             pltpu.VMEM((half, width), jnp.bfloat16),
             pltpu.VMEM((2, max(counts), width), jnp.bfloat16),
-            pltpu.VMEM((max(counts), both), jnp.float32),
             pltpu.VMEM((max(counts), half), jnp.bfloat16),
             dma((len(chunks),)),
             dma((tiles,)),
@@ -317,14 +330,13 @@
     mine = {0: own}
     front = [lax.ppermute(c, AXIS, ahead) for c in own]
     rear = [lax.ppermute(c, AXIS, back) for c in own]
+    front[0], rear[0], shipped, small = lax.optimization_barrier(
+        (front[0], rear[0], shipped, small)
+    )
     mine[1] = front + rear
     for s in range(2, half):
         front = [lax.ppermute(c, AXIS, ahead) for c in front]
         rear = [lax.ppermute(c, AXIS, back) for c in rear]
-        if s == 2:
-            front[0], rear[0], shipped, small = lax.optimization_barrier(
-                (front[0], rear[0], shipped, small)
-            )
         mine[s] = front + rear
     at_shift = lax.dynamic_index_in_dim(jnp.asarray(neighbours), me, 0, keepdims=False)
     picked = at_shift[:, None] == jnp.arange(devices)[None, :]
@@ -340,9 +352,10 @@
     block_latents = lax.all_to_all(shipped, AXIS, split_axis=0, concat_axis=0, tiled=True)
 
     parts = {}
-    for steps in ([half], list(range(half - 1, -1, -1))):
-        both = [mine[s] + [lax.ppermute(c, AXIS, across) for c in mine[s]] for s in steps]
-        for s, (part, rest) in zip(steps, mlp(both, gate_up, down_proj)):
+    groups = [[half], [half - 1], list(range(half - 2, -1, -1))]
+    for group in groups:
+        both = [mine[s] + [lax.ppermute(c, AXIS, across) for c in mine[s]] for s in group]
+        for s, (part, rest) in zip(group, mlp(both, gate_up, down_proj)):
             parts[s] = (part, lax.ppermute(rest, AXIS, across))
 
     def contribution(s, k, flow):

time: 231 us -> 228 us (0.987)
  Pallas kernels: 60.1 us -> 72.2 us
  waiting for transfers between devices: 93.1 us -> 81.9 us
  local copies, waits for them, and re-layouts: 10.7 us -> 6.88 us
    ppermute x4, waiting for transfers between devices: 6 us -> 18.2 us  [per_device(): rear = [lax.ppermute(c, AXIS, back) for c in rear]]
    ppermute x2, waiting for transfers between devices: 8.18 us -> 0.01 us  [per_device(): rear = [lax.ppermute(c, AXIS, back) for c in own]]
    ppermute x2, waiting for transfers between devices: 8.06 us -> 0.01 us  [per_device(): front = [lax.ppermute(c, AXIS, ahead) for c in own]]
    ppermute x14, waiting for transfers between devices: 39.4 us -> 32.4 us  [per_device(): lax.ppermute(value, AXIS, course[way])]
    pallas_call x2 -> x3, Pallas kernels: 47 us -> 53.4 us  [mlp(): pl.pallas_call(functools.partial(mlp_kernel, sizes, tile), in_specs=[anyw...]
    pallas_call x2, Pallas kernels: 12.3 us -> 18.1 us  [attend(): pl.pallas_call(attend_kernel, grid_spec=pltpu.PrefetchScalarGridSpec(num_...]
    unnamed x76 -> x64, local copies, waits for them, and re-layouts: 9.41 us -> 5.6 us
    ppermute x4, starting transfers between devices: 3.03 us -> 5.78 us  [per_device(): front = [lax.ppermute(c, AXIS, ahead) for c in front]]
  transfers between devices with their start and end apart: 51 -> 51, of which waited for: 23 -> 21; matrix products, arithmetic and copies ran while one was open for 7% -> 8% of each run, Pallas kernels for 26% -> 32%
where the time goes in v7:
time: 228 us; the launch traced here: 226 us
  waiting for transfers between devices  81.9 us (36%)
  Pallas kernels  72.2 us (32%)
  starting transfers between devices  44.8 us (20%)
  other arithmetic  19.2 us (8%)
  local copies, waits for them, and re-layouts  6.88 us (3%)
    pallas_call x3, Pallas kernels, mlp(): pl.pallas_call(functools.partial(mlp_kernel, sizes, tile), in_specs=[anyw...  53.4 us
    ppermute x14, waiting for transfers between devices, per_device(): lax.ppermute(value, AXIS, course[way])  32.4 us
    ppermute x4, waiting for transfers between devices, per_device(): rear = [lax.ppermute(c, AXIS, back) for c in rear]  18.2 us
    pallas_call x2, Pallas kernels, attend(): pl.pallas_call(attend_kernel, grid_spec=pltpu.PrefetchScalarGridSpec(num_...  18.1 us
    ppermute x4, waiting for transfers between devices, per_device(): front = [lax.ppermute(c, AXIS, ahead) for c in front]  15.3 us
    ppermute x14, starting transfers between devices, per_device(): lax.ppermute(value, AXIS, course[way])  14.5 us
    convert_element_type x5, other arithmetic, contribution(): return (weight[:, None] * both).astype(jnp.bfloat16)  8.26 us
    all_to_all x1, waiting for transfers between devices, per_device(): small = lax.all_to_all(small, AXIS, split_axis=0, concat_axis=0, tiled=True)  7.48 us
  transfers between devices with their start and end apart: 51, of which 21 were waited for; matrix products, arithmetic and copies ran while one was open for 8% of the time, Pallas kernels for 32%

profile of v7, /device:TPU:20, one launch (start us, length us, event | category | flops | bytes accessed | tf_op | source)
XLA Modules:
  0.0 226.0 jit_solution(8677344031674000768)
XLA Ops:
  1.1 1.6 collective-permute-start.1
  2.7 1.6 collective-permute-start.3
  4.3 0.9 convert_reduce_fusion.2
  5.2 0.7 multiply_add_fusion
  6.1 0.8 select_reduce_fusion.1
  6.9 0.7 pad_add_fusion
  7.6 5.1 %all-to-all-start = ((s32[16,1,66]{2,1,0:T(1,128)}), s32[16,1,66]{2,1,0:T(1,128)S(1)}, u32[]{:S(2)}, u32[]{:S(2)}) async-start(s32[16,1,66]{2,1,0:T(1,128)} %bitcast.2), calls=%async_computation | async-start | bytes 16384 | tf_op jit(solution)/shard_map/all_to_all | solution.py:325
  13.3 1.3 copy-done.2
  14.6 0.7 ship.1
  15.4 1.5 copy-done.1
  16.8 7.5 %all-to-all-done = s32[16,1,66]{2,1,0:T(1,128)S(1)} async-done(((s32[16,1,66]{2,1,0:T(1,128)}), s32[16,1,66]{2,1,0:T(1,128)S(1)}, u32[]{:S(2)}, u32[]{:S(2)}) %all-to-all-start) | async-done | bytes 4256 | tf_op jit(solution)/shard_map/all_to_all | solution.py:325
  24.3 1.5 collective-permute-start.4
  25.8 0.6 collective-permute-start.7
  26.4 0.7 collective-permute-start.6
  27.0 1.4 collective-permute-start.5
  28.4 9.3 %collective-permute-done.4.refs_0_ = bf16[32,7168]{1,0:T(8,128)(2,1)S(1)} collective-permute-done((bf16[32,7168]{1,0:T(8,128)(2,1)S(1)}, bf16[32,7168]{1,0:T(8,128)(2,1)S(1)}, u32[]{:S(2)}, u32[]{:S(2)}) %collective-permute-start.4) | collective-permute-done | bytes 458784 | tf_op jit(solution)/shard_map/ppermute | solution.py:338
  37.8 1.5 collective-permute-start.8
  40.2 0.7 dynamic-slice_bitcast_fusion
  40.9 8.5 %collective-permute-done.6.refs_2_ = bf16[32,7168]{1,0:T(8,128)(2,1)} collective-permute-done((bf16[32,7168]{1,0:T(8,128)(2,1)}, bf16[32,7168]{1,0:T(8,128)(2,1)}, u32[]{:S(2)}, u32[]{:S(2)}) %collective-permute-start.6) | collective-permute-done | bytes 458784 | tf_op jit(solution)/shard_map/ppermute | solution.py:339
  50.0 1.5 collective-permute-start.9
  51.4 6.0 %collective-permute-done.8.refs_0_ = bf16[32,7168]{1,0:T(8,128)(2,1)S(1)} collective-permute-done((bf16[32,7168]{1,0:T(8,128)(2,1)S(1)}, bf16[32,7168]{1,0:T(8,128)(2,1)S(1)}, u32[]{:S(2)}, u32[]{:S(2)}) %collective-permute-start.8) | collective-permute-done | bytes 458784 | tf_op jit(solution)/shard_map/ppermute | solution.py:338
  57.4 1.5 collective-permute-start.12
  59.9 9.1 %collective-permute-done.10.refs_2_ = bf16[32,7168]{1,0:T(8,128)(2,1)S(1)} collective-permute-done((bf16[32,7168]{1,0:T(8,128)(2,1)}, bf16[32,7168]{1,0:T(8,128)(2,1)S(1)}, u32[]{:S(2)}, u32[]{:S(2)}) %collective-permute-start.10) | collective-permute-done | bytes 458784 | tf_op jit(solution)/shard_map/ppermute | solution.py:339
  69.0 7.1 %collective-permute-done.12.refs_0_ = bf16[32,7168]{1,0:T(8,128)(2,1)} collective-permute-done((bf16[32,7168]{1,0:T(8,128)(2,1)S(1)}, bf16[32,7168]{1,0:T(8,128)(2,1)}, u32[]{:S(2)}, u32[]{:S(2)}) %collective-permute-start.12) | collective-permute-done | bytes 458784 | tf_op jit(solution)/shard_map/ppermute | solution.py:350
  76.1 1.4 collective-permute-done.13.refs_1_
  77.5 0.8 copy-done.13
  78.7 0.8 copy-done.15
  81.6 5.2 %all-to-all-start.1 = ((bf16[32,64,576]{2,1,0:T(8,128)(2,1)}), bf16[32,64,576]{2,1,0:T(8,128)(2,1)S(1)}, u32[]{:S(2)}, u32[]{:S(2)}) async-start(bf16[32,64,576]{2,1,0:T(8,128)(2,1)} %copy-done.1), calls=%async_computation.1 | async-start | bytes 5242880 | tf_op jit(solution)/shard_map/all_to_all | solution.py:352
  88.2 11.1 %mlp.3 = (bf16[64,7168]{1,0:T(8,128)(2,1)S(1)}, bf16[64,7168]{1,0:T(8,128)(2,1)S(1)}) custom-call(bf16[32,7168]{1,0:T(8,128)(2,1)} %collective-permute-done.12.refs_0_, bf16[32,7168]{1,0:T(8,128)(2,1)} %collective-permute-done.13.refs_1_, bf16[32,7168]{1,0:T(8,128)(2,1)} %collective-permute-done.14.refs_2_, ...), custom_call_target="tpu_custom_call" | custom-call | flops 2818572288 | bytes 25690112 | tf_op jit(solution)/shard_map/mlp/pallas_call | solution.py:138
  101.3 28.9 %mlp.4 = (bf16[128,7168]{1,0:T(8,128)(2,1)}, bf16[128,7168]{1,0:T(8,128)(2,1)}, bf16[128,7168]{1,0:T(8,128)(2,1)}, bf16[128,7168]{1,0:T(8,128)(2,1)}, bf16[64,71...) custom-call(bf16[32,7168]{1,0:T(8,128)(2,1)S(1)} %copy-done.14, bf16[32,7168]{1,0:T(8,128)(2,1)S(1)} %copy-done.16, ...), custom_call_target="tpu_custom_call" | custom-call | flops 14092861440 | bytes 40370176 | tf_op jit(solution)/shard_map/mlp/pallas_call | solution.py:138
  130.6 13.4 %mlp.5 = (bf16[128,7168]{1,0:T(8,128)(2,1)S(1)}, bf16[128,7168]{1,0:T(8,128)(2,1)S(1)}) custom-call(bf16[32,7168]{1,0:T(8,128)(2,1)S(1)} %collective-permute-done.8.refs_0_, bf16[32,7168]{1,0:T(8,128)(2,1)S(1)} %copy-done.8, bf16[32,7168]{1,0:T(8,128)(2,1)S(1)} %copy-done.6, bf16[32,7168]{1,0:T(8,128)(2,1)S(1)} %copy-done.4, ...), custom_call_target="tpu_custom_call" | custom-call | flops 5637144576 | bytes 29360128 | tf_op jit(solution)/shard_map/mlp/pallas_call | solution.py:138
  144.8 2.3 %multiply_convert_fusion.15 = (bf16[32,7168]{1,0:T(8,128)(2,1)S(1)}, bf16[32,7168]{1,0:T(8,128)(2,1)}) fusion(bf16[64,7168]{1,0:T(8,128)(2,1)} %collective-permute-done.16, bf16[64,7168]{1,0:T(8,128)(2,1)S(1)} %get-tuple-element.99, f32[32]{0:T(128)S(1)} %get-tuple-element.216, f32[32]{0:T(128)S(1)} %get-tuple-element.202), kind=kLoop, calls=%fused_computation.28 | loop fusion | flops 2293760 | bytes 2752768 | tf_op jit(solution)/shard_map/convert_element_type | solution.py:369
  147.6 1.5 collective-permute-start.38
  149.1 1.0 multiply_convert_fusion.1
  150.2 1.7 multiply_convert_fusion.3
  152.2 1.7 multiply_convert_fusion.7
  154.2 1.6 multiply_convert_fusion.11
  155.9 4.1 %collective-permute-done.17 = bf16[32,7168]{1,0:T(8,128)(2,1)} collective-permute-done((bf16[32,7168]{1,0:T(8,128)(2,1)S(1)}, bf16[32,7168]{1,0:T(8,128)(2,1)}, u32[]{:S(2)}, u32[]{:S(2)}) %collective-permute-start.17) | collective-permute-done | bytes 458784 | tf_op jit(solution)/shard_map/ppermute | solution.py:398
  160.4 1.5 add_convert_fusion.5
  161.9 1.5 collective-permute-start.43
  164.0 1.3 add_convert_fusion.11
  165.3 1.5 collective-permute-start.36
  167.4 7.4 %attend.2 = bf16[16,64,512]{2,1,0:T(8,128)(2,1)S(1)} custom-call(s32[32]{0:T(128)S(1)} %select_reduce_fusion.3.order_ref, s32[17]{0:T(128)S(1)} %get-tuple-element.218.start_ref, s32[32]{0:T(128)S(1)} %get-tuple-element.219.length_ref, bf16[32,64,576]{2,1,0:T(8,128)(2,1)S(1)} %copy-done, bf16[32,1,576]{2,1,0:T(2,128)(2,1)S(1)} %copy.34.own_ref, ...), custom_call_target="tpu_custom_call" | custom-call | flops 150994944 | bytes 4587520 | tf_op jit(solution)/shard_map/attend/pallas_call | solution.py:233
  174.8 0.7 collective-permute-done.43
  175.5 1.7 collective-permute-done.44
  177.4 2.1 collective-permute-start.45
  179.5 5.8 %collective-permute-done.36 = bf16[32,7168]{1,0:T(8,128)(2,1)S(1)} collective-permute-done((bf16[32,7168]{1,0:T(8,128)(2,1)}, bf16[32,7168]{1,0:T(8,128)(2,1)S(1)}, u32[]{:S(2)}, u32[]{:S(2)}) %collective-permute-start.36) | collective-permute-done | bytes 458784 | tf_op jit(solution)/shard_map/ppermute | solution.py:398
  185.3 1.7 collective-permute-done.37
  187.2 1.3 collective-permute-start.39
  188.5 0.8 collective-permute-start.40
  189.3 5.8 %collective-permute-done.45 = bf16[32,7168]{1,0:T(8,128)(2,1)S(1)} collective-permute-done((bf16[32,7168]{1,0:T(8,128)(2,1)S(1)}, bf16[32,7168]{1,0:T(8,128)(2,1)S(1)}, u32[]{:S(2)}, u32[]{:S(2)}) %collective-permute-start.45) | collective-permute-done | bytes 458784 | tf_op jit(solution)/shard_map/ppermute | solution.py:398
  195.1 1.7 collective-permute-done.46
  197.1 1.3 collective-permute-start.47
  198.3 0.8 collective-permute-start.48
  199.1 5.8 %collective-permute-done.39 = bf16[32,7168]{1,0:T(8,128)(2,1)S(1)} collective-permute-done((bf16[32,7168]{1,0:T(8,128)(2,1)S(1)}, bf16[32,7168]{1,0:T(8,128)(2,1)S(1)}, u32[]{:S(2)}, u32[]{:S(2)}) %collective-permute-start.39) | collective-permute-done | bytes 458784 | tf_op jit(solution)/shard_map/ppermute | solution.py:398
  205.0 1.7 collective-permute-done.40
  206.9 1.3 collective-permute-start.41
  208.2 0.8 collective-permute-start.42
  209.0 10.7 %attend.3 = bf16[16,64,512]{2,1,0:T(8,128)(2,1)S(1)} custom-call(s32[32]{0:T(128)S(1)} %select_reduce_fusion.3.order_ref, s32[17]{0:T(128)S(1)} %get-tuple-element.217.start_ref, s32[32]{0:T(128)S(1)} %get-tuple-element.219.length_ref, bf16[32,64,576]{2,1,0:T(8,128)(2,1)S(1)} %copy-done, bf16[32,1,576]{2,1,0:T(2,128)(2,1)S(1)} %copy.34.own_ref, ...), custom_call_target="tpu_custom_call" | custom-call | flops 150994944 | bytes 4587520 | tf_op jit(solution)/shard_map/attend/pallas_call | solution.py:233
  219.6 1.5 pad_maximum_fusion
  221.2 1.6 collective-permute-done.41
  222.7 1.4 collective-permute-done.42
  224.1 0.9 add_convert_fusion
  225.1 0.9 add_convert_fusion.6
  (150 shorter events, 14.8 us)
Async XLA Ops:
  0.6 23.7 %collective-permute-start = (bf16[32,7168]{1,0:T(8,128)(2,1)}, bf16[32,7168]{1,0:T(8,128)(2,1)S(1)}, u32[]{:S(2)}, u32[]{:S(2)}) collective-permute-start(bf16[32,7168]{1,0:T(8,128)(2,1)} %refs_16_), channel_id=1, source_target_pairs={{0,4},{1,5},{4,8},{5,9},{8,12},{9,13},{12,14},{13,15},{14,10},{15,... | collective-permute-start | bytes 1376264 | tf_op jit(solution)/shard_map/ppermute | solution.py:331
  1.1 23.2 %collective-permute-start.1 = (bf16[32,7168]{1,0:T(8,128)(2,1)}, bf16[32,7168]{1,0:T(8,128)(2,1)}, u32[]{:S(2)}, u32[]{:S(2)}) collective-permute-start(bf16[32,7168]{1,0:T(8,128)(2,1)} %refs_16_), channel_id=1, source_target_pairs={{4,0},{5,1},{8,4},{9,5},{12,8},{13,9},{14,12},{15,13},{10,14},{11,... | collective-permute-start | bytes 1376264 | tf_op jit(solution)/shard_map/ppermute | solution.py:332
  2.7 23.1 %collective-permute-start.3 = (bf16[32,7168]{1,0:T(8,128)(2,1)}, bf16[32,7168]{1,0:T(8,128)(2,1)}, u32[]{:S(2)}, u32[]{:S(2)}) collective-permute-start(bf16[32,7168]{1,0:T(8,128)(2,1)} %refs_17_), channel_id=1, source_target_pairs={{4,0},{5,1},{8,4},{9,5},{12,8},{13,9},{14,12},{15,13},{10,14},{11,... | collective-permute-start | bytes 1376264 | tf_op jit(solution)/shard_map/ppermute | solution.py:332
  7.6 16.7 %all-to-all-start = ((s32[16,1,66]{2,1,0:T(1,128)}), s32[16,1,66]{2,1,0:T(1,128)S(1)}, u32[]{:S(2)}, u32[]{:S(2)}) async-start(s32[16,1,66]{2,1,0:T(1,128)} %bitcast.2), calls=%async_computation | async-start | bytes 16384 | tf_op jit(solution)/shard_map/all_to_all | solution.py:325
  12.7 14.3 %collective-permute-start.2 = (bf16[32,7168]{1,0:T(8,128)(2,1)}, bf16[32,7168]{1,0:T(8,128)(2,1)}, u32[]{:S(2)}, u32[]{:S(2)}) collective-permute-start(bf16[32,7168]{1,0:T(8,128)(2,1)} %refs_17_), channel_id=1, source_target_pairs={{0,4},{1,5},{4,8},{5,9},{8,12},{9,13},{12,14},{13,15},{14,10},{15,... | collective-permute-start | bytes 1376264 | tf_op jit(solution)/shard_map/ppermute | solution.py:331
  14.6 25.6 %copy-start.29 = (bf16[32,576]{1,0:T(8,128)(2,1)S(1)}, bf16[32,576]{1,0:T(8,128)(2,1)}, u32[]{:S(2)}) copy-start(bf16[32,576]{1,0:T(8,128)(2,1)} %param.24) | copy-start | bytes 110596
  24.3 13.5 %collective-permute-start.4 = (bf16[32,7168]{1,0:T(8,128)(2,1)S(1)}, bf16[32,7168]{1,0:T(8,128)(2,1)S(1)}, u32[]{:S(2)}, u32[]{:S(2)}) collective-permute-start(bf16[32,7168]{1,0:T(8,128)(2,1)S(1)} %collective-permute-done.refs_8_), channel_id=1, source_target_pairs={{0,4},{1,5},{4,8},{5,9},{8,12},{9,13},{12,14},{13,15},{14,10},{15,... | collective-permute-start | bytes 1376264 | tf_op jit(solution)/shard_map/ppermute | solution.py:338
  25.8 13.8 %collective-permute-start.7 = (bf16[32,7168]{1,0:T(8,128)(2,1)}, bf16[32,7168]{1,0:T(8,128)(2,1)}, u32[]{:S(2)}, u32[]{:S(2)}) collective-permute-start(bf16[32,7168]{1,0:T(8,128)(2,1)} %collective-permute-done.3.refs_11_), channel_id=1, source_target_pairs={{4,0},{5,1},{8,4},{9,5},{12,8},{13,9},{14,12},{15,13},{10,14},{11,... | collective-permute-start | bytes 1376264 | tf_op jit(solution)/shard_map/ppermute | solution.py:339
  26.4 23.0 %collective-permute-start.6 = (bf16[32,7168]{1,0:T(8,128)(2,1)}, bf16[32,7168]{1,0:T(8,128)(2,1)}, u32[]{:S(2)}, u32[]{:S(2)}) collective-permute-start(bf16[32,7168]{1,0:T(8,128)(2,1)} %collective-permute-done.1.refs_10_), channel_id=1, source_target_pairs={{4,0},{5,1},{8,4},{9,5},{12,8},{13,9},{14,12},{15,13},{10,14},{11,... | collective-permute-start | bytes 1376264 | tf_op jit(solution)/shard_map/ppermute | solution.py:339
  27.0 22.9 %collective-permute-start.5 = (bf16[32,7168]{1,0:T(8,128)(2,1)}, bf16[32,7168]{1,0:T(8,128)(2,1)S(1)}, u32[]{:S(2)}, u32[]{:S(2)}) collective-permute-start(bf16[32,7168]{1,0:T(8,128)(2,1)} %collective-permute-done.2.refs_9_), channel_id=1, source_target_pairs={{0,4},{1,5},{4,8},{5,9},{8,12},{9,13},{12,14},{13,15},{14,10},{15,... | collective-permute-start | bytes 1376264 | tf_op jit(solution)/shard_map/ppermute | solution.py:338
  37.8 19.7 %collective-permute-start.8 = (bf16[32,7168]{1,0:T(8,128)(2,1)S(1)}, bf16[32,7168]{1,0:T(8,128)(2,1)S(1)}, u32[]{:S(2)}, u32[]{:S(2)}) collective-permute-start(bf16[32,7168]{1,0:T(8,128)(2,1)S(1)} %collective-permute-done.4.refs_0_), channel_id=1, source_target_pairs={{0,4},{1,5},{4,8},{5,9},{8,12},{9,13},{12,14},{13,15},{14,10},{15,... | collective-permute-start | bytes 1376264 | tf_op jit(solution)/shard_map/ppermute | solution.py:338
  39.6 19.6 %collective-permute-start.11 = (bf16[32,7168]{1,0:T(8,128)(2,1)}, bf16[32,7168]{1,0:T(8,128)(2,1)S(1)}, u32[]{:S(2)}, u32[]{:S(2)}) collective-permute-start(bf16[32,7168]{1,0:T(8,128)(2,1)} %collective-permute-done.7.refs_3_), channel_id=1, source_target_pairs={{4,0},{5,1},{8,4},{9,5},{12,8},{13,9},{14,12},{15,13},{10,14},{11,... | collective-permute-start | bytes 1376264 | tf_op jit(solution)/shard_map/ppermute | solution.py:339
  49.4 19.6 %collective-permute-start.10 = (bf16[32,7168]{1,0:T(8,128)(2,1)}, bf16[32,7168]{1,0:T(8,128)(2,1)S(1)}, u32[]{:S(2)}, u32[]{:S(2)}) collective-permute-start(bf16[32,7168]{1,0:T(8,128)(2,1)} %collective-permute-done.6.refs_2_), channel_id=1, source_target_pairs={{4,0},{5,1},{8,4},{9,5},{12,8},{13,9},{14,12},{15,13},{10,14},{11,... | collective-permute-start | bytes 1376264 | tf_op jit(solution)/shard_map/ppermute | solution.py:339
  50.0 19.0 %collective-permute-start.9 = (bf16[32,7168]{1,0:T(8,128)(2,1)S(1)}, bf16[32,7168]{1,0:T(8,128)(2,1)S(1)}, u32[]{:S(2)}, u32[]{:S(2)}) collective-permute-start(bf16[32,7168]{1,0:T(8,128)(2,1)S(1)} %collective-permute-done.5.refs_1_), channel_id=1, source_target_pairs={{0,4},{1,5},{4,8},{5,9},{8,12},{9,13},{12,14},{13,15},{14,10},{15,... | collective-permute-start | bytes 1376264 | tf_op jit(solution)/shard_map/ppermute | solution.py:338
  57.4 18.6 %collective-permute-start.12 = (bf16[32,7168]{1,0:T(8,128)(2,1)S(1)}, bf16[32,7168]{1,0:T(8,128)(2,1)}, u32[]{:S(2)}, u32[]{:S(2)}) collective-permute-start(bf16[32,7168]{1,0:T(8,128)(2,1)S(1)} %collective-permute-done.8.refs_0_), channel_id=1, source_target_pairs={{0,4},{1,5},{4,8},{5,9},{8,12},{9,13},{12,14},{13,15},{14,10},{15,... | collective-permute-start | bytes 1376264 | tf_op jit(solution)/shard_map/ppermute | solution.py:350
  59.1 22.5 %copy-start.3 = (bf16[32,7168]{1,0:T(8,128)(2,1)}, bf16[32,7168]{1,0:T(8,128)(2,1)S(1)}, u32[]{:S(2)}) copy-start(bf16[32,7168]{1,0:T(8,128)(2,1)S(1)} %collective-permute-done.11.refs_3_) | copy-start | bytes 1376260
  59.1 18.3 %collective-permute-start.13 = (bf16[32,7168]{1,0:T(8,128)(2,1)S(1)}, bf16[32,7168]{1,0:T(8,128)(2,1)}, u32[]{:S(2)}, u32[]{:S(2)}) collective-permute-start(bf16[32,7168]{1,0:T(8,128)(2,1)S(1)} %collective-permute-done.11.refs_3_), channel_id=1, source_target_pairs={{4,0},{5,1},{8,4},{9,5},{12,8},{13,9},{14,12},{15,13},{10,14},{11,... | collective-permute-start | bytes 1376264 | tf_op jit(solution)/shard_map/ppermute | solution.py:350
  69.0 12.6 %copy-start.5 = (bf16[32,7168]{1,0:T(8,128)(2,1)}, bf16[32,7168]{1,0:T(8,128)(2,1)S(1)}, u32[]{:S(2)}) copy-start(bf16[32,7168]{1,0:T(8,128)(2,1)S(1)} %collective-permute-done.10.refs_2_) | copy-start | bytes 1376260
  69.0 12.6 %copy-start.7 = (bf16[32,7168]{1,0:T(8,128)(2,1)}, bf16[32,7168]{1,0:T(8,128)(2,1)S(1)}, u32[]{:S(2)}) copy-start(bf16[32,7168]{1,0:T(8,128)(2,1)S(1)} %collective-permute-done.9.refs_1_) | copy-start | bytes 1376260
  77.4 3.2 %collective-permute-start.18 = (bf16[32,7168]{1,0:T(8,128)(2,1)S(1)}, bf16[32,7168]{1,0:T(8,128)(2,1)}, u32[]{:S(2)}, u32[]{:S(2)}) collective-permute-start(bf16[32,7168]{1,0:T(8,128)(2,1)S(1)} %collective-permute-done.4.refs_0_), channel_id=1, source_target_pairs={{0,1},{1,0},{2,3},{3,2},{4,5},{5,4},{6,7},{7,6},{8,9},{9,8},{10,11... | collective-permute-start | bytes 1376264 | tf_op jit(solution)/shard_map/ppermute | solution.py:357
  78.2 2.8 %collective-permute-start.19 = (bf16[32,7168]{1,0:T(8,128)(2,1)S(1)}, bf16[32,7168]{1,0:T(8,128)(2,1)}, u32[]{:S(2)}, u32[]{:S(2)}) collective-permute-start(bf16[32,7168]{1,0:T(8,128)(2,1)S(1)} %collective-permute-done.5.refs_1_), channel_id=1, source_target_pairs={{0,1},{1,0},{2,3},{3,2},{4,5},{5,4},{6,7},{7,6},{8,9},{9,8},{10,11... | collective-permute-start | bytes 1376264 | tf_op jit(solution)/shard_map/ppermute | solution.py:357
  80.0 6.8 %collective-permute-start.20 = (bf16[32,7168]{1,0:T(8,128)(2,1)}, bf16[32,7168]{1,0:T(8,128)(2,1)}, u32[]{:S(2)}, u32[]{:S(2)}) collective-permute-start(bf16[32,7168]{1,0:T(8,128)(2,1)} %collective-permute-done.6.refs_2_), channel_id=1, source_target_pairs={{0,1},{1,0},{2,3},{3,2},{4,5},{5,4},{6,7},{7,6},{8,9},{9,8},{10,11... | collective-permute-start | bytes 1376264 | tf_op jit(solution)/shard_map/ppermute | solution.py:357
  80.0 7.0 %collective-permute-start.21 = (bf16[32,7168]{1,0:T(8,128)(2,1)}, bf16[32,7168]{1,0:T(8,128)(2,1)}, u32[]{:S(2)}, u32[]{:S(2)}) collective-permute-start(bf16[32,7168]{1,0:T(8,128)(2,1)} %collective-permute-done.7.refs_3_), channel_id=1, source_target_pairs={{0,1},{1,0},{2,3},{3,2},{4,5},{5,4},{6,7},{7,6},{8,9},{9,8},{10,11... | collective-permute-start | bytes 1376264 | tf_op jit(solution)/shard_map/ppermute | solution.py:357
  80.5 6.8 %collective-permute-start.22 = (bf16[32,7168]{1,0:T(8,128)(2,1)}, bf16[32,7168]{1,0:T(8,128)(2,1)}, u32[]{:S(2)}, u32[]{:S(2)}) collective-permute-start(bf16[32,7168]{1,0:T(8,128)(2,1)} %copy-done.11), channel_id=1, source_target_pairs={{0,1},{1,0},{2,3},{3,2},{4,5},{5,4},{6,7},{7,6},{8,9},{9,8},{10,11... | collective-permute-start | bytes 1376264 | tf_op jit(solution)/shard_map/ppermute | solution.py:357
  80.6 6.9 %collective-permute-start.14 = (bf16[32,7168]{1,0:T(8,128)(2,1)}, bf16[32,7168]{1,0:T(8,128)(2,1)}, u32[]{:S(2)}, u32[]{:S(2)}) collective-permute-start(bf16[32,7168]{1,0:T(8,128)(2,1)} %collective-permute-done.12.refs_0_), channel_id=1, source_target_pairs={{0,1},{1,0},{2,3},{3,2},{4,5},{5,4},{6,7},{7,6},{8,9},{9,8},{10,11... | collective-permute-start | bytes 1376264 | tf_op jit(solution)/shard_map/ppermute | solution.py:357
  81.0 6.8 %collective-permute-start.15 = (bf16[32,7168]{1,0:T(8,128)(2,1)}, bf16[32,7168]{1,0:T(8,128)(2,1)}, u32[]{:S(2)}, u32[]{:S(2)}) collective-permute-start(bf16[32,7168]{1,0:T(8,128)(2,1)} %collective-permute-done.13.refs_1_), channel_id=1, source_target_pairs={{0,1},{1,0},{2,3},{3,2},{4,5},{5,4},{6,7},{7,6},{8,9},{9,8},{10,11... | collective-permute-start | bytes 1376264 | tf_op jit(solution)/shard_map/ppermute | solution.py:357
  81.6 78.4 %all-to-all-start.1 = ((bf16[32,64,576]{2,1,0:T(8,128)(2,1)}), bf16[32,64,576]{2,1,0:T(8,128)(2,1)S(1)}, u32[]{:S(2)}, u32[]{:S(2)}) async-start(bf16[32,64,576]{2,1,0:T(8,128)(2,1)} %copy-done.1), calls=%async_computation.1 | async-start | bytes 5242880 | tf_op jit(solution)/shard_map/all_to_all | solution.py:352
  86.8 12.5 %collective-permute-start.23 = (bf16[32,7168]{1,0:T(8,128)(2,1)}, bf16[32,7168]{1,0:T(8,128)(2,1)S(1)}, u32[]{:S(2)}, u32[]{:S(2)}) collective-permute-start(bf16[32,7168]{1,0:T(8,128)(2,1)} %collective-permute-done.2.refs_9_), channel_id=1, source_target_pairs={{0,1},{1,0},{2,3},{3,2},{4,5},{5,4},{6,7},{7,6},{8,9},{9,8},{10,11... | collective-permute-start | bytes 1376264 | tf_op jit(solution)/shard_map/ppermute | solution.py:357
  87.0 12.7 %collective-permute-start.24 = (bf16[32,7168]{1,0:T(8,128)(2,1)}, bf16[32,7168]{1,0:T(8,128)(2,1)S(1)}, u32[]{:S(2)}, u32[]{:S(2)}) collective-permute-start(bf16[32,7168]{1,0:T(8,128)(2,1)} %collective-permute-done.1.refs_10_), channel_id=1, source_target_pairs={{0,1},{1,0},{2,3},{3,2},{4,5},{5,4},{6,7},{7,6},{8,9},{9,8},{10,11... | collective-permute-start | bytes 1376264 | tf_op jit(solution)/shard_map/ppermute | solution.py:357
  87.4 12.5 %collective-permute-start.25 = (bf16[32,7168]{1,0:T(8,128)(2,1)}, bf16[32,7168]{1,0:T(8,128)(2,1)S(1)}, u32[]{:S(2)}, u32[]{:S(2)}) collective-permute-start(bf16[32,7168]{1,0:T(8,128)(2,1)} %collective-permute-done.3.refs_11_), channel_id=1, source_target_pairs={{0,1},{1,0},{2,3},{3,2},{4,5},{5,4},{6,7},{7,6},{8,9},{9,8},{10,11... | collective-permute-start | bytes 1376264 | tf_op jit(solution)/shard_map/ppermute | solution.py:357
  87.5 12.8 %collective-permute-start.26 = (bf16[32,7168]{1,0:T(8,128)(2,1)}, bf16[32,7168]{1,0:T(8,128)(2,1)S(1)}, u32[]{:S(2)}, u32[]{:S(2)}) collective-permute-start(bf16[32,7168]{1,0:T(8,128)(2,1)} %refs_16_), channel_id=1, source_target_pairs={{0,1},{1,0},{2,3},{3,2},{4,5},{5,4},{6,7},{7,6},{8,9},{9,8},{10,11... | collective-permute-start | bytes 1376264 | tf_op jit(solution)/shard_map/ppermute | solution.py:357
  87.9 12.6 %collective-permute-start.27 = (bf16[32,7168]{1,0:T(8,128)(2,1)}, bf16[32,7168]{1,0:T(8,128)(2,1)S(1)}, u32[]{:S(2)}, u32[]{:S(2)}) collective-permute-start(bf16[32,7168]{1,0:T(8,128)(2,1)} %refs_17_), channel_id=1, source_target_pairs={{0,1},{1,0},{2,3},{3,2},{4,5},{5,4},{6,7},{7,6},{8,9},{9,8},{10,11... | collective-permute-start | bytes 1376264 | tf_op jit(solution)/shard_map/ppermute | solution.py:357
  88.1 13.1 %copy-start.9 = (bf16[32,7168]{1,0:T(8,128)(2,1)S(1)}, bf16[32,7168]{1,0:T(8,128)(2,1)}, u32[]{:S(2)}) copy-start(bf16[32,7168]{1,0:T(8,128)(2,1)} %refs_16_) | copy-start | bytes 1376260
  88.1 13.1 %copy-start.10 = (bf16[32,7168]{1,0:T(8,128)(2,1)S(1)}, bf16[32,7168]{1,0:T(8,128)(2,1)}, u32[]{:S(2)}) copy-start(bf16[32,7168]{1,0:T(8,128)(2,1)} %refs_17_) | copy-start | bytes 1376260
  88.2 13.1 %copy-start.12 = (bf16[32,7168]{1,0:T(8,128)(2,1)S(1)}, bf16[32,7168]{1,0:T(8,128)(2,1)}, u32[]{:S(2)}) copy-start(bf16[32,7168]{1,0:T(8,128)(2,1)} %copy-done.11) | copy-start | bytes 1376260
  88.2 13.1 %copy-start.14 = (bf16[32,7168]{1,0:T(8,128)(2,1)S(1)}, bf16[32,7168]{1,0:T(8,128)(2,1)}, u32[]{:S(2)}) copy-start(bf16[32,7168]{1,0:T(8,128)(2,1)} %copy-done.13) | copy-start | bytes 1376260
  88.2 13.1 %copy-start.16 = (bf16[32,7168]{1,0:T(8,128)(2,1)S(1)}, bf16[32,7168]{1,0:T(8,128)(2,1)}, u32[]{:S(2)}) copy-start(bf16[32,7168]{1,0:T(8,128)(2,1)} %copy-done.15) | copy-start | bytes 1376260
  99.3 30.8 %collective-permute-start.30 = (bf16[32,7168]{1,0:T(8,128)(2,1)S(1)}, bf16[32,7168]{1,0:T(8,128)(2,1)S(1)}, u32[]{:S(2)}, u32[]{:S(2)}) collective-permute-start(bf16[32,7168]{1,0:T(8,128)(2,1)S(1)} %collective-permute-done.8.refs_0_), channel_id=1, source_target_pairs={{0,1},{1,0},{2,3},{3,2},{4,5},{5,4},{6,7},{7,6},{8,9},{9,8},{10,11... | collective-permute-start | bytes 1376264 | tf_op jit(solution)/shard_map/ppermute | solution.py:357
  99.8 30.9 %collective-permute-start.31 = (bf16[32,7168]{1,0:T(8,128)(2,1)S(1)}, bf16[32,7168]{1,0:T(8,128)(2,1)S(1)}, u32[]{:S(2)}, u32[]{:S(2)}) collective-permute-start(bf16[32,7168]{1,0:T(8,128)(2,1)S(1)} %copy-done.8), channel_id=1, source_target_pairs={{0,1},{1,0},{2,3},{3,2},{4,5},{5,4},{6,7},{7,6},{8,9},{9,8},{10,11... | collective-permute-start | bytes 1376264 | tf_op jit(solution)/shard_map/ppermute | solution.py:357
  99.9 30.7 %collective-permute-start.32 = (bf16[32,7168]{1,0:T(8,128)(2,1)S(1)}, bf16[32,7168]{1,0:T(8,128)(2,1)S(1)}, u32[]{:S(2)}, u32[]{:S(2)}) collective-permute-start(bf16[32,7168]{1,0:T(8,128)(2,1)S(1)} %copy-done.6), channel_id=1, source_target_pairs={{0,1},{1,0},{2,3},{3,2},{4,5},{5,4},{6,7},{7,6},{8,9},{9,8},{10,11... | collective-permute-start | bytes 1376264 | tf_op jit(solution)/shard_map/ppermute | solution.py:357
  100.3 30.3 %collective-permute-start.33 = (bf16[32,7168]{1,0:T(8,128)(2,1)S(1)}, bf16[32,7168]{1,0:T(8,128)(2,1)S(1)}, u32[]{:S(2)}, u32[]{:S(2)}) collective-permute-start(bf16[32,7168]{1,0:T(8,128)(2,1)S(1)} %copy-done.4), channel_id=1, source_target_pairs={{0,1},{1,0},{2,3},{3,2},{4,5},{5,4},{6,7},{7,6},{8,9},{9,8},{10,11... | collective-permute-start | bytes 1376264 | tf_op jit(solution)/shard_map/ppermute | solution.py:357
  100.5 44.3 %collective-permute-start.16 = (bf16[64,7168]{1,0:T(8,128)(2,1)S(1)}, bf16[64,7168]{1,0:T(8,128)(2,1)}, u32[]{:S(2)}, u32[]{:S(2)}) collective-permute-start(bf16[64,7168]{1,0:T(8,128)(2,1)S(1)} %get-tuple-element.100), channel_id=1, source_target_pairs={{0,1},{1,0},{2,3},{3,2},{4,5},{5,4},{6,7},{7,6},{8,9},{9,8},{10,11... | collective-permute-start | bytes 2752520 | tf_op jit(solution)/shard_map/ppermute | solution.py:359
  130.2 17.5 %collective-permute-start.35 = (bf16[64,7168]{1,0:T(8,128)(2,1)}, bf16[64,7168]{1,0:T(8,128)(2,1)S(1)}, u32[]{:S(2)}, u32[]{:S(2)}) collective-permute-start(bf16[64,7168]{1,0:T(8,128)(2,1)} %get-tuple-element.122), channel_id=1, source_target_pairs={{0,1},{1,0},{2,3},{3,2},{4,5},{5,4},{6,7},{7,6},{8,9},{9,8},{10,11... | collective-permute-start | bytes 2752520 | tf_op jit(solution)/shard_map/ppermute | solution.py:359
  144.1 6.1 %collective-permute-start.34 = (bf16[128,7168]{1,0:T(8,128)(2,1)S(1)}, bf16[128,7168]{1,0:T(8,128)(2,1)S(1)}, u32[]{:S(2)}, u32[]{:S(2)}) collective-permute-start(bf16[128,7168]{1,0:T(8,128)(2,1)S(1)} %get-tuple-element.120), channel_id=1, source_target_pairs={{0,1},{1,0},{2,3},{3,2},{4,5},{5,4},{6,7},{7,6},{8,9},{9,8},{10,11... | collective-permute-start | bytes 5505032 | tf_op jit(solution)/shard_map/ppermute | solution.py:359
  144.3 7.6 %collective-permute-start.29 = (bf16[128,7168]{1,0:T(8,128)(2,1)}, bf16[128,7168]{1,0:T(8,128)(2,1)S(1)}, u32[]{:S(2)}, u32[]{:S(2)}) collective-permute-start(bf16[128,7168]{1,0:T(8,128)(2,1)} %get-tuple-element.114), channel_id=1, source_target_pairs={{0,1},{1,0},{2,3},{3,2},{4,5},{5,4},{6,7},{7,6},{8,9},{9,8},{10,11... | collective-permute-start | bytes 5505032 | tf_op jit(solution)/shard_map/ppermute | solution.py:359
  144.6 9.2 %collective-permute-start.28 = (bf16[128,7168]{1,0:T(8,128)(2,1)}, bf16[128,7168]{1,0:T(8,128)(2,1)S(1)}, u32[]{:S(2)}, u32[]{:S(2)}) collective-permute-start(bf16[128,7168]{1,0:T(8,128)(2,1)} %get-tuple-element.112), channel_id=1, source_target_pairs={{0,1},{1,0},{2,3},{3,2},{4,5},{5,4},{6,7},{7,6},{8,9},{9,8},{10,11... | collective-permute-start | bytes 5505032 | tf_op jit(solution)/shard_map/ppermute | solution.py:359
  147.1 12.9 %collective-permute-start.17 = (bf16[32,7168]{1,0:T(8,128)(2,1)S(1)}, bf16[32,7168]{1,0:T(8,128)(2,1)}, u32[]{:S(2)}, u32[]{:S(2)}) collective-permute-start(bf16[32,7168]{1,0:T(8,128)(2,1)S(1)} %get-tuple-element.197), channel_id=1, source_target_pairs={{0,4},{1,5},{4,8},{5,9},{8,12},{9,13},{12,14},{13,15},{14,10},{15,... | collective-permute-start | bytes 1376264 | tf_op jit(solution)/shard_map/ppermute | solution.py:398
  147.6 12.8 %collective-permute-start.38 = (bf16[32,7168]{1,0:T(8,128)(2,1)}, bf16[32,7168]{1,0:T(8,128)(2,1)}, u32[]{:S(2)}, u32[]{:S(2)}) collective-permute-start(bf16[32,7168]{1,0:T(8,128)(2,1)} %get-tuple-element.198), channel_id=1, source_target_pairs={{4,0},{5,1},{8,4},{9,5},{12,8},{13,9},{14,12},{15,13},{10,14},{11,... | collective-permute-start | bytes 1376264 | tf_op jit(solution)/shard_map/ppermute | solution.py:398
  161.9 13.5 %collective-permute-start.43 = (bf16[32,7168]{1,0:T(8,128)(2,1)S(1)}, bf16[32,7168]{1,0:T(8,128)(2,1)S(1)}, u32[]{:S(2)}, u32[]{:S(2)}) collective-permute-start(bf16[32,7168]{1,0:T(8,128)(2,1)S(1)} %add_convert_fusion.5), channel_id=1, source_target_pairs={{4,0},{5,1},{8,4},{9,5},{12,8},{13,9},{14,12},{15,13},{10,14},{11,... | collective-permute-start | bytes 1376264 | tf_op jit(solution)/shard_map/ppermute | solution.py:398
  163.5 13.7 %collective-permute-start.44 = (bf16[32,7168]{1,0:T(8,128)(2,1)}, bf16[32,7168]{1,0:T(8,128)(2,1)S(1)}, u32[]{:S(2)}, u32[]{:S(2)}) collective-permute-start(bf16[32,7168]{1,0:T(8,128)(2,1)} %get-tuple-element.161), channel_id=1, source_target_pairs={{0,4},{1,5},{4,8},{5,9},{8,12},{9,13},{12,14},{13,15},{14,10},{15,... | collective-permute-start | bytes 1376264 | tf_op jit(solution)/shard_map/ppermute | solution.py:398
  165.3 20.0 %collective-permute-start.36 = (bf16[32,7168]{1,0:T(8,128)(2,1)}, bf16[32,7168]{1,0:T(8,128)(2,1)S(1)}, u32[]{:S(2)}, u32[]{:S(2)}) collective-permute-start(bf16[32,7168]{1,0:T(8,128)(2,1)} %get-tuple-element.127), channel_id=1, source_target_pairs={{4,0},{5,1},{8,4},{9,5},{12,8},{13,9},{14,12},{15,13},{10,14},{11,... | collective-permute-start | bytes 1376264 | tf_op jit(solution)/shard_map/ppermute | solution.py:398
  166.8 20.2 %collective-permute-start.37 = (bf16[32,7168]{1,0:T(8,128)(2,1)S(1)}, bf16[32,7168]{1,0:T(8,128)(2,1)S(1)}, u32[]{:S(2)}, u32[]{:S(2)}) collective-permute-start(bf16[32,7168]{1,0:T(8,128)(2,1)S(1)} %add_convert_fusion.11), channel_id=1, source_target_pairs={{0,4},{1,5},{4,8},{5,9},{8,12},{9,13},{12,14},{13,15},{14,10},{15,... | collective-permute-start | bytes 1376264 | tf_op jit(solution)/shard_map/ppermute | solution.py:398
  177.3 19.5 %copy-start.21 = (bf16[32,7168]{1,0:T(8,128)(2,1)S(1)}, bf16[32,7168]{1,0:T(8,128)(2,1)}, u32[]{:S(2)}) copy-start(bf16[32,7168]{1,0:T(8,128)(2,1)} %get-tuple-element.171) | copy-start | bytes 1376260
  177.4 19.5 %copy-start.20 = (bf16[32,7168]{1,0:T(8,128)(2,1)S(1)}, bf16[32,7168]{1,0:T(8,128)(2,1)}, u32[]{:S(2)}) copy-start(bf16[32,7168]{1,0:T(8,128)(2,1)} %get-tuple-element.169) | copy-start | bytes 1376260
  177.4 17.7 %collective-permute-start.45 = (bf16[32,7168]{1,0:T(8,128)(2,1)S(1)}, bf16[32,7168]{1,0:T(8,128)(2,1)S(1)}, u32[]{:S(2)}, u32[]{:S(2)}) collective-permute-start(bf16[32,7168]{1,0:T(8,128)(2,1)S(1)} %add_convert_fusion.4), channel_id=1, source_target_pairs={{4,0},{5,1},{8,4},{9,5},{12,8},{13,9},{14,12},{15,13},{10,14},{11,... | collective-permute-start | bytes 1376264 | tf_op jit(solution)/shard_map/ppermute | solution.py:398
  179.5 17.3 %collective-permute-start.46 = (bf16[32,7168]{1,0:T(8,128)(2,1)S(1)}, bf16[32,7168]{1,0:T(8,128)(2,1)S(1)}, u32[]{:S(2)}, u32[]{:S(2)}) collective-permute-start(bf16[32,7168]{1,0:T(8,128)(2,1)S(1)} %add_convert_fusion.3), channel_id=1, source_target_pairs={{0,4},{1,5},{4,8},{5,9},{8,12},{9,13},{12,14},{13,15},{14,10},{15,... | collective-permute-start | bytes 1376264 | tf_op jit(solution)/shard_map/ppermute | solution.py:398
  187.1 19.5 %copy-start.19 = (bf16[32,7168]{1,0:T(8,128)(2,1)S(1)}, bf16[32,7168]{1,0:T(8,128)(2,1)}, u32[]{:S(2)}) copy-start(bf16[32,7168]{1,0:T(8,128)(2,1)} %get-tuple-element.151) | copy-start | bytes 1376260
  187.2 19.5 %copy-start.18 = (bf16[32,7168]{1,0:T(8,128)(2,1)S(1)}, bf16[32,7168]{1,0:T(8,128)(2,1)}, u32[]{:S(2)}) copy-start(bf16[32,7168]{1,0:T(8,128)(2,1)} %get-tuple-element.149) | copy-start | bytes 1376260
  187.2 17.7 %collective-permute-start.39 = (bf16[32,7168]{1,0:T(8,128)(2,1)S(1)}, bf16[32,7168]{1,0:T(8,128)(2,1)S(1)}, u32[]{:S(2)}, u32[]{:S(2)}) collective-permute-start(bf16[32,7168]{1,0:T(8,128)(2,1)S(1)} %add_convert_fusion.10), channel_id=1, source_target_pairs={{4,0},{5,1},{8,4},{9,5},{12,8},{13,9},{14,12},{15,13},{10,14},{11,... | collective-permute-start | bytes 1376264 | tf_op jit(solution)/shard_map/ppermute | solution.py:398
  188.5 18.1 %collective-permute-start.40 = (bf16[32,7168]{1,0:T(8,128)(2,1)S(1)}, bf16[32,7168]{1,0:T(8,128)(2,1)S(1)}, u32[]{:S(2)}, u32[]{:S(2)}) collective-permute-start(bf16[32,7168]{1,0:T(8,128)(2,1)S(1)} %add_convert_fusion.9), channel_id=1, source_target_pairs={{0,4},{1,5},{4,8},{5,9},{8,12},{9,13},{12,14},{13,15},{14,10},{15,... | collective-permute-start | bytes 1376264 | tf_op jit(solution)/shard_map/ppermute | solution.py:398
  197.1 24.1 %collective-permute-start.47 = (bf16[32,7168]{1,0:T(8,128)(2,1)S(1)}, bf16[32,7168]{1,0:T(8,128)(2,1)S(1)}, u32[]{:S(2)}, u32[]{:S(2)}) collective-permute-start(bf16[32,7168]{1,0:T(8,128)(2,1)S(1)} %add_convert_fusion.2), channel_id=1, source_target_pairs={{4,0},{5,1},{8,4},{9,5},{12,8},{13,9},{14,12},{15,13},{10,14},{11,... | collective-permute-start | bytes 1376264 | tf_op jit(solution)/shard_map/ppermute | solution.py:398
  198.3 22.8 %collective-permute-start.48 = (bf16[32,7168]{1,0:T(8,128)(2,1)S(1)}, bf16[32,7168]{1,0:T(8,128)(2,1)S(1)}, u32[]{:S(2)}, u32[]{:S(2)}) collective-permute-start(bf16[32,7168]{1,0:T(8,128)(2,1)S(1)} %add_convert_fusion.1), channel_id=1, source_target_pairs={{0,4},{1,5},{4,8},{5,9},{8,12},{9,13},{12,14},{13,15},{14,10},{15,... | collective-permute-start | bytes 1376264 | tf_op jit(solution)/shard_map/ppermute | solution.py:398
  206.9 15.8 %collective-permute-start.41 = (bf16[32,7168]{1,0:T(8,128)(2,1)S(1)}, bf16[32,7168]{1,0:T(8,128)(2,1)S(1)}, u32[]{:S(2)}, u32[]{:S(2)}) collective-permute-start(bf16[32,7168]{1,0:T(8,128)(2,1)S(1)} %add_convert_fusion.8), channel_id=1, source_target_pairs={{4,0},{5,1},{8,4},{9,5},{12,8},{13,9},{14,12},{15,13},{10,14},{11,... | collective-permute-start | bytes 1376264 | tf_op jit(solution)/shard_map/ppermute | solution.py:398
  208.2 16.0 %collective-permute-start.42 = (bf16[32,7168]{1,0:T(8,128)(2,1)S(1)}, bf16[32,7168]{1,0:T(8,128)(2,1)S(1)}, u32[]{:S(2)}, u32[]{:S(2)}) collective-permute-start(bf16[32,7168]{1,0:T(8,128)(2,1)S(1)} %add_convert_fusion.7), channel_id=1, source_target_pairs={{0,4},{1,5},{4,8},{5,9},{8,12},{9,13},{12,14},{13,15},{14,10},{15,... | collective-permute-start | bytes 1376264 | tf_op jit(solution)/shard_map/ppermute | solution.py:398
  (19 other events, 110.8 us)

commit v8 on v5

--- a/solution.py
+++ b/solution.py
@@ -297,15 +297,18 @@
         other = [lax.ppermute(c, AXIS, across) for c in mine]
         return mlp(mine, other, gate_up, down_proj)
 
+    first = min(2, half - 1)
+    near, _ = lax.optimization_barrier((front[1] + rear[1] + own, front[first][1:]))
+    results = {1: work(1, near)}
+    last_rear, results[1] = lax.optimization_barrier((rear[half - 1][1], results[1]))
     front[half] = [lax.ppermute(front[half - 1][0], AXIS, ahead)]
-    rear[half] = [lax.ppermute(rear[half - 1][1], AXIS, back)]
+    rear[half] = [lax.ppermute(last_rear, AXIS, back)]
     front, rear, shipped, shift_gates = lax.optimization_barrier(
         (front, rear, shipped, shift_gates)
     )
     block_latents = lax.all_to_all(shipped, AXIS, split_axis=0, concat_axis=0, tiled=True)
-    results = {}
-    for s in range(half, 0, -1):
-        results[s] = work(s, front[s] + rear[s] + (own if s == 1 else []))
+    for s in range(half, 1, -1):
+        results[s] = work(s, front[s] + rear[s])
     parts = {s: (part, lax.ppermute(rest, AXIS, across)) for s, (part, rest) in results.items()}
 
     def contribution(s, k, flow):

time: 227 us -> 239 us (1.053)
  Pallas kernels: 61 us -> 70.2 us
  local copies, waits for them, and re-layouts: 7.47 us -> 11.4 us
  other arithmetic: 21.6 us -> 18.2 us
    pallas_call x2, Pallas kernels: 8.2 us -> 18 us  [attend(): pl.pallas_call(attend_kernel, grid_spec=pltpu.PrefetchScalarGridSpec(num_...]
    ppermute x4, waiting for transfers between devices: 15.3 us -> 6.99 us  [per_device(): front[s] = [lax.ppermute(c, AXIS, ahead) for c in front[s - 1]]]
    ppermute x2, waiting for transfers between devices: 0.01 us -> 7.96 us  [per_device(): front = {1: [lax.ppermute(c, AXIS, ahead) for c in own]}]
    ppermute x4, waiting for transfers between devices: 17.8 us -> 11.3 us  [per_device(): rear[s] = [lax.ppermute(c, AXIS, back) for c in rear[s - 1]]]
    ppermute x14, waiting for transfers between devices: 40.5 us -> 45.4 us  [per_device(): lax.ppermute(value, AXIS, course[way])]
    unnamed x62 -> x54, local copies, waits for them, and re-layouts: 6.21 us -> 10.1 us
    convert_element_type x4, other arithmetic: 10.7 us -> 7.55 us  [contribution(): return (weight[:, None] * both).astype(jnp.bfloat16)]
  transfers between devices with their start and end apart: 50 -> 50, of which waited for: 21 -> 13; matrix products, arithmetic and copies ran while one was open for 9% -> 7% of each run, Pallas kernels for 27% -> 30%
where the time goes in v8:
time: 239 us; the launch traced here: 235 us
  waiting for transfers between devices  87.7 us (37%)
  Pallas kernels  70.2 us (29%)
  starting transfers between devices  46.3 us (19%)
  other arithmetic  18.2 us (8%)
  local copies, waits for them, and re-layouts  11.4 us (5%)
    pallas_call x4, Pallas kernels, mlp(): pl.pallas_call(functools.partial(mlp_kernel, sizes, tile), in_specs=[anyw...  51.4 us
    ppermute x14, waiting for transfers between devices, per_device(): lax.ppermute(value, AXIS, course[way])  45.4 us
    pallas_call x2, Pallas kernels, attend(): pl.pallas_call(attend_kernel, grid_spec=pltpu.PrefetchScalarGridSpec(num_...  18 us
    ppermute x14, starting transfers between devices, per_device(): lax.ppermute(value, AXIS, course[way])  14.5 us
    ppermute x4, waiting for transfers between devices, per_device(): rear[s] = [lax.ppermute(c, AXIS, back) for c in rear[s - 1]]  11.3 us
    unnamed x54, local copies, waits for them, and re-layouts  10.1 us
    ppermute x1, waiting for transfers between devices, per_device(): front[half] = [lax.ppermute(front[half - 1][0], AXIS, ahead)]  9.38 us
    ppermute x2, waiting for transfers between devices, per_device(): front = {1: [lax.ppermute(c, AXIS, ahead) for c in own]}  7.96 us
  transfers between devices with their start and end apart: 50, of which 13 were waited for; matrix products, arithmetic and copies ran while one was open for 7% of the time, Pallas kernels for 30%

profile of v8, /device:TPU:20, one launch (start us, length us, event | category | flops | bytes accessed | tf_op | source)
XLA Modules:
  0.0 234.9 jit_solution(17396116348676001408)
XLA Ops:
  1.6 1.6 collective-permute-start.1
  3.2 1.6 collective-permute-start.8
  4.7 0.9 convert_reduce_fusion.2
  5.7 0.7 multiply_add_fusion
  6.4 8.0 %collective-permute-done.2.refs_1_ = bf16[32,7168]{1,0:T(8,128)(2,1)S(1)} collective-permute-done((bf16[32,7168]{1,0:T(8,128)(2,1)}, bf16[32,7168]{1,0:T(8,128)(2,1)S(1)}, u32[]{:S(2)}, u32[]{:S(2)}) %collective-permute-start.2) | collective-permute-done | bytes 458784 | tf_op jit(solution)/shard_map/ppermute | solution.py:279
  14.9 0.8 select_reduce_fusion.1
  15.8 0.7 pad_add_fusion
  16.5 6.2 %all-to-all-start = ((s32[16,1,66]{2,1,0:T(1,128)}), s32[16,1,66]{2,1,0:T(1,128)S(1)}, u32[]{:S(2)}, u32[]{:S(2)}) async-start(s32[16,1,66]{2,1,0:T(1,128)} %bitcast.2), calls=%async_computation | async-start | bytes 16384 | tf_op jit(solution)/shard_map/all_to_all | solution.py:274
  22.7 1.3 copy-done.4
  24.0 0.7 ship.1
  24.8 1.5 copy-done.1
  26.3 6.7 %all-to-all-done = s32[16,1,66]{2,1,0:T(1,128)S(1)} async-done(((s32[16,1,66]{2,1,0:T(1,128)}), s32[16,1,66]{2,1,0:T(1,128)S(1)}, u32[]{:S(2)}, u32[]{:S(2)}) %all-to-all-start) | async-done | bytes 4256 | tf_op jit(solution)/shard_map/all_to_all | solution.py:274
  33.0 1.4 collective-permute-start.3
  34.3 0.7 collective-permute-start.9
  35.0 1.6 collective-permute-start.10
  36.6 0.8 copy-done.15
  37.4 0.7 dynamic-slice_bitcast_fusion
  38.6 7.0 %collective-permute-done.3.refs_0_ = bf16[32,7168]{1,0:T(8,128)(2,1)} collective-permute-done((bf16[32,7168]{1,0:T(8,128)(2,1)S(1)}, bf16[32,7168]{1,0:T(8,128)(2,1)}, u32[]{:S(2)}, u32[]{:S(2)}) %collective-permute-start.3) | collective-permute-done | bytes 458784 | tf_op jit(solution)/shard_map/ppermute | solution.py:293
  45.5 2.6 %collective-permute-done.9.refs_2_ = bf16[32,7168]{1,0:T(8,128)(2,1)} collective-permute-done((bf16[32,7168]{1,0:T(8,128)(2,1)}, bf16[32,7168]{1,0:T(8,128)(2,1)}, u32[]{:S(2)}, u32[]{:S(2)}) %collective-permute-start.9) | collective-permute-done | bytes 458784 | tf_op jit(solution)/shard_map/ppermute | solution.py:294
  48.1 8.3 %collective-permute-done.10.refs_3_ = bf16[32,7168]{1,0:T(8,128)(2,1)S(1)} collective-permute-done((bf16[32,7168]{1,0:T(8,128)(2,1)}, bf16[32,7168]{1,0:T(8,128)(2,1)S(1)}, u32[]{:S(2)}, u32[]{:S(2)}) %collective-permute-start.10) | collective-permute-done | bytes 458784 | tf_op jit(solution)/shard_map/ppermute | solution.py:294
  57.2 1.5 collective-permute-start.6
  58.7 1.5 collective-permute-start.5
  60.8 0.6 collective-permute-start.12
  61.3 1.0 copy-done.10
  62.4 1.0 copy-done.12
  63.4 1.0 copy-done.14
  64.4 1.0 copy-done.16
  65.4 14.9 %mlp.4 = (bf16[192,7168]{1,0:T(8,128)(2,1)S(1)}, bf16[192,7168]{1,0:T(8,128)(2,1)}) custom-call(bf16[32,7168]{1,0:T(8,128)(2,1)S(1)} %copy-done.16, bf16[32,7168]{1,0:T(8,128)(2,1)S(1)} %copy-done.14, bf16[32,7168]{1,0:T(8,128)(2,1)} %collective-permute-done.1.refs_2_, bf16[32,7168]{1,0:T(8,128)(2,1)} %collective-permute-done.8.refs_3_, ...), custom_call_target="tpu_custom_call" | custom-call | flops 8455716864 | bytes 33030144 | tf_op jit(solution)/shard_map/mlp/pallas_call | solution.py:91
  80.3 1.5 copy-done.2
  82.3 0.6 collective-permute-start.19
  82.9 1.5 collective-permute-start.7
  84.8 9.4 %collective-permute-done.7.refs_0_ = bf16[32,7168]{1,0:T(8,128)(2,1)} collective-permute-done((bf16[32,7168]{1,0:T(8,128)(2,1)}, bf16[32,7168]{1,0:T(8,128)(2,1)}, u32[]{:S(2)}, u32[]{:S(2)}) %collective-permute-start.7) | collective-permute-done | bytes 458784 | tf_op jit(solution)/shard_map/ppermute | solution.py:304
  95.8 6.5 %all-to-all-start.1 = ((bf16[32,64,576]{2,1,0:T(8,128)(2,1)}), bf16[32,64,576]{2,1,0:T(8,128)(2,1)S(1)}, u32[]{:S(2)}, u32[]{:S(2)}) async-start(bf16[32,64,576]{2,1,0:T(8,128)(2,1)} %copy-done.1), calls=%async_computation.1 | async-start | bytes 5242880 | tf_op jit(solution)/shard_map/all_to_all | solution.py:309
  103.0 11.2 %mlp.5 = (bf16[64,7168]{1,0:T(8,128)(2,1)S(1)}, bf16[64,7168]{1,0:T(8,128)(2,1)S(1)}) custom-call(bf16[32,7168]{1,0:T(8,128)(2,1)} %collective-permute-done.7.refs_0_, bf16[32,7168]{1,0:T(8,128)(2,1)} %collective-permute-done.19.refs_1_, bf16[32,7168]{1,0:T(8,128)(2,1)} %collective-permute-done.20.refs_2_, bf16[32,7168]{1,0:T(8,128)(2,1)} %collective-permute-done.21.refs_3_, ...), custom_call_target="tpu_custom_call" | custom-call | flops 2818572288 | bytes 25690112 | tf_op jit(solution)/shard_map/mlp/pallas_call | solution.py:91
  115.4 12.7 %mlp.6 = (bf16[128,7168]{1,0:T(8,128)(2,1)S(1)}, bf16[128,7168]{1,0:T(8,128)(2,1)S(1)}) custom-call(bf16[32,7168]{1,0:T(8,128)(2,1)} %collective-permute-done.3.refs_0_, bf16[32,7168]{1,0:T(8,128)(2,1)S(1)} %collective-permute-done.4.refs_1_, bf16[32,7168]{1,0:T(8,128)(2,1)} %collective-permute-done.9.refs_2_, bf16[32,7168]{1,0:T(8,128)(2,1)S(1)} %copy-done.6, ...), custom_call_target="tpu_custom_call" | custom-call | flops 5637144576 | bytes 29360128 | tf_op jit(solution)/shard_map/mlp/pallas_call | solution.py:91
  128.8 12.6 %mlp.7 = (bf16[128,7168]{1,0:T(8,128)(2,1)S(1)}, bf16[128,7168]{1,0:T(8,128)(2,1)S(1)}) custom-call(bf16[32,7168]{1,0:T(8,128)(2,1)} %collective-permute-done.5.refs_0_, bf16[32,7168]{1,0:T(8,128)(2,1)S(1)} %copy-done.8, bf16[32,7168]{1,0:T(8,128)(2,1)} %collective-permute-done.11.refs_2_, bf16[32,7168]{1,0:T(8,128)(2,1)} %collective-permute-done.12.refs_3_, ...), custom_call_target="tpu_custom_call" | custom-call | flops 5637144576 | bytes 29360128 | tf_op jit(solution)/shard_map/mlp/pallas_call | solution.py:91
  141.6 2.3 multiply_convert_fusion.15
  143.9 1.5 collective-permute-start.37
  145.9 1.5 multiply_convert_fusion.7
  147.4 0.8 copy-done.3
  148.2 2.1 multiply_convert_fusion.1
  150.3 1.7 multiply_convert_fusion.3
  152.0 17.3 %collective-permute-done.23 = bf16[32,7168]{1,0:T(8,128)(2,1)} collective-permute-done((bf16[32,7168]{1,0:T(8,128)(2,1)S(1)}, bf16[32,7168]{1,0:T(8,128)(2,1)}, u32[]{:S(2)}, u32[]{:S(2)}) %collective-permute-start.23) | collective-permute-done | bytes 458784 | tf_op jit(solution)/shard_map/ppermute | solution.py:357
  169.2 1.0 collective-permute-done.37
  170.2 1.3 add_convert_fusion.11
  171.6 2.0 collective-permute-start.36
  173.6 1.3 add_convert_fusion.5
  175.0 2.0 collective-permute-start.43
  176.9 10.2 %attend.2 = bf16[16,64,512]{2,1,0:T(8,128)(2,1)S(1)} custom-call(s32[32]{0:T(128)S(1)} %select_reduce_fusion.3.order_ref, s32[17]{0:T(128)S(1)} %get-tuple-element.220.start_ref, s32[32]{0:T(128)S(1)} %get-tuple-element.221.length_ref, bf16[32,64,576]{2,1,0:T(8,128)(2,1)S(1)} %copy-done, bf16[32,1,576]{2,1,0:T(2,128)(2,1)S(1)} %copy.34.own_ref, ...), custom_call_target="tpu_custom_call" | custom-call | flops 150994944 | bytes 4587520 | tf_op jit(solution)/shard_map/attend/pallas_call | solution.py:182
  187.6 2.0 collective-permute-start.39
  189.6 5.5 %collective-permute-done.42 = bf16[32,7168]{1,0:T(8,128)(2,1)S(1)} collective-permute-done((bf16[32,7168]{1,0:T(8,128)(2,1)S(1)}, bf16[32,7168]{1,0:T(8,128)(2,1)S(1)}, u32[]{:S(2)}, u32[]{:S(2)}) %collective-permute-start.42) | collective-permute-done | bytes 458784 | tf_op jit(solution)/shard_map/ppermute | solution.py:357
  195.3 0.6 collective-permute-start.44
  195.9 1.5 collective-permute-start.45
  197.4 7.5 %collective-permute-done.38 = bf16[32,7168]{1,0:T(8,128)(2,1)S(1)} collective-permute-done((bf16[32,7168]{1,0:T(8,128)(2,1)S(1)}, bf16[32,7168]{1,0:T(8,128)(2,1)S(1)}, u32[]{:S(2)}, u32[]{:S(2)}) %collective-permute-start.38) | collective-permute-done | bytes 458784 | tf_op jit(solution)/shard_map/ppermute | solution.py:357
  205.1 0.6 collective-permute-start.40
  205.7 1.5 collective-permute-start.41
  207.2 7.5 %collective-permute-done.44 = bf16[32,7168]{1,0:T(8,128)(2,1)S(1)} collective-permute-done((bf16[32,7168]{1,0:T(8,128)(2,1)S(1)}, bf16[32,7168]{1,0:T(8,128)(2,1)S(1)}, u32[]{:S(2)}, u32[]{:S(2)}) %collective-permute-start.44) | collective-permute-done | bytes 458784 | tf_op jit(solution)/shard_map/ppermute | solution.py:357
  215.0 0.6 collective-permute-start.46
  215.5 1.5 collective-permute-start.47
  217.0 7.8 %attend.3 = bf16[16,64,512]{2,1,0:T(8,128)(2,1)S(1)} custom-call(s32[32]{0:T(128)S(1)} %select_reduce_fusion.3.order_ref, s32[17]{0:T(128)S(1)} %get-tuple-element.219.start_ref, s32[32]{0:T(128)S(1)} %get-tuple-element.221.length_ref, bf16[32,64,576]{2,1,0:T(8,128)(2,1)S(1)} %copy-done, bf16[32,1,576]{2,1,0:T(2,128)(2,1)S(1)} %copy.34.own_ref, ...), custom_call_target="tpu_custom_call" | custom-call | flops 150994944 | bytes 4587520 | tf_op jit(solution)/shard_map/attend/pallas_call | solution.py:182
  224.9 1.5 pad_maximum_fusion
  226.4 6.6 %collective-permute-done.46 = bf16[32,7168]{1,0:T(8,128)(2,1)S(1)} collective-permute-done((bf16[32,7168]{1,0:T(8,128)(2,1)S(1)}, bf16[32,7168]{1,0:T(8,128)(2,1)S(1)}, u32[]{:S(2)}, u32[]{:S(2)}) %collective-permute-start.46) | collective-permute-done | bytes 458784 | tf_op jit(solution)/shard_map/ppermute | solution.py:357
  233.0 0.9 add_convert_fusion.6
  233.9 0.9 add_convert_fusion
  (138 shorter events, 10.4 us)
Async XLA Ops:
  0.6 56.4 %copy-start.26 = (bf16[32,576]{1,0:T(8,128)(2,1)S(1)}, bf16[32,576]{1,0:T(8,128)(2,1)}, u32[]{:S(2)}) copy-start(bf16[32,576]{1,0:T(8,128)(2,1)} %param.24) | copy-start | bytes 110596
  0.6 13.7 %collective-permute-start.2 = (bf16[32,7168]{1,0:T(8,128)(2,1)}, bf16[32,7168]{1,0:T(8,128)(2,1)S(1)}, u32[]{:S(2)}, u32[]{:S(2)}) collective-permute-start(bf16[32,7168]{1,0:T(8,128)(2,1)} %refs_5_), channel_id=1, source_target_pairs={{0,4},{1,5},{4,8},{5,9},{8,12},{9,13},{12,14},{13,15},{14,10},{15,... | collective-permute-start | bytes 1376264 | tf_op jit(solution)/shard_map/ppermute | solution.py:279
  1.1 31.8 %collective-permute-start = (bf16[32,7168]{1,0:T(8,128)(2,1)}, bf16[32,7168]{1,0:T(8,128)(2,1)S(1)}, u32[]{:S(2)}, u32[]{:S(2)}) collective-permute-start(bf16[32,7168]{1,0:T(8,128)(2,1)} %refs_4_), channel_id=1, source_target_pairs={{0,4},{1,5},{4,8},{5,9},{8,12},{9,13},{12,14},{13,15},{14,10},{15,... | collective-permute-start | bytes 1376264 | tf_op jit(solution)/shard_map/ppermute | solution.py:279
  1.6 31.4 %collective-permute-start.1 = (bf16[32,7168]{1,0:T(8,128)(2,1)}, bf16[32,7168]{1,0:T(8,128)(2,1)}, u32[]{:S(2)}, u32[]{:S(2)}) collective-permute-start(bf16[32,7168]{1,0:T(8,128)(2,1)} %refs_4_), channel_id=1, source_target_pairs={{4,0},{5,1},{8,4},{9,5},{12,8},{13,9},{14,12},{15,13},{10,14},{11,... | collective-permute-start | bytes 1376264 | tf_op jit(solution)/shard_map/ppermute | solution.py:280
  3.2 31.8 %collective-permute-start.8 = (bf16[32,7168]{1,0:T(8,128)(2,1)}, bf16[32,7168]{1,0:T(8,128)(2,1)}, u32[]{:S(2)}, u32[]{:S(2)}) collective-permute-start(bf16[32,7168]{1,0:T(8,128)(2,1)} %refs_5_), channel_id=1, source_target_pairs={{4,0},{5,1},{8,4},{9,5},{12,8},{13,9},{14,12},{15,13},{10,14},{11,... | collective-permute-start | bytes 1376264 | tf_op jit(solution)/shard_map/ppermute | solution.py:280
  14.3 42.8 %copy-start.13 = (bf16[32,7168]{1,0:T(8,128)(2,1)}, bf16[32,7168]{1,0:T(8,128)(2,1)S(1)}, u32[]{:S(2)}) copy-start(bf16[32,7168]{1,0:T(8,128)(2,1)S(1)} %collective-permute-done.2.refs_1_) | copy-start | bytes 1376260
  14.3 22.3 %collective-permute-start.4 = (bf16[32,7168]{1,0:T(8,128)(2,1)S(1)}, bf16[32,7168]{1,0:T(8,128)(2,1)S(1)}, u32[]{:S(2)}, u32[]{:S(2)}) collective-permute-start(bf16[32,7168]{1,0:T(8,128)(2,1)S(1)} %collective-permute-done.2.refs_1_), channel_id=1, source_target_pairs={{0,4},{1,5},{4,8},{5,9},{8,12},{9,13},{12,14},{13,15},{14,10},{15,... | collective-permute-start | bytes 1376264 | tf_op jit(solution)/shard_map/ppermute | solution.py:293
  16.5 16.5 %all-to-all-start = ((s32[16,1,66]{2,1,0:T(1,128)}), s32[16,1,66]{2,1,0:T(1,128)S(1)}, u32[]{:S(2)}, u32[]{:S(2)}) async-start(s32[16,1,66]{2,1,0:T(1,128)} %bitcast.2), calls=%async_computation | async-start | bytes 16384 | tf_op jit(solution)/shard_map/all_to_all | solution.py:274
  24.0 32.4 %copy-start.9 = (bf16[32,7168]{1,0:T(8,128)(2,1)S(1)}, bf16[32,7168]{1,0:T(8,128)(2,1)}, u32[]{:S(2)}) copy-start(bf16[32,7168]{1,0:T(8,128)(2,1)} %refs_4_) | copy-start | bytes 1376260
  24.0 32.4 %copy-start.11 = (bf16[32,7168]{1,0:T(8,128)(2,1)S(1)}, bf16[32,7168]{1,0:T(8,128)(2,1)}, u32[]{:S(2)}) copy-start(bf16[32,7168]{1,0:T(8,128)(2,1)} %refs_5_) | copy-start | bytes 1376260
  33.0 12.6 %collective-permute-start.3 = (bf16[32,7168]{1,0:T(8,128)(2,1)S(1)}, bf16[32,7168]{1,0:T(8,128)(2,1)}, u32[]{:S(2)}, u32[]{:S(2)}) collective-permute-start(bf16[32,7168]{1,0:T(8,128)(2,1)S(1)} %collective-permute-done.refs_0_), channel_id=1, source_target_pairs={{0,4},{1,5},{4,8},{5,9},{8,12},{9,13},{12,14},{13,15},{14,10},{15,... | collective-permute-start | bytes 1376264 | tf_op jit(solution)/shard_map/ppermute | solution.py:293
  34.3 13.8 %collective-permute-start.9 = (bf16[32,7168]{1,0:T(8,128)(2,1)}, bf16[32,7168]{1,0:T(8,128)(2,1)}, u32[]{:S(2)}, u32[]{:S(2)}) collective-permute-start(bf16[32,7168]{1,0:T(8,128)(2,1)} %collective-permute-done.1.refs_2_), channel_id=1, source_target_pairs={{4,0},{5,1},{8,4},{9,5},{12,8},{13,9},{14,12},{15,13},{10,14},{11,... | collective-permute-start | bytes 1376264 | tf_op jit(solution)/shard_map/ppermute | solution.py:294
  35.0 21.4 %collective-permute-start.10 = (bf16[32,7168]{1,0:T(8,128)(2,1)}, bf16[32,7168]{1,0:T(8,128)(2,1)S(1)}, u32[]{:S(2)}, u32[]{:S(2)}) collective-permute-start(bf16[32,7168]{1,0:T(8,128)(2,1)} %collective-permute-done.8.refs_3_), channel_id=1, source_target_pairs={{4,0},{5,1},{8,4},{9,5},{12,8},{13,9},{14,12},{15,13},{10,14},{11,... | collective-permute-start | bytes 1376264 | tf_op jit(solution)/shard_map/ppermute | solution.py:294
  36.6 19.8 %collective-permute-start.13 = (bf16[32,7168]{1,0:T(8,128)(2,1)S(1)}, bf16[32,7168]{1,0:T(8,128)(2,1)}, u32[]{:S(2)}, u32[]{:S(2)}) collective-permute-start(bf16[32,7168]{1,0:T(8,128)(2,1)S(1)} %collective-permute-done.refs_0_), channel_id=1, source_target_pairs={{0,1},{1,0},{2,3},{3,2},{4,5},{5,4},{6,7},{7,6},{8,9},{9,8},{10,11... | collective-permute-start | bytes 1376264 | tf_op jit(solution)/shard_map/ppermute | solution.py:297
  38.1 19.2 %collective-permute-start.14 = (bf16[32,7168]{1,0:T(8,128)(2,1)S(1)}, bf16[32,7168]{1,0:T(8,128)(2,1)S(1)}, u32[]{:S(2)}, u32[]{:S(2)}) collective-permute-start(bf16[32,7168]{1,0:T(8,128)(2,1)S(1)} %collective-permute-done.2.refs_1_), channel_id=1, source_target_pairs={{0,1},{1,0},{2,3},{3,2},{4,5},{5,4},{6,7},{7,6},{8,9},{9,8},{10,11... | collective-permute-start | bytes 1376264 | tf_op jit(solution)/shard_map/ppermute | solution.py:297
  45.5 13.2 %collective-permute-start.15 = (bf16[32,7168]{1,0:T(8,128)(2,1)}, bf16[32,7168]{1,0:T(8,128)(2,1)S(1)}, u32[]{:S(2)}, u32[]{:S(2)}) collective-permute-start(bf16[32,7168]{1,0:T(8,128)(2,1)} %collective-permute-done.1.refs_2_), channel_id=1, source_target_pairs={{0,1},{1,0},{2,3},{3,2},{4,5},{5,4},{6,7},{7,6},{8,9},{9,8},{10,11... | collective-permute-start | bytes 1376264 | tf_op jit(solution)/shard_map/ppermute | solution.py:297
  48.1 12.1 %collective-permute-start.16 = (bf16[32,7168]{1,0:T(8,128)(2,1)}, bf16[32,7168]{1,0:T(8,128)(2,1)S(1)}, u32[]{:S(2)}, u32[]{:S(2)}) collective-permute-start(bf16[32,7168]{1,0:T(8,128)(2,1)} %collective-permute-done.8.refs_3_), channel_id=1, source_target_pairs={{0,1},{1,0},{2,3},{3,2},{4,5},{5,4},{6,7},{7,6},{8,9},{9,8},{10,11... | collective-permute-start | bytes 1376264 | tf_op jit(solution)/shard_map/ppermute | solution.py:297
  56.4 23.9 %copy-start.5 = (bf16[32,7168]{1,0:T(8,128)(2,1)}, bf16[32,7168]{1,0:T(8,128)(2,1)S(1)}, u32[]{:S(2)}) copy-start(bf16[32,7168]{1,0:T(8,128)(2,1)S(1)} %collective-permute-done.10.refs_3_) | copy-start | bytes 1376260
  56.4 4.4 %collective-permute-start.17 = (bf16[32,7168]{1,0:T(8,128)(2,1)S(1)}, bf16[32,7168]{1,0:T(8,128)(2,1)S(1)}, u32[]{:S(2)}, u32[]{:S(2)}) collective-permute-start(bf16[32,7168]{1,0:T(8,128)(2,1)S(1)} %copy-done.9), channel_id=1, source_target_pairs={{0,1},{1,0},{2,3},{3,2},{4,5},{5,4},{6,7},{7,6},{8,9},{9,8},{10,11... | collective-permute-start | bytes 1376264 | tf_op jit(solution)/shard_map/ppermute | solution.py:297
  56.4 4.9 %collective-permute-start.18 = (bf16[32,7168]{1,0:T(8,128)(2,1)S(1)}, bf16[32,7168]{1,0:T(8,128)(2,1)S(1)}, u32[]{:S(2)}, u32[]{:S(2)}) collective-permute-start(bf16[32,7168]{1,0:T(8,128)(2,1)S(1)} %copy-done.11), channel_id=1, source_target_pairs={{0,1},{1,0},{2,3},{3,2},{4,5},{5,4},{6,7},{7,6},{8,9},{9,8},{10,11... | collective-permute-start | bytes 1376264 | tf_op jit(solution)/shard_map/ppermute | solution.py:297
  57.2 27.5 %collective-permute-start.6 = (bf16[32,7168]{1,0:T(8,128)(2,1)S(1)}, bf16[32,7168]{1,0:T(8,128)(2,1)S(1)}, u32[]{:S(2)}, u32[]{:S(2)}) collective-permute-start(bf16[32,7168]{1,0:T(8,128)(2,1)S(1)} %collective-permute-done.4.refs_1_), channel_id=1, source_target_pairs={{0,4},{1,5},{4,8},{5,9},{8,12},{9,13},{12,14},{13,15},{14,10},{15,... | collective-permute-start | bytes 1376264 | tf_op jit(solution)/shard_map/ppermute | solution.py:293
  58.7 24.1 %collective-permute-start.5 = (bf16[32,7168]{1,0:T(8,128)(2,1)}, bf16[32,7168]{1,0:T(8,128)(2,1)}, u32[]{:S(2)}, u32[]{:S(2)}) collective-permute-start(bf16[32,7168]{1,0:T(8,128)(2,1)} %collective-permute-done.3.refs_0_), channel_id=1, source_target_pairs={{0,4},{1,5},{4,8},{5,9},{8,12},{9,13},{12,14},{13,15},{14,10},{15,... | collective-permute-start | bytes 1376264 | tf_op jit(solution)/shard_map/ppermute | solution.py:293
  60.2 24.5 %collective-permute-start.11 = (bf16[32,7168]{1,0:T(8,128)(2,1)}, bf16[32,7168]{1,0:T(8,128)(2,1)}, u32[]{:S(2)}, u32[]{:S(2)}) collective-permute-start(bf16[32,7168]{1,0:T(8,128)(2,1)} %collective-permute-done.9.refs_2_), channel_id=1, source_target_pairs={{4,0},{5,1},{8,4},{9,5},{12,8},{13,9},{14,12},{15,13},{10,14},{11,... | collective-permute-start | bytes 1376264 | tf_op jit(solution)/shard_map/ppermute | solution.py:294
  60.8 21.5 %collective-permute-start.12 = (bf16[32,7168]{1,0:T(8,128)(2,1)S(1)}, bf16[32,7168]{1,0:T(8,128)(2,1)}, u32[]{:S(2)}, u32[]{:S(2)}) collective-permute-start(bf16[32,7168]{1,0:T(8,128)(2,1)S(1)} %collective-permute-done.10.refs_3_), channel_id=1, source_target_pairs={{4,0},{5,1},{8,4},{9,5},{12,8},{13,9},{14,12},{15,13},{10,14},{11,... | collective-permute-start | bytes 1376264 | tf_op jit(solution)/shard_map/ppermute | solution.py:294
  82.3 11.8 %collective-permute-start.19 = (bf16[32,7168]{1,0:T(8,128)(2,1)}, bf16[32,7168]{1,0:T(8,128)(2,1)}, u32[]{:S(2)}, u32[]{:S(2)}) collective-permute-start(bf16[32,7168]{1,0:T(8,128)(2,1)} %collective-permute-done.12.refs_3_), channel_id=1, source_target_pairs={{4,0},{5,1},{8,4},{9,5},{12,8},{13,9},{14,12},{15,13},{10,14},{11,... | collective-permute-start | bytes 1376264 | tf_op jit(solution)/shard_map/ppermute | solution.py:305
  82.9 11.3 %collective-permute-start.7 = (bf16[32,7168]{1,0:T(8,128)(2,1)}, bf16[32,7168]{1,0:T(8,128)(2,1)}, u32[]{:S(2)}, u32[]{:S(2)}) collective-permute-start(bf16[32,7168]{1,0:T(8,128)(2,1)} %collective-permute-done.5.refs_0_), channel_id=1, source_target_pairs={{0,4},{1,5},{4,8},{5,9},{8,12},{9,13},{12,14},{13,15},{14,10},{15,... | collective-permute-start | bytes 1376264 | tf_op jit(solution)/shard_map/ppermute | solution.py:304
  84.7 11.0 %copy-start.7 = (bf16[32,7168]{1,0:T(8,128)(2,1)}, bf16[32,7168]{1,0:T(8,128)(2,1)S(1)}, u32[]{:S(2)}) copy-start(bf16[32,7168]{1,0:T(8,128)(2,1)S(1)} %collective-permute-done.6.refs_1_) | copy-start | bytes 1376260
  94.1 8.2 %collective-permute-start.20 = (bf16[32,7168]{1,0:T(8,128)(2,1)}, bf16[32,7168]{1,0:T(8,128)(2,1)}, u32[]{:S(2)}, u32[]{:S(2)}) collective-permute-start(bf16[32,7168]{1,0:T(8,128)(2,1)} %collective-permute-done.7.refs_0_), channel_id=1, source_target_pairs={{0,1},{1,0},{2,3},{3,2},{4,5},{5,4},{6,7},{7,6},{8,9},{9,8},{10,11... | collective-permute-start | bytes 1376264 | tf_op jit(solution)/shard_map/ppermute | solution.py:297
  94.4 8.2 %collective-permute-start.21 = (bf16[32,7168]{1,0:T(8,128)(2,1)}, bf16[32,7168]{1,0:T(8,128)(2,1)}, u32[]{:S(2)}, u32[]{:S(2)}) collective-permute-start(bf16[32,7168]{1,0:T(8,128)(2,1)} %collective-permute-done.19.refs_1_), channel_id=1, source_target_pairs={{0,1},{1,0},{2,3},{3,2},{4,5},{5,4},{6,7},{7,6},{8,9},{9,8},{10,11... | collective-permute-start | bytes 1376264 | tf_op jit(solution)/shard_map/ppermute | solution.py:297
  95.2 19.1 %collective-permute-start.25 = (bf16[32,7168]{1,0:T(8,128)(2,1)}, bf16[32,7168]{1,0:T(8,128)(2,1)}, u32[]{:S(2)}, u32[]{:S(2)}) collective-permute-start(bf16[32,7168]{1,0:T(8,128)(2,1)} %collective-permute-done.3.refs_0_), channel_id=1, source_target_pairs={{0,1},{1,0},{2,3},{3,2},{4,5},{5,4},{6,7},{7,6},{8,9},{9,8},{10,11... | collective-permute-start | bytes 1376264 | tf_op jit(solution)/shard_map/ppermute | solution.py:297
  95.2 19.4 %collective-permute-start.26 = (bf16[32,7168]{1,0:T(8,128)(2,1)S(1)}, bf16[32,7168]{1,0:T(8,128)(2,1)}, u32[]{:S(2)}, u32[]{:S(2)}) collective-permute-start(bf16[32,7168]{1,0:T(8,128)(2,1)S(1)} %collective-permute-done.4.refs_1_), channel_id=1, source_target_pairs={{0,1},{1,0},{2,3},{3,2},{4,5},{5,4},{6,7},{7,6},{8,9},{9,8},{10,11... | collective-permute-start | bytes 1376264 | tf_op jit(solution)/shard_map/ppermute | solution.py:297
  95.7 19.2 %collective-permute-start.27 = (bf16[32,7168]{1,0:T(8,128)(2,1)}, bf16[32,7168]{1,0:T(8,128)(2,1)}, u32[]{:S(2)}, u32[]{:S(2)}) collective-permute-start(bf16[32,7168]{1,0:T(8,128)(2,1)} %collective-permute-done.9.refs_2_), channel_id=1, source_target_pairs={{0,1},{1,0},{2,3},{3,2},{4,5},{5,4},{6,7},{7,6},{8,9},{9,8},{10,11... | collective-permute-start | bytes 1376264 | tf_op jit(solution)/shard_map/ppermute | solution.py:297
  95.8 73.5 %all-to-all-start.1 = ((bf16[32,64,576]{2,1,0:T(8,128)(2,1)}), bf16[32,64,576]{2,1,0:T(8,128)(2,1)S(1)}, u32[]{:S(2)}, u32[]{:S(2)}) async-start(bf16[32,64,576]{2,1,0:T(8,128)(2,1)} %copy-done.1), calls=%async_computation.1 | async-start | bytes 5242880 | tf_op jit(solution)/shard_map/all_to_all | solution.py:309
  102.3 12.8 %collective-permute-start.28 = (bf16[32,7168]{1,0:T(8,128)(2,1)}, bf16[32,7168]{1,0:T(8,128)(2,1)S(1)}, u32[]{:S(2)}, u32[]{:S(2)}) collective-permute-start(bf16[32,7168]{1,0:T(8,128)(2,1)} %copy-done.5), channel_id=1, source_target_pairs={{0,1},{1,0},{2,3},{3,2},{4,5},{5,4},{6,7},{7,6},{8,9},{9,8},{10,11... | collective-permute-start | bytes 1376264 | tf_op jit(solution)/shard_map/ppermute | solution.py:297
  102.6 11.7 %copy-start.8 = (bf16[32,7168]{1,0:T(8,128)(2,1)S(1)}, bf16[32,7168]{1,0:T(8,128)(2,1)}, u32[]{:S(2)}) copy-start(bf16[32,7168]{1,0:T(8,128)(2,1)} %copy-done.7) | copy-start | bytes 1376260
  102.6 12.8 %copy-start.6 = (bf16[32,7168]{1,0:T(8,128)(2,1)S(1)}, bf16[32,7168]{1,0:T(8,128)(2,1)}, u32[]{:S(2)}) copy-start(bf16[32,7168]{1,0:T(8,128)(2,1)} %copy-done.5) | copy-start | bytes 1376260
  102.6 25.6 %collective-permute-start.30 = (bf16[32,7168]{1,0:T(8,128)(2,1)}, bf16[32,7168]{1,0:T(8,128)(2,1)S(1)}, u32[]{:S(2)}, u32[]{:S(2)}) collective-permute-start(bf16[32,7168]{1,0:T(8,128)(2,1)} %collective-permute-done.5.refs_0_), channel_id=1, source_target_pairs={{0,1},{1,0},{2,3},{3,2},{4,5},{5,4},{6,7},{7,6},{8,9},{9,8},{10,11... | collective-permute-start | bytes 1376264 | tf_op jit(solution)/shard_map/ppermute | solution.py:297
  114.3 14.1 %collective-permute-start.31 = (bf16[32,7168]{1,0:T(8,128)(2,1)S(1)}, bf16[32,7168]{1,0:T(8,128)(2,1)S(1)}, u32[]{:S(2)}, u32[]{:S(2)}) collective-permute-start(bf16[32,7168]{1,0:T(8,128)(2,1)S(1)} %copy-done.8), channel_id=1, source_target_pairs={{0,1},{1,0},{2,3},{3,2},{4,5},{5,4},{6,7},{7,6},{8,9},{9,8},{10,11... | collective-permute-start | bytes 1376264 | tf_op jit(solution)/shard_map/ppermute | solution.py:297
  114.6 14.2 %collective-permute-start.32 = (bf16[32,7168]{1,0:T(8,128)(2,1)}, bf16[32,7168]{1,0:T(8,128)(2,1)S(1)}, u32[]{:S(2)}, u32[]{:S(2)}) collective-permute-start(bf16[32,7168]{1,0:T(8,128)(2,1)} %collective-permute-done.11.refs_2_), channel_id=1, source_target_pairs={{0,1},{1,0},{2,3},{3,2},{4,5},{5,4},{6,7},{7,6},{8,9},{9,8},{10,11... | collective-permute-start | bytes 1376264 | tf_op jit(solution)/shard_map/ppermute | solution.py:297
  114.9 13.9 %collective-permute-start.33 = (bf16[32,7168]{1,0:T(8,128)(2,1)}, bf16[32,7168]{1,0:T(8,128)(2,1)S(1)}, u32[]{:S(2)}, u32[]{:S(2)}) collective-permute-start(bf16[32,7168]{1,0:T(8,128)(2,1)} %collective-permute-done.12.refs_3_), channel_id=1, source_target_pairs={{0,1},{1,0},{2,3},{3,2},{4,5},{5,4},{6,7},{7,6},{8,9},{9,8},{10,11... | collective-permute-start | bytes 1376264 | tf_op jit(solution)/shard_map/ppermute | solution.py:297
  115.1 26.5 %collective-permute-start.22 = (bf16[64,7168]{1,0:T(8,128)(2,1)S(1)}, bf16[64,7168]{1,0:T(8,128)(2,1)}, u32[]{:S(2)}, u32[]{:S(2)}) collective-permute-start(bf16[64,7168]{1,0:T(8,128)(2,1)S(1)} %get-tuple-element.110), channel_id=1, source_target_pairs={{0,1},{1,0},{2,3},{3,2},{4,5},{5,4},{6,7},{7,6},{8,9},{9,8},{10,11... | collective-permute-start | bytes 2752520 | tf_op jit(solution)/shard_map/ppermute | solution.py:312
  128.2 19.2 %collective-permute-start.24 = (bf16[192,7168]{1,0:T(8,128)(2,1)}, bf16[192,7168]{1,0:T(8,128)(2,1)S(1)}, u32[]{:S(2)}, u32[]{:S(2)}) collective-permute-start(bf16[192,7168]{1,0:T(8,128)(2,1)} %get-tuple-element.112), channel_id=1, source_target_pairs={{0,1},{1,0},{2,3},{3,2},{4,5},{5,4},{6,7},{7,6},{8,9},{9,8},{10,11... | collective-permute-start | bytes 8257544 | tf_op jit(solution)/shard_map/ppermute | solution.py:312
  128.4 17.5 %collective-permute-start.29 = (bf16[128,7168]{1,0:T(8,128)(2,1)S(1)}, bf16[128,7168]{1,0:T(8,128)(2,1)S(1)}, u32[]{:S(2)}, u32[]{:S(2)}) collective-permute-start(bf16[128,7168]{1,0:T(8,128)(2,1)S(1)} %get-tuple-element.118), channel_id=1, source_target_pairs={{0,1},{1,0},{2,3},{3,2},{4,5},{5,4},{6,7},{7,6},{8,9},{9,8},{10,11... | collective-permute-start | bytes 5505032 | tf_op jit(solution)/shard_map/ppermute | solution.py:312
  141.3 9.0 %collective-permute-start.34 = (bf16[128,7168]{1,0:T(8,128)(2,1)S(1)}, bf16[128,7168]{1,0:T(8,128)(2,1)S(1)}, u32[]{:S(2)}, u32[]{:S(2)}) collective-permute-start(bf16[128,7168]{1,0:T(8,128)(2,1)S(1)} %get-tuple-element.124), channel_id=1, source_target_pairs={{0,1},{1,0},{2,3},{3,2},{4,5},{5,4},{6,7},{7,6},{8,9},{9,8},{10,11... | collective-permute-start | bytes 5505032 | tf_op jit(solution)/shard_map/ppermute | solution.py:312
  143.9 26.4 %collective-permute-start.37 = (bf16[32,7168]{1,0:T(8,128)(2,1)}, bf16[32,7168]{1,0:T(8,128)(2,1)}, u32[]{:S(2)}, u32[]{:S(2)}) collective-permute-start(bf16[32,7168]{1,0:T(8,128)(2,1)} %get-tuple-element.200), channel_id=1, source_target_pairs={{4,0},{5,1},{8,4},{9,5},{12,8},{13,9},{14,12},{15,13},{10,14},{11,... | collective-permute-start | bytes 1376264 | tf_op jit(solution)/shard_map/ppermute | solution.py:357
  145.4 23.9 %collective-permute-start.23 = (bf16[32,7168]{1,0:T(8,128)(2,1)S(1)}, bf16[32,7168]{1,0:T(8,128)(2,1)}, u32[]{:S(2)}, u32[]{:S(2)}) collective-permute-start(bf16[32,7168]{1,0:T(8,128)(2,1)S(1)} %get-tuple-element.199), channel_id=1, source_target_pairs={{0,4},{1,5},{4,8},{5,9},{8,12},{9,13},{12,14},{13,15},{14,10},{15,... | collective-permute-start | bytes 1376264 | tf_op jit(solution)/shard_map/ppermute | solution.py:357
  171.5 15.7 %collective-permute-start.35 = (bf16[32,7168]{1,0:T(8,128)(2,1)}, bf16[32,7168]{1,0:T(8,128)(2,1)S(1)}, u32[]{:S(2)}, u32[]{:S(2)}) collective-permute-start(bf16[32,7168]{1,0:T(8,128)(2,1)} %get-tuple-element.129), channel_id=1, source_target_pairs={{4,0},{5,1},{8,4},{9,5},{12,8},{13,9},{14,12},{15,13},{10,14},{11,... | collective-permute-start | bytes 1376264 | tf_op jit(solution)/shard_map/ppermute | solution.py:357
  171.6 15.6 %collective-permute-start.36 = (bf16[32,7168]{1,0:T(8,128)(2,1)S(1)}, bf16[32,7168]{1,0:T(8,128)(2,1)S(1)}, u32[]{:S(2)}, u32[]{:S(2)}) collective-permute-start(bf16[32,7168]{1,0:T(8,128)(2,1)S(1)} %add_convert_fusion.11), channel_id=1, source_target_pairs={{0,4},{1,5},{4,8},{5,9},{8,12},{9,13},{12,14},{13,15},{14,10},{15,... | collective-permute-start | bytes 1376264 | tf_op jit(solution)/shard_map/ppermute | solution.py:357
  174.9 20.2 %collective-permute-start.42 = (bf16[32,7168]{1,0:T(8,128)(2,1)S(1)}, bf16[32,7168]{1,0:T(8,128)(2,1)S(1)}, u32[]{:S(2)}, u32[]{:S(2)}) collective-permute-start(bf16[32,7168]{1,0:T(8,128)(2,1)S(1)} %add_convert_fusion.5), channel_id=1, source_target_pairs={{4,0},{5,1},{8,4},{9,5},{12,8},{13,9},{14,12},{15,13},{10,14},{11,... | collective-permute-start | bytes 1376264 | tf_op jit(solution)/shard_map/ppermute | solution.py:357
  175.0 20.1 %collective-permute-start.43 = (bf16[32,7168]{1,0:T(8,128)(2,1)}, bf16[32,7168]{1,0:T(8,128)(2,1)S(1)}, u32[]{:S(2)}, u32[]{:S(2)}) collective-permute-start(bf16[32,7168]{1,0:T(8,128)(2,1)} %get-tuple-element.163), channel_id=1, source_target_pairs={{0,4},{1,5},{4,8},{5,9},{8,12},{9,13},{12,14},{13,15},{14,10},{15,... | collective-permute-start | bytes 1376264 | tf_op jit(solution)/shard_map/ppermute | solution.py:357
  176.9 10.3 %copy-start.19 = (bf16[32,7168]{1,0:T(8,128)(2,1)S(1)}, bf16[32,7168]{1,0:T(8,128)(2,1)}, u32[]{:S(2)}) copy-start(bf16[32,7168]{1,0:T(8,128)(2,1)} %get-tuple-element.145) | copy-start | bytes 1376260
  176.9 10.4 %copy-start.18 = (bf16[32,7168]{1,0:T(8,128)(2,1)S(1)}, bf16[32,7168]{1,0:T(8,128)(2,1)}, u32[]{:S(2)}) copy-start(bf16[32,7168]{1,0:T(8,128)(2,1)} %get-tuple-element.147) | copy-start | bytes 1376260
  187.4 17.5 %copy-start.25 = (bf16[32,7168]{1,0:T(8,128)(2,1)S(1)}, bf16[32,7168]{1,0:T(8,128)(2,1)}, u32[]{:S(2)}) copy-start(bf16[32,7168]{1,0:T(8,128)(2,1)} %get-tuple-element.151) | copy-start | bytes 1376260
  187.5 17.5 %copy-start.24 = (bf16[32,7168]{1,0:T(8,128)(2,1)S(1)}, bf16[32,7168]{1,0:T(8,128)(2,1)}, u32[]{:S(2)}) copy-start(bf16[32,7168]{1,0:T(8,128)(2,1)} %get-tuple-element.153) | copy-start | bytes 1376260
  187.5 17.4 %collective-permute-start.38 = (bf16[32,7168]{1,0:T(8,128)(2,1)S(1)}, bf16[32,7168]{1,0:T(8,128)(2,1)S(1)}, u32[]{:S(2)}, u32[]{:S(2)}) collective-permute-start(bf16[32,7168]{1,0:T(8,128)(2,1)S(1)} %add_convert_fusion.10), channel_id=1, source_target_pairs={{4,0},{5,1},{8,4},{9,5},{12,8},{13,9},{14,12},{15,13},{10,14},{11,... | collective-permute-start | bytes 1376264 | tf_op jit(solution)/shard_map/ppermute | solution.py:357
  187.6 17.3 %collective-permute-start.39 = (bf16[32,7168]{1,0:T(8,128)(2,1)S(1)}, bf16[32,7168]{1,0:T(8,128)(2,1)S(1)}, u32[]{:S(2)}, u32[]{:S(2)}) collective-permute-start(bf16[32,7168]{1,0:T(8,128)(2,1)S(1)} %add_convert_fusion.9), channel_id=1, source_target_pairs={{0,4},{1,5},{4,8},{5,9},{8,12},{9,13},{12,14},{13,15},{14,10},{15,... | collective-permute-start | bytes 1376264 | tf_op jit(solution)/shard_map/ppermute | solution.py:357
  195.2 19.5 %copy-start.23 = (bf16[32,7168]{1,0:T(8,128)(2,1)S(1)}, bf16[32,7168]{1,0:T(8,128)(2,1)}, u32[]{:S(2)}) copy-start(bf16[32,7168]{1,0:T(8,128)(2,1)} %get-tuple-element.171) | copy-start | bytes 1376260
  195.3 19.5 %copy-start.22 = (bf16[32,7168]{1,0:T(8,128)(2,1)S(1)}, bf16[32,7168]{1,0:T(8,128)(2,1)}, u32[]{:S(2)}) copy-start(bf16[32,7168]{1,0:T(8,128)(2,1)} %get-tuple-element.173) | copy-start | bytes 1376260
  195.3 19.4 %collective-permute-start.44 = (bf16[32,7168]{1,0:T(8,128)(2,1)S(1)}, bf16[32,7168]{1,0:T(8,128)(2,1)S(1)}, u32[]{:S(2)}, u32[]{:S(2)}) collective-permute-start(bf16[32,7168]{1,0:T(8,128)(2,1)S(1)} %add_convert_fusion.4), channel_id=1, source_target_pairs={{4,0},{5,1},{8,4},{9,5},{12,8},{13,9},{14,12},{15,13},{10,14},{11,... | collective-permute-start | bytes 1376264 | tf_op jit(solution)/shard_map/ppermute | solution.py:357
  195.9 18.8 %collective-permute-start.45 = (bf16[32,7168]{1,0:T(8,128)(2,1)S(1)}, bf16[32,7168]{1,0:T(8,128)(2,1)S(1)}, u32[]{:S(2)}, u32[]{:S(2)}) collective-permute-start(bf16[32,7168]{1,0:T(8,128)(2,1)S(1)} %add_convert_fusion.3), channel_id=1, source_target_pairs={{0,4},{1,5},{4,8},{5,9},{8,12},{9,13},{12,14},{13,15},{14,10},{15,... | collective-permute-start | bytes 1376264 | tf_op jit(solution)/shard_map/ppermute | solution.py:357
  205.1 21.2 %collective-permute-start.40 = (bf16[32,7168]{1,0:T(8,128)(2,1)S(1)}, bf16[32,7168]{1,0:T(8,128)(2,1)S(1)}, u32[]{:S(2)}, u32[]{:S(2)}) collective-permute-start(bf16[32,7168]{1,0:T(8,128)(2,1)S(1)} %add_convert_fusion.8), channel_id=1, source_target_pairs={{4,0},{5,1},{8,4},{9,5},{12,8},{13,9},{14,12},{15,13},{10,14},{11,... | collective-permute-start | bytes 1376264 | tf_op jit(solution)/shard_map/ppermute | solution.py:357
  205.7 20.6 %collective-permute-start.41 = (bf16[32,7168]{1,0:T(8,128)(2,1)S(1)}, bf16[32,7168]{1,0:T(8,128)(2,1)S(1)}, u32[]{:S(2)}, u32[]{:S(2)}) collective-permute-start(bf16[32,7168]{1,0:T(8,128)(2,1)S(1)} %add_convert_fusion.7), channel_id=1, source_target_pairs={{0,4},{1,5},{4,8},{5,9},{8,12},{9,13},{12,14},{13,15},{14,10},{15,... | collective-permute-start | bytes 1376264 | tf_op jit(solution)/shard_map/ppermute | solution.py:357
  215.0 18.0 %collective-permute-start.46 = (bf16[32,7168]{1,0:T(8,128)(2,1)S(1)}, bf16[32,7168]{1,0:T(8,128)(2,1)S(1)}, u32[]{:S(2)}, u32[]{:S(2)}) collective-permute-start(bf16[32,7168]{1,0:T(8,128)(2,1)S(1)} %add_convert_fusion.2), channel_id=1, source_target_pairs={{4,0},{5,1},{8,4},{9,5},{12,8},{13,9},{14,12},{15,13},{10,14},{11,... | collective-permute-start | bytes 1376264 | tf_op jit(solution)/shard_map/ppermute | solution.py:357
  215.5 17.5 %collective-permute-start.47 = (bf16[32,7168]{1,0:T(8,128)(2,1)S(1)}, bf16[32,7168]{1,0:T(8,128)(2,1)S(1)}, u32[]{:S(2)}, u32[]{:S(2)}) collective-permute-start(bf16[32,7168]{1,0:T(8,128)(2,1)S(1)} %add_convert_fusion.1), channel_id=1, source_target_pairs={{0,4},{1,5},{4,8},{5,9},{8,12},{9,13},{12,14},{13,15},{14,10},{15,... | collective-permute-start | bytes 1376264 | tf_op jit(solution)/shard_map/ppermute | solution.py:357
  (13 other events, 44.4 us)

commit v9 on v5

--- a/solution.py
+++ b/solution.py
@@ -278,9 +278,7 @@
     sizes = [prefill_count, decode_count]
     front = {1: [lax.ppermute(c, AXIS, ahead) for c in own]}
     rear = {1: [lax.ppermute(c, AXIS, back) for c in own]}
-    front[1][0], rear[1][0], shipped, small = lax.optimization_barrier(
-        (front[1][0], rear[1][0], shipped, small)
-    )
+    rear[1][1], shipped, small = lax.optimization_barrier((rear[1][1], shipped, small))
     at_shift = lax.dynamic_index_in_dim(jnp.asarray(neighbours), me, 0, keepdims=False)
     picked = at_shift[:, None] == jnp.arange(devices)[None, :]
     shift_gates = jnp.sum(jnp.where(picked[:, :, None], small[None, :, :row_count], 0), axis=1)

time: 227 us -> 222 us (0.978)
  waiting for transfers between devices: 89.6 us -> 85.1 us
  local copies, waits for them, and re-layouts: 7.47 us -> 4.92 us
    ppermute x4, waiting for transfers between devices: 15.3 us -> 1.82 us  [per_device(): front[s] = [lax.ppermute(c, AXIS, ahead) for c in front[s - 1]]]
    ppermute x4, waiting for transfers between devices: 17.8 us -> 30.1 us  [per_device(): rear[s] = [lax.ppermute(c, AXIS, back) for c in rear[s - 1]]]
    all_to_all x1, waiting for transfers between devices: 7.45 us -> 0.01 us  [per_device(): small = lax.all_to_all(small, AXIS, split_axis=0, concat_axis=0, tiled=True)]
    ppermute x1, waiting for transfers between devices: 1.17 us -> 7.54 us  [per_device(): rear[half] = [lax.ppermute(rear[half - 1][1], AXIS, back)]]
    ppermute x1, waiting for transfers between devices: 7.31 us -> 1.18 us  [per_device(): front[half] = [lax.ppermute(front[half - 1][0], AXIS, ahead)]]
    ppermute x2, waiting for transfers between devices: 0.01 us -> 4.59 us  [per_device(): rear = {1: [lax.ppermute(c, AXIS, back) for c in own]}]
    ppermute x4, starting transfers between devices: 5.73 us -> 2.24 us  [per_device(): front[s] = [lax.ppermute(c, AXIS, ahead) for c in front[s - 1]]]
    ppermute x4, starting transfers between devices: 2.38 us -> 5.86 us  [per_device(): rear[s] = [lax.ppermute(c, AXIS, back) for c in rear[s - 1]]]
  transfers between devices with their start and end apart: 50 -> 50, of which waited for: 21 -> 22; matrix products, arithmetic and copies ran while one was open for 9% -> 9% of each run, Pallas kernels for 27% -> 28%
where the time goes in v9:
time: 222 us; the launch traced here: 220 us
  waiting for transfers between devices  85.1 us (38%)
  Pallas kernels  61.8 us (28%)
  starting transfers between devices  45.1 us (20%)
  other arithmetic  21.6 us (10%)
  local copies, waits for them, and re-layouts  4.92 us (2%)
    pallas_call x4, Pallas kernels, mlp(): pl.pallas_call(functools.partial(mlp_kernel, sizes, tile), in_specs=[anyw...  52.1 us
    ppermute x14, waiting for transfers between devices, per_device(): lax.ppermute(value, AXIS, course[way])  39.8 us
    ppermute x4, waiting for transfers between devices, per_device(): rear[s] = [lax.ppermute(c, AXIS, back) for c in rear[s - 1]]  30.1 us
    ppermute x14, starting transfers between devices, per_device(): lax.ppermute(value, AXIS, course[way])  14.5 us
    convert_element_type x4, other arithmetic, contribution(): return (weight[:, None] * both).astype(jnp.bfloat16)  10.7 us
    pallas_call x2, Pallas kernels, attend(): pl.pallas_call(attend_kernel, grid_spec=pltpu.PrefetchScalarGridSpec(num_...  9.02 us
    ppermute x1, waiting for transfers between devices, per_device(): rear[half] = [lax.ppermute(rear[half - 1][1], AXIS, back)]  7.54 us
    all_to_all x1, starting transfers between devices, per_device(): small = lax.all_to_all(small, AXIS, split_axis=0, concat_axis=0, tiled=True)  6.13 us
  transfers between devices with their start and end apart: 50, of which 22 were waited for; matrix products, arithmetic and copies ran while one was open for 9% of the time, Pallas kernels for 28%

profile of v9, /device:TPU:20, one launch (start us, length us, event | category | flops | bytes accessed | tf_op | source)
XLA Modules:
  0.0 219.6 jit_solution(434303480130837665)
XLA Ops:
  0.6 1.6 collective-permute-start.8
  2.7 0.9 convert_reduce_fusion.2
  3.6 0.7 multiply_add_fusion
  4.5 0.8 select_reduce_fusion.1
  5.3 0.7 pad_add_fusion
  6.0 6.1 %all-to-all-start = ((s32[16,1,66]{2,1,0:T(1,128)}), s32[16,1,66]{2,1,0:T(1,128)S(1)}, u32[]{:S(2)}, u32[]{:S(2)}) async-start(s32[16,1,66]{2,1,0:T(1,128)} %bitcast.2), calls=%async_computation | async-start | bytes 16384 | tf_op jit(solution)/shard_map/all_to_all | solution.py:274
  12.2 1.5 collective-permute-start.7
  14.2 1.3 copy-done.2
  15.5 0.7 ship.1
  16.3 1.5 copy-done.1
  17.7 0.8 copy-done.15
  18.5 1.5 collective-permute-start.10
  20.5 0.7 dynamic-slice_bitcast_fusion
  21.2 4.6 %collective-permute-done.7.refs_2_ = bf16[32,7168]{1,0:T(8,128)(2,1)} collective-permute-done((bf16[32,7168]{1,0:T(8,128)(2,1)}, bf16[32,7168]{1,0:T(8,128)(2,1)}, u32[]{:S(2)}, u32[]{:S(2)}) %collective-permute-start.7) | collective-permute-done | bytes 458784 | tf_op jit(solution)/shard_map/ppermute | solution.py:280
  25.8 1.5 collective-permute-start.9
  27.9 7.7 %collective-permute-done.10.refs_3_ = bf16[32,7168]{1,0:T(8,128)(2,1)S(1)} collective-permute-done((bf16[32,7168]{1,0:T(8,128)(2,1)}, bf16[32,7168]{1,0:T(8,128)(2,1)S(1)}, u32[]{:S(2)}, u32[]{:S(2)}) %collective-permute-start.10) | collective-permute-done | bytes 458784 | tf_op jit(solution)/shard_map/ppermute | solution.py:292
  35.6 1.5 collective-permute-start.12
  37.9 7.5 %collective-permute-done.9.refs_2_ = bf16[32,7168]{1,0:T(8,128)(2,1)S(1)} collective-permute-done((bf16[32,7168]{1,0:T(8,128)(2,1)}, bf16[32,7168]{1,0:T(8,128)(2,1)S(1)}, u32[]{:S(2)}, u32[]{:S(2)}) %collective-permute-start.9) | collective-permute-done | bytes 458784 | tf_op jit(solution)/shard_map/ppermute | solution.py:292
  45.4 1.5 collective-permute-start.11
  47.5 7.8 %collective-permute-done.12.refs_3_ = bf16[32,7168]{1,0:T(8,128)(2,1)S(1)} collective-permute-done((bf16[32,7168]{1,0:T(8,128)(2,1)S(1)}, bf16[32,7168]{1,0:T(8,128)(2,1)S(1)}, u32[]{:S(2)}, u32[]{:S(2)}) %collective-permute-start.12) | collective-permute-done | bytes 458784 | tf_op jit(solution)/shard_map/ppermute | solution.py:292
  55.2 1.5 collective-permute-start.13
  57.8 7.3 %collective-permute-done.11.refs_2_ = bf16[32,7168]{1,0:T(8,128)(2,1)S(1)} collective-permute-done((bf16[32,7168]{1,0:T(8,128)(2,1)S(1)}, bf16[32,7168]{1,0:T(8,128)(2,1)S(1)}, u32[]{:S(2)}, u32[]{:S(2)}) %collective-permute-start.11) | collective-permute-done | bytes 458784 | tf_op jit(solution)/shard_map/ppermute | solution.py:292
  65.1 1.6 collective-permute-done.5.refs_1_
  66.7 7.5 %collective-permute-done.13.refs_1_ = bf16[32,7168]{1,0:T(8,128)(2,1)} collective-permute-done((bf16[32,7168]{1,0:T(8,128)(2,1)S(1)}, bf16[32,7168]{1,0:T(8,128)(2,1)}, u32[]{:S(2)}, u32[]{:S(2)}) %collective-permute-start.13) | collective-permute-done | bytes 458784 | tf_op jit(solution)/shard_map/ppermute | solution.py:299
  74.2 1.2 collective-permute-done.6.refs_0_
  76.9 5.1 %all-to-all-start.1 = ((bf16[32,64,576]{2,1,0:T(8,128)(2,1)}), bf16[32,64,576]{2,1,0:T(8,128)(2,1)S(1)}, u32[]{:S(2)}, u32[]{:S(2)}) async-start(bf16[32,64,576]{2,1,0:T(8,128)(2,1)} %copy-done.1), calls=%async_computation.1 | async-start | bytes 5242880 | tf_op jit(solution)/shard_map/all_to_all | solution.py:303
  82.7 11.9 %mlp.4 = (bf16[64,7168]{1,0:T(8,128)(2,1)S(1)}, bf16[64,7168]{1,0:T(8,128)(2,1)}) custom-call(bf16[32,7168]{1,0:T(8,128)(2,1)} %collective-permute-done.6.refs_0_, bf16[32,7168]{1,0:T(8,128)(2,1)} %collective-permute-done.13.refs_1_, bf16[32,7168]{1,0:T(8,128)(2,1)} %collective-permute-done.14.refs_2_, bf16[32,7168]{1,0:T(8,128)(2,1)} %collective-permute-done.15.refs_3_, ...), custom_call_target="tpu_custom_call" | custom-call | flops 2818572288 | bytes 25690112 | tf_op jit(solution)/shard_map/mlp/pallas_call | solution.py:91
  95.9 12.6 %mlp.7 = (bf16[128,7168]{1,0:T(8,128)(2,1)S(1)}, bf16[128,7168]{1,0:T(8,128)(2,1)S(1)}) custom-call(bf16[32,7168]{1,0:T(8,128)(2,1)} %collective-permute-done.4.refs_0_, bf16[32,7168]{1,0:T(8,128)(2,1)} %collective-permute-done.5.refs_1_, bf16[32,7168]{1,0:T(8,128)(2,1)S(1)} %copy-done.12, bf16[32,7168]{1,0:T(8,128)(2,1)S(1)} %copy-done.10, ...), custom_call_target="tpu_custom_call" | custom-call | flops 5637144576 | bytes 29360128 | tf_op jit(solution)/shard_map/mlp/pallas_call | solution.py:91
  110.0 12.3 %mlp.6 = (bf16[128,7168]{1,0:T(8,128)(2,1)S(1)}, bf16[128,7168]{1,0:T(8,128)(2,1)S(1)}) custom-call(bf16[32,7168]{1,0:T(8,128)(2,1)S(1)} %copy-done.4, bf16[32,7168]{1,0:T(8,128)(2,1)S(1)} %copy-done.8, bf16[32,7168]{1,0:T(8,128)(2,1)S(1)} %copy-done.6, bf16[32,7168]{1,0:T(8,128)(2,1)S(1)} %collective-permute-done.10.refs_3_, ...), custom_call_target="tpu_custom_call" | custom-call | flops 5637144576 | bytes 29360128 | tf_op jit(solution)/shard_map/mlp/pallas_call | solution.py:91
  122.9 15.3 %mlp.5 = (bf16[192,7168]{1,0:T(8,128)(2,1)S(1)}, bf16[192,7168]{1,0:T(8,128)(2,1)}) custom-call(bf16[32,7168]{1,0:T(8,128)(2,1)} %collective-permute-done.refs_0_, bf16[32,7168]{1,0:T(8,128)(2,1)} %collective-permute-done.1.refs_1_, bf16[32,7168]{1,0:T(8,128)(2,1)} %collective-permute-done.7.refs_2_, bf16[32,7168]{1,0:T(8,128)(2,1)S(1)} %copy-done.16, ...), custom_call_target="tpu_custom_call" | custom-call | flops 8455716864 | bytes 33030144 | tf_op jit(solution)/shard_map/mlp/pallas_call | solution.py:91
  138.4 2.3 %multiply_convert_fusion.15 = (bf16[32,7168]{1,0:T(8,128)(2,1)S(1)}, bf16[32,7168]{1,0:T(8,128)(2,1)}) fusion(bf16[64,7168]{1,0:T(8,128)(2,1)} %collective-permute-done.16, bf16[64,7168]{1,0:T(8,128)(2,1)S(1)} %get-tuple-element.93, f32[32]{0:T(128)S(1)} %get-tuple-element.206, f32[32]{0:T(128)S(1)} %get-tuple-element.192), kind=kLoop, calls=%fused_computation.28 | loop fusion | flops 2293760 | bytes 2752768 | tf_op jit(solution)/shard_map/convert_element_type | solution.py:323
  141.3 1.5 collective-permute-start.37
  142.7 3.2 %multiply_convert_fusion.3 = (bf16[32,7168]{1,0:T(8,128)(2,1)}, bf16[32,7168]{1,0:T(8,128)(2,1)}, bf16[32,7168]{1,0:T(8,128)(2,1)}, bf16[32,7168]{1,0:T(8,128)(2,1)}) fusion(bf16[128,7168]{1,0:T(8,128)(2,1)} %collective-permute-done.34, bf16[128,7168]{1,0:T(8,128)(2,1)S(1)} %get-tuple-element.111, f32[32]{0:T(128)S(1)} %get-tuple-element.194, ...), kind=kLoop, calls=%fused_computation.16 | loop fusion | flops 4587520 | bytes 5505536 | tf_op jit(solution)/shard_map/convert_element_type | solution.py:323
  145.9 3.1 %multiply_convert_fusion.7 = (bf16[32,7168]{1,0:T(8,128)(2,1)}, bf16[32,7168]{1,0:T(8,128)(2,1)}, bf16[32,7168]{1,0:T(8,128)(2,1)}, bf16[32,7168]{1,0:T(8,128)(2,1)S(1)}) fusion(bf16[128,7168]{1,0:T(8,128)(2,1)} %collective-permute-done.29, bf16[128,7168]{1,0:T(8,128)(2,1)S(1)} %get-tuple-element.105, f32[32]{0:T(128)S(1)} %get-tuple-element.198, ...), kind=kLoop, calls=%fused_computation.20 | loop fusion | flops 4587520 | bytes 5505536 | tf_op jit(solution)/shard_map/convert_element_type | solution.py:323
  149.0 2.1 multiply_convert_fusion.1
  151.2 2.4 %collective-permute-done.17 = bf16[32,7168]{1,0:T(8,128)(2,1)} collective-permute-done((bf16[32,7168]{1,0:T(8,128)(2,1)S(1)}, bf16[32,7168]{1,0:T(8,128)(2,1)}, u32[]{:S(2)}, u32[]{:S(2)}) %collective-permute-start.17) | collective-permute-done | bytes 458784 | tf_op jit(solution)/shard_map/ppermute | solution.py:352
  154.1 1.5 add_convert_fusion.5
  155.6 1.5 collective-permute-start.42
  157.7 1.3 add_convert_fusion.11
  158.9 1.5 collective-permute-start.35
  161.0 4.1 %attend.2 = bf16[16,64,512]{2,1,0:T(8,128)(2,1)S(1)} custom-call(s32[32]{0:T(128)S(1)} %select_reduce_fusion.3.order_ref, s32[17]{0:T(128)S(1)} %get-tuple-element.208.start_ref, s32[32]{0:T(128)S(1)} %get-tuple-element.209.length_ref, bf16[32,64,576]{2,1,0:T(8,128)(2,1)S(1)} %copy-done, bf16[32,1,576]{2,1,0:T(2,128)(2,1)S(1)} %copy.34.own_ref, ...), custom_call_target="tpu_custom_call" | custom-call | flops 150994944 | bytes 4587520 | tf_op jit(solution)/shard_map/attend/pallas_call | solution.py:182
  165.1 4.0 %collective-permute-done.42 = bf16[32,7168]{1,0:T(8,128)(2,1)S(1)} collective-permute-done((bf16[32,7168]{1,0:T(8,128)(2,1)S(1)}, bf16[32,7168]{1,0:T(8,128)(2,1)S(1)}, u32[]{:S(2)}, u32[]{:S(2)}) %collective-permute-start.42) | collective-permute-done | bytes 458784 | tf_op jit(solution)/shard_map/ppermute | solution.py:352
  169.1 1.7 collective-permute-done.43
  171.1 1.3 collective-permute-start.44
  172.3 0.8 collective-permute-start.45
  173.1 5.8 %collective-permute-done.35 = bf16[32,7168]{1,0:T(8,128)(2,1)S(1)} collective-permute-done((bf16[32,7168]{1,0:T(8,128)(2,1)}, bf16[32,7168]{1,0:T(8,128)(2,1)S(1)}, u32[]{:S(2)}, u32[]{:S(2)}) %collective-permute-start.35) | collective-permute-done | bytes 458784 | tf_op jit(solution)/shard_map/ppermute | solution.py:352
  178.9 1.7 collective-permute-done.36
  180.9 1.3 collective-permute-start.38
  182.1 0.8 collective-permute-start.39
  182.9 5.8 %collective-permute-done.44 = bf16[32,7168]{1,0:T(8,128)(2,1)S(1)} collective-permute-done((bf16[32,7168]{1,0:T(8,128)(2,1)S(1)}, bf16[32,7168]{1,0:T(8,128)(2,1)S(1)}, u32[]{:S(2)}, u32[]{:S(2)}) %collective-permute-start.44) | collective-permute-done | bytes 458784 | tf_op jit(solution)/shard_map/ppermute | solution.py:352
  188.8 1.7 collective-permute-done.45
  190.7 1.3 collective-permute-start.46
  192.0 0.8 collective-permute-start.47
  192.8 5.8 %collective-permute-done.38 = bf16[32,7168]{1,0:T(8,128)(2,1)S(1)} collective-permute-done((bf16[32,7168]{1,0:T(8,128)(2,1)S(1)}, bf16[32,7168]{1,0:T(8,128)(2,1)S(1)}, u32[]{:S(2)}, u32[]{:S(2)}) %collective-permute-start.38) | collective-permute-done | bytes 458784 | tf_op jit(solution)/shard_map/ppermute | solution.py:352
  198.6 1.7 collective-permute-done.39
  200.5 1.3 collective-permute-start.40
  201.8 0.8 collective-permute-start.41
  202.6 4.9 %attend.3 = bf16[16,64,512]{2,1,0:T(8,128)(2,1)S(1)} custom-call(s32[32]{0:T(128)S(1)} %select_reduce_fusion.3.order_ref, s32[17]{0:T(128)S(1)} %get-tuple-element.207.start_ref, s32[32]{0:T(128)S(1)} %get-tuple-element.209.length_ref, bf16[32,64,576]{2,1,0:T(8,128)(2,1)S(1)} %copy-done, bf16[32,1,576]{2,1,0:T(2,128)(2,1)S(1)} %copy.34.own_ref, ...), custom_call_target="tpu_custom_call" | custom-call | flops 150994944 | bytes 4587520 | tf_op jit(solution)/shard_map/attend/pallas_call | solution.py:182
  207.6 1.5 pad_maximum_fusion
  209.1 1.0 collective-permute-done.47
  210.1 6.3 %collective-permute-done.40 = bf16[32,7168]{1,0:T(8,128)(2,1)S(1)} collective-permute-done((bf16[32,7168]{1,0:T(8,128)(2,1)S(1)}, bf16[32,7168]{1,0:T(8,128)(2,1)S(1)}, u32[]{:S(2)}, u32[]{:S(2)}) %collective-permute-start.40) | collective-permute-done | bytes 458784 | tf_op jit(solution)/shard_map/ppermute | solution.py:352
  216.4 1.4 collective-permute-done.41
  217.8 0.9 add_convert_fusion
  218.7 0.9 add_convert_fusion.6
  (138 shorter events, 13.8 us)
Async XLA Ops:
  0.6 37.1 %copy-start.26 = (bf16[32,576]{1,0:T(8,128)(2,1)S(1)}, bf16[32,576]{1,0:T(8,128)(2,1)}, u32[]{:S(2)}) copy-start(bf16[32,576]{1,0:T(8,128)(2,1)} %param.24) | copy-start | bytes 110596
  0.6 17.1 %collective-permute-start.8 = (bf16[32,7168]{1,0:T(8,128)(2,1)}, bf16[32,7168]{1,0:T(8,128)(2,1)S(1)}, u32[]{:S(2)}, u32[]{:S(2)}) collective-permute-start(bf16[32,7168]{1,0:T(8,128)(2,1)} %refs_5_.1), channel_id=1, source_target_pairs={{4,0},{5,1},{8,4},{9,5},{12,8},{13,9},{14,12},{15,13},{10,14},{11,... | collective-permute-start | bytes 1376264 | tf_op jit(solution)/shard_map/ppermute | solution.py:280
  2.3 17.7 %collective-permute-start = (bf16[32,7168]{1,0:T(8,128)(2,1)}, bf16[32,7168]{1,0:T(8,128)(2,1)}, u32[]{:S(2)}, u32[]{:S(2)}) collective-permute-start(bf16[32,7168]{1,0:T(8,128)(2,1)} %refs_4_.1), channel_id=1, source_target_pairs={{0,4},{1,5},{4,8},{5,9},{8,12},{9,13},{12,14},{13,15},{14,10},{15,... | collective-permute-start | bytes 1376264 | tf_op jit(solution)/shard_map/ppermute | solution.py:279
  6.0 11.7 %all-to-all-start = ((s32[16,1,66]{2,1,0:T(1,128)}), s32[16,1,66]{2,1,0:T(1,128)S(1)}, u32[]{:S(2)}, u32[]{:S(2)}) async-start(s32[16,1,66]{2,1,0:T(1,128)} %bitcast.2), calls=%async_computation | async-start | bytes 16384 | tf_op jit(solution)/shard_map/all_to_all | solution.py:274
  12.2 13.7 %collective-permute-start.7 = (bf16[32,7168]{1,0:T(8,128)(2,1)}, bf16[32,7168]{1,0:T(8,128)(2,1)}, u32[]{:S(2)}, u32[]{:S(2)}) collective-permute-start(bf16[32,7168]{1,0:T(8,128)(2,1)} %refs_4_.1), channel_id=1, source_target_pairs={{4,0},{5,1},{8,4},{9,5},{12,8},{13,9},{14,12},{15,13},{10,14},{11,... | collective-permute-start | bytes 1376264 | tf_op jit(solution)/shard_map/ppermute | solution.py:280
  13.6 13.7 %collective-permute-start.1 = (bf16[32,7168]{1,0:T(8,128)(2,1)}, bf16[32,7168]{1,0:T(8,128)(2,1)}, u32[]{:S(2)}, u32[]{:S(2)}) collective-permute-start(bf16[32,7168]{1,0:T(8,128)(2,1)} %refs_5_.1), channel_id=1, source_target_pairs={{0,4},{1,5},{4,8},{5,9},{8,12},{9,13},{12,14},{13,15},{14,10},{15,... | collective-permute-start | bytes 1376264 | tf_op jit(solution)/shard_map/ppermute | solution.py:279
  18.5 17.0 %collective-permute-start.10 = (bf16[32,7168]{1,0:T(8,128)(2,1)}, bf16[32,7168]{1,0:T(8,128)(2,1)S(1)}, u32[]{:S(2)}, u32[]{:S(2)}) collective-permute-start(bf16[32,7168]{1,0:T(8,128)(2,1)} %copy-done.15), channel_id=1, source_target_pairs={{4,0},{5,1},{8,4},{9,5},{12,8},{13,9},{14,12},{15,13},{10,14},{11,... | collective-permute-start | bytes 1376264 | tf_op jit(solution)/shard_map/ppermute | solution.py:292
  20.0 17.1 %collective-permute-start.2 = (bf16[32,7168]{1,0:T(8,128)(2,1)}, bf16[32,7168]{1,0:T(8,128)(2,1)S(1)}, u32[]{:S(2)}, u32[]{:S(2)}) collective-permute-start(bf16[32,7168]{1,0:T(8,128)(2,1)} %collective-permute-done.refs_0_), channel_id=1, source_target_pairs={{0,4},{1,5},{4,8},{5,9},{8,12},{9,13},{12,14},{13,15},{14,10},{15,... | collective-permute-start | bytes 1376264 | tf_op jit(solution)/shard_map/ppermute | solution.py:291
  20.5 74.1 %collective-permute-start.22 = (bf16[32,7168]{1,0:T(8,128)(2,1)}, bf16[32,7168]{1,0:T(8,128)(2,1)}, u32[]{:S(2)}, u32[]{:S(2)}) collective-permute-start(bf16[32,7168]{1,0:T(8,128)(2,1)} %refs_4_.1), channel_id=1, source_target_pairs={{0,1},{1,0},{2,3},{3,2},{4,5},{5,4},{6,7},{7,6},{8,9},{9,8},{10,11... | collective-permute-start | bytes 1376264 | tf_op jit(solution)/shard_map/ppermute | solution.py:295
  25.8 19.6 %collective-permute-start.9 = (bf16[32,7168]{1,0:T(8,128)(2,1)}, bf16[32,7168]{1,0:T(8,128)(2,1)S(1)}, u32[]{:S(2)}, u32[]{:S(2)}) collective-permute-start(bf16[32,7168]{1,0:T(8,128)(2,1)} %collective-permute-done.7.refs_2_), channel_id=1, source_target_pairs={{4,0},{5,1},{8,4},{9,5},{12,8},{13,9},{14,12},{15,13},{10,14},{11,... | collective-permute-start | bytes 1376264 | tf_op jit(solution)/shard_map/ppermute | solution.py:292
  27.3 19.6 %collective-permute-start.3 = (bf16[32,7168]{1,0:T(8,128)(2,1)}, bf16[32,7168]{1,0:T(8,128)(2,1)S(1)}, u32[]{:S(2)}, u32[]{:S(2)}) collective-permute-start(bf16[32,7168]{1,0:T(8,128)(2,1)} %collective-permute-done.1.refs_1_), channel_id=1, source_target_pairs={{0,4},{1,5},{4,8},{5,9},{8,12},{9,13},{12,14},{13,15},{14,10},{15,... | collective-permute-start | bytes 1376264 | tf_op jit(solution)/shard_map/ppermute | solution.py:291
  35.6 19.7 %collective-permute-start.12 = (bf16[32,7168]{1,0:T(8,128)(2,1)S(1)}, bf16[32,7168]{1,0:T(8,128)(2,1)S(1)}, u32[]{:S(2)}, u32[]{:S(2)}) collective-permute-start(bf16[32,7168]{1,0:T(8,128)(2,1)S(1)} %collective-permute-done.10.refs_3_), channel_id=1, source_target_pairs={{4,0},{5,1},{8,4},{9,5},{12,8},{13,9},{14,12},{15,13},{10,14},{11,... | collective-permute-start | bytes 1376264 | tf_op jit(solution)/shard_map/ppermute | solution.py:292
  37.1 39.8 %copy-start.3 = (bf16[32,7168]{1,0:T(8,128)(2,1)}, bf16[32,7168]{1,0:T(8,128)(2,1)S(1)}, u32[]{:S(2)}) copy-start(bf16[32,7168]{1,0:T(8,128)(2,1)S(1)} %collective-permute-done.2.refs_0_) | copy-start | bytes 1376260
  37.1 19.8 %collective-permute-start.4 = (bf16[32,7168]{1,0:T(8,128)(2,1)S(1)}, bf16[32,7168]{1,0:T(8,128)(2,1)}, u32[]{:S(2)}, u32[]{:S(2)}) collective-permute-start(bf16[32,7168]{1,0:T(8,128)(2,1)S(1)} %collective-permute-done.2.refs_0_), channel_id=1, source_target_pairs={{0,4},{1,5},{4,8},{5,9},{8,12},{9,13},{12,14},{13,15},{14,10},{15,... | collective-permute-start | bytes 1376264 | tf_op jit(solution)/shard_map/ppermute | solution.py:291
  45.4 31.5 %copy-start.5 = (bf16[32,7168]{1,0:T(8,128)(2,1)}, bf16[32,7168]{1,0:T(8,128)(2,1)S(1)}, u32[]{:S(2)}) copy-start(bf16[32,7168]{1,0:T(8,128)(2,1)S(1)} %collective-permute-done.9.refs_2_) | copy-start | bytes 1376260
  45.4 19.7 %collective-permute-start.11 = (bf16[32,7168]{1,0:T(8,128)(2,1)S(1)}, bf16[32,7168]{1,0:T(8,128)(2,1)S(1)}, u32[]{:S(2)}, u32[]{:S(2)}) collective-permute-start(bf16[32,7168]{1,0:T(8,128)(2,1)S(1)} %collective-permute-done.9.refs_2_), channel_id=1, source_target_pairs={{4,0},{5,1},{8,4},{9,5},{12,8},{13,9},{14,12},{15,13},{10,14},{11,... | collective-permute-start | bytes 1376264 | tf_op jit(solution)/shard_map/ppermute | solution.py:292
  46.9 30.0 %copy-start.7 = (bf16[32,7168]{1,0:T(8,128)(2,1)}, bf16[32,7168]{1,0:T(8,128)(2,1)S(1)}, u32[]{:S(2)}) copy-start(bf16[32,7168]{1,0:T(8,128)(2,1)S(1)} %collective-permute-done.3.refs_1_) | copy-start | bytes 1376260
  46.9 19.8 %collective-permute-start.5 = (bf16[32,7168]{1,0:T(8,128)(2,1)S(1)}, bf16[32,7168]{1,0:T(8,128)(2,1)}, u32[]{:S(2)}, u32[]{:S(2)}) collective-permute-start(bf16[32,7168]{1,0:T(8,128)(2,1)S(1)} %collective-permute-done.3.refs_1_), channel_id=1, source_target_pairs={{0,4},{1,5},{4,8},{5,9},{8,12},{9,13},{12,14},{13,15},{14,10},{15,... | collective-permute-start | bytes 1376264 | tf_op jit(solution)/shard_map/ppermute | solution.py:291
  55.2 21.7 %copy-start.9 = (bf16[32,7168]{1,0:T(8,128)(2,1)}, bf16[32,7168]{1,0:T(8,128)(2,1)S(1)}, u32[]{:S(2)}) copy-start(bf16[32,7168]{1,0:T(8,128)(2,1)S(1)} %collective-permute-done.12.refs_3_) | copy-start | bytes 1376260
  55.2 19.0 %collective-permute-start.13 = (bf16[32,7168]{1,0:T(8,128)(2,1)S(1)}, bf16[32,7168]{1,0:T(8,128)(2,1)}, u32[]{:S(2)}, u32[]{:S(2)}) collective-permute-start(bf16[32,7168]{1,0:T(8,128)(2,1)S(1)} %collective-permute-done.12.refs_3_), channel_id=1, source_target_pairs={{4,0},{5,1},{8,4},{9,5},{12,8},{13,9},{14,12},{15,13},{10,14},{11,... | collective-permute-start | bytes 1376264 | tf_op jit(solution)/shard_map/ppermute | solution.py:299
  56.8 18.6 %collective-permute-start.6 = (bf16[32,7168]{1,0:T(8,128)(2,1)}, bf16[32,7168]{1,0:T(8,128)(2,1)}, u32[]{:S(2)}, u32[]{:S(2)}) collective-permute-start(bf16[32,7168]{1,0:T(8,128)(2,1)} %collective-permute-done.4.refs_0_), channel_id=1, source_target_pairs={{0,4},{1,5},{4,8},{5,9},{8,12},{9,13},{12,14},{13,15},{14,10},{15,... | collective-permute-start | bytes 1376264 | tf_op jit(solution)/shard_map/ppermute | solution.py:298
  75.4 6.6 %collective-permute-start.14 = (bf16[32,7168]{1,0:T(8,128)(2,1)}, bf16[32,7168]{1,0:T(8,128)(2,1)}, u32[]{:S(2)}, u32[]{:S(2)}) collective-permute-start(bf16[32,7168]{1,0:T(8,128)(2,1)} %collective-permute-done.6.refs_0_), channel_id=1, source_target_pairs={{0,1},{1,0},{2,3},{3,2},{4,5},{5,4},{6,7},{7,6},{8,9},{9,8},{10,11... | collective-permute-start | bytes 1376264 | tf_op jit(solution)/shard_map/ppermute | solution.py:295
  75.4 6.9 %collective-permute-start.15 = (bf16[32,7168]{1,0:T(8,128)(2,1)}, bf16[32,7168]{1,0:T(8,128)(2,1)}, u32[]{:S(2)}, u32[]{:S(2)}) collective-permute-start(bf16[32,7168]{1,0:T(8,128)(2,1)} %collective-permute-done.13.refs_1_), channel_id=1, source_target_pairs={{0,1},{1,0},{2,3},{3,2},{4,5},{5,4},{6,7},{7,6},{8,9},{9,8},{10,11... | collective-permute-start | bytes 1376264 | tf_op jit(solution)/shard_map/ppermute | solution.py:295
  76.4 18.5 %collective-permute-start.30 = (bf16[32,7168]{1,0:T(8,128)(2,1)}, bf16[32,7168]{1,0:T(8,128)(2,1)}, u32[]{:S(2)}, u32[]{:S(2)}) collective-permute-start(bf16[32,7168]{1,0:T(8,128)(2,1)} %collective-permute-done.4.refs_0_), channel_id=1, source_target_pairs={{0,1},{1,0},{2,3},{3,2},{4,5},{5,4},{6,7},{7,6},{8,9},{9,8},{10,11... | collective-permute-start | bytes 1376264 | tf_op jit(solution)/shard_map/ppermute | solution.py:295
  76.4 18.8 %collective-permute-start.31 = (bf16[32,7168]{1,0:T(8,128)(2,1)}, bf16[32,7168]{1,0:T(8,128)(2,1)}, u32[]{:S(2)}, u32[]{:S(2)}) collective-permute-start(bf16[32,7168]{1,0:T(8,128)(2,1)} %collective-permute-done.5.refs_1_), channel_id=1, source_target_pairs={{0,1},{1,0},{2,3},{3,2},{4,5},{5,4},{6,7},{7,6},{8,9},{9,8},{10,11... | collective-permute-start | bytes 1376264 | tf_op jit(solution)/shard_map/ppermute | solution.py:295
  76.9 76.7 %all-to-all-start.1 = ((bf16[32,64,576]{2,1,0:T(8,128)(2,1)}), bf16[32,64,576]{2,1,0:T(8,128)(2,1)S(1)}, u32[]{:S(2)}, u32[]{:S(2)}) async-start(bf16[32,64,576]{2,1,0:T(8,128)(2,1)} %copy-done.1), calls=%async_computation.1 | async-start | bytes 5242880 | tf_op jit(solution)/shard_map/all_to_all | solution.py:303
  82.0 13.3 %collective-permute-start.32 = (bf16[32,7168]{1,0:T(8,128)(2,1)}, bf16[32,7168]{1,0:T(8,128)(2,1)S(1)}, u32[]{:S(2)}, u32[]{:S(2)}) collective-permute-start(bf16[32,7168]{1,0:T(8,128)(2,1)} %copy-done.11), channel_id=1, source_target_pairs={{0,1},{1,0},{2,3},{3,2},{4,5},{5,4},{6,7},{7,6},{8,9},{9,8},{10,11... | collective-permute-start | bytes 1376264 | tf_op jit(solution)/shard_map/ppermute | solution.py:295
  82.2 13.5 %collective-permute-start.33 = (bf16[32,7168]{1,0:T(8,128)(2,1)}, bf16[32,7168]{1,0:T(8,128)(2,1)S(1)}, u32[]{:S(2)}, u32[]{:S(2)}) collective-permute-start(bf16[32,7168]{1,0:T(8,128)(2,1)} %copy-done.9), channel_id=1, source_target_pairs={{0,1},{1,0},{2,3},{3,2},{4,5},{5,4},{6,7},{7,6},{8,9},{9,8},{10,11... | collective-permute-start | bytes 1376264 | tf_op jit(solution)/shard_map/ppermute | solution.py:295
  82.7 13.2 %copy-start.10 = (bf16[32,7168]{1,0:T(8,128)(2,1)S(1)}, bf16[32,7168]{1,0:T(8,128)(2,1)}, u32[]{:S(2)}) copy-start(bf16[32,7168]{1,0:T(8,128)(2,1)} %copy-done.9) | copy-start | bytes 1376260
  82.7 13.2 %copy-start.12 = (bf16[32,7168]{1,0:T(8,128)(2,1)S(1)}, bf16[32,7168]{1,0:T(8,128)(2,1)}, u32[]{:S(2)}) copy-start(bf16[32,7168]{1,0:T(8,128)(2,1)} %copy-done.11) | copy-start | bytes 1376260
  94.6 14.9 %copy-start.16 = (bf16[32,7168]{1,0:T(8,128)(2,1)S(1)}, bf16[32,7168]{1,0:T(8,128)(2,1)}, u32[]{:S(2)}) copy-start(bf16[32,7168]{1,0:T(8,128)(2,1)} %copy-done.15) | copy-start | bytes 1376260
  94.6 13.9 %collective-permute-start.23 = (bf16[32,7168]{1,0:T(8,128)(2,1)S(1)}, bf16[32,7168]{1,0:T(8,128)(2,1)S(1)}, u32[]{:S(2)}, u32[]{:S(2)}) collective-permute-start(bf16[32,7168]{1,0:T(8,128)(2,1)S(1)} %copy-done.14), channel_id=1, source_target_pairs={{0,1},{1,0},{2,3},{3,2},{4,5},{5,4},{6,7},{7,6},{8,9},{9,8},{10,11... | collective-permute-start | bytes 1376264 | tf_op jit(solution)/shard_map/ppermute | solution.py:295
  94.8 14.1 %collective-permute-start.25 = (bf16[32,7168]{1,0:T(8,128)(2,1)S(1)}, bf16[32,7168]{1,0:T(8,128)(2,1)S(1)}, u32[]{:S(2)}, u32[]{:S(2)}) collective-permute-start(bf16[32,7168]{1,0:T(8,128)(2,1)S(1)} %copy-done.4), channel_id=1, source_target_pairs={{0,1},{1,0},{2,3},{3,2},{4,5},{5,4},{6,7},{7,6},{8,9},{9,8},{10,11... | collective-permute-start | bytes 1376264 | tf_op jit(solution)/shard_map/ppermute | solution.py:295
  95.2 13.9 %collective-permute-start.26 = (bf16[32,7168]{1,0:T(8,128)(2,1)S(1)}, bf16[32,7168]{1,0:T(8,128)(2,1)S(1)}, u32[]{:S(2)}, u32[]{:S(2)}) collective-permute-start(bf16[32,7168]{1,0:T(8,128)(2,1)S(1)} %copy-done.8), channel_id=1, source_target_pairs={{0,1},{1,0},{2,3},{3,2},{4,5},{5,4},{6,7},{7,6},{8,9},{9,8},{10,11... | collective-permute-start | bytes 1376264 | tf_op jit(solution)/shard_map/ppermute | solution.py:295
  95.4 14.1 %collective-permute-start.27 = (bf16[32,7168]{1,0:T(8,128)(2,1)S(1)}, bf16[32,7168]{1,0:T(8,128)(2,1)S(1)}, u32[]{:S(2)}, u32[]{:S(2)}) collective-permute-start(bf16[32,7168]{1,0:T(8,128)(2,1)S(1)} %copy-done.6), channel_id=1, source_target_pairs={{0,1},{1,0},{2,3},{3,2},{4,5},{5,4},{6,7},{7,6},{8,9},{9,8},{10,11... | collective-permute-start | bytes 1376264 | tf_op jit(solution)/shard_map/ppermute | solution.py:295
  95.7 13.9 %collective-permute-start.28 = (bf16[32,7168]{1,0:T(8,128)(2,1)S(1)}, bf16[32,7168]{1,0:T(8,128)(2,1)S(1)}, u32[]{:S(2)}, u32[]{:S(2)}) collective-permute-start(bf16[32,7168]{1,0:T(8,128)(2,1)S(1)} %collective-permute-done.10.refs_3_), channel_id=1, source_target_pairs={{0,1},{1,0},{2,3},{3,2},{4,5},{5,4},{6,7},{7,6},{8,9},{9,8},{10,11... | collective-permute-start | bytes 1376264 | tf_op jit(solution)/shard_map/ppermute | solution.py:295
  108.6 13.8 %collective-permute-start.18 = (bf16[32,7168]{1,0:T(8,128)(2,1)}, bf16[32,7168]{1,0:T(8,128)(2,1)S(1)}, u32[]{:S(2)}, u32[]{:S(2)}) collective-permute-start(bf16[32,7168]{1,0:T(8,128)(2,1)} %collective-permute-done.refs_0_), channel_id=1, source_target_pairs={{0,1},{1,0},{2,3},{3,2},{4,5},{5,4},{6,7},{7,6},{8,9},{9,8},{10,11... | collective-permute-start | bytes 1376264 | tf_op jit(solution)/shard_map/ppermute | solution.py:295
  109.0 13.6 %collective-permute-start.19 = (bf16[32,7168]{1,0:T(8,128)(2,1)}, bf16[32,7168]{1,0:T(8,128)(2,1)S(1)}, u32[]{:S(2)}, u32[]{:S(2)}) collective-permute-start(bf16[32,7168]{1,0:T(8,128)(2,1)} %collective-permute-done.1.refs_1_), channel_id=1, source_target_pairs={{0,1},{1,0},{2,3},{3,2},{4,5},{5,4},{6,7},{7,6},{8,9},{9,8},{10,11... | collective-permute-start | bytes 1376264 | tf_op jit(solution)/shard_map/ppermute | solution.py:295
  109.1 13.8 %collective-permute-start.20 = (bf16[32,7168]{1,0:T(8,128)(2,1)}, bf16[32,7168]{1,0:T(8,128)(2,1)S(1)}, u32[]{:S(2)}, u32[]{:S(2)}) collective-permute-start(bf16[32,7168]{1,0:T(8,128)(2,1)} %collective-permute-done.7.refs_2_), channel_id=1, source_target_pairs={{0,1},{1,0},{2,3},{3,2},{4,5},{5,4},{6,7},{7,6},{8,9},{9,8},{10,11... | collective-permute-start | bytes 1376264 | tf_op jit(solution)/shard_map/ppermute | solution.py:295
  109.5 13.4 %collective-permute-start.21 = (bf16[32,7168]{1,0:T(8,128)(2,1)S(1)}, bf16[32,7168]{1,0:T(8,128)(2,1)S(1)}, u32[]{:S(2)}, u32[]{:S(2)}) collective-permute-start(bf16[32,7168]{1,0:T(8,128)(2,1)S(1)} %copy-done.16), channel_id=1, source_target_pairs={{0,1},{1,0},{2,3},{3,2},{4,5},{5,4},{6,7},{7,6},{8,9},{9,8},{10,11... | collective-permute-start | bytes 1376264 | tf_op jit(solution)/shard_map/ppermute | solution.py:295
  109.7 13.3 %copy-start.13 = (bf16[32,7168]{1,0:T(8,128)(2,1)S(1)}, bf16[32,7168]{1,0:T(8,128)(2,1)}, u32[]{:S(2)}) copy-start(bf16[32,7168]{1,0:T(8,128)(2,1)} %refs_4_.1) | copy-start | bytes 1376260
  109.7 28.8 %collective-permute-start.16 = (bf16[64,7168]{1,0:T(8,128)(2,1)}, bf16[64,7168]{1,0:T(8,128)(2,1)}, u32[]{:S(2)}, u32[]{:S(2)}) collective-permute-start(bf16[64,7168]{1,0:T(8,128)(2,1)} %get-tuple-element.94), channel_id=1, source_target_pairs={{0,1},{1,0},{2,3},{3,2},{4,5},{5,4},{6,7},{7,6},{8,9},{9,8},{10,11... | collective-permute-start | bytes 2752520 | tf_op jit(solution)/shard_map/ppermute | solution.py:307
  122.3 20.4 %collective-permute-start.34 = (bf16[128,7168]{1,0:T(8,128)(2,1)S(1)}, bf16[128,7168]{1,0:T(8,128)(2,1)}, u32[]{:S(2)}, u32[]{:S(2)}) collective-permute-start(bf16[128,7168]{1,0:T(8,128)(2,1)S(1)} %get-tuple-element.112), channel_id=1, source_target_pairs={{0,1},{1,0},{2,3},{3,2},{4,5},{5,4},{6,7},{7,6},{8,9},{9,8},{10,11... | collective-permute-start | bytes 5505032 | tf_op jit(solution)/shard_map/ppermute | solution.py:307
  122.6 23.4 %collective-permute-start.29 = (bf16[128,7168]{1,0:T(8,128)(2,1)S(1)}, bf16[128,7168]{1,0:T(8,128)(2,1)}, u32[]{:S(2)}, u32[]{:S(2)}) collective-permute-start(bf16[128,7168]{1,0:T(8,128)(2,1)S(1)} %get-tuple-element.106), channel_id=1, source_target_pairs={{0,1},{1,0},{2,3},{3,2},{4,5},{5,4},{6,7},{7,6},{8,9},{9,8},{10,11... | collective-permute-start | bytes 5505032 | tf_op jit(solution)/shard_map/ppermute | solution.py:307
  138.2 10.8 %collective-permute-start.24 = (bf16[192,7168]{1,0:T(8,128)(2,1)}, bf16[192,7168]{1,0:T(8,128)(2,1)S(1)}, u32[]{:S(2)}, u32[]{:S(2)}) collective-permute-start(bf16[192,7168]{1,0:T(8,128)(2,1)} %get-tuple-element.100), channel_id=1, source_target_pairs={{0,1},{1,0},{2,3},{3,2},{4,5},{5,4},{6,7},{7,6},{8,9},{9,8},{10,11... | collective-permute-start | bytes 8257544 | tf_op jit(solution)/shard_map/ppermute | solution.py:307
  140.7 12.9 %collective-permute-start.17 = (bf16[32,7168]{1,0:T(8,128)(2,1)S(1)}, bf16[32,7168]{1,0:T(8,128)(2,1)}, u32[]{:S(2)}, u32[]{:S(2)}) collective-permute-start(bf16[32,7168]{1,0:T(8,128)(2,1)S(1)} %get-tuple-element.187), channel_id=1, source_target_pairs={{0,4},{1,5},{4,8},{5,9},{8,12},{9,13},{12,14},{13,15},{14,10},{15,... | collective-permute-start | bytes 1376264 | tf_op jit(solution)/shard_map/ppermute | solution.py:352
  141.3 12.8 %collective-permute-start.37 = (bf16[32,7168]{1,0:T(8,128)(2,1)}, bf16[32,7168]{1,0:T(8,128)(2,1)}, u32[]{:S(2)}, u32[]{:S(2)}) collective-permute-start(bf16[32,7168]{1,0:T(8,128)(2,1)} %get-tuple-element.188), channel_id=1, source_target_pairs={{4,0},{5,1},{8,4},{9,5},{12,8},{13,9},{14,12},{15,13},{10,14},{11,... | collective-permute-start | bytes 1376264 | tf_op jit(solution)/shard_map/ppermute | solution.py:352
  155.6 13.5 %collective-permute-start.42 = (bf16[32,7168]{1,0:T(8,128)(2,1)S(1)}, bf16[32,7168]{1,0:T(8,128)(2,1)S(1)}, u32[]{:S(2)}, u32[]{:S(2)}) collective-permute-start(bf16[32,7168]{1,0:T(8,128)(2,1)S(1)} %add_convert_fusion.5), channel_id=1, source_target_pairs={{4,0},{5,1},{8,4},{9,5},{12,8},{13,9},{14,12},{15,13},{10,14},{11,... | collective-permute-start | bytes 1376264 | tf_op jit(solution)/shard_map/ppermute | solution.py:352
  157.1 13.7 %collective-permute-start.43 = (bf16[32,7168]{1,0:T(8,128)(2,1)}, bf16[32,7168]{1,0:T(8,128)(2,1)S(1)}, u32[]{:S(2)}, u32[]{:S(2)}) collective-permute-start(bf16[32,7168]{1,0:T(8,128)(2,1)} %get-tuple-element.151), channel_id=1, source_target_pairs={{0,4},{1,5},{4,8},{5,9},{8,12},{9,13},{12,14},{13,15},{14,10},{15,... | collective-permute-start | bytes 1376264 | tf_op jit(solution)/shard_map/ppermute | solution.py:352
  158.9 20.0 %collective-permute-start.35 = (bf16[32,7168]{1,0:T(8,128)(2,1)}, bf16[32,7168]{1,0:T(8,128)(2,1)S(1)}, u32[]{:S(2)}, u32[]{:S(2)}) collective-permute-start(bf16[32,7168]{1,0:T(8,128)(2,1)} %get-tuple-element.117), channel_id=1, source_target_pairs={{4,0},{5,1},{8,4},{9,5},{12,8},{13,9},{14,12},{15,13},{10,14},{11,... | collective-permute-start | bytes 1376264 | tf_op jit(solution)/shard_map/ppermute | solution.py:352
  160.5 20.2 %collective-permute-start.36 = (bf16[32,7168]{1,0:T(8,128)(2,1)S(1)}, bf16[32,7168]{1,0:T(8,128)(2,1)S(1)}, u32[]{:S(2)}, u32[]{:S(2)}) collective-permute-start(bf16[32,7168]{1,0:T(8,128)(2,1)S(1)} %add_convert_fusion.11), channel_id=1, source_target_pairs={{0,4},{1,5},{4,8},{5,9},{8,12},{9,13},{12,14},{13,15},{14,10},{15,... | collective-permute-start | bytes 1376264 | tf_op jit(solution)/shard_map/ppermute | solution.py:352
  165.1 15.5 %copy-start.17 = (bf16[32,7168]{1,0:T(8,128)(2,1)S(1)}, bf16[32,7168]{1,0:T(8,128)(2,1)}, u32[]{:S(2)}) copy-start(bf16[32,7168]{1,0:T(8,128)(2,1)} %get-tuple-element.135) | copy-start | bytes 1376260
  170.9 19.5 %copy-start.25 = (bf16[32,7168]{1,0:T(8,128)(2,1)S(1)}, bf16[32,7168]{1,0:T(8,128)(2,1)}, u32[]{:S(2)}) copy-start(bf16[32,7168]{1,0:T(8,128)(2,1)} %get-tuple-element.161) | copy-start | bytes 1376260
  171.0 19.5 %copy-start.24 = (bf16[32,7168]{1,0:T(8,128)(2,1)S(1)}, bf16[32,7168]{1,0:T(8,128)(2,1)}, u32[]{:S(2)}) copy-start(bf16[32,7168]{1,0:T(8,128)(2,1)} %get-tuple-element.159) | copy-start | bytes 1376260
  171.1 17.7 %collective-permute-start.44 = (bf16[32,7168]{1,0:T(8,128)(2,1)S(1)}, bf16[32,7168]{1,0:T(8,128)(2,1)S(1)}, u32[]{:S(2)}, u32[]{:S(2)}) collective-permute-start(bf16[32,7168]{1,0:T(8,128)(2,1)S(1)} %add_convert_fusion.4), channel_id=1, source_target_pairs={{4,0},{5,1},{8,4},{9,5},{12,8},{13,9},{14,12},{15,13},{10,14},{11,... | collective-permute-start | bytes 1376264 | tf_op jit(solution)/shard_map/ppermute | solution.py:352
  172.3 18.1 %collective-permute-start.45 = (bf16[32,7168]{1,0:T(8,128)(2,1)S(1)}, bf16[32,7168]{1,0:T(8,128)(2,1)S(1)}, u32[]{:S(2)}, u32[]{:S(2)}) collective-permute-start(bf16[32,7168]{1,0:T(8,128)(2,1)S(1)} %add_convert_fusion.3), channel_id=1, source_target_pairs={{0,4},{1,5},{4,8},{5,9},{8,12},{9,13},{12,14},{13,15},{14,10},{15,... | collective-permute-start | bytes 1376264 | tf_op jit(solution)/shard_map/ppermute | solution.py:352
  180.7 19.6 %copy-start.23 = (bf16[32,7168]{1,0:T(8,128)(2,1)S(1)}, bf16[32,7168]{1,0:T(8,128)(2,1)}, u32[]{:S(2)}) copy-start(bf16[32,7168]{1,0:T(8,128)(2,1)} %get-tuple-element.141) | copy-start | bytes 1376260
  180.9 19.5 %copy-start.22 = (bf16[32,7168]{1,0:T(8,128)(2,1)S(1)}, bf16[32,7168]{1,0:T(8,128)(2,1)}, u32[]{:S(2)}) copy-start(bf16[32,7168]{1,0:T(8,128)(2,1)} %get-tuple-element.139) | copy-start | bytes 1376260
  180.9 17.7 %collective-permute-start.38 = (bf16[32,7168]{1,0:T(8,128)(2,1)S(1)}, bf16[32,7168]{1,0:T(8,128)(2,1)S(1)}, u32[]{:S(2)}, u32[]{:S(2)}) collective-permute-start(bf16[32,7168]{1,0:T(8,128)(2,1)S(1)} %add_convert_fusion.10), channel_id=1, source_target_pairs={{4,0},{5,1},{8,4},{9,5},{12,8},{13,9},{14,12},{15,13},{10,14},{11,... | collective-permute-start | bytes 1376264 | tf_op jit(solution)/shard_map/ppermute | solution.py:352
  182.1 18.1 %collective-permute-start.39 = (bf16[32,7168]{1,0:T(8,128)(2,1)S(1)}, bf16[32,7168]{1,0:T(8,128)(2,1)S(1)}, u32[]{:S(2)}, u32[]{:S(2)}) collective-permute-start(bf16[32,7168]{1,0:T(8,128)(2,1)S(1)} %add_convert_fusion.9), channel_id=1, source_target_pairs={{0,4},{1,5},{4,8},{5,9},{8,12},{9,13},{12,14},{13,15},{14,10},{15,... | collective-permute-start | bytes 1376264 | tf_op jit(solution)/shard_map/ppermute | solution.py:352
  190.7 18.4 %collective-permute-start.46 = (bf16[32,7168]{1,0:T(8,128)(2,1)S(1)}, bf16[32,7168]{1,0:T(8,128)(2,1)S(1)}, u32[]{:S(2)}, u32[]{:S(2)}) collective-permute-start(bf16[32,7168]{1,0:T(8,128)(2,1)S(1)} %add_convert_fusion.2), channel_id=1, source_target_pairs={{4,0},{5,1},{8,4},{9,5},{12,8},{13,9},{14,12},{15,13},{10,14},{11,... | collective-permute-start | bytes 1376264 | tf_op jit(solution)/shard_map/ppermute | solution.py:352
  192.0 18.1 %collective-permute-start.47 = (bf16[32,7168]{1,0:T(8,128)(2,1)S(1)}, bf16[32,7168]{1,0:T(8,128)(2,1)S(1)}, u32[]{:S(2)}, u32[]{:S(2)}) collective-permute-start(bf16[32,7168]{1,0:T(8,128)(2,1)S(1)} %add_convert_fusion.1), channel_id=1, source_target_pairs={{0,4},{1,5},{4,8},{5,9},{8,12},{9,13},{12,14},{13,15},{14,10},{15,... | collective-permute-start | bytes 1376264 | tf_op jit(solution)/shard_map/ppermute | solution.py:352
  200.5 15.8 %collective-permute-start.40 = (bf16[32,7168]{1,0:T(8,128)(2,1)S(1)}, bf16[32,7168]{1,0:T(8,128)(2,1)S(1)}, u32[]{:S(2)}, u32[]{:S(2)}) collective-permute-start(bf16[32,7168]{1,0:T(8,128)(2,1)S(1)} %add_convert_fusion.8), channel_id=1, source_target_pairs={{4,0},{5,1},{8,4},{9,5},{12,8},{13,9},{14,12},{15,13},{10,14},{11,... | collective-permute-start | bytes 1376264 | tf_op jit(solution)/shard_map/ppermute | solution.py:352
  201.8 16.0 %collective-permute-start.41 = (bf16[32,7168]{1,0:T(8,128)(2,1)S(1)}, bf16[32,7168]{1,0:T(8,128)(2,1)S(1)}, u32[]{:S(2)}, u32[]{:S(2)}) collective-permute-start(bf16[32,7168]{1,0:T(8,128)(2,1)S(1)} %add_convert_fusion.7), channel_id=1, source_target_pairs={{0,4},{1,5},{4,8},{5,9},{8,12},{9,13},{12,14},{13,15},{14,10},{15,... | collective-permute-start | bytes 1376264 | tf_op jit(solution)/shard_map/ppermute | solution.py:352
  (13 other events, 113.1 us)
